TPU v7x, 32 devices: a whole 2x2x4 slice. The times are simulated.
32 devices in a mesh: parts: 2 (over y), wide: 4 (over x, core), tensor: 4 (over z).
Axes of the slice: x: 2, y: 2, z: 4, core: 2. Of those that a mesh axis runs over, the one named last changes fastest.
Arguments:
- tokens: bfloat16 [2048, 8192], P(('parts', 'wide'), 'tensor'), parts along dimension 0, may hold values from -300 to 300
- attention_norm_gain: bfloat16 [8192], P('tensor'), may hold values from 0.099609375 to 1.8984375
- key_value_weight: bfloat16 [8192, 2048], P('tensor'), may hold values from -0.0625 to 0.0625
- adapter_down_weight: bfloat16 [64, 8192, 128], P(('parts', 'wide'), 'tensor'), parts along dimension 0, may hold values from -0.0625 to 0.0625
- adapter_up_weight: bfloat16 [64, 64, 2048], P(('parts', 'wide'), None, 'tensor'), parts along dimension 0, may hold values from -0.75 to 0.75
- request_adapter: int32 [2048], P(('parts', 'wide')), parts along dimension 0, may hold values from 0 to 31, as said below
- adapter_storage_row: int32 [64], P('parts'), parts along dimension 0, may hold values from 0 to 31, as said below
- cached_token_length: int32 [2048], P(('parts', 'wide')), parts along dimension 0, may hold values from 1 to 8192
Outputs:
- kv_entries: bfloat16 [2048, 2048], P(('parts', 'wide'), 'tensor'), parts along dimension 0
There are 2 independent parts, one for each index of `parts`. A program takes and returns all parts, laid end to end along the dimension named above; an argument that names none is the same for every part. Nothing has to cross between parts.
Inputs may be any that keep to these rules, and one draw needn't show every extreme that they name: A permutation; adapter a lies in storage row adapter_storage_row[a], held by wide index adapter_storage_row[a] // 8. `request_adapter`: among the 256 requests of one wide index, at most 104 have adapters held by any one wide index; one wide index holds the adapters of exactly 104 requests of every wide index.
All inputs are finite; a program needn't handle non-finite values.
Results may differ from a plain program's by a relative error of at most 0.0057.
Values may be sent and summed in bfloat16 or wider, within the bound.
No kernel may reach another device: no remote copies, remote signals or barrier semaphores. Data moves between devices by JAX's collectives and lax.ppermute only.
A program may use at most 64 MiB of HBM per device.

v0:
```python
import functools
import math

import jax
import jax.numpy as jnp
from jax import lax
from jax.experimental import pallas as pl
from jax.experimental.pallas import tpu as pltpu
from jax.sharding import PartitionSpec as P

MODEL_WIDTH = 8192
HEAD = 128
EPSILON = 1e-05
ROPE_BASE = 500000.0
F32 = jnp.float32
BF16 = jnp.bfloat16


def iota(shape, axis):
    return lax.broadcasted_iota(jnp.int32, shape, axis)


def call(kernel, name, outs, vmem=(), hbm=(), after=(), scratch=(), flops=0, moved=0, limit=16, hbm_outs=0):
    def body(*refs):
        keep = len(vmem) + len(hbm)
        kernel(*refs[:keep], *refs[keep + len(after) :])

    return pl.pallas_call(
        body,
        out_shape=outs,
        in_specs=[pl.BlockSpec(memory_space=pltpu.VMEM)] * len(vmem)
        + [pl.BlockSpec(memory_space=pltpu.HBM)] * len(hbm)
        + [pl.BlockSpec(memory_space=pl.ANY)] * len(after),
        out_specs=[pl.BlockSpec(memory_space=pltpu.HBM)] * hbm_outs
        + [pl.BlockSpec(memory_space=pltpu.VMEM)] * (len(outs) - hbm_outs),
        scratch_shapes=scratch,
        compiler_params=pltpu.CompilerParams(vmem_limit_bytes=limit * 1024 * 1024),
        cost_estimate=pl.CostEstimate(flops=flops, bytes_accessed=moved, transcendentals=0),
        name=name,
    )(*vmem, *hbm, *after)


def shape(dims, dtype):
    return jax.ShapeDtypeStruct(dims, dtype)


def to_column(row, count):
    spread = iota((count, row.shape[1]), 0) == iota((count, row.shape[1]), 1)
    return jnp.sum(jnp.where(spread, row, 0.0), axis=1, keepdims=True)


def places(req, table, n_wide, per_dev):
    rows = req.shape[1]
    me = lax.axis_index("wide").astype(jnp.int32)
    stored = jnp.zeros_like(req)
    for a in range(table.shape[0]):
        stored = jnp.where(req == a, table[a], stored)
    owner = lax.div(stored, per_dev)
    slot = stored - owner * per_dev
    pad = -(-n_wide // 16) * 16
    hit = owner == (iota((pad, rows), 0) ^ me)
    earlier = (iota((rows, rows), 0) <= iota((rows, rows), 1)).astype(BF16)
    count = jnp.dot(hit.astype(BF16), earlier, preferred_element_type=F32)
    return jnp.where(hit, count.astype(jnp.int32) - 1, -1), slot


def dispatch_kernel(order, n_wide, per_dev, cap, req_hbm, table_hbm, tok_hbm, gain_hbm, *refs):
    xs = refs[: len(order)]
    wide_gain_ref, req_ref, table_ref, tok_ref, gain_ref, x_ref, sems, out_sems = refs[
        len(order) :
    ]
    rows, depth = tok_ref.shape
    height = x_ref.shape[1]
    loads = [
        pltpu.make_async_copy(req_hbm, req_ref, sems.at[0]),
        pltpu.make_async_copy(table_hbm, table_ref, sems.at[1]),
        pltpu.make_async_copy(tok_hbm, tok_ref, sems.at[2]),
        pltpu.make_async_copy(gain_hbm, gain_ref, sems.at[3]),
    ]
    for copy in loads:
        copy.start()
    loads[0].wait()
    loads[1].wait()
    place, slot = places(req_ref[...], table_ref, n_wide, per_dev)
    slots = jnp.broadcast_to(slot.astype(F32), (16, rows)).astype(BF16)
    picks, slot_rows = [], []
    for k in order:
        pick = (iota((HEAD, rows), 0) == place[k : k + 1]).astype(BF16)
        slot_rows.append(
            lax.dot_general(slots, pick, (((1,), (1,)), ((), ())), preferred_element_type=F32)
        )
        picks.append(pick[:height])
    loads[3].wait()
    wide_gain_ref[...] = gain_ref[...].astype(F32)
    loads[2].wait()
    stores = []
    for j, k in enumerate(order):
        y = jnp.dot(picks[j], tok_ref[...], preferred_element_type=F32)
        first = jnp.where(iota((height, HEAD), 0) == cap, slot_rows[j][:1], y[:, :HEAD])
        x_ref[j, :, :HEAD] = first.astype(BF16)
        x_ref[j, :, HEAD:] = y[:, HEAD:].astype(BF16)
        copy = pltpu.make_async_copy(x_ref.at[j], xs[j], out_sems.at[j])
        copy.start()
        stores.append(copy)
    for copy in stores:
        copy.wait()


def base_kernel(offsets, cols, gain_hbm, tok_hbm, weight_hbm, *refs):
    count = len(offsets)
    outs = refs[:count]
    gain_ref, tok_ref, buf, acc_ref, sems = refs[count:]
    steps, chunk, _ = buf.shape
    copies = [
        pltpu.make_async_copy(weight_hbm.at[pl.ds(i * chunk, chunk)], buf.at[i], sems.at[2 + i])
        for i in range(steps)
    ]
    loads = [
        pltpu.make_async_copy(gain_hbm, gain_ref, sems.at[0]),
        pltpu.make_async_copy(tok_hbm, tok_ref, sems.at[1]),
    ]
    for copy in loads + copies:
        copy.start()
    for copy in loads:
        copy.wait()
    spot = lax.axis_index("tensor").astype(jnp.int32)
    for i in range(steps):
        pieces = []
        for b in range(i * chunk // HEAD, (i + 1) * chunk // HEAD):
            piece = tok_ref[:, b * HEAD : (b + 1) * HEAD].astype(F32) * gain_ref[b : b + 1]
            pieces.append(piece.astype(BF16))
        x = jnp.concatenate(pieces, axis=1)
        copies[i].wait()
        for j, k in enumerate(offsets):
            start = pl.multiple_of((spot ^ k) * cols, HEAD)
            y = jnp.dot(x, buf[i, :, pl.ds(start, cols)], preferred_element_type=F32)
            if i > 0:
                y = y + acc_ref[j]
            if i < steps - 1:
                acc_ref[j] = y
            else:
                outs[j][...] = y.astype(outs[j].dtype)


def pair_kernel(count, *refs):
    for j in range(count):
        total = refs[j][...] + refs[count + j][...].astype(F32)
        refs[2 * count + j][...] = total.astype(BF16)


def scaled_down_kernel(gain_ref, down_hbm, out_ref, buf, sems):
    per_dev, depth, rank = down_hbm.shape
    copies = [pltpu.make_async_copy(down_hbm.at[a], buf.at[a], sems.at[a]) for a in range(per_dev)]
    for copy in copies:
        copy.start()
    columns = []
    for b in range(depth // HEAD):
        columns.append(to_column(gain_ref[b : b + 1], HEAD))
    for a in range(per_dev):
        copies[a].wait()
        for b in range(depth // HEAD):
            span = slice(b * HEAD, (b + 1) * HEAD)
            out_ref[span, a * rank : (a + 1) * rank] = (
                buf[a, span].astype(F32) * columns[b]
            ).astype(BF16)


def aux_kernel(n_wide, per_dev, req_hbm, table_hbm, tok_hbm, sq_ref, *refs):
    sels = refs[:n_wide]
    req_ref, table_ref, tok_ref, sems = refs[n_wide:]
    copies = [
        pltpu.make_async_copy(req_hbm, req_ref, sems.at[0]),
        pltpu.make_async_copy(table_hbm, table_ref, sems.at[1]),
        pltpu.make_async_copy(tok_hbm, tok_ref, sems.at[2]),
    ]
    for copy in copies:
        copy.start()
    for copy in copies:
        copy.wait()
    rows = tok_ref.shape[0]
    place, _ = places(req_ref[...], table_ref, n_wide, per_dev)
    place = place.astype(F32)
    for k in range(n_wide):
        column = to_column(place[k : k + 1], rows).astype(jnp.int32)
        sels[k][...] = (iota((rows, HEAD), 1) == column).astype(BF16)
    tok = tok_ref[...]
    gram = lax.dot_general(tok, tok, (((1,), (1,)), ((), ())), preferred_element_type=F32)
    diag = iota((rows, rows), 0) == iota((rows, rows), 1)
    sq = jnp.sum(jnp.where(diag, gram, 0.0), axis=0, keepdims=True)
    block = jnp.zeros((8, HEAD), F32)
    for p in range(3):
        part = sq.astype(BF16).astype(F32)
        sq = sq - part
        for i in range(rows // HEAD):
            term = part[:, i * HEAD : (i + 1) * HEAD]
            block = jnp.where(iota((8, HEAD), 0) == p * (rows // HEAD) + i, term, block)
    sq_ref[...] = block


def slot_column(x_ref, cap):
    height = x_ref.shape[0]
    base = cap // 16 * 16
    row = x_ref[base : base + 16, :HEAD].astype(F32)[cap - base : cap - base + 1]
    column = to_column(row, height)
    return jnp.where(iota((height, 1), 0) < cap, column, -1.0)


def down_kernel(count, cap, with_sq, *refs):
    xs, down_ref = refs[:count], refs[count]
    sq_ref = refs[count + 1] if with_sq else None
    out_ref = refs[-1]
    height, depth = xs[0].shape
    rank = HEAD
    x = jnp.concatenate([x[...] for x in xs], axis=0) if count > 1 else xs[0][...]
    slot = [slot_column(x, cap) for x in xs]
    slot = jnp.concatenate(slot, axis=0) if count > 1 else slot[0]
    low = jnp.zeros((count * height, rank), F32)
    for g in range(down_ref.shape[1] // (2 * rank)):
        y = jnp.dot(
            x, down_ref[:, 2 * g * rank : 2 * (g + 1) * rank], preferred_element_type=F32
        )
        low = jnp.where(slot == 2 * g, y[:, :rank], low)
        low = jnp.where(slot == 2 * g + 1, y[:, rank:], low)
    for j in range(count):
        part = low[j * height : (j + 1) * height]
        if j == 0 and with_sq:
            tail = [jnp.zeros((cap, rank), F32), sq_ref[...]]
            if height > cap + 8:
                tail.append(jnp.zeros((height - cap - 8, rank), F32))
            part = part + jnp.concatenate(tail, axis=0)
        out_ref[j] = part.astype(BF16)


def low_sum_kernel(count, *refs):
    left, right, out_ref = refs[0], refs[1], refs[2 + count]
    out_ref[...] = (left[...].astype(F32) + right[...].astype(F32)).astype(BF16)
    if count:
        total = refs[2][...]
        for b in refs[3 : 2 + count]:
            total = total + b[...].astype(F32)
        refs[3 + count][...] = total


def head_is_key(heads, h):
    if heads % 2 == 0:
        return h % 2 == 0
    return (lax.axis_index("tensor").astype(jnp.int32) * heads + h) % 2 == 0


def up_kernel(count, n_parts, cap, with_sq, *refs):
    xs = refs[:count]
    parts = refs[count : count + n_parts]
    up_ref = refs[count + n_parts]
    outs = refs[count + n_parts + 1 :]
    per_dev, half, cols = up_ref.shape
    heads = cols // HEAD
    height, rank = parts[0].shape[1:]
    up = up_ref[...].reshape(per_dev * half, cols)
    sums = []
    for j in range(count):
        low = parts[0][j].astype(F32)
        for part in parts[1:]:
            low = low + part[j].astype(F32)
        sums.append(low)
    if with_sq:
        outs[count][...] = sums[0][cap : cap + 8]
    low = jnp.concatenate(sums, axis=0) if count > 1 else sums[0]
    slot = [slot_column(x, cap) for x in xs]
    slot = jnp.concatenate(slot, axis=0) if count > 1 else slot[0]
    left = iota((count * height, rank), 1) < half
    turned = pltpu.roll(low, half, 1)
    wide = []
    for source in (jnp.where(left, low, turned), jnp.where(left, turned, low)):
        pieces = []
        for g in range(per_dev // 2):
            mine = slot == jnp.where(left, 2.0 * g, 2.0 * g + 1)
            pieces.append(jnp.where(mine, source, 0.0).astype(BF16))
        wide.append(jnp.concatenate(pieces, axis=1))
    for h in range(heads):
        key = head_is_key(heads, h)
        if isinstance(key, bool):
            lhs = wide[0] if key else wide[1]
        else:
            lhs = jnp.where(key, wide[0].astype(F32), wide[1].astype(F32)).astype(BF16)
        span = slice(h * HEAD, (h + 1) * HEAD)
        y = jnp.dot(lhs, up[:, span], preferred_element_type=F32).astype(BF16)
        for j in range(count):
            outs[j][:, span] = y[j * height : (j + 1) * height]


def placed(sels, deltas):
    height, cols = deltas[0].shape
    blocks = []
    for delta in deltas:
        blocks.append(delta[...])
        if height < HEAD:
            blocks.append(jnp.zeros((HEAD - height, cols), BF16))
    lhs = jnp.concatenate([sel[...] for sel in sels], axis=1) if len(sels) > 1 else sels[0][...]
    return jnp.dot(lhs, jnp.concatenate(blocks, axis=0), preferred_element_type=F32)


def gather_kernel(n_base, count, sq_ref, *refs):
    base = refs[:n_base]
    deltas = refs[n_base : n_base + count]
    sels = refs[n_base + count : n_base + 2 * count]
    out_ref, scale_ref = refs[-2:]
    rows, cols = out_ref.shape
    pieces = rows // HEAD
    squares = []
    for i in range(pieces):
        total = sq_ref[i : i + 1]
        for p in range(1, 3):
            total = total + sq_ref[p * pieces + i : p * pieces + i + 1]
        squares.append(total)
    square = to_column(jnp.concatenate(squares, axis=1), rows)
    scale = lax.rsqrt(square * (1.0 / MODEL_WIDTH) + EPSILON)
    scale_ref[...] = jnp.broadcast_to(scale, (rows, HEAD))
    total = base[0][...]
    for b in base[1:]:
        total = total + b[...].astype(F32)
    out_ref[...] = total + placed(sels, deltas)


def finish_kernel(sum_ref, scale_ref, delta_ref, sel_ref, cos_ref, sin_ref, out_ref):
    rows, cols = out_ref.shape
    total = sum_ref[...] + placed([sel_ref], [delta_ref])
    heads = cols // HEAD
    scale = scale_ref[...]
    for h in range(heads):
        span = slice(h * HEAD, (h + 1) * HEAD)
        x = total[:, span] * scale
        key = head_is_key(heads, h)
        if key is False:
            out_ref[:, span] = x.astype(BF16)
            continue
        y = x * cos_ref[...] + pltpu.roll(x, HEAD // 2, 1) * sin_ref[...]
        if key is not True:
            y = jnp.where(key, y, x)
        out_ref[:, span] = y.astype(BF16)


def local(
    mesh_shape,
    tokens,
    attention_norm_gain,
    key_value_weight,
    adapter_down_weight,
    adapter_up_weight,
    request_adapter,
    adapter_storage_row,
    cached_token_length,
):
    n_wide, n_tensor = mesh_shape["wide"], mesh_shape["tensor"]
    rows, depth = tokens.shape
    per_dev, _, rank = adapter_down_weight.shape
    cols = adapter_up_weight.shape[2]
    cap = 104 if n_wide <= 4 else 64
    height = -(-(cap + 8) // 16) * 16
    req = request_adapter.reshape(1, rows)
    gain = attention_norm_gain.reshape(depth // HEAD, HEAD)

    def over(axis, array, k):
        size = mesh_shape[axis]
        return lax.ppermute(array, axis, [(i, i ^ k) for i in range(size)])

    small = [pltpu.VMEM((1, rows), jnp.int32), pltpu.SMEM(adapter_storage_row.shape, jnp.int32)]
    last = 2
    first = [0, 1] + list(range(3, n_wide))

    def dispatch(order, after):
        *blocks, wide_gain = call(
            functools.partial(dispatch_kernel, order, n_wide, per_dev, cap),
            "dispatch",
            [shape((height, depth), BF16)] * len(order) + [shape(gain.shape, F32)],
            hbm=(req, adapter_storage_row, tokens, gain),
            hbm_outs=len(order),
            after=after,
            scratch=small
            + [
                pltpu.VMEM((rows, depth), BF16),
                pltpu.VMEM(gain.shape, BF16),
                pltpu.VMEM((len(order), height, depth), BF16),
                pltpu.SemaphoreType.DMA((4,)),
                pltpu.SemaphoreType.DMA((len(order),)),
            ],
            flops=2 * len(order) * height * rows * depth,
            moved=2 * rows * depth * 4,
            limit=63,
        )
        return blocks, wide_gain

    held = [None] * n_wide
    early = list(range(n_wide - 1, 2, -1))
    blocks, wide_gain = dispatch(early, ())
    for k, block in zip(early, blocks):
        held[k] = over("wide", block, k)
    blocks, wide_gain = dispatch([last, 1, 0], (wide_gain,))
    held[0] = blocks[2]
    held[last], held[1] = over("wide", blocks[0], last), over("wide", blocks[1], 1)

    twos = list(range(2, n_tensor, 2))
    far = [k ^ 1 for k in twos]
    offsets = far + [1] + twos + [0]
    chunk = math.gcd(depth, 512)
    steps = depth // chunk
    sums = call(
        functools.partial(base_kernel, offsets, cols),
        "base",
        [shape((rows, cols), BF16)] * (len(far) + 1) + [shape((rows, cols), F32)] * (len(twos) + 1),
        hbm=(wide_gain, tokens, key_value_weight),
        scratch=[
            pltpu.VMEM(gain.shape, F32),
            pltpu.VMEM((rows, depth), BF16),
            pltpu.VMEM((steps, chunk, key_value_weight.shape[1]), BF16),
            pltpu.VMEM((len(offsets), rows, cols), F32),
            pltpu.SemaphoreType.DMA((2 + steps,)),
        ],
        flops=2 * rows * depth * cols * n_tensor,
        moved=2 * depth * cols * n_tensor,
        limit=52,
    )
    away, near, own, base = sums[: len(far)], sums[len(far)], sums[len(far) + 1 : -1], sums[-1]
    beside = [over("tensor", p, 1) for p in away]
    near = over("tensor", near, 1)
    (down,) = call(
        scaled_down_kernel,
        "scaled_down",
        [shape((depth, per_dev * rank), BF16)],
        vmem=(wide_gain,),
        hbm=(adapter_down_weight,),
        after=(base,),
        scratch=[
            pltpu.VMEM((per_dev, depth, rank), BF16),
            pltpu.SemaphoreType.DMA((per_dev,)),
        ],
        flops=4 * depth * per_dev * rank,
        moved=4 * depth * per_dev * rank,
    )
    half_size = HEAD // 2
    freq_index = jnp.arange(half_size).astype(F32)
    inverse = jnp.exp(freq_index * (-2.0 / HEAD) * math.log(ROPE_BASE))
    angles = cached_token_length.astype(F32)[:, None] * inverse[None, :]
    cosine, sine = jnp.cos(angles), jnp.sin(angles)
    cosine = jnp.concatenate([cosine, cosine], axis=1)
    sine = jnp.concatenate([-sine, sine], axis=1)

    pairs = call(
        functools.partial(pair_kernel, len(twos)),
        "pair_sums",
        [shape((rows, cols), BF16)] * len(twos),
        vmem=(*own, *beside),
        after=(down, cosine, sine, held[1]),
        moved=8 * rows * cols * len(twos),
    )
    pairs_here = pairs
    pairs = [over("tensor", p, k) for p, k in zip(pairs, twos)]

    def down_block(group, extra, after):
        xs = [held[k] for k in group]
        (low,) = call(
            functools.partial(down_kernel, len(xs), cap, bool(extra)),
            "down_block",
            [shape((len(xs), height, rank), BF16)],
            vmem=(*xs, down, *extra),
            after=after,
            flops=2 * len(xs) * height * depth * rank * per_dev,
            moved=2 * per_dev * depth * rank,
        )
        return low

    def up_block(group, parts, with_sq, after):
        xs = [held[k] for k in group]
        outs = [shape((height, cols), BF16)] * len(xs)
        if with_sq:
            outs = outs + [shape((8, HEAD), F32)]
        return call(
            functools.partial(up_kernel, len(xs), len(parts), cap, with_sq),
            "up_block",
            outs,
            vmem=(*xs, *parts, adapter_up_weight),
            after=after,
            flops=2 * len(xs) * height * per_dev * rank * cols,
            moved=2 * per_dev * rank * cols,
        )

    low = down_block(first, (), (pairs_here[0],))
    sq, *sels = call(
        functools.partial(aux_kernel, n_wide, per_dev),
        "aux",
        [shape((8, HEAD), F32)] + [shape((rows, HEAD), BF16)] * n_wide,
        hbm=(req, adapter_storage_row, tokens),
        after=(low,),
        scratch=small + [pltpu.VMEM((rows, depth), BF16), pltpu.SemaphoreType.DMA((3,))],
        flops=2 * rows * rows * depth,
        moved=2 * rows * depth,
    )
    step = 1
    while True:
        other = over("tensor", low, step)
        if step * 2 >= n_tensor:
            break
        adds = (base, near) if step == 1 else ()
        outs = [shape(low.shape, BF16)] + [shape((rows, cols), F32)] * (step == 1)
        low, *extra = call(
            functools.partial(low_sum_kernel, len(adds)), "low_sum", outs, vmem=(low, other, *adds), after=(sq,)
        )
        if extra:
            (base,) = extra
        step *= 2
    low_last = down_block([last], (sq,), (low,))
    last_parts = [low_last] + [over("tensor", low_last, k) for k in range(n_tensor - 1, 0, -1)]
    ups = up_block(first, [low, other], False, (low_last,))
    deltas = [u if k == 0 else over("wide", u, k) for k, u in zip(first, ups)]
    up, square = up_block([last], last_parts, True, (ups[0],))
    delta = over("wide", up, last)
    total, scale = call(
        functools.partial(gather_kernel, 1 + len(pairs), len(first)),
        "gather",
        [shape((rows, cols), F32), shape((rows, HEAD), F32)],
        vmem=(square, base, *pairs, *deltas, *[sels[k] for k in first]),
        after=(up,),
        flops=2 * rows * cols * HEAD * len(first),
    )
    return call(
        finish_kernel,
        "finish",
        [shape((rows, cols), BF16)],
        vmem=(total, scale, delta, sels[last], cosine, sine),
        flops=2 * rows * cols * HEAD,
    )[0]


def solution(mesh):
    return jax.shard_map(
        functools.partial(local, dict(mesh.shape)),
        mesh=mesh,
        in_specs=(
            P(("parts", "wide"), "tensor"),
            P("tensor"),
            P("tensor", None),
            P(("parts", "wide"), "tensor", None),
            P(("parts", "wide"), None, "tensor"),
            P(("parts", "wide")),
            P("parts"),
            P(("parts", "wide")),
        ),
        out_specs=P(("parts", "wide"), "tensor"),
        check_vma=False,
    )
```

profile of v0, /device:TPU:0, one launch (start us, length us, event | category | flops | bytes accessed | tf_op | source)
XLA Modules:
  0.0 56.3 jit_solution(7506484319623917679)
XLA Ops:
  0.0 3.0 %dispatch.2 = (bf16[112,2048]{1,0:T(8,128)(2,1)}, f32[16,128]{1,0:T(8,128)}) custom-call(s32[1,256]{1,0:T(1,128)} %bitcast.2, s32[32]{0:T(128)} %refs_1_.9, bf16[256,2048]{1,0:T(8,128)(2,1)} %refs_2_.7, bf16[16,128]{1,0:T(8,128)(2,1)} %bitcast.5), custom_call_target="tpu_custom_call" | custom-call | flops 117440512 | bytes 4194304 | tf_op jit(solution)/shard_map/dispatch/pallas_call | solution.py:28
  3.0 2.4 %collective-permute-start.2 = (bf16[112,2048]{1,0:T(8,128)(2,1)}, bf16[112,2048]{1,0:T(8,128)(2,1)S(1)}, u32[]{:S(2)}, u32[]{:S(2)}) collective-permute-start(bf16[112,2048]{1,0:T(8,128)(2,1)} %get-tuple-element.35), channel_id=1, source_target_pairs={{0,12},{4,8},{8,4},{12,0},{1,13},{5,9},{9,5},{13,1},{2,14},{6,10},... | collective-permute-start | bytes 1376264 | tf_op jit(solution)/shard_map/ppermute | solution.py:364
  5.4 3.3 %dispatch.3 = (bf16[112,2048]{1,0:T(8,128)(2,1)}, bf16[112,2048]{1,0:T(8,128)(2,1)}, bf16[112,2048]{1,0:T(8,128)(2,1)}, f32[16,128]{1,0:T(8,128)}) custom-call(s32[1,256]{1,0:T(1,128)} %bitcast.3, s32[32]{0:T(128)} %refs_1_.9, bf16[256,2048]{1,0:T(8,128)(2,1)} %refs_2_.7, bf16[16,128]{1,0:T(8,128)(2,1)} %bitcast.6, f32[16,128]{1,0:T(8,128)} %get-tuple-element.29.refs_4_), custom_call_target="tpu_custom_call" | custom-call | flops 352321536 | bytes 4194304 | tf_op jit(solution)/shard_map/dispatch/pallas_call | solution.py:28
  9.6 0.7 %copy-done.4 = f32[16,128]{1,0:T(8,128)S(1)} copy-done((f32[16,128]{1,0:T(8,128)S(1)}, f32[16,128]{1,0:T(8,128)}, u32[]{:S(2)}) %copy-start.4) | copy-done | bytes 8216
  10.3 4.8 %base.1 = (bf16[256,512]{1,0:T(8,128)(2,1)S(1)}, bf16[256,512]{1,0:T(8,128)(2,1)S(1)}, f32[256,512]{1,0:T(8,128)S(1)}, f32[256,512]{1,0:T(8,128)S(1)}) custom-call(f32[16,128]{1,0:T(8,128)S(1)} %copy-done.4, bf16[256,2048]{1,0:T(8,128)(2,1)} %refs_2_.7, bf16[2048,2048]{1,0:T(8,128)(2,1)} %refs_2_.6), custom_call_target="tpu_custom_call" | custom-call | flops 2147483648 | bytes 8388608 | tf_op jit(solution)/shard_map/base/pallas_call | solution.py:28
  15.1 1.8 %collective-permute-start.3 = (bf16[256,512]{1,0:T(8,128)(2,1)S(1)}, bf16[256,512]{1,0:T(8,128)(2,1)S(1)}, u32[]{:S(2)}, u32[]{:S(2)}) collective-permute-start(bf16[256,512]{1,0:T(8,128)(2,1)S(1)} %get-tuple-element.37), channel_id=1, source_target_pairs={{0,1},{1,0},{2,3},{3,2},{4,5},{5,4},{6,7},{7,6},{8,9},{9,8},{10,11... | collective-permute-start | bytes 786440 | tf_op jit(solution)/shard_map/ppermute | solution.py:364
  17.9 1.9 %scaled_down.1.refs_2_.refs_3_.refs_1_ = bf16[2048,1024]{1,0:T(8,128)(2,1)S(1)} custom-call(f32[16,128]{1,0:T(8,128)S(1)} %copy-done.4, bf16[8,2048,128]{2,1,0:T(8,128)(2,1)S(1)} %copy-done.1, f32[256,512]{1,0:T(8,128)S(1)} %get-tuple-element.32.refs_2_), custom_call_target="tpu_custom_call" | custom-call | flops 8388608 | bytes 8388608 | tf_op jit(solution)/shard_map/scaled_down/pallas_call | solution.py:28
  19.9 4.4 %collective-permute-done.3.refs_1_ = bf16[256,512]{1,0:T(8,128)(2,1)S(1)} collective-permute-done((bf16[256,512]{1,0:T(8,128)(2,1)S(1)}, bf16[256,512]{1,0:T(8,128)(2,1)S(1)}, u32[]{:S(2)}, u32[]{:S(2)}) %collective-permute-start.3) | collective-permute-done | bytes 262176 | tf_op jit(solution)/shard_map/ppermute | solution.py:364
  24.4 1.6 %down_block.2.refs_3_.refs_0_ = bf16[3,112,128]{2,1,0:T(8,128)(2,1)S(1)} custom-call(bf16[112,2048]{1,0:T(8,128)(2,1)S(1)} %copy-done.3, bf16[112,2048]{1,0:T(8,128)(2,1)S(1)} %collective-permute-done.1.refs_5_.refs_1_, bf16[112,2048]{1,0:T(8,128)(2,1)S(1)} %collective-permute-done.2.refs_2_, bf16[2048,1024]{1,0:T(8,128)(2,1)S(1)} %scaled_down.1.refs_2_.refs_3_.refs_1_, ...), custom_call_target="tpu_custom_call" | custom-call | flops 1409286144 | bytes 4194304 | tf_op jit(solution)/shard_map/down_block/pallas_call | solution.py:28
  26.0 1.9 %collective-permute-start.4 = (bf16[3,112,128]{2,1,0:T(8,128)(2,1)S(1)}, bf16[3,112,128]{2,1,0:T(8,128)(2,1)S(1)}, u32[]{:S(2)}, u32[]{:S(2)}) collective-permute-start(bf16[3,112,128]{2,1,0:T(8,128)(2,1)S(1)} %down_block.2.refs_3_.refs_0_), channel_id=1, source_target_pairs={{0,1},{1,0},{2,3},{3,2},{4,5},{5,4},{6,7},{7,6},{8,9},{9,8},{10,11... | collective-permute-start | bytes 258056 | tf_op jit(solution)/shard_map/ppermute | solution.py:364
  27.9 2.6 %collective-permute-start.10 = (bf16[256,512]{1,0:T(8,128)(2,1)S(1)}, bf16[256,512]{1,0:T(8,128)(2,1)S(1)}, u32[]{:S(2)}, u32[]{:S(2)}) collective-permute-start(bf16[256,512]{1,0:T(8,128)(2,1)S(1)} %pair_sums.1.refs_4_), channel_id=1, source_target_pairs={{0,2},{1,3},{2,0},{3,1},{4,6},{5,7},{6,4},{7,5},{8,10},{9,11},{10,... | collective-permute-start | bytes 786440 | tf_op jit(solution)/shard_map/ppermute | solution.py:364
  30.4 1.1 %aux.1 = (f32[8,128]{1,0:T(8,128)S(1)}, bf16[256,128]{1,0:T(8,128)(2,1)S(1)}, bf16[256,128]{1,0:T(8,128)(2,1)S(1)}, bf16[256,128]{1,0:T(8,128)(2,1)S(1)}, bf16[256,128]{1,0:T(8,128)(2,1)S(1)}) custom-call(s32[1,256]{1,0:T(1,128)S(1)} %bitcast.4, s32[32]{0:T(128)S(1)} %copy-done.6, bf16[256,2048]{1,0:T(8,128)(2,1)S(1)} %copy-done, ...), custom_call_target="tpu_custom_call" | custom-call | flops 268435456 | bytes 1048576 | tf_op jit(solution)/shard_map/aux/pallas_call | solution.py:28
  31.5 1.3 %collective-permute-done.5.refs_3_ = bf16[256,512]{1,0:T(8,128)(2,1)S(1)} collective-permute-done((bf16[256,512]{1,0:T(8,128)(2,1)S(1)}, bf16[256,512]{1,0:T(8,128)(2,1)S(1)}, u32[]{:S(2)}, u32[]{:S(2)}) %collective-permute-start.5) | collective-permute-done | bytes 262176 | tf_op jit(solution)/shard_map/ppermute | solution.py:364
  32.9 1.9 %collective-permute-done.4.refs_1_ = bf16[3,112,128]{2,1,0:T(8,128)(2,1)S(1)} collective-permute-done((bf16[3,112,128]{2,1,0:T(8,128)(2,1)S(1)}, bf16[3,112,128]{2,1,0:T(8,128)(2,1)S(1)}, u32[]{:S(2)}, u32[]{:S(2)}) %collective-permute-start.4) | collective-permute-done | bytes 86048 | tf_op jit(solution)/shard_map/ppermute | solution.py:364
  35.5 0.8 %down_block.3.refs_6_.refs_1_ = bf16[1,112,128]{2,1,0:T(8,128)(2,1)S(1)} custom-call(bf16[112,2048]{1,0:T(8,128)(2,1)S(1)} %collective-permute-done.refs_0_, bf16[2048,1024]{1,0:T(8,128)(2,1)S(1)} %scaled_down.1.refs_2_.refs_3_.refs_1_, f32[8,128]{1,0:T(8,128)S(1)} %get-tuple-element.38.refs_4_.refs_2_, bf16[3,112,128]{2,1,0:T(8,128)(2,1)S(1)} %get-tuple-element.40.refs_3_), custom_call_target="tpu_custom_call" | custom-call | flops 469762048 | bytes 4194304 | tf_op jit(solution)/shard_map/down_block/pallas_call | solution.py:28
  36.3 2.6 %collective-permute-start.8 = (bf16[1,112,128]{2,1,0:T(8,128)(2,1)S(1)}, bf16[1,112,128]{2,1,0:T(8,128)(2,1)S(1)}, u32[]{:S(2)}, u32[]{:S(2)}) collective-permute-start(bf16[1,112,128]{2,1,0:T(8,128)(2,1)S(1)} %down_block.3.refs_6_.refs_1_), channel_id=1, source_target_pairs={{0,1},{1,0},{2,3},{3,2},{4,5},{5,4},{6,7},{7,6},{8,9},{9,8},{10,11... | collective-permute-start | bytes 86024 | tf_op jit(solution)/shard_map/ppermute | solution.py:364
  38.9 2.4 %collective-permute-start.6 = (bf16[1,112,128]{2,1,0:T(8,128)(2,1)S(1)}, bf16[1,112,128]{2,1,0:T(8,128)(2,1)S(1)}, u32[]{:S(2)}, u32[]{:S(2)}) collective-permute-start(bf16[1,112,128]{2,1,0:T(8,128)(2,1)S(1)} %down_block.3.refs_6_.refs_1_), channel_id=1, source_target_pairs={{0,3},{1,2},{2,1},{3,0},{4,7},{5,6},{6,5},{7,4},{8,11},{9,10},{10,... | collective-permute-start | bytes 86024 | tf_op jit(solution)/shard_map/ppermute | solution.py:364
  41.3 5.1 %collective-permute-done.9.refs_4_ = bf16[3,112,128]{2,1,0:T(8,128)(2,1)S(1)} collective-permute-done((bf16[3,112,128]{2,1,0:T(8,128)(2,1)S(1)}, bf16[3,112,128]{2,1,0:T(8,128)(2,1)S(1)}, u32[]{:S(2)}, u32[]{:S(2)}) %collective-permute-start.9) | collective-permute-done | bytes 86048 | tf_op jit(solution)/shard_map/ppermute | solution.py:364
  46.4 0.8 %up_block.2 = (bf16[112,512]{1,0:T(8,128)(2,1)S(1)}, bf16[112,512]{1,0:T(8,128)(2,1)S(1)}, bf16[112,512]{1,0:T(8,128)(2,1)S(1)}) custom-call(bf16[112,2048]{1,0:T(8,128)(2,1)S(1)} %copy-done.3, bf16[112,2048]{1,0:T(8,128)(2,1)S(1)} %collective-permute-done.1.refs_5_.refs_1_, bf16[112,2048]{1,0:T(8,128)(2,1)S(1)} %collective-permute-done.2.refs_2_, ...), custom_call_target="tpu_custom_call" | custom-call | flops 352321536 | bytes 1048576 | tf_op jit(solution)/shard_map/up_block/pallas_call | solution.py:28
  47.3 1.5 %collective-permute-start.12 = (bf16[112,512]{1,0:T(8,128)(2,1)S(1)}, bf16[112,512]{1,0:T(8,128)(2,1)S(1)}, u32[]{:S(2)}, u32[]{:S(2)}) collective-permute-start(bf16[112,512]{1,0:T(8,128)(2,1)S(1)} %get-tuple-element.45), channel_id=1, source_target_pairs={{0,12},{4,8},{8,4},{12,0},{1,13},{5,9},{9,5},{13,1},{2,14},{6,10},... | collective-permute-start | bytes 344072 | tf_op jit(solution)/shard_map/ppermute | solution.py:364
  49.3 0.7 %collective-permute-start.13 = (bf16[112,512]{1,0:T(8,128)(2,1)S(1)}, bf16[112,512]{1,0:T(8,128)(2,1)S(1)}, u32[]{:S(2)}, u32[]{:S(2)}) collective-permute-start(bf16[112,512]{1,0:T(8,128)(2,1)S(1)} %get-tuple-element.49.refs_9_), channel_id=1, source_target_pairs={{0,8},{4,12},{8,0},{12,4},{1,9},{5,13},{9,1},{13,5},{2,10},{6,14},... | collective-permute-start | bytes 344072 | tf_op jit(solution)/shard_map/ppermute | solution.py:364
  50.0 2.4 %collective-permute-done.12.refs_5_ = bf16[112,512]{1,0:T(8,128)(2,1)S(1)} collective-permute-done((bf16[112,512]{1,0:T(8,128)(2,1)S(1)}, bf16[112,512]{1,0:T(8,128)(2,1)S(1)}, u32[]{:S(2)}, u32[]{:S(2)}) %collective-permute-start.12) | collective-permute-done | bytes 114720 | tf_op jit(solution)/shard_map/ppermute | solution.py:364
  52.6 2.7 %collective-permute-done.13.refs_2_ = bf16[112,512]{1,0:T(8,128)(2,1)S(1)} collective-permute-done((bf16[112,512]{1,0:T(8,128)(2,1)S(1)}, bf16[112,512]{1,0:T(8,128)(2,1)S(1)}, u32[]{:S(2)}, u32[]{:S(2)}) %collective-permute-start.13) | collective-permute-done | bytes 114720 | tf_op jit(solution)/shard_map/ppermute | solution.py:364
  55.3 1.0 %finish.1 = bf16[256,512]{1,0:T(8,128)(2,1)} custom-call(f32[256,512]{1,0:T(8,128)S(1)} %get-tuple-element.50.refs_0_, f32[256,128]{1,0:T(8,128)S(1)} %get-tuple-element.51.refs_1_, bf16[112,512]{1,0:T(8,128)(2,1)S(1)} %collective-permute-done.13.refs_2_, bf16[256,128]{1,0:T(8,128)(2,1)S(1)} %get-tuple-element.52.refs_3_, ...), custom_call_target="tpu_custom_call" | custom-call | flops 33554432 | tf_op jit(solution)/shard_map/finish/pallas_call | solution.py:28
  (37 shorter events, 3.4 us)
Async XLA Ops:
  3.0 21.4 %collective-permute-start.2 = (bf16[112,2048]{1,0:T(8,128)(2,1)}, bf16[112,2048]{1,0:T(8,128)(2,1)S(1)}, u32[]{:S(2)}, u32[]{:S(2)}) collective-permute-start(bf16[112,2048]{1,0:T(8,128)(2,1)} %get-tuple-element.35), channel_id=1, source_target_pairs={{0,12},{4,8},{8,4},{12,0},{1,13},{5,9},{9,5},{13,1},{2,14},{6,10},... | collective-permute-start | bytes 1376264 | tf_op jit(solution)/shard_map/ppermute | solution.py:364
  8.8 26.8 %collective-permute-start = (bf16[112,2048]{1,0:T(8,128)(2,1)}, bf16[112,2048]{1,0:T(8,128)(2,1)S(1)}, u32[]{:S(2)}, u32[]{:S(2)}) collective-permute-start(bf16[112,2048]{1,0:T(8,128)(2,1)} %get-tuple-element.30), channel_id=1, source_target_pairs={{0,8},{4,12},{8,0},{12,4},{1,9},{5,13},{9,1},{13,5},{2,10},{6,14},... | collective-permute-start | bytes 1376264 | tf_op jit(solution)/shard_map/ppermute | solution.py:364
  9.4 14.9 %collective-permute-start.1 = (bf16[112,2048]{1,0:T(8,128)(2,1)}, bf16[112,2048]{1,0:T(8,128)(2,1)S(1)}, u32[]{:S(2)}, u32[]{:S(2)}) collective-permute-start(bf16[112,2048]{1,0:T(8,128)(2,1)} %get-tuple-element.34), channel_id=1, source_target_pairs={{0,4},{4,0},{8,12},{12,8},{1,5},{5,1},{9,13},{13,9},{2,6},{6,2},{1... | collective-permute-start | bytes 1376264 | tf_op jit(solution)/shard_map/ppermute | solution.py:364
  9.6 0.7 %copy-start.4 = (f32[16,128]{1,0:T(8,128)S(1)}, f32[16,128]{1,0:T(8,128)}, u32[]{:S(2)}) copy-start(f32[16,128]{1,0:T(8,128)} %get-tuple-element.31.refs_0_) | copy-start | bytes 24580
  10.3 6.9 %copy-start.7 = (s32[256]{0:T(256)S(1)}, s32[256]{0:T(256)}, u32[]{:S(2)}) copy-start(s32[256]{0:T(256)} %param.15) | copy-start | bytes 3076
  10.3 7.6 %copy-start.1 = (bf16[8,2048,128]{2,1,0:T(8,128)(2,1)S(1)}, bf16[8,2048,128]{2,1,0:T(8,128)(2,1)}, u32[]{:S(2)}) copy-start(bf16[8,2048,128]{2,1,0:T(8,128)(2,1)} %refs_1_.8) | copy-start | bytes 12582916
  15.1 9.2 %collective-permute-start.3 = (bf16[256,512]{1,0:T(8,128)(2,1)S(1)}, bf16[256,512]{1,0:T(8,128)(2,1)S(1)}, u32[]{:S(2)}, u32[]{:S(2)}) collective-permute-start(bf16[256,512]{1,0:T(8,128)(2,1)S(1)} %get-tuple-element.37), channel_id=1, source_target_pairs={{0,1},{1,0},{2,3},{3,2},{4,5},{5,4},{6,7},{7,6},{8,9},{9,8},{10,11... | collective-permute-start | bytes 786440 | tf_op jit(solution)/shard_map/ppermute | solution.py:364
  16.9 15.9 %collective-permute-start.5 = (bf16[256,512]{1,0:T(8,128)(2,1)S(1)}, bf16[256,512]{1,0:T(8,128)(2,1)S(1)}, u32[]{:S(2)}, u32[]{:S(2)}) collective-permute-start(bf16[256,512]{1,0:T(8,128)(2,1)S(1)} %get-tuple-element.39), channel_id=1, source_target_pairs={{0,1},{1,0},{2,3},{3,2},{4,5},{5,4},{6,7},{7,6},{8,9},{9,8},{10,11... | collective-permute-start | bytes 786440 | tf_op jit(solution)/shard_map/ppermute | solution.py:364
  19.9 4.5 %copy-start.3 = (bf16[112,2048]{1,0:T(8,128)(2,1)S(1)}, bf16[112,2048]{1,0:T(8,128)(2,1)}, u32[]{:S(2)}) copy-start(bf16[112,2048]{1,0:T(8,128)(2,1)} %get-tuple-element.33.refs_0_) | copy-start | bytes 1376260
  24.3 6.1 %copy-start = (bf16[256,2048]{1,0:T(8,128)(2,1)S(1)}, bf16[256,2048]{1,0:T(8,128)(2,1)}, u32[]{:S(2)}) copy-start(bf16[256,2048]{1,0:T(8,128)(2,1)} %refs_2_.7) | copy-start | bytes 3145732
  24.4 6.1 %copy-start.5 = (s32[256]{0:T(256)S(1)}, s32[256]{0:T(256)}, u32[]{:S(2)}) copy-start(s32[256]{0:T(256)} %param.13) | copy-start | bytes 3076
  24.4 6.1 %copy-start.6 = (s32[32]{0:T(128)S(1)}, s32[32]{0:T(128)}, u32[]{:S(2)}) copy-start(s32[32]{0:T(128)} %refs_1_.9) | copy-start | bytes 388
  26.0 20.4 %copy-start.2 = (bf16[8,64,512]{2,1,0:T(8,128)(2,1)S(1)}, bf16[8,64,512]{2,1,0:T(8,128)(2,1)}, u32[]{:S(2)}) copy-start(bf16[8,64,512]{2,1,0:T(8,128)(2,1)} %refs_5_.3) | copy-start | bytes 1572868
  26.0 8.8 %collective-permute-start.4 = (bf16[3,112,128]{2,1,0:T(8,128)(2,1)S(1)}, bf16[3,112,128]{2,1,0:T(8,128)(2,1)S(1)}, u32[]{:S(2)}, u32[]{:S(2)}) collective-permute-start(bf16[3,112,128]{2,1,0:T(8,128)(2,1)S(1)} %down_block.2.refs_3_.refs_0_), channel_id=1, source_target_pairs={{0,1},{1,0},{2,3},{3,2},{4,5},{5,4},{6,7},{7,6},{8,9},{9,8},{10,11... | collective-permute-start | bytes 258056 | tf_op jit(solution)/shard_map/ppermute | solution.py:364
  27.9 22.1 %collective-permute-start.10 = (bf16[256,512]{1,0:T(8,128)(2,1)S(1)}, bf16[256,512]{1,0:T(8,128)(2,1)S(1)}, u32[]{:S(2)}, u32[]{:S(2)}) collective-permute-start(bf16[256,512]{1,0:T(8,128)(2,1)S(1)} %pair_sums.1.refs_4_), channel_id=1, source_target_pairs={{0,2},{1,3},{2,0},{3,1},{4,6},{5,7},{6,4},{7,5},{8,10},{9,11},{10,... | collective-permute-start | bytes 786440 | tf_op jit(solution)/shard_map/ppermute | solution.py:364
  34.9 11.6 %collective-permute-start.9 = (bf16[3,112,128]{2,1,0:T(8,128)(2,1)S(1)}, bf16[3,112,128]{2,1,0:T(8,128)(2,1)S(1)}, u32[]{:S(2)}, u32[]{:S(2)}) collective-permute-start(bf16[3,112,128]{2,1,0:T(8,128)(2,1)S(1)} %get-tuple-element.40.refs_3_), channel_id=1, source_target_pairs={{0,2},{1,3},{2,0},{3,1},{4,6},{5,7},{6,4},{7,5},{8,10},{9,11},{10,... | collective-permute-start | bytes 258056 | tf_op jit(solution)/shard_map/ppermute | solution.py:364
  36.3 11.1 %collective-permute-start.8 = (bf16[1,112,128]{2,1,0:T(8,128)(2,1)S(1)}, bf16[1,112,128]{2,1,0:T(8,128)(2,1)S(1)}, u32[]{:S(2)}, u32[]{:S(2)}) collective-permute-start(bf16[1,112,128]{2,1,0:T(8,128)(2,1)S(1)} %down_block.3.refs_6_.refs_1_), channel_id=1, source_target_pairs={{0,1},{1,0},{2,3},{3,2},{4,5},{5,4},{6,7},{7,6},{8,9},{9,8},{10,11... | collective-permute-start | bytes 86024 | tf_op jit(solution)/shard_map/ppermute | solution.py:364
  38.8 10.0 %collective-permute-start.7 = (bf16[1,112,128]{2,1,0:T(8,128)(2,1)S(1)}, bf16[1,112,128]{2,1,0:T(8,128)(2,1)S(1)}, u32[]{:S(2)}, u32[]{:S(2)}) collective-permute-start(bf16[1,112,128]{2,1,0:T(8,128)(2,1)S(1)} %down_block.3.refs_6_.refs_1_), channel_id=1, source_target_pairs={{0,2},{1,3},{2,0},{3,1},{4,6},{5,7},{6,4},{7,5},{8,10},{9,11},{10,... | collective-permute-start | bytes 86024 | tf_op jit(solution)/shard_map/ppermute | solution.py:364
  38.9 10.0 %collective-permute-start.6 = (bf16[1,112,128]{2,1,0:T(8,128)(2,1)S(1)}, bf16[1,112,128]{2,1,0:T(8,128)(2,1)S(1)}, u32[]{:S(2)}, u32[]{:S(2)}) collective-permute-start(bf16[1,112,128]{2,1,0:T(8,128)(2,1)S(1)} %down_block.3.refs_6_.refs_1_), channel_id=1, source_target_pairs={{0,3},{1,2},{2,1},{3,0},{4,7},{5,6},{6,5},{7,4},{8,11},{9,10},{10,... | collective-permute-start | bytes 86024 | tf_op jit(solution)/shard_map/ppermute | solution.py:364
  47.3 2.7 %collective-permute-start.11 = (bf16[112,512]{1,0:T(8,128)(2,1)S(1)}, bf16[112,512]{1,0:T(8,128)(2,1)S(1)}, u32[]{:S(2)}, u32[]{:S(2)}) collective-permute-start(bf16[112,512]{1,0:T(8,128)(2,1)S(1)} %get-tuple-element.44), channel_id=1, source_target_pairs={{0,4},{4,0},{8,12},{12,8},{1,5},{5,1},{9,13},{13,9},{2,6},{6,2},{1... | collective-permute-start | bytes 344072 | tf_op jit(solution)/shard_map/ppermute | solution.py:364
  47.3 5.0 %collective-permute-start.12 = (bf16[112,512]{1,0:T(8,128)(2,1)S(1)}, bf16[112,512]{1,0:T(8,128)(2,1)S(1)}, u32[]{:S(2)}, u32[]{:S(2)}) collective-permute-start(bf16[112,512]{1,0:T(8,128)(2,1)S(1)} %get-tuple-element.45), channel_id=1, source_target_pairs={{0,12},{4,8},{8,4},{12,0},{1,13},{5,9},{9,5},{13,1},{2,14},{6,10},... | collective-permute-start | bytes 344072 | tf_op jit(solution)/shard_map/ppermute | solution.py:364
  49.3 6.1 %collective-permute-start.13 = (bf16[112,512]{1,0:T(8,128)(2,1)S(1)}, bf16[112,512]{1,0:T(8,128)(2,1)S(1)}, u32[]{:S(2)}, u32[]{:S(2)}) collective-permute-start(bf16[112,512]{1,0:T(8,128)(2,1)S(1)} %get-tuple-element.49.refs_9_), channel_id=1, source_target_pairs={{0,8},{4,12},{8,0},{12,4},{1,9},{5,13},{9,1},{13,5},{2,10},{6,14},... | collective-permute-start | bytes 344072 | tf_op jit(solution)/shard_map/ppermute | solution.py:364
where the time goes:
time: 56.6 us; the launch traced here: 56.3 us
  Pallas kernels  19.1 us (34%)
  waiting for transfers between devices  17.9 us (32%)
  starting transfers between devices  17.7 us (31%)
  local copies, waits for them, and re-layouts  0.73 us (1%)
  other arithmetic  0.68 us (1%)
    pallas_call x13, Pallas kernels, call(): pl.pallas_call(body, out_shape=outs, in_specs=[pl.BlockSpec(memory_space=...  19.1 us
    ppermute x14, waiting for transfers between devices, over(): return lax.ppermute(array, axis, [(i, i ^ k) for i in range(size)])  17.9 us
    ppermute x14, starting transfers between devices, over(): return lax.ppermute(array, axis, [(i, i ^ k) for i in range(size)])  17.7 us
  transfers between devices with their start and end apart: 14, of which 6 were waited for; matrix products, arithmetic and copies ran while one was open for 1% of the time, Pallas kernels for 27%

commit v1 on v0

--- a/solution.py
+++ b/solution.py
@@ -142,10 +142,11 @@
                 outs[j][...] = y.astype(outs[j].dtype)
 
 
-def pair_kernel(count, *refs):
+def pair_kernel(count, start, *refs):
     for j in range(count):
-        total = refs[j][...] + refs[count + j][...].astype(F32)
-        refs[2 * count + j][...] = total.astype(BF16)
+        out_ref = refs[2 * count + j]
+        rows = slice(start, start + out_ref.shape[0])
+        out_ref[...] = (refs[j][rows] + refs[count + j][rows].astype(F32)).astype(BF16)
 
 
 def scaled_down_kernel(gain_ref, down_hbm, out_ref, buf, sems):
@@ -231,14 +232,12 @@
         out_ref[j] = part.astype(BF16)
 
 
-def low_sum_kernel(count, *refs):
-    left, right, out_ref = refs[0], refs[1], refs[2 + count]
-    out_ref[...] = (left[...].astype(F32) + right[...].astype(F32)).astype(BF16)
-    if count:
-        total = refs[2][...]
-        for b in refs[3 : 2 + count]:
-            total = total + b[...].astype(F32)
-        refs[3 + count][...] = total
+def low_sum_kernel(left_ref, right_ref, *refs):
+    out_ref = refs[len(refs) // 2]
+    total = left_ref[...].astype(F32) + right_ref[...].astype(F32)
+    out_ref[...] = total.astype(BF16)
+    if len(refs) > 1:
+        refs[2][...] = refs[0][...]
 
 
 def head_is_key(heads, h):
@@ -299,10 +298,18 @@
     return jnp.dot(lhs, jnp.concatenate(blocks, axis=0), preferred_element_type=F32)
 
 
-def gather_kernel(n_base, count, sq_ref, *refs):
-    base = refs[:n_base]
-    deltas = refs[n_base : n_base + count]
-    sels = refs[n_base + count : n_base + 2 * count]
+def base_sum_kernel(n_pairs, base_ref, *refs):
+    out_ref = refs[n_pairs]
+    half = refs[0].shape[0] if n_pairs else 0
+    out_ref[...] = base_ref[...]
+    for top in refs[:n_pairs]:
+        out_ref[:half] += top[...].astype(F32)
+
+
+def gather_kernel(n_pairs, count, sq_ref, base_ref, near_ref, *refs):
+    bottoms = refs[:n_pairs]
+    deltas = refs[n_pairs : n_pairs + count]
+    sels = refs[n_pairs + count : n_pairs + 2 * count]
     out_ref, scale_ref = refs[-2:]
     rows, cols = out_ref.shape
     pieces = rows // HEAD
@@ -315,15 +322,22 @@
     square = to_column(jnp.concatenate(squares, axis=1), rows)
     scale = lax.rsqrt(square * (1.0 / MODEL_WIDTH) + EPSILON)
     scale_ref[...] = jnp.broadcast_to(scale, (rows, HEAD))
-    total = base[0][...]
-    for b in base[1:]:
-        total = total + b[...].astype(F32)
-    out_ref[...] = total + placed(sels, deltas)
-
-
-def finish_kernel(sum_ref, scale_ref, delta_ref, sel_ref, cos_ref, sin_ref, out_ref):
+    total = base_ref[...] + near_ref[...].astype(F32) + placed(sels, deltas)
+    if bottoms:
+        half = rows - bottoms[0].shape[0]
+        lower = total[half:]
+        for bottom in bottoms:
+            lower = lower + bottom[...].astype(F32)
+        out_ref[:half] = total[:half]
+        out_ref[half:] = lower
+    else:
+        out_ref[...] = total
+
+
+def finish_kernel(count, sum_ref, scale_ref, cos_ref, sin_ref, *refs):
+    deltas, sels, out_ref = refs[:count], refs[count : 2 * count], refs[2 * count]
     rows, cols = out_ref.shape
-    total = sum_ref[...] + placed([sel_ref], [delta_ref])
+    total = sum_ref[...] + placed(sels, deltas)
     heads = cols // HEAD
     scale = scale_ref[...]
     for h in range(heads):
@@ -364,8 +378,7 @@
         return lax.ppermute(array, axis, [(i, i ^ k) for i in range(size)])
 
     small = [pltpu.VMEM((1, rows), jnp.int32), pltpu.SMEM(adapter_storage_row.shape, jnp.int32)]
-    last = 2
-    first = [0, 1] + list(range(3, n_wide))
+    first, last = [0, 1], list(range(2, n_wide))
 
     def dispatch(order, after):
         *blocks, wide_gain = call(
@@ -389,14 +402,10 @@
         )
         return blocks, wide_gain
 
-    held = [None] * n_wide
-    early = list(range(n_wide - 1, 2, -1))
-    blocks, wide_gain = dispatch(early, ())
-    for k, block in zip(early, blocks):
-        held[k] = over("wide", block, k)
-    blocks, wide_gain = dispatch([last, 1, 0], (wide_gain,))
-    held[0] = blocks[2]
-    held[last], held[1] = over("wide", blocks[0], last), over("wide", blocks[1], 1)
+    order = list(range(n_wide - 1, -1, -1))
+    blocks, wide_gain = dispatch(order, ())
+    held = [blocks[n_wide - 1 - k] for k in range(n_wide)]
+    held[1:] = [over("wide", held[k], k) for k in range(1, n_wide)]
 
     twos = list(range(2, n_tensor, 2))
     far = [k ^ 1 for k in twos]
@@ -421,7 +430,6 @@
     )
     away, near, own, base = sums[: len(far)], sums[len(far)], sums[len(far) + 1 : -1], sums[-1]
     beside = [over("tensor", p, 1) for p in away]
-    near = over("tensor", near, 1)
     (down,) = call(
         scaled_down_kernel,
         "scaled_down",
@@ -444,16 +452,16 @@
     cosine = jnp.concatenate([cosine, cosine], axis=1)
     sine = jnp.concatenate([-sine, sine], axis=1)
 
-    pairs = call(
-        functools.partial(pair_kernel, len(twos)),
-        "pair_sums",
-        [shape((rows, cols), BF16)] * len(twos),
-        vmem=(*own, *beside),
-        after=(down, cosine, sine, held[1]),
-        moved=8 * rows * cols * len(twos),
-    )
-    pairs_here = pairs
-    pairs = [over("tensor", p, k) for p, k in zip(pairs, twos)]
+    def pair_sums(start, after):
+        pairs = call(
+            functools.partial(pair_kernel, len(twos), start),
+            "pair_sums",
+            [shape((rows // 2, cols), BF16)] * len(twos),
+            vmem=(*own, *beside),
+            after=after,
+            moved=4 * rows * cols * len(twos),
+        )
+        return pairs[-1], [over("tensor", p, k) for p, k in zip(pairs, twos)]
 
     def down_block(group, extra, after):
         xs = [held[k] for k in group]
@@ -483,7 +491,7 @@
             moved=2 * per_dev * rank * cols,
         )
 
-    low = down_block(first, (), (pairs_here[0],))
+    low = down_block(first, (), ())
     sq, *sels = call(
         functools.partial(aux_kernel, n_wide, per_dev),
         "aux",
@@ -494,38 +502,50 @@
         flops=2 * rows * rows * depth,
         moved=2 * rows * depth,
     )
+    pair, tops = pair_sums(0, (sq, cosine, sine))
     step = 1
     while True:
         other = over("tensor", low, step)
         if step * 2 >= n_tensor:
             break
-        adds = (base, near) if step == 1 else ()
-        outs = [shape(low.shape, BF16)] + [shape((rows, cols), F32)] * (step == 1)
-        low, *extra = call(
-            functools.partial(low_sum_kernel, len(adds)), "low_sum", outs, vmem=(low, other, *adds), after=(sq,)
-        )
-        if extra:
-            (base,) = extra
+        more = (near,) if step == 1 else ()
+        low, *handed = call(
+            low_sum_kernel,
+            "low_sum",
+            [shape(low.shape, BF16)] + [shape((rows, cols), BF16)] * len(more),
+            vmem=(low, other, *more),
+            after=(pair,),
+        )
+        if handed:
+            near = over("tensor", handed[0], 1)
         step *= 2
-    low_last = down_block([last], (sq,), (low,))
+    (base,) = call(
+        functools.partial(base_sum_kernel, len(tops)),
+        "base_sum",
+        [shape((rows, cols), F32)],
+        vmem=(base, *tops),
+        after=(low,),
+    )
+    low_last = down_block(last, (sq,), (base,))
     last_parts = [low_last] + [over("tensor", low_last, k) for k in range(n_tensor - 1, 0, -1)]
     ups = up_block(first, [low, other], False, (low_last,))
     deltas = [u if k == 0 else over("wide", u, k) for k, u in zip(first, ups)]
-    up, square = up_block([last], last_parts, True, (ups[0],))
-    delta = over("wide", up, last)
+    pair, bottoms = pair_sums(rows // 2, (ups[0],))
+    *ups, square = up_block(last, last_parts, True, (pair,))
+    last_deltas = [over("wide", u, k) for k, u in zip(last, ups)]
     total, scale = call(
-        functools.partial(gather_kernel, 1 + len(pairs), len(first)),
+        functools.partial(gather_kernel, len(bottoms), len(first)),
         "gather",
         [shape((rows, cols), F32), shape((rows, HEAD), F32)],
-        vmem=(square, base, *pairs, *deltas, *[sels[k] for k in first]),
-        after=(up,),
+        vmem=(square, base, near, *bottoms, *deltas, *[sels[k] for k in first]),
+        after=(ups[0],),
         flops=2 * rows * cols * HEAD * len(first),
     )
     return call(
-        finish_kernel,
+        functools.partial(finish_kernel, len(last)),
         "finish",
         [shape((rows, cols), BF16)],
-        vmem=(total, scale, delta, sels[last], cosine, sine),
+        vmem=(total, scale, cosine, sine, *last_deltas, *[sels[k] for k in last]),
         flops=2 * rows * cols * HEAD,
     )[0]
 

time: 56.6 us -> 53.4 us (0.943)
  waiting for transfers between devices: 17.9 us -> 14.8 us
  Pallas kernels: 19.1 us -> 16.2 us
  starting transfers between devices: 17.7 us -> 20.6 us
    ppermute x14 -> x15, waiting for transfers between devices: 17.9 us -> 14.8 us  [over(): return lax.ppermute(array, axis, [(i, i ^ k) for i in range(size)])]
    pallas_call x13 -> x14, Pallas kernels: 19.1 us -> 16.2 us  [call(): pl.pallas_call(body, out_shape=outs, in_specs=[pl.BlockSpec(memory_space=...]
    ppermute x14 -> x15, starting transfers between devices: 17.7 us -> 20.6 us  [over(): return lax.ppermute(array, axis, [(i, i ^ k) for i in range(size)])]
  transfers between devices with their start and end apart: 14 -> 15, of which waited for: 6 -> 6; matrix products, arithmetic and copies ran while one was open for 1% -> 1% of each run, Pallas kernels for 27% -> 22%
where the time goes in v1:
time: 53.4 us; the launch traced here: 53.2 us
  starting transfers between devices  20.6 us (39%)
  Pallas kernels  16.2 us (30%)
  waiting for transfers between devices  14.8 us (28%)
  local copies, waits for them, and re-layouts  0.73 us (1%)
  other arithmetic  0.68 us (1%)
    ppermute x15, starting transfers between devices, over(): return lax.ppermute(array, axis, [(i, i ^ k) for i in range(size)])  20.6 us
    pallas_call x14, Pallas kernels, call(): pl.pallas_call(body, out_shape=outs, in_specs=[pl.BlockSpec(memory_space=...  16.2 us
    ppermute x15, waiting for transfers between devices, over(): return lax.ppermute(array, axis, [(i, i ^ k) for i in range(size)])  14.8 us
  transfers between devices with their start and end apart: 15, of which 6 were waited for; matrix products, arithmetic and copies ran while one was open for 1% of the time, Pallas kernels for 22%

profile of v1, /device:TPU:0, one launch (start us, length us, event | category | flops | bytes accessed | tf_op | source)
XLA Modules:
  0.0 53.2 jit_solution(9842875704896915345)
XLA Ops:
  0.0 3.5 %dispatch.1 = (bf16[112,2048]{1,0:T(8,128)(2,1)}, bf16[112,2048]{1,0:T(8,128)(2,1)}, bf16[112,2048]{1,0:T(8,128)(2,1)}, bf16[112,2048]{1,0:T(8,128)(2,1)}, f32[16,128]{1,0:T(8,128)}) custom-call(s32[1,256]{1,0:T(1,128)} %bitcast.2, s32[32]{0:T(128)} %refs_1_.7, bf16[256,2048]{1,0:T(8,128)(2,1)} %refs_2_.5, bf16[16,128]{1,0:T(8,128)(2,1)} %bitcast.4), custom_call_target="tpu_custom_call" | custom-call | flops 469762048 | bytes 4194304 | tf_op jit(solution)/shard_map/dispatch/pallas_call | solution.py:28
  3.5 3.0 %collective-permute-start = (bf16[112,2048]{1,0:T(8,128)(2,1)}, bf16[112,2048]{1,0:T(8,128)(2,1)S(1)}, u32[]{:S(2)}, u32[]{:S(2)}) collective-permute-start(bf16[112,2048]{1,0:T(8,128)(2,1)} %get-tuple-element.28), channel_id=1, source_target_pairs={{0,8},{4,12},{8,0},{12,4},{1,9},{5,13},{9,1},{13,5},{2,10},{6,14},... | collective-permute-start | bytes 1376264 | tf_op jit(solution)/shard_map/ppermute | solution.py:378
  6.7 0.7 %copy-done.4 = f32[16,128]{1,0:T(8,128)S(1)} copy-done((f32[16,128]{1,0:T(8,128)S(1)}, f32[16,128]{1,0:T(8,128)}, u32[]{:S(2)}) %copy-start.4) | copy-done | bytes 8216
  7.4 4.8 %base.1 = (bf16[256,512]{1,0:T(8,128)(2,1)S(1)}, bf16[256,512]{1,0:T(8,128)(2,1)S(1)}, f32[256,512]{1,0:T(8,128)S(1)}, f32[256,512]{1,0:T(8,128)S(1)}) custom-call(f32[16,128]{1,0:T(8,128)S(1)} %copy-done.4, bf16[256,2048]{1,0:T(8,128)(2,1)} %refs_2_.5, bf16[2048,2048]{1,0:T(8,128)(2,1)} %refs_2_.4), custom_call_target="tpu_custom_call" | custom-call | flops 2147483648 | bytes 8388608 | tf_op jit(solution)/shard_map/base/pallas_call | solution.py:28
  12.2 2.1 %collective-permute-start.3 = (bf16[256,512]{1,0:T(8,128)(2,1)S(1)}, bf16[256,512]{1,0:T(8,128)(2,1)S(1)}, u32[]{:S(2)}, u32[]{:S(2)}) collective-permute-start(bf16[256,512]{1,0:T(8,128)(2,1)S(1)} %get-tuple-element.36), channel_id=1, source_target_pairs={{0,1},{1,0},{2,3},{3,2},{4,5},{5,4},{6,7},{7,6},{8,9},{9,8},{10,11... | collective-permute-start | bytes 786440 | tf_op jit(solution)/shard_map/ppermute | solution.py:378
  14.9 2.0 %scaled_down.1.refs_2_ = bf16[2048,1024]{1,0:T(8,128)(2,1)S(1)} custom-call(f32[16,128]{1,0:T(8,128)S(1)} %copy-done.4, bf16[8,2048,128]{2,1,0:T(8,128)(2,1)S(1)} %copy-done, f32[256,512]{1,0:T(8,128)S(1)} %get-tuple-element.31.refs_2_.refs_0_), custom_call_target="tpu_custom_call" | custom-call | flops 8388608 | bytes 8388608 | tf_op jit(solution)/shard_map/scaled_down/pallas_call | solution.py:28
  17.0 1.1 %down_block.2.refs_3_.refs_0_ = bf16[2,112,128]{2,1,0:T(8,128)(2,1)S(1)} custom-call(bf16[112,2048]{1,0:T(8,128)(2,1)S(1)} %copy-done.3, bf16[112,2048]{1,0:T(8,128)(2,1)S(1)} %collective-permute-done.2.refs_1_, bf16[2048,1024]{1,0:T(8,128)(2,1)S(1)} %scaled_down.1.refs_2_), custom_call_target="tpu_custom_call" | custom-call | flops 939524096 | bytes 4194304 | tf_op jit(solution)/shard_map/down_block/pallas_call | solution.py:28
  18.2 1.1 %aux.1 = (f32[8,128]{1,0:T(8,128)S(1)}, bf16[256,128]{1,0:T(8,128)(2,1)S(1)}, bf16[256,128]{1,0:T(8,128)(2,1)S(1)}, bf16[256,128]{1,0:T(8,128)(2,1)S(1)}, bf16[256,128]{1,0:T(8,128)(2,1)S(1)}) custom-call(s32[1,256]{1,0:T(1,128)S(1)} %bitcast.3, s32[32]{0:T(128)S(1)} %copy-done.6, bf16[256,2048]{1,0:T(8,128)(2,1)S(1)} %copy-done.1, ...), custom_call_target="tpu_custom_call" | custom-call | flops 268435456 | bytes 1048576 | tf_op jit(solution)/shard_map/aux/pallas_call | solution.py:28
  19.3 1.5 %collective-permute-done.3.refs_1_ = bf16[256,512]{1,0:T(8,128)(2,1)S(1)} collective-permute-done((bf16[256,512]{1,0:T(8,128)(2,1)S(1)}, bf16[256,512]{1,0:T(8,128)(2,1)S(1)}, u32[]{:S(2)}, u32[]{:S(2)}) %collective-permute-start.3) | collective-permute-done | bytes 262176 | tf_op jit(solution)/shard_map/ppermute | solution.py:378
  20.8 2.8 %collective-permute-start.4 = (bf16[128,512]{1,0:T(8,128)(2,1)S(1)}, bf16[128,512]{1,0:T(8,128)(2,1)S(1)}, u32[]{:S(2)}, u32[]{:S(2)}) collective-permute-start(bf16[128,512]{1,0:T(8,128)(2,1)S(1)} %pair_sums.2.refs_3_), channel_id=1, source_target_pairs={{0,2},{1,3},{2,0},{3,1},{4,6},{5,7},{6,4},{7,5},{8,10},{9,11},{10,... | collective-permute-start | bytes 393224 | tf_op jit(solution)/shard_map/ppermute | solution.py:378
  23.6 1.6 %collective-permute-start.5 = (bf16[2,112,128]{2,1,0:T(8,128)(2,1)S(1)}, bf16[2,112,128]{2,1,0:T(8,128)(2,1)S(1)}, u32[]{:S(2)}, u32[]{:S(2)}) collective-permute-start(bf16[2,112,128]{2,1,0:T(8,128)(2,1)S(1)} %down_block.2.refs_3_.refs_0_), channel_id=1, source_target_pairs={{0,1},{1,0},{2,3},{3,2},{4,5},{5,4},{6,7},{7,6},{8,9},{9,8},{10,11... | collective-permute-start | bytes 172040 | tf_op jit(solution)/shard_map/ppermute | solution.py:378
  25.2 2.6 %collective-permute-done.5.refs_1_ = bf16[2,112,128]{2,1,0:T(8,128)(2,1)S(1)} collective-permute-done((bf16[2,112,128]{2,1,0:T(8,128)(2,1)S(1)}, bf16[2,112,128]{2,1,0:T(8,128)(2,1)S(1)}, u32[]{:S(2)}, u32[]{:S(2)}) %collective-permute-start.5) | collective-permute-done | bytes 57376 | tf_op jit(solution)/shard_map/ppermute | solution.py:378
  27.8 1.6 %collective-permute-start.9 = (bf16[2,112,128]{2,1,0:T(8,128)(2,1)S(1)}, bf16[2,112,128]{2,1,0:T(8,128)(2,1)S(1)}, u32[]{:S(2)}, u32[]{:S(2)}) collective-permute-start(bf16[2,112,128]{2,1,0:T(8,128)(2,1)S(1)} %get-tuple-element.38.refs_2_), channel_id=1, source_target_pairs={{0,2},{1,3},{2,0},{3,1},{4,6},{5,7},{6,4},{7,5},{8,10},{9,11},{10,... | collective-permute-start | bytes 172040 | tf_op jit(solution)/shard_map/ppermute | solution.py:378
  29.4 0.9 %collective-permute-start.10 = (bf16[256,512]{1,0:T(8,128)(2,1)S(1)}, bf16[256,512]{1,0:T(8,128)(2,1)S(1)}, u32[]{:S(2)}, u32[]{:S(2)}) collective-permute-start(bf16[256,512]{1,0:T(8,128)(2,1)S(1)} %get-tuple-element.41), channel_id=1, source_target_pairs={{0,1},{1,0},{2,3},{3,2},{4,5},{5,4},{6,7},{7,6},{8,9},{9,8},{10,11... | collective-permute-start | bytes 786440 | tf_op jit(solution)/shard_map/ppermute | solution.py:378
  30.4 1.2 %down_block.3.refs_5_.refs_2_ = bf16[2,112,128]{2,1,0:T(8,128)(2,1)S(1)} custom-call(bf16[112,2048]{1,0:T(8,128)(2,1)S(1)} %collective-permute-done.refs_0_, bf16[112,2048]{1,0:T(8,128)(2,1)S(1)} %collective-permute-done.1.refs_1_, bf16[2048,1024]{1,0:T(8,128)(2,1)S(1)} %scaled_down.1.refs_2_, f32[8,128]{1,0:T(8,128)S(1)} %get-tuple-element.34.refs_2_.refs_3_, ...), custom_call_target="tpu_custom_call" | custom-call | flops 939524096 | bytes 4194304 | tf_op jit(solution)/shard_map/down_block/pallas_call | solution.py:28
  31.6 3.8 %collective-permute-start.6 = (bf16[2,112,128]{2,1,0:T(8,128)(2,1)S(1)}, bf16[2,112,128]{2,1,0:T(8,128)(2,1)S(1)}, u32[]{:S(2)}, u32[]{:S(2)}) collective-permute-start(bf16[2,112,128]{2,1,0:T(8,128)(2,1)S(1)} %down_block.3.refs_5_.refs_2_), channel_id=1, source_target_pairs={{0,3},{1,2},{2,1},{3,0},{4,7},{5,6},{6,5},{7,4},{8,11},{9,10},{10,... | collective-permute-start | bytes 172040 | tf_op jit(solution)/shard_map/ppermute | solution.py:378
  35.4 0.6 %collective-permute-start.8 = (bf16[2,112,128]{2,1,0:T(8,128)(2,1)S(1)}, bf16[2,112,128]{2,1,0:T(8,128)(2,1)S(1)}, u32[]{:S(2)}, u32[]{:S(2)}) collective-permute-start(bf16[2,112,128]{2,1,0:T(8,128)(2,1)S(1)} %down_block.3.refs_5_.refs_2_), channel_id=1, source_target_pairs={{0,1},{1,0},{2,3},{3,2},{4,5},{5,4},{6,7},{7,6},{8,9},{9,8},{10,11... | collective-permute-start | bytes 172040 | tf_op jit(solution)/shard_map/ppermute | solution.py:378
  36.7 2.4 %collective-permute-start.11 = (bf16[128,512]{1,0:T(8,128)(2,1)S(1)}, bf16[128,512]{1,0:T(8,128)(2,1)S(1)}, u32[]{:S(2)}, u32[]{:S(2)}) collective-permute-start(bf16[128,512]{1,0:T(8,128)(2,1)S(1)} %pair_sums.3.refs_7_), channel_id=1, source_target_pairs={{0,2},{1,3},{2,0},{3,1},{4,6},{5,7},{6,4},{7,5},{8,10},{9,11},{10,... | collective-permute-start | bytes 393224 | tf_op jit(solution)/shard_map/ppermute | solution.py:378
  39.0 1.1 %collective-permute-done.6.refs_3_ = bf16[2,112,128]{2,1,0:T(8,128)(2,1)S(1)} collective-permute-done((bf16[2,112,128]{2,1,0:T(8,128)(2,1)S(1)}, bf16[2,112,128]{2,1,0:T(8,128)(2,1)S(1)}, u32[]{:S(2)}, u32[]{:S(2)}) %collective-permute-start.6) | collective-permute-done | bytes 57376 | tf_op jit(solution)/shard_map/ppermute | solution.py:378
  40.1 4.5 %collective-permute-done.7.refs_4_ = bf16[2,112,128]{2,1,0:T(8,128)(2,1)S(1)} collective-permute-done((bf16[2,112,128]{2,1,0:T(8,128)(2,1)S(1)}, bf16[2,112,128]{2,1,0:T(8,128)(2,1)S(1)}, u32[]{:S(2)}, u32[]{:S(2)}) %collective-permute-start.7) | collective-permute-done | bytes 57376 | tf_op jit(solution)/shard_map/ppermute | solution.py:378
  45.2 1.6 %collective-permute-start.13 = (bf16[112,512]{1,0:T(8,128)(2,1)S(1)}, bf16[112,512]{1,0:T(8,128)(2,1)S(1)}, u32[]{:S(2)}, u32[]{:S(2)}) collective-permute-start(bf16[112,512]{1,0:T(8,128)(2,1)S(1)} %get-tuple-element.45.refs_8_), channel_id=1, source_target_pairs={{0,8},{4,12},{8,0},{12,4},{1,9},{5,13},{9,1},{13,5},{2,10},{6,14},... | collective-permute-start | bytes 344072 | tf_op jit(solution)/shard_map/ppermute | solution.py:378
  47.0 3.3 %collective-permute-done.13.refs_4_ = bf16[112,512]{1,0:T(8,128)(2,1)S(1)} collective-permute-done((bf16[112,512]{1,0:T(8,128)(2,1)S(1)}, bf16[112,512]{1,0:T(8,128)(2,1)S(1)}, u32[]{:S(2)}, u32[]{:S(2)}) %collective-permute-start.13) | collective-permute-done | bytes 114720 | tf_op jit(solution)/shard_map/ppermute | solution.py:378
  50.4 1.8 %collective-permute-done.14.refs_5_ = bf16[112,512]{1,0:T(8,128)(2,1)S(1)} collective-permute-done((bf16[112,512]{1,0:T(8,128)(2,1)S(1)}, bf16[112,512]{1,0:T(8,128)(2,1)S(1)}, u32[]{:S(2)}, u32[]{:S(2)}) %collective-permute-start.14) | collective-permute-done | bytes 114720 | tf_op jit(solution)/shard_map/ppermute | solution.py:378
  52.2 1.0 %finish.1 = bf16[256,512]{1,0:T(8,128)(2,1)} custom-call(f32[256,512]{1,0:T(8,128)S(1)} %get-tuple-element.46.refs_0_, f32[256,128]{1,0:T(8,128)S(1)} %get-tuple-element.47.refs_1_, f32[256,128]{1,0:T(8,128)S(1)} %get-tuple-element.54.refs_3_.refs_2_, f32[256,128]{1,0:T(8,128)S(1)} %get-tuple-element.55.refs_4_.refs_3_, ...), custom_call_target="tpu_custom_call" | custom-call | flops 33554432 | tf_op jit(solution)/shard_map/finish/pallas_call | solution.py:28
  (40 shorter events, 2.5 us)
Async XLA Ops:
  3.5 26.9 %collective-permute-start = (bf16[112,2048]{1,0:T(8,128)(2,1)}, bf16[112,2048]{1,0:T(8,128)(2,1)S(1)}, u32[]{:S(2)}, u32[]{:S(2)}) collective-permute-start(bf16[112,2048]{1,0:T(8,128)(2,1)} %get-tuple-element.28), channel_id=1, source_target_pairs={{0,8},{4,12},{8,0},{12,4},{1,9},{5,13},{9,1},{13,5},{2,10},{6,14},... | collective-permute-start | bytes 1376264 | tf_op jit(solution)/shard_map/ppermute | solution.py:378
  6.5 23.9 %collective-permute-start.1 = (bf16[112,2048]{1,0:T(8,128)(2,1)}, bf16[112,2048]{1,0:T(8,128)(2,1)S(1)}, u32[]{:S(2)}, u32[]{:S(2)}) collective-permute-start(bf16[112,2048]{1,0:T(8,128)(2,1)} %get-tuple-element.29), channel_id=1, source_target_pairs={{0,12},{4,8},{8,4},{12,0},{1,13},{5,9},{9,5},{13,1},{2,14},{6,10},... | collective-permute-start | bytes 1376264 | tf_op jit(solution)/shard_map/ppermute | solution.py:378
  6.5 10.5 %collective-permute-start.2 = (bf16[112,2048]{1,0:T(8,128)(2,1)}, bf16[112,2048]{1,0:T(8,128)(2,1)S(1)}, u32[]{:S(2)}, u32[]{:S(2)}) collective-permute-start(bf16[112,2048]{1,0:T(8,128)(2,1)} %get-tuple-element.33), channel_id=1, source_target_pairs={{0,4},{4,0},{8,12},{12,8},{1,5},{5,1},{9,13},{13,9},{2,6},{6,2},{1... | collective-permute-start | bytes 1376264 | tf_op jit(solution)/shard_map/ppermute | solution.py:378
  6.7 0.7 %copy-start.4 = (f32[16,128]{1,0:T(8,128)S(1)}, f32[16,128]{1,0:T(8,128)}, u32[]{:S(2)}) copy-start(f32[16,128]{1,0:T(8,128)} %get-tuple-element.30.refs_0_) | copy-start | bytes 24580
  7.4 6.9 %copy-start.7 = (s32[256]{0:T(256)S(1)}, s32[256]{0:T(256)}, u32[]{:S(2)}) copy-start(s32[256]{0:T(256)} %param.15) | copy-start | bytes 3076
  7.4 7.5 %copy-start = (bf16[8,2048,128]{2,1,0:T(8,128)(2,1)S(1)}, bf16[8,2048,128]{2,1,0:T(8,128)(2,1)}, u32[]{:S(2)}) copy-start(bf16[8,2048,128]{2,1,0:T(8,128)(2,1)} %refs_1_.6) | copy-start | bytes 12582916
  12.2 8.6 %collective-permute-start.3 = (bf16[256,512]{1,0:T(8,128)(2,1)S(1)}, bf16[256,512]{1,0:T(8,128)(2,1)S(1)}, u32[]{:S(2)}, u32[]{:S(2)}) collective-permute-start(bf16[256,512]{1,0:T(8,128)(2,1)S(1)} %get-tuple-element.36), channel_id=1, source_target_pairs={{0,1},{1,0},{2,3},{3,2},{4,5},{5,4},{6,7},{7,6},{8,9},{9,8},{10,11... | collective-permute-start | bytes 786440 | tf_op jit(solution)/shard_map/ppermute | solution.py:378
  14.9 2.2 %copy-start.3 = (bf16[112,2048]{1,0:T(8,128)(2,1)S(1)}, bf16[112,2048]{1,0:T(8,128)(2,1)}, u32[]{:S(2)}) copy-start(bf16[112,2048]{1,0:T(8,128)(2,1)} %get-tuple-element.32.refs_0_) | copy-start | bytes 1376260
  16.8 1.4 %copy-start.1 = (bf16[256,2048]{1,0:T(8,128)(2,1)S(1)}, bf16[256,2048]{1,0:T(8,128)(2,1)}, u32[]{:S(2)}) copy-start(bf16[256,2048]{1,0:T(8,128)(2,1)} %refs_2_.5) | copy-start | bytes 3145732
  16.9 1.4 %copy-start.5 = (s32[256]{0:T(256)S(1)}, s32[256]{0:T(256)}, u32[]{:S(2)}) copy-start(s32[256]{0:T(256)} %param.13) | copy-start | bytes 3076
  16.9 1.4 %copy-start.6 = (s32[32]{0:T(128)S(1)}, s32[32]{0:T(128)}, u32[]{:S(2)}) copy-start(s32[32]{0:T(128)} %refs_1_.7) | copy-start | bytes 388
  20.8 15.2 %copy-start.2 = (bf16[8,64,512]{2,1,0:T(8,128)(2,1)S(1)}, bf16[8,64,512]{2,1,0:T(8,128)(2,1)}, u32[]{:S(2)}) copy-start(bf16[8,64,512]{2,1,0:T(8,128)(2,1)} %refs_6_.1) | copy-start | bytes 1572868
  20.8 9.5 %collective-permute-start.4 = (bf16[128,512]{1,0:T(8,128)(2,1)S(1)}, bf16[128,512]{1,0:T(8,128)(2,1)S(1)}, u32[]{:S(2)}, u32[]{:S(2)}) collective-permute-start(bf16[128,512]{1,0:T(8,128)(2,1)S(1)} %pair_sums.2.refs_3_), channel_id=1, source_target_pairs={{0,2},{1,3},{2,0},{3,1},{4,6},{5,7},{6,4},{7,5},{8,10},{9,11},{10,... | collective-permute-start | bytes 393224 | tf_op jit(solution)/shard_map/ppermute | solution.py:378
  23.6 4.2 %collective-permute-start.5 = (bf16[2,112,128]{2,1,0:T(8,128)(2,1)S(1)}, bf16[2,112,128]{2,1,0:T(8,128)(2,1)S(1)}, u32[]{:S(2)}, u32[]{:S(2)}) collective-permute-start(bf16[2,112,128]{2,1,0:T(8,128)(2,1)S(1)} %down_block.2.refs_3_.refs_0_), channel_id=1, source_target_pairs={{0,1},{1,0},{2,3},{3,2},{4,5},{5,4},{6,7},{7,6},{8,9},{9,8},{10,11... | collective-permute-start | bytes 172040 | tf_op jit(solution)/shard_map/ppermute | solution.py:378
  27.8 8.2 %collective-permute-start.9 = (bf16[2,112,128]{2,1,0:T(8,128)(2,1)S(1)}, bf16[2,112,128]{2,1,0:T(8,128)(2,1)S(1)}, u32[]{:S(2)}, u32[]{:S(2)}) collective-permute-start(bf16[2,112,128]{2,1,0:T(8,128)(2,1)S(1)} %get-tuple-element.38.refs_2_), channel_id=1, source_target_pairs={{0,2},{1,3},{2,0},{3,1},{4,6},{5,7},{6,4},{7,5},{8,10},{9,11},{10,... | collective-permute-start | bytes 172040 | tf_op jit(solution)/shard_map/ppermute | solution.py:378
  29.4 17.4 %collective-permute-start.10 = (bf16[256,512]{1,0:T(8,128)(2,1)S(1)}, bf16[256,512]{1,0:T(8,128)(2,1)S(1)}, u32[]{:S(2)}, u32[]{:S(2)}) collective-permute-start(bf16[256,512]{1,0:T(8,128)(2,1)S(1)} %get-tuple-element.41), channel_id=1, source_target_pairs={{0,1},{1,0},{2,3},{3,2},{4,5},{5,4},{6,7},{7,6},{8,9},{9,8},{10,11... | collective-permute-start | bytes 786440 | tf_op jit(solution)/shard_map/ppermute | solution.py:378
  31.6 8.6 %collective-permute-start.6 = (bf16[2,112,128]{2,1,0:T(8,128)(2,1)S(1)}, bf16[2,112,128]{2,1,0:T(8,128)(2,1)S(1)}, u32[]{:S(2)}, u32[]{:S(2)}) collective-permute-start(bf16[2,112,128]{2,1,0:T(8,128)(2,1)S(1)} %down_block.3.refs_5_.refs_2_), channel_id=1, source_target_pairs={{0,3},{1,2},{2,1},{3,0},{4,7},{5,6},{6,5},{7,4},{8,11},{9,10},{10,... | collective-permute-start | bytes 172040 | tf_op jit(solution)/shard_map/ppermute | solution.py:378
  35.4 9.2 %collective-permute-start.7 = (bf16[2,112,128]{2,1,0:T(8,128)(2,1)S(1)}, bf16[2,112,128]{2,1,0:T(8,128)(2,1)S(1)}, u32[]{:S(2)}, u32[]{:S(2)}) collective-permute-start(bf16[2,112,128]{2,1,0:T(8,128)(2,1)S(1)} %down_block.3.refs_5_.refs_2_), channel_id=1, source_target_pairs={{0,2},{1,3},{2,0},{3,1},{4,6},{5,7},{6,4},{7,5},{8,10},{9,11},{10,... | collective-permute-start | bytes 172040 | tf_op jit(solution)/shard_map/ppermute | solution.py:378
  35.4 9.2 %collective-permute-start.8 = (bf16[2,112,128]{2,1,0:T(8,128)(2,1)S(1)}, bf16[2,112,128]{2,1,0:T(8,128)(2,1)S(1)}, u32[]{:S(2)}, u32[]{:S(2)}) collective-permute-start(bf16[2,112,128]{2,1,0:T(8,128)(2,1)S(1)} %down_block.3.refs_5_.refs_2_), channel_id=1, source_target_pairs={{0,1},{1,0},{2,3},{3,2},{4,5},{5,4},{6,7},{7,6},{8,9},{9,8},{10,11... | collective-permute-start | bytes 172040 | tf_op jit(solution)/shard_map/ppermute | solution.py:378
  36.7 10.1 %collective-permute-start.11 = (bf16[128,512]{1,0:T(8,128)(2,1)S(1)}, bf16[128,512]{1,0:T(8,128)(2,1)S(1)}, u32[]{:S(2)}, u32[]{:S(2)}) collective-permute-start(bf16[128,512]{1,0:T(8,128)(2,1)S(1)} %pair_sums.3.refs_7_), channel_id=1, source_target_pairs={{0,2},{1,3},{2,0},{3,1},{4,6},{5,7},{6,4},{7,5},{8,10},{9,11},{10,... | collective-permute-start | bytes 393224 | tf_op jit(solution)/shard_map/ppermute | solution.py:378
  40.1 6.6 %collective-permute-start.12 = (bf16[112,512]{1,0:T(8,128)(2,1)S(1)}, bf16[112,512]{1,0:T(8,128)(2,1)S(1)}, u32[]{:S(2)}, u32[]{:S(2)}) collective-permute-start(bf16[112,512]{1,0:T(8,128)(2,1)S(1)} %get-tuple-element.42), channel_id=1, source_target_pairs={{0,4},{4,0},{8,12},{12,8},{1,5},{5,1},{9,13},{13,9},{2,6},{6,2},{1... | collective-permute-start | bytes 344072 | tf_op jit(solution)/shard_map/ppermute | solution.py:378
  45.2 5.2 %collective-permute-start.13 = (bf16[112,512]{1,0:T(8,128)(2,1)S(1)}, bf16[112,512]{1,0:T(8,128)(2,1)S(1)}, u32[]{:S(2)}, u32[]{:S(2)}) collective-permute-start(bf16[112,512]{1,0:T(8,128)(2,1)S(1)} %get-tuple-element.45.refs_8_), channel_id=1, source_target_pairs={{0,8},{4,12},{8,0},{12,4},{1,9},{5,13},{9,1},{13,5},{2,10},{6,14},... | collective-permute-start | bytes 344072 | tf_op jit(solution)/shard_map/ppermute | solution.py:378
  46.8 5.4 %collective-permute-start.14 = (bf16[112,512]{1,0:T(8,128)(2,1)S(1)}, bf16[112,512]{1,0:T(8,128)(2,1)S(1)}, u32[]{:S(2)}, u32[]{:S(2)}) collective-permute-start(bf16[112,512]{1,0:T(8,128)(2,1)S(1)} %get-tuple-element.48), channel_id=1, source_target_pairs={{0,12},{4,8},{8,4},{12,0},{1,13},{5,9},{9,5},{13,1},{2,14},{6,10},... | collective-permute-start | bytes 344072 | tf_op jit(solution)/shard_map/ppermute | solution.py:378

commit v2 on v1

--- a/solution.py
+++ b/solution.py
@@ -229,7 +229,8 @@
             if height > cap + 8:
                 tail.append(jnp.zeros((height - cap - 8, rank), F32))
             part = part + jnp.concatenate(tail, axis=0)
-        out_ref[j] = part.astype(BF16)
+        for i in range(j, out_ref.shape[0], count):
+            out_ref[i] = part.astype(BF16)
 
 
 def low_sum_kernel(left_ref, right_ref, *refs):
@@ -257,10 +258,8 @@
     up = up_ref[...].reshape(per_dev * half, cols)
     sums = []
     for j in range(count):
-        low = parts[0][j].astype(F32)
-        for part in parts[1:]:
-            low = low + part[j].astype(F32)
-        sums.append(low)
+        terms = [part[i].astype(F32) for part in parts for i in range(j, part.shape[0], count)]
+        sums.append(sum(terms[1:], terms[0]))
     if with_sq:
         outs[count][...] = sums[0][cap : cap + 8]
     low = jnp.concatenate(sums, axis=0) if count > 1 else sums[0]
@@ -463,12 +462,12 @@
         )
         return pairs[-1], [over("tensor", p, k) for p, k in zip(pairs, twos)]
 
-    def down_block(group, extra, after):
+    def down_block(group, extra, after, copies=1):
         xs = [held[k] for k in group]
         (low,) = call(
             functools.partial(down_kernel, len(xs), cap, bool(extra)),
             "down_block",
-            [shape((len(xs), height, rank), BF16)],
+            [shape((copies * len(xs), height, rank), BF16)],
             vmem=(*xs, down, *extra),
             after=after,
             flops=2 * len(xs) * height * depth * rank * per_dev,
@@ -526,9 +525,9 @@
         vmem=(base, *tops),
         after=(low,),
     )
-    low_last = down_block(last, (sq,), (base,))
-    last_parts = [low_last] + [over("tensor", low_last, k) for k in range(n_tensor - 1, 0, -1)]
-    ups = up_block(first, [low, other], False, (low_last,))
+    low_last = down_block(last, (sq,), (base,), n_tensor)
+    last_parts = [lax.all_to_all(low_last, "tensor", 0, 0, tiled=True)]
+    ups = up_block(first, [low, other], False, (last_parts[0],))
     deltas = [u if k == 0 else over("wide", u, k) for k, u in zip(first, ups)]
     pair, bottoms = pair_sums(rows // 2, (ups[0],))
     *ups, square = up_block(last, last_parts, True, (pair,))

time: 53.4 us -> 62.8 us (1.18)
  local copies, waits for them, and re-layouts: 0.73 us -> 4.14 us
  starting transfers between devices: 20.6 us -> 23.9 us
  waiting for transfers between devices: 14.8 us -> 16.3 us
  Pallas kernels: 16.2 us -> 17.1 us
    all_to_all x0 -> x1, starting transfers between devices: none -> 4.55 us  [local(): last_parts = [lax.all_to_all(low_last, 'tensor', 0, 0, tiled=True)]]
    unnamed x16 -> x44, local copies, waits for them, and re-layouts: 0.73 us -> 4.14 us
    ppermute x15 -> x12, waiting for transfers between devices: 14.8 us -> 16.3 us  [over(): return lax.ppermute(array, axis, [(i, i ^ k) for i in range(size)])]
    ppermute x15 -> x12, starting transfers between devices: 20.6 us -> 19.4 us  [over(): return lax.ppermute(array, axis, [(i, i ^ k) for i in range(size)])]
    pallas_call x14, Pallas kernels: 16.2 us -> 17.1 us  [call(): pl.pallas_call(body, out_shape=outs, in_specs=[pl.BlockSpec(memory_space=...]
  transfers between devices with their start and end apart: 15 -> 13, of which waited for: 6 -> 7; matrix products, arithmetic and copies ran while one was open for 1% -> 1% of each run, Pallas kernels for 22% -> 18%
where the time goes in v2:
time: 62.8 us; the launch traced here: 62.5 us
  starting transfers between devices  23.9 us (38%)
  Pallas kernels  17.1 us (27%)
  waiting for transfers between devices  16.3 us (26%)
  local copies, waits for them, and re-layouts  4.14 us (7%)
  other arithmetic  0.68 us (1%)
    ppermute x12, starting transfers between devices, over(): return lax.ppermute(array, axis, [(i, i ^ k) for i in range(size)])  19.4 us
    pallas_call x14, Pallas kernels, call(): pl.pallas_call(body, out_shape=outs, in_specs=[pl.BlockSpec(memory_space=...  17.1 us
    ppermute x12, waiting for transfers between devices, over(): return lax.ppermute(array, axis, [(i, i ^ k) for i in range(size)])  16.3 us
    all_to_all x1, starting transfers between devices, local(): last_parts = [lax.all_to_all(low_last, 'tensor', 0, 0, tiled=True)]  4.55 us
    unnamed x44, local copies, waits for them, and re-layouts  4.14 us
  transfers between devices with their start and end apart: 13, of which 7 were waited for; matrix products, arithmetic and copies ran while one was open for 1% of the time, Pallas kernels for 18%

profile of v2, /device:TPU:0, one launch (start us, length us, event | category | flops | bytes accessed | tf_op | source)
XLA Modules:
  0.0 62.5 jit_solution(10566076125461203330)
XLA Ops:
  0.0 3.5 %dispatch.1 = (bf16[112,2048]{1,0:T(8,128)(2,1)}, bf16[112,2048]{1,0:T(8,128)(2,1)}, bf16[112,2048]{1,0:T(8,128)(2,1)}, bf16[112,2048]{1,0:T(8,128)(2,1)}, f32[16,128]{1,0:T(8,128)}) custom-call(s32[1,256]{1,0:T(1,128)} %bitcast.2, s32[32]{0:T(128)} %refs_1_.7, bf16[256,2048]{1,0:T(8,128)(2,1)} %refs_2_.5, bf16[16,128]{1,0:T(8,128)(2,1)} %bitcast.4), custom_call_target="tpu_custom_call" | custom-call | flops 469762048 | bytes 4194304 | tf_op jit(solution)/shard_map/dispatch/pallas_call | solution.py:28
  3.5 3.0 %collective-permute-start = (bf16[112,2048]{1,0:T(8,128)(2,1)}, bf16[112,2048]{1,0:T(8,128)(2,1)S(1)}, u32[]{:S(2)}, u32[]{:S(2)}) collective-permute-start(bf16[112,2048]{1,0:T(8,128)(2,1)} %get-tuple-element.28), channel_id=1, source_target_pairs={{0,8},{4,12},{8,0},{12,4},{1,9},{5,13},{9,1},{13,5},{2,10},{6,14},... | collective-permute-start | bytes 1376264 | tf_op jit(solution)/shard_map/ppermute | solution.py:377
  7.4 4.8 %base.1 = (bf16[256,512]{1,0:T(8,128)(2,1)S(1)}, bf16[256,512]{1,0:T(8,128)(2,1)S(1)}, f32[256,512]{1,0:T(8,128)S(1)}, f32[256,512]{1,0:T(8,128)S(1)}) custom-call(f32[16,128]{1,0:T(8,128)S(1)} %copy-done.17, bf16[256,2048]{1,0:T(8,128)(2,1)} %refs_2_.5, bf16[2048,2048]{1,0:T(8,128)(2,1)} %refs_2_.4), custom_call_target="tpu_custom_call" | custom-call | flops 2147483648 | bytes 8388608 | tf_op jit(solution)/shard_map/base/pallas_call | solution.py:28
  12.2 2.1 %collective-permute-start.3 = (bf16[256,512]{1,0:T(8,128)(2,1)S(1)}, bf16[256,512]{1,0:T(8,128)(2,1)S(1)}, u32[]{:S(2)}, u32[]{:S(2)}) collective-permute-start(bf16[256,512]{1,0:T(8,128)(2,1)S(1)} %get-tuple-element.36), channel_id=1, source_target_pairs={{0,1},{1,0},{2,3},{3,2},{4,5},{5,4},{6,7},{7,6},{8,9},{9,8},{10,11... | collective-permute-start | bytes 786440 | tf_op jit(solution)/shard_map/ppermute | solution.py:377
  14.9 1.9 %scaled_down.1.refs_2_ = bf16[2048,1024]{1,0:T(8,128)(2,1)S(1)} custom-call(f32[16,128]{1,0:T(8,128)S(1)} %copy-done.17, bf16[8,2048,128]{2,1,0:T(8,128)(2,1)S(1)} %copy-done, f32[256,512]{1,0:T(8,128)S(1)} %get-tuple-element.31.refs_2_.refs_0_), custom_call_target="tpu_custom_call" | custom-call | flops 8388608 | bytes 8388608 | tf_op jit(solution)/shard_map/scaled_down/pallas_call | solution.py:28
  17.0 1.1 %down_block.2.refs_3_.refs_0_ = bf16[2,112,128]{2,1,0:T(8,128)(2,1)S(1)} custom-call(bf16[112,2048]{1,0:T(8,128)(2,1)S(1)} %copy-done.3, bf16[112,2048]{1,0:T(8,128)(2,1)S(1)} %collective-permute-done.2.refs_1_, bf16[2048,1024]{1,0:T(8,128)(2,1)S(1)} %scaled_down.1.refs_2_), custom_call_target="tpu_custom_call" | custom-call | flops 939524096 | bytes 4194304 | tf_op jit(solution)/shard_map/down_block/pallas_call | solution.py:28
  18.2 1.1 %aux.1 = (f32[8,128]{1,0:T(8,128)S(1)}, bf16[256,128]{1,0:T(8,128)(2,1)S(1)}, bf16[256,128]{1,0:T(8,128)(2,1)S(1)}, bf16[256,128]{1,0:T(8,128)(2,1)S(1)}, bf16[256,128]{1,0:T(8,128)(2,1)S(1)}) custom-call(s32[1,256]{1,0:T(1,128)S(1)} %bitcast.3, s32[32]{0:T(128)S(1)} %copy-done.19, bf16[256,2048]{1,0:T(8,128)(2,1)S(1)} %copy-done.1, ...), custom_call_target="tpu_custom_call" | custom-call | flops 268435456 | bytes 1048576 | tf_op jit(solution)/shard_map/aux/pallas_call | solution.py:28
  19.3 1.4 %collective-permute-done.3.refs_1_ = bf16[256,512]{1,0:T(8,128)(2,1)S(1)} collective-permute-done((bf16[256,512]{1,0:T(8,128)(2,1)S(1)}, bf16[256,512]{1,0:T(8,128)(2,1)S(1)}, u32[]{:S(2)}, u32[]{:S(2)}) %collective-permute-start.3) | collective-permute-done | bytes 262176 | tf_op jit(solution)/shard_map/ppermute | solution.py:377
  21.5 2.7 %collective-permute-start.4 = (bf16[128,512]{1,0:T(8,128)(2,1)S(1)}, bf16[128,512]{1,0:T(8,128)(2,1)S(1)}, u32[]{:S(2)}, u32[]{:S(2)}) collective-permute-start(bf16[128,512]{1,0:T(8,128)(2,1)S(1)} %pair_sums.2.refs_3_), channel_id=1, source_target_pairs={{0,2},{1,3},{2,0},{3,1},{4,6},{5,7},{6,4},{7,5},{8,10},{9,11},{10,... | collective-permute-start | bytes 393224 | tf_op jit(solution)/shard_map/ppermute | solution.py:377
  24.3 1.6 %collective-permute-start.5 = (bf16[2,112,128]{2,1,0:T(8,128)(2,1)S(1)}, bf16[2,112,128]{2,1,0:T(8,128)(2,1)S(1)}, u32[]{:S(2)}, u32[]{:S(2)}) collective-permute-start(bf16[2,112,128]{2,1,0:T(8,128)(2,1)S(1)} %down_block.2.refs_3_.refs_0_), channel_id=1, source_target_pairs={{0,1},{1,0},{2,3},{3,2},{4,5},{5,4},{6,7},{7,6},{8,9},{9,8},{10,11... | collective-permute-start | bytes 172040 | tf_op jit(solution)/shard_map/ppermute | solution.py:377
  25.8 2.6 %collective-permute-done.5.refs_1_ = bf16[2,112,128]{2,1,0:T(8,128)(2,1)S(1)} collective-permute-done((bf16[2,112,128]{2,1,0:T(8,128)(2,1)S(1)}, bf16[2,112,128]{2,1,0:T(8,128)(2,1)S(1)}, u32[]{:S(2)}, u32[]{:S(2)}) %collective-permute-start.5) | collective-permute-done | bytes 57376 | tf_op jit(solution)/shard_map/ppermute | solution.py:377
  28.5 1.7 %collective-permute-done.4.refs_1_ = bf16[128,512]{1,0:T(8,128)(2,1)S(1)} collective-permute-done((bf16[128,512]{1,0:T(8,128)(2,1)S(1)}, bf16[128,512]{1,0:T(8,128)(2,1)S(1)}, u32[]{:S(2)}, u32[]{:S(2)}) %collective-permute-start.4) | collective-permute-done | bytes 131104 | tf_op jit(solution)/shard_map/ppermute | solution.py:377
  30.3 1.2 %down_block.3 = bf16[8,112,128]{2,1,0:T(8,128)(2,1)S(1)} custom-call(bf16[112,2048]{1,0:T(8,128)(2,1)S(1)} %collective-permute-done.refs_0_, bf16[112,2048]{1,0:T(8,128)(2,1)S(1)} %collective-permute-done.1.refs_1_, bf16[2048,1024]{1,0:T(8,128)(2,1)S(1)} %scaled_down.1.refs_2_, f32[8,128]{1,0:T(8,128)S(1)} %get-tuple-element.34.refs_2_.refs_3_, ...), custom_call_target="tpu_custom_call" | custom-call | flops 939524096 | bytes 4194304 | tf_op jit(solution)/shard_map/down_block/pallas_call | solution.py:28
  32.1 4.6 %all-to-all-start = ((bf16[8,112,128]{2,1,0:T(8,128)(2,1)}), bf16[8,112,128]{2,1,0:T(8,128)(2,1)S(1)}, u32[]{:S(2)}, u32[]{:S(2)}) async-start(bf16[8,112,128]{2,1,0:T(8,128)(2,1)} %copy-done.8), calls=%async_computation | async-start | bytes 458752 | tf_op jit(solution)/shard_map/all_to_all | solution.py:529
  36.7 2.0 %collective-permute-start.7 = (bf16[256,512]{1,0:T(8,128)(2,1)}, bf16[256,512]{1,0:T(8,128)(2,1)}, u32[]{:S(2)}, u32[]{:S(2)}) collective-permute-start(bf16[256,512]{1,0:T(8,128)(2,1)} %copy-done.20), channel_id=1, source_target_pairs={{0,1},{1,0},{2,3},{3,2},{4,5},{5,4},{6,7},{7,6},{8,9},{9,8},{10,11... | collective-permute-start | bytes 786440 | tf_op jit(solution)/shard_map/ppermute | solution.py:377
  38.7 2.4 %collective-permute-start.6 = (bf16[2,112,128]{2,1,0:T(8,128)(2,1)S(1)}, bf16[2,112,128]{2,1,0:T(8,128)(2,1)S(1)}, u32[]{:S(2)}, u32[]{:S(2)}) collective-permute-start(bf16[2,112,128]{2,1,0:T(8,128)(2,1)S(1)} %get-tuple-element.38.refs_2_), channel_id=1, source_target_pairs={{0,2},{1,3},{2,0},{3,1},{4,6},{5,7},{6,4},{7,5},{8,10},{9,11},{10,... | collective-permute-start | bytes 172040 | tf_op jit(solution)/shard_map/ppermute | solution.py:377
  41.0 6.0 %collective-permute-done.6.refs_3_ = bf16[2,112,128]{2,1,0:T(8,128)(2,1)S(1)} collective-permute-done((bf16[2,112,128]{2,1,0:T(8,128)(2,1)S(1)}, bf16[2,112,128]{2,1,0:T(8,128)(2,1)S(1)}, u32[]{:S(2)}, u32[]{:S(2)}) %collective-permute-start.6) | collective-permute-done | bytes 57376 | tf_op jit(solution)/shard_map/ppermute | solution.py:377
  47.1 1.0 %copy-done.5 = bf16[112,2048]{1,0:T(8,128)(2,1)S(1)} copy-done((bf16[112,2048]{1,0:T(8,128)(2,1)S(1)}, bf16[112,2048]{1,0:T(8,128)(2,1)}, u32[]{:S(2)}) %copy-start.5) | copy-done | bytes 458776
  49.7 3.4 %collective-permute-start.8 = (bf16[128,512]{1,0:T(8,128)(2,1)S(1)}, bf16[128,512]{1,0:T(8,128)(2,1)S(1)}, u32[]{:S(2)}, u32[]{:S(2)}) collective-permute-start(bf16[128,512]{1,0:T(8,128)(2,1)S(1)} %pair_sums.3.refs_4_), channel_id=1, source_target_pairs={{0,2},{1,3},{2,0},{3,1},{4,6},{5,7},{6,4},{7,5},{8,10},{9,11},{10,... | collective-permute-start | bytes 393224 | tf_op jit(solution)/shard_map/ppermute | solution.py:377
  53.8 1.6 %collective-permute-start.10 = (bf16[112,512]{1,0:T(8,128)(2,1)S(1)}, bf16[112,512]{1,0:T(8,128)(2,1)S(1)}, u32[]{:S(2)}, u32[]{:S(2)}) collective-permute-start(bf16[112,512]{1,0:T(8,128)(2,1)S(1)} %get-tuple-element.45.refs_8_), channel_id=1, source_target_pairs={{0,8},{4,12},{8,0},{12,4},{1,9},{5,13},{9,1},{13,5},{2,10},{6,14},... | collective-permute-start | bytes 344072 | tf_op jit(solution)/shard_map/ppermute | solution.py:377
  55.7 1.8 %collective-permute-done.8.refs_3_ = bf16[128,512]{1,0:T(8,128)(2,1)S(1)} collective-permute-done((bf16[128,512]{1,0:T(8,128)(2,1)S(1)}, bf16[128,512]{1,0:T(8,128)(2,1)S(1)}, u32[]{:S(2)}, u32[]{:S(2)}) %collective-permute-start.8) | collective-permute-done | bytes 131104 | tf_op jit(solution)/shard_map/ppermute | solution.py:377
  57.5 1.2 %gather.1 = (f32[256,512]{1,0:T(8,128)S(1)}, f32[256,128]{1,0:T(8,128)S(1)}) custom-call(f32[8,128]{1,0:T(8,128)S(1)} %get-tuple-element.40.refs_0_, f32[256,512]{1,0:T(8,128)S(1)} %base_sum.1.refs_4_.refs_1_, bf16[256,512]{1,0:T(8,128)(2,1)} %collective-permute-done.7.refs_2_, bf16[128,512]{1,0:T(8,128)(2,1)S(1)} %collective-permute-done.8.refs_3_, ...), custom_call_target="tpu_custom_call" | custom-call | flops 67108864 | tf_op jit(solution)/shard_map/gather/pallas_call | solution.py:28
  58.7 1.1 %collective-permute-done.10.refs_4_ = bf16[112,512]{1,0:T(8,128)(2,1)S(1)} collective-permute-done((bf16[112,512]{1,0:T(8,128)(2,1)S(1)}, bf16[112,512]{1,0:T(8,128)(2,1)S(1)}, u32[]{:S(2)}, u32[]{:S(2)}) %collective-permute-start.10) | collective-permute-done | bytes 114720 | tf_op jit(solution)/shard_map/ppermute | solution.py:377
  59.8 1.7 %collective-permute-done.11.refs_5_ = bf16[112,512]{1,0:T(8,128)(2,1)S(1)} collective-permute-done((bf16[112,512]{1,0:T(8,128)(2,1)S(1)}, bf16[112,512]{1,0:T(8,128)(2,1)S(1)}, u32[]{:S(2)}, u32[]{:S(2)}) %collective-permute-start.11) | collective-permute-done | bytes 114720 | tf_op jit(solution)/shard_map/ppermute | solution.py:377
  (64 shorter events, 6.7 us)
Async XLA Ops:
  3.5 26.7 %collective-permute-start = (bf16[112,2048]{1,0:T(8,128)(2,1)}, bf16[112,2048]{1,0:T(8,128)(2,1)S(1)}, u32[]{:S(2)}, u32[]{:S(2)}) collective-permute-start(bf16[112,2048]{1,0:T(8,128)(2,1)} %get-tuple-element.28), channel_id=1, source_target_pairs={{0,8},{4,12},{8,0},{12,4},{1,9},{5,13},{9,1},{13,5},{2,10},{6,14},... | collective-permute-start | bytes 1376264 | tf_op jit(solution)/shard_map/ppermute | solution.py:377
  6.5 23.7 %collective-permute-start.1 = (bf16[112,2048]{1,0:T(8,128)(2,1)}, bf16[112,2048]{1,0:T(8,128)(2,1)S(1)}, u32[]{:S(2)}, u32[]{:S(2)}) collective-permute-start(bf16[112,2048]{1,0:T(8,128)(2,1)} %get-tuple-element.29), channel_id=1, source_target_pairs={{0,12},{4,8},{8,4},{12,0},{1,13},{5,9},{9,5},{13,1},{2,14},{6,10},... | collective-permute-start | bytes 1376264 | tf_op jit(solution)/shard_map/ppermute | solution.py:377
  6.5 10.5 %collective-permute-start.2 = (bf16[112,2048]{1,0:T(8,128)(2,1)}, bf16[112,2048]{1,0:T(8,128)(2,1)S(1)}, u32[]{:S(2)}, u32[]{:S(2)}) collective-permute-start(bf16[112,2048]{1,0:T(8,128)(2,1)} %get-tuple-element.33), channel_id=1, source_target_pairs={{0,4},{4,0},{8,12},{12,8},{1,5},{5,1},{9,13},{13,9},{2,6},{6,2},{1... | collective-permute-start | bytes 1376264 | tf_op jit(solution)/shard_map/ppermute | solution.py:377
  7.4 7.5 %copy-start = (bf16[8,2048,128]{2,1,0:T(8,128)(2,1)S(1)}, bf16[8,2048,128]{2,1,0:T(8,128)(2,1)}, u32[]{:S(2)}) copy-start(bf16[8,2048,128]{2,1,0:T(8,128)(2,1)} %refs_1_.6) | copy-start | bytes 12582916
  12.2 8.6 %collective-permute-start.3 = (bf16[256,512]{1,0:T(8,128)(2,1)S(1)}, bf16[256,512]{1,0:T(8,128)(2,1)S(1)}, u32[]{:S(2)}, u32[]{:S(2)}) collective-permute-start(bf16[256,512]{1,0:T(8,128)(2,1)S(1)} %get-tuple-element.36), channel_id=1, source_target_pairs={{0,1},{1,0},{2,3},{3,2},{4,5},{5,4},{6,7},{7,6},{8,9},{9,8},{10,11... | collective-permute-start | bytes 786440 | tf_op jit(solution)/shard_map/ppermute | solution.py:377
  17.0 13.2 %copy-start.4 = (bf16[112,2048]{1,0:T(8,128)(2,1)}, bf16[112,2048]{1,0:T(8,128)(2,1)S(1)}, u32[]{:S(2)}) copy-start(bf16[112,2048]{1,0:T(8,128)(2,1)S(1)} %collective-permute-done.2.refs_1_) | copy-start | bytes 1376260
  19.3 10.9 %copy-start.9 = (bf16[256,128]{1,0:T(8,128)(2,1)}, bf16[256,128]{1,0:T(8,128)(2,1)S(1)}, u32[]{:S(2)}) copy-start(bf16[256,128]{1,0:T(8,128)(2,1)S(1)} %get-tuple-element.49.refs_6_) | copy-start | bytes 196612
  19.3 10.9 %copy-start.11 = (bf16[256,128]{1,0:T(8,128)(2,1)}, bf16[256,128]{1,0:T(8,128)(2,1)S(1)}, u32[]{:S(2)}) copy-start(bf16[256,128]{1,0:T(8,128)(2,1)S(1)} %get-tuple-element.50.refs_7_) | copy-start | bytes 196612
  19.3 10.9 %copy-start.13 = (bf16[256,128]{1,0:T(8,128)(2,1)}, bf16[256,128]{1,0:T(8,128)(2,1)S(1)}, u32[]{:S(2)}) copy-start(bf16[256,128]{1,0:T(8,128)(2,1)S(1)} %get-tuple-element.43.refs_6_) | copy-start | bytes 196612
  19.3 10.9 %copy-start.15 = (bf16[256,128]{1,0:T(8,128)(2,1)}, bf16[256,128]{1,0:T(8,128)(2,1)S(1)}, u32[]{:S(2)}) copy-start(bf16[256,128]{1,0:T(8,128)(2,1)S(1)} %get-tuple-element.44.refs_7_) | copy-start | bytes 196612
  21.5 25.5 %copy-start.2 = (bf16[8,64,512]{2,1,0:T(8,128)(2,1)S(1)}, bf16[8,64,512]{2,1,0:T(8,128)(2,1)}, u32[]{:S(2)}) copy-start(bf16[8,64,512]{2,1,0:T(8,128)(2,1)} %refs_3_.1) | copy-start | bytes 1572868
  21.5 8.6 %collective-permute-start.4 = (bf16[128,512]{1,0:T(8,128)(2,1)S(1)}, bf16[128,512]{1,0:T(8,128)(2,1)S(1)}, u32[]{:S(2)}, u32[]{:S(2)}) collective-permute-start(bf16[128,512]{1,0:T(8,128)(2,1)S(1)} %pair_sums.2.refs_3_), channel_id=1, source_target_pairs={{0,2},{1,3},{2,0},{3,1},{4,6},{5,7},{6,4},{7,5},{8,10},{9,11},{10,... | collective-permute-start | bytes 393224 | tf_op jit(solution)/shard_map/ppermute | solution.py:377
  24.3 4.2 %collective-permute-start.5 = (bf16[2,112,128]{2,1,0:T(8,128)(2,1)S(1)}, bf16[2,112,128]{2,1,0:T(8,128)(2,1)S(1)}, u32[]{:S(2)}, u32[]{:S(2)}) collective-permute-start(bf16[2,112,128]{2,1,0:T(8,128)(2,1)S(1)} %down_block.2.refs_3_.refs_0_), channel_id=1, source_target_pairs={{0,1},{1,0},{2,3},{3,2},{4,5},{5,4},{6,7},{7,6},{8,9},{9,8},{10,11... | collective-permute-start | bytes 172040 | tf_op jit(solution)/shard_map/ppermute | solution.py:377
  32.1 15.0 %all-to-all-start = ((bf16[8,112,128]{2,1,0:T(8,128)(2,1)}), bf16[8,112,128]{2,1,0:T(8,128)(2,1)S(1)}, u32[]{:S(2)}, u32[]{:S(2)}) async-start(bf16[8,112,128]{2,1,0:T(8,128)(2,1)} %copy-done.8), calls=%async_computation | async-start | bytes 458752 | tf_op jit(solution)/shard_map/all_to_all | solution.py:529
  36.7 19.0 %collective-permute-start.7 = (bf16[256,512]{1,0:T(8,128)(2,1)}, bf16[256,512]{1,0:T(8,128)(2,1)}, u32[]{:S(2)}, u32[]{:S(2)}) collective-permute-start(bf16[256,512]{1,0:T(8,128)(2,1)} %copy-done.20), channel_id=1, source_target_pairs={{0,1},{1,0},{2,3},{3,2},{4,5},{5,4},{6,7},{7,6},{8,9},{9,8},{10,11... | collective-permute-start | bytes 786440 | tf_op jit(solution)/shard_map/ppermute | solution.py:377
  38.7 8.4 %collective-permute-start.6 = (bf16[2,112,128]{2,1,0:T(8,128)(2,1)S(1)}, bf16[2,112,128]{2,1,0:T(8,128)(2,1)S(1)}, u32[]{:S(2)}, u32[]{:S(2)}) collective-permute-start(bf16[2,112,128]{2,1,0:T(8,128)(2,1)S(1)} %get-tuple-element.38.refs_2_), channel_id=1, source_target_pairs={{0,2},{1,3},{2,0},{3,1},{4,6},{5,7},{6,4},{7,5},{8,10},{9,11},{10,... | collective-permute-start | bytes 172040 | tf_op jit(solution)/shard_map/ppermute | solution.py:377
  48.1 9.4 %copy-start.14 = (bf16[256,128]{1,0:T(8,128)(2,1)S(1)}, bf16[256,128]{1,0:T(8,128)(2,1)}, u32[]{:S(2)}) copy-start(bf16[256,128]{1,0:T(8,128)(2,1)} %copy-done.13) | copy-start | bytes 196612
  48.1 9.4 %copy-start.16 = (bf16[256,128]{1,0:T(8,128)(2,1)S(1)}, bf16[256,128]{1,0:T(8,128)(2,1)}, u32[]{:S(2)}) copy-start(bf16[256,128]{1,0:T(8,128)(2,1)} %copy-done.15) | copy-start | bytes 196612
  48.1 13.4 %copy-start.10 = (bf16[256,128]{1,0:T(8,128)(2,1)S(1)}, bf16[256,128]{1,0:T(8,128)(2,1)}, u32[]{:S(2)}) copy-start(bf16[256,128]{1,0:T(8,128)(2,1)} %copy-done.9) | copy-start | bytes 196612
  48.1 13.4 %copy-start.12 = (bf16[256,128]{1,0:T(8,128)(2,1)S(1)}, bf16[256,128]{1,0:T(8,128)(2,1)}, u32[]{:S(2)}) copy-start(bf16[256,128]{1,0:T(8,128)(2,1)} %copy-done.11) | copy-start | bytes 196612
  49.7 7.8 %collective-permute-start.8 = (bf16[128,512]{1,0:T(8,128)(2,1)S(1)}, bf16[128,512]{1,0:T(8,128)(2,1)S(1)}, u32[]{:S(2)}, u32[]{:S(2)}) collective-permute-start(bf16[128,512]{1,0:T(8,128)(2,1)S(1)} %pair_sums.3.refs_4_), channel_id=1, source_target_pairs={{0,2},{1,3},{2,0},{3,1},{4,6},{5,7},{6,4},{7,5},{8,10},{9,11},{10,... | collective-permute-start | bytes 393224 | tf_op jit(solution)/shard_map/ppermute | solution.py:377
  53.1 2.5 %collective-permute-start.9 = (bf16[112,512]{1,0:T(8,128)(2,1)S(1)}, bf16[112,512]{1,0:T(8,128)(2,1)S(1)}, u32[]{:S(2)}, u32[]{:S(2)}) collective-permute-start(bf16[112,512]{1,0:T(8,128)(2,1)S(1)} %get-tuple-element.42), channel_id=1, source_target_pairs={{0,4},{4,0},{8,12},{12,8},{1,5},{5,1},{9,13},{13,9},{2,6},{6,2},{1... | collective-permute-start | bytes 344072 | tf_op jit(solution)/shard_map/ppermute | solution.py:377
  53.8 6.0 %collective-permute-start.10 = (bf16[112,512]{1,0:T(8,128)(2,1)S(1)}, bf16[112,512]{1,0:T(8,128)(2,1)S(1)}, u32[]{:S(2)}, u32[]{:S(2)}) collective-permute-start(bf16[112,512]{1,0:T(8,128)(2,1)S(1)} %get-tuple-element.45.refs_8_), channel_id=1, source_target_pairs={{0,8},{4,12},{8,0},{12,4},{1,9},{5,13},{9,1},{13,5},{2,10},{6,14},... | collective-permute-start | bytes 344072 | tf_op jit(solution)/shard_map/ppermute | solution.py:377
  55.3 6.1 %collective-permute-start.11 = (bf16[112,512]{1,0:T(8,128)(2,1)S(1)}, bf16[112,512]{1,0:T(8,128)(2,1)S(1)}, u32[]{:S(2)}, u32[]{:S(2)}) collective-permute-start(bf16[112,512]{1,0:T(8,128)(2,1)S(1)} %get-tuple-element.48), channel_id=1, source_target_pairs={{0,12},{4,8},{8,4},{12,0},{1,13},{5,9},{9,5},{13,1},{2,14},{6,10},... | collective-permute-start | bytes 344072 | tf_op jit(solution)/shard_map/ppermute | solution.py:377
  (11 other events, 19.1 us)

commit v3 on v1

--- a/solution.py
+++ b/solution.py
@@ -149,6 +149,22 @@
         out_ref[...] = (refs[j][rows] + refs[count + j][rows].astype(F32)).astype(BF16)
 
 
+def pair_low_kernel(count, near_ref, low_ref, other_ref, *refs):
+    outs, sent_ref = refs[2 * count : -1], refs[-1]
+    cols = refs[0].shape[1]
+    half = refs[0].shape[0] // 2
+    for j in range(count):
+        total = (refs[j][:half] + refs[count + j][:half].astype(F32)).astype(BF16)
+        for h in range(cols // HEAD):
+            outs[j][h * half : (h + 1) * half] = total[:, h * HEAD : (h + 1) * HEAD]
+    base = cols // HEAD * half
+    groups, height, _ = low_ref.shape
+    for i in range(groups):
+        total = low_ref[i].astype(F32) + other_ref[i].astype(F32)
+        outs[0][base + i * height : base + (i + 1) * height] = total.astype(BF16)
+    sent_ref[...] = near_ref[...]
+
+
 def scaled_down_kernel(gain_ref, down_hbm, out_ref, buf, sems):
     per_dev, depth, rank = down_hbm.shape
     copies = [pltpu.make_async_copy(down_hbm.at[a], buf.at[a], sems.at[a]) for a in range(per_dev)]
@@ -232,12 +248,18 @@
         out_ref[j] = part.astype(BF16)
 
 
-def low_sum_kernel(left_ref, right_ref, *refs):
-    out_ref = refs[len(refs) // 2]
-    total = left_ref[...].astype(F32) + right_ref[...].astype(F32)
-    out_ref[...] = total.astype(BF16)
-    if len(refs) > 1:
-        refs[2][...] = refs[0][...]
+def low_term(ref, i, groups, height):
+    if len(ref.shape) == 3:
+        return ref[i].astype(F32)
+    start = ref.shape[0] - (groups - i) * height
+    return ref[start : start + height].astype(F32)
+
+
+def low_sum_kernel(left_ref, right_ref, out_ref):
+    groups, height, _ = out_ref.shape
+    for i in range(groups):
+        left = low_term(left_ref, i, groups, height)
+        out_ref[i] = (left + low_term(right_ref, i, groups, height)).astype(BF16)
 
 
 def head_is_key(heads, h):
@@ -253,14 +275,12 @@
     outs = refs[count + n_parts + 1 :]
     per_dev, half, cols = up_ref.shape
     heads = cols // HEAD
-    height, rank = parts[0].shape[1:]
+    height, rank = outs[0].shape[0], 2 * half
     up = up_ref[...].reshape(per_dev * half, cols)
     sums = []
     for j in range(count):
-        low = parts[0][j].astype(F32)
-        for part in parts[1:]:
-            low = low + part[j].astype(F32)
-        sums.append(low)
+        terms = [low_term(part, j, count, height) for part in parts]
+        sums.append(sum(terms[1:], terms[0]))
     if with_sq:
         outs[count][...] = sums[0][cap : cap + 8]
     low = jnp.concatenate(sums, axis=0) if count > 1 else sums[0]
@@ -298,18 +318,10 @@
     return jnp.dot(lhs, jnp.concatenate(blocks, axis=0), preferred_element_type=F32)
 
 
-def base_sum_kernel(n_pairs, base_ref, *refs):
-    out_ref = refs[n_pairs]
-    half = refs[0].shape[0] if n_pairs else 0
-    out_ref[...] = base_ref[...]
-    for top in refs[:n_pairs]:
-        out_ref[:half] += top[...].astype(F32)
-
-
 def gather_kernel(n_pairs, count, sq_ref, base_ref, near_ref, *refs):
-    bottoms = refs[:n_pairs]
-    deltas = refs[n_pairs : n_pairs + count]
-    sels = refs[n_pairs + count : n_pairs + 2 * count]
+    tops, bottoms = refs[:n_pairs], refs[n_pairs : 2 * n_pairs]
+    deltas = refs[2 * n_pairs : 2 * n_pairs + count]
+    sels = refs[2 * n_pairs + count : 2 * n_pairs + 2 * count]
     out_ref, scale_ref = refs[-2:]
     rows, cols = out_ref.shape
     pieces = rows // HEAD
@@ -323,15 +335,17 @@
     scale = lax.rsqrt(square * (1.0 / MODEL_WIDTH) + EPSILON)
     scale_ref[...] = jnp.broadcast_to(scale, (rows, HEAD))
     total = base_ref[...] + near_ref[...].astype(F32) + placed(sels, deltas)
-    if bottoms:
-        half = rows - bottoms[0].shape[0]
-        lower = total[half:]
-        for bottom in bottoms:
-            lower = lower + bottom[...].astype(F32)
-        out_ref[:half] = total[:half]
-        out_ref[half:] = lower
-    else:
-        out_ref[...] = total
+    half = rows // 2
+    lower = total[half:]
+    for bottom in bottoms:
+        lower = lower + bottom[...].astype(F32)
+    out_ref[half:] = lower
+    for h in range(cols // HEAD):
+        span = slice(h * HEAD, (h + 1) * HEAD)
+        upper = total[:half, span]
+        for top in tops:
+            upper = upper + top[h * half : (h + 1) * half].astype(F32)
+        out_ref[:half, span] = upper
 
 
 def finish_kernel(count, sum_ref, scale_ref, cos_ref, sin_ref, *refs):
@@ -452,17 +466,6 @@
     cosine = jnp.concatenate([cosine, cosine], axis=1)
     sine = jnp.concatenate([-sine, sine], axis=1)
 
-    def pair_sums(start, after):
-        pairs = call(
-            functools.partial(pair_kernel, len(twos), start),
-            "pair_sums",
-            [shape((rows // 2, cols), BF16)] * len(twos),
-            vmem=(*own, *beside),
-            after=after,
-            moved=4 * rows * cols * len(twos),
-        )
-        return pairs[-1], [over("tensor", p, k) for p, k in zip(pairs, twos)]
-
     def down_block(group, extra, after):
         xs = [held[k] for k in group]
         (low,) = call(
@@ -502,42 +505,49 @@
         flops=2 * rows * rows * depth,
         moved=2 * rows * depth,
     )
-    pair, tops = pair_sums(0, (sq, cosine, sine))
-    step = 1
-    while True:
-        other = over("tensor", low, step)
-        if step * 2 >= n_tensor:
-            break
-        more = (near,) if step == 1 else ()
-        low, *handed = call(
+    half = rows // 2
+    upper = cols // HEAD * half
+    other = over("tensor", low, 1)
+    *pairs, near = call(
+        functools.partial(pair_low_kernel, len(twos)),
+        "pair_low_sums",
+        [shape((upper + len(first) * height, HEAD), BF16)]
+        + [shape((upper, HEAD), BF16)] * (len(twos) - 1)
+        + [shape((rows, cols), BF16)],
+        vmem=(near, low, other, *own, *beside),
+        after=(sq, cosine, sine),
+    )
+    tops = [over("tensor", p, k) for p, k in zip(pairs, twos)]
+    near = over("tensor", near, 1)
+    done = pairs[0]
+    low, other = pairs[0], tops[0]
+    for step in range(2, n_tensor.bit_length() - 1):
+        (low,) = call(
             low_sum_kernel,
             "low_sum",
-            [shape(low.shape, BF16)] + [shape((rows, cols), BF16)] * len(more),
-            vmem=(low, other, *more),
-            after=(pair,),
+            [shape((len(first), height, rank), BF16)],
+            vmem=(low, other),
         )
-        if handed:
-            near = over("tensor", handed[0], 1)
-        step *= 2
-    (base,) = call(
-        functools.partial(base_sum_kernel, len(tops)),
-        "base_sum",
-        [shape((rows, cols), F32)],
-        vmem=(base, *tops),
-        after=(low,),
-    )
-    low_last = down_block(last, (sq,), (base,))
+        other = over("tensor", low, 2**step)
+    low_last = down_block(last, (sq,), (done,))
     last_parts = [low_last] + [over("tensor", low_last, k) for k in range(n_tensor - 1, 0, -1)]
     ups = up_block(first, [low, other], False, (low_last,))
     deltas = [u if k == 0 else over("wide", u, k) for k, u in zip(first, ups)]
-    pair, bottoms = pair_sums(rows // 2, (ups[0],))
-    *ups, square = up_block(last, last_parts, True, (pair,))
+    pairs = call(
+        functools.partial(pair_kernel, len(twos), half),
+        "pair_sums",
+        [shape((half, cols), BF16)] * len(twos),
+        vmem=(*own, *beside),
+        after=(ups[0],),
+    )
+    bottoms = [over("tensor", p, k) for p, k in zip(pairs, twos)]
+    *ups, square = up_block(last, last_parts, True, (pairs[0],))
     last_deltas = [over("wide", u, k) for k, u in zip(last, ups)]
     total, scale = call(
         functools.partial(gather_kernel, len(bottoms), len(first)),
         "gather",
         [shape((rows, cols), F32), shape((rows, HEAD), F32)],
-        vmem=(square, base, near, *bottoms, *deltas, *[sels[k] for k in first]),
+        vmem=(square, base, near, *tops, *bottoms, *deltas, *[sels[k] for k in first]),
         after=(ups[0],),
         flops=2 * rows * cols * HEAD * len(first),
     )

time: 53.4 us -> 50.4 us (0.944)
  starting transfers between devices: 20.6 us -> 16 us
  waiting for transfers between devices: 14.8 us -> 16.4 us
    ppermute x15 -> x14, starting transfers between devices: 20.6 us -> 16 us  [over(): return lax.ppermute(array, axis, [(i, i ^ k) for i in range(size)])]
    ppermute x15 -> x14, waiting for transfers between devices: 14.8 us -> 16.4 us  [over(): return lax.ppermute(array, axis, [(i, i ^ k) for i in range(size)])]
    pallas_call x14 -> x12, Pallas kernels: 16.2 us -> 16.2 us  [call(): pl.pallas_call(body, out_shape=outs, in_specs=[pl.BlockSpec(memory_space=...]
  transfers between devices with their start and end apart: 15 -> 14, of which waited for: 6 -> 8; matrix products, arithmetic and copies ran while one was open for 1% -> 1% of each run, Pallas kernels for 22% -> 23%
where the time goes in v3:
time: 50.4 us; the launch traced here: 50.2 us
  waiting for transfers between devices  16.4 us (33%)
  Pallas kernels  16.2 us (32%)
  starting transfers between devices  16 us (32%)
  local copies, waits for them, and re-layouts  0.73 us (1%)
  other arithmetic  0.68 us (1%)
    ppermute x14, waiting for transfers between devices, over(): return lax.ppermute(array, axis, [(i, i ^ k) for i in range(size)])  16.4 us
    pallas_call x12, Pallas kernels, call(): pl.pallas_call(body, out_shape=outs, in_specs=[pl.BlockSpec(memory_space=...  16.2 us
    ppermute x14, starting transfers between devices, over(): return lax.ppermute(array, axis, [(i, i ^ k) for i in range(size)])  16 us
  transfers between devices with their start and end apart: 14, of which 8 were waited for; matrix products, arithmetic and copies ran while one was open for 1% of the time, Pallas kernels for 23%

profile of v3, /device:TPU:0, one launch (start us, length us, event | category | flops | bytes accessed | tf_op | source)
XLA Modules:
  0.0 50.2 jit_solution(12509647148727261622)
XLA Ops:
  0.0 3.5 %dispatch.1 = (bf16[112,2048]{1,0:T(8,128)(2,1)}, bf16[112,2048]{1,0:T(8,128)(2,1)}, bf16[112,2048]{1,0:T(8,128)(2,1)}, bf16[112,2048]{1,0:T(8,128)(2,1)}, f32[16,128]{1,0:T(8,128)}) custom-call(s32[1,256]{1,0:T(1,128)} %bitcast.2, s32[32]{0:T(128)} %refs_1_.7, bf16[256,2048]{1,0:T(8,128)(2,1)} %refs_2_.5, bf16[16,128]{1,0:T(8,128)(2,1)} %bitcast.4), custom_call_target="tpu_custom_call" | custom-call | flops 469762048 | bytes 4194304 | tf_op jit(solution)/shard_map/dispatch/pallas_call | solution.py:28
  3.5 3.0 %collective-permute-start = (bf16[112,2048]{1,0:T(8,128)(2,1)}, bf16[112,2048]{1,0:T(8,128)(2,1)S(1)}, u32[]{:S(2)}, u32[]{:S(2)}) collective-permute-start(bf16[112,2048]{1,0:T(8,128)(2,1)} %get-tuple-element.28), channel_id=1, source_target_pairs={{0,8},{4,12},{8,0},{12,4},{1,9},{5,13},{9,1},{13,5},{2,10},{6,14},... | collective-permute-start | bytes 1376264 | tf_op jit(solution)/shard_map/ppermute | solution.py:392
  6.7 0.7 %copy-done.4 = f32[16,128]{1,0:T(8,128)S(1)} copy-done((f32[16,128]{1,0:T(8,128)S(1)}, f32[16,128]{1,0:T(8,128)}, u32[]{:S(2)}) %copy-start.4) | copy-done | bytes 8216
  7.4 4.8 %base.1 = (bf16[256,512]{1,0:T(8,128)(2,1)S(1)}, bf16[256,512]{1,0:T(8,128)(2,1)S(1)}, f32[256,512]{1,0:T(8,128)S(1)}, f32[256,512]{1,0:T(8,128)S(1)}) custom-call(f32[16,128]{1,0:T(8,128)S(1)} %copy-done.4, bf16[256,2048]{1,0:T(8,128)(2,1)} %refs_2_.5, bf16[2048,2048]{1,0:T(8,128)(2,1)} %refs_2_.4), custom_call_target="tpu_custom_call" | custom-call | flops 2147483648 | bytes 8388608 | tf_op jit(solution)/shard_map/base/pallas_call | solution.py:28
  12.2 2.1 %collective-permute-start.4 = (bf16[256,512]{1,0:T(8,128)(2,1)S(1)}, bf16[256,512]{1,0:T(8,128)(2,1)S(1)}, u32[]{:S(2)}, u32[]{:S(2)}) collective-permute-start(bf16[256,512]{1,0:T(8,128)(2,1)S(1)} %get-tuple-element.37), channel_id=1, source_target_pairs={{0,1},{1,0},{2,3},{3,2},{4,5},{5,4},{6,7},{7,6},{8,9},{9,8},{10,11... | collective-permute-start | bytes 786440 | tf_op jit(solution)/shard_map/ppermute | solution.py:392
  14.9 2.0 %scaled_down.1.refs_2_ = bf16[2048,1024]{1,0:T(8,128)(2,1)S(1)} custom-call(f32[16,128]{1,0:T(8,128)S(1)} %copy-done.4, bf16[8,2048,128]{2,1,0:T(8,128)(2,1)S(1)} %copy-done, f32[256,512]{1,0:T(8,128)S(1)} %get-tuple-element.31.refs_2_.refs_1_), custom_call_target="tpu_custom_call" | custom-call | flops 8388608 | bytes 8388608 | tf_op jit(solution)/shard_map/scaled_down/pallas_call | solution.py:28
  16.9 1.1 %down_block.2.refs_3_.refs_1_ = bf16[2,112,128]{2,1,0:T(8,128)(2,1)S(1)} custom-call(bf16[112,2048]{1,0:T(8,128)(2,1)S(1)} %copy-done.3, bf16[112,2048]{1,0:T(8,128)(2,1)S(1)} %collective-permute-done.2.refs_1_, bf16[2048,1024]{1,0:T(8,128)(2,1)S(1)} %scaled_down.1.refs_2_), custom_call_target="tpu_custom_call" | custom-call | flops 939524096 | bytes 4194304 | tf_op jit(solution)/shard_map/down_block/pallas_call | solution.py:28
  18.3 1.1 %aux.1 = (f32[8,128]{1,0:T(8,128)S(1)}, bf16[256,128]{1,0:T(8,128)(2,1)S(1)}, bf16[256,128]{1,0:T(8,128)(2,1)S(1)}, bf16[256,128]{1,0:T(8,128)(2,1)S(1)}, bf16[256,128]{1,0:T(8,128)(2,1)S(1)}) custom-call(s32[1,256]{1,0:T(1,128)S(1)} %bitcast.3, s32[32]{0:T(128)S(1)} %copy-done.6, bf16[256,2048]{1,0:T(8,128)(2,1)S(1)} %copy-done.1, ...), custom_call_target="tpu_custom_call" | custom-call | flops 268435456 | bytes 1048576 | tf_op jit(solution)/shard_map/aux/pallas_call | solution.py:28
  19.4 1.7 %collective-permute-done.4.refs_4_.refs_1_ = bf16[256,512]{1,0:T(8,128)(2,1)S(1)} collective-permute-done((bf16[256,512]{1,0:T(8,128)(2,1)S(1)}, bf16[256,512]{1,0:T(8,128)(2,1)S(1)}, u32[]{:S(2)}, u32[]{:S(2)}) %collective-permute-start.4) | collective-permute-done | bytes 262176 | tf_op jit(solution)/shard_map/ppermute | solution.py:392
  21.1 1.2 %collective-permute-done.3.refs_2_ = bf16[2,112,128]{2,1,0:T(8,128)(2,1)S(1)} collective-permute-done((bf16[2,112,128]{2,1,0:T(8,128)(2,1)S(1)}, bf16[2,112,128]{2,1,0:T(8,128)(2,1)S(1)}, u32[]{:S(2)}, u32[]{:S(2)}) %collective-permute-start.3) | collective-permute-done | bytes 57376 | tf_op jit(solution)/shard_map/ppermute | solution.py:392
  22.3 2.7 %collective-permute-start.8 = (bf16[736,128]{1,0:T(8,128)(2,1)S(1)}, bf16[736,128]{1,0:T(8,128)(2,1)S(1)}, u32[]{:S(2)}, u32[]{:S(2)}) collective-permute-start(bf16[736,128]{1,0:T(8,128)(2,1)S(1)} %get-tuple-element.38.refs_4_.refs_2_), channel_id=1, source_target_pairs={{0,2},{1,3},{2,0},{3,1},{4,6},{5,7},{6,4},{7,5},{8,10},{9,11},{10,... | collective-permute-start | bytes 565256 | tf_op jit(solution)/shard_map/ppermute | solution.py:392
  25.0 1.5 %collective-permute-start.9 = (bf16[256,512]{1,0:T(8,128)(2,1)S(1)}, bf16[256,512]{1,0:T(8,128)(2,1)S(1)}, u32[]{:S(2)}, u32[]{:S(2)}) collective-permute-start(bf16[256,512]{1,0:T(8,128)(2,1)S(1)} %get-tuple-element.41), channel_id=1, source_target_pairs={{0,1},{1,0},{2,3},{3,2},{4,5},{5,4},{6,7},{7,6},{8,9},{9,8},{10,11... | collective-permute-start | bytes 786440 | tf_op jit(solution)/shard_map/ppermute | solution.py:392
  26.5 1.1 %down_block.3.refs_5_.refs_2_ = bf16[2,112,128]{2,1,0:T(8,128)(2,1)S(1)} custom-call(bf16[112,2048]{1,0:T(8,128)(2,1)S(1)} %collective-permute-done.refs_0_, bf16[112,2048]{1,0:T(8,128)(2,1)S(1)} %collective-permute-done.1.refs_1_, bf16[2048,1024]{1,0:T(8,128)(2,1)S(1)} %scaled_down.1.refs_2_, f32[8,128]{1,0:T(8,128)S(1)} %get-tuple-element.34.refs_5_.refs_3_, ...), custom_call_target="tpu_custom_call" | custom-call | flops 939524096 | bytes 4194304 | tf_op jit(solution)/shard_map/down_block/pallas_call | solution.py:28
  27.6 1.6 %collective-permute-start.7 = (bf16[2,112,128]{2,1,0:T(8,128)(2,1)S(1)}, bf16[2,112,128]{2,1,0:T(8,128)(2,1)S(1)}, u32[]{:S(2)}, u32[]{:S(2)}) collective-permute-start(bf16[2,112,128]{2,1,0:T(8,128)(2,1)S(1)} %down_block.3.refs_5_.refs_2_), channel_id=1, source_target_pairs={{0,1},{1,0},{2,3},{3,2},{4,5},{5,4},{6,7},{7,6},{8,9},{9,8},{10,11... | collective-permute-start | bytes 172040 | tf_op jit(solution)/shard_map/ppermute | solution.py:392
  29.2 2.6 %collective-permute-start.6 = (bf16[2,112,128]{2,1,0:T(8,128)(2,1)S(1)}, bf16[2,112,128]{2,1,0:T(8,128)(2,1)S(1)}, u32[]{:S(2)}, u32[]{:S(2)}) collective-permute-start(bf16[2,112,128]{2,1,0:T(8,128)(2,1)S(1)} %down_block.3.refs_5_.refs_2_), channel_id=1, source_target_pairs={{0,2},{1,3},{2,0},{3,1},{4,6},{5,7},{6,4},{7,5},{8,10},{9,11},{10,... | collective-permute-start | bytes 172040 | tf_op jit(solution)/shard_map/ppermute | solution.py:392
  32.1 1.3 %collective-permute-done.8.refs_3_ = bf16[736,128]{1,0:T(8,128)(2,1)S(1)} collective-permute-done((bf16[736,128]{1,0:T(8,128)(2,1)S(1)}, bf16[736,128]{1,0:T(8,128)(2,1)S(1)}, u32[]{:S(2)}, u32[]{:S(2)}) %collective-permute-start.8) | collective-permute-done | bytes 188448 | tf_op jit(solution)/shard_map/ppermute | solution.py:392
  33.4 0.6 %up_block.2 = (bf16[112,512]{1,0:T(8,128)(2,1)S(1)}, bf16[112,512]{1,0:T(8,128)(2,1)S(1)}) custom-call(bf16[112,2048]{1,0:T(8,128)(2,1)S(1)} %copy-done.3, bf16[112,2048]{1,0:T(8,128)(2,1)S(1)} %collective-permute-done.2.refs_1_, bf16[736,128]{1,0:T(8,128)(2,1)S(1)} %get-tuple-element.38.refs_4_.refs_2_, ...), custom_call_target="tpu_custom_call" | custom-call | flops 234881024 | bytes 1048576 | tf_op jit(solution)/shard_map/up_block/pallas_call | solution.py:28
  34.4 4.9 %collective-permute-done.7.refs_5_ = bf16[2,112,128]{2,1,0:T(8,128)(2,1)S(1)} collective-permute-done((bf16[2,112,128]{2,1,0:T(8,128)(2,1)S(1)}, bf16[2,112,128]{2,1,0:T(8,128)(2,1)S(1)}, u32[]{:S(2)}, u32[]{:S(2)}) %collective-permute-start.7) | collective-permute-done | bytes 57376 | tf_op jit(solution)/shard_map/ppermute | solution.py:392
  39.3 1.3 %collective-permute-done.5.refs_3_ = bf16[2,112,128]{2,1,0:T(8,128)(2,1)S(1)} collective-permute-done((bf16[2,112,128]{2,1,0:T(8,128)(2,1)S(1)}, bf16[2,112,128]{2,1,0:T(8,128)(2,1)S(1)}, u32[]{:S(2)}, u32[]{:S(2)}) %collective-permute-start.5) | collective-permute-done | bytes 57376 | tf_op jit(solution)/shard_map/ppermute | solution.py:392
  41.6 1.3 %collective-permute-start.12 = (bf16[112,512]{1,0:T(8,128)(2,1)S(1)}, bf16[112,512]{1,0:T(8,128)(2,1)S(1)}, u32[]{:S(2)}, u32[]{:S(2)}) collective-permute-start(bf16[112,512]{1,0:T(8,128)(2,1)S(1)} %get-tuple-element.45.refs_9_), channel_id=1, source_target_pairs={{0,8},{4,12},{8,0},{12,4},{1,9},{5,13},{9,1},{13,5},{2,10},{6,14},... | collective-permute-start | bytes 344072 | tf_op jit(solution)/shard_map/ppermute | solution.py:392
  42.9 1.4 %collective-permute-done.10.refs_4_ = bf16[128,512]{1,0:T(8,128)(2,1)S(1)} collective-permute-done((bf16[128,512]{1,0:T(8,128)(2,1)S(1)}, bf16[128,512]{1,0:T(8,128)(2,1)S(1)}, u32[]{:S(2)}, u32[]{:S(2)}) %collective-permute-start.10) | collective-permute-done | bytes 131104 | tf_op jit(solution)/shard_map/ppermute | solution.py:392
  44.5 2.1 %collective-permute-done.13.refs_5_ = bf16[112,512]{1,0:T(8,128)(2,1)S(1)} collective-permute-done((bf16[112,512]{1,0:T(8,128)(2,1)S(1)}, bf16[112,512]{1,0:T(8,128)(2,1)S(1)}, u32[]{:S(2)}, u32[]{:S(2)}) %collective-permute-start.13) | collective-permute-done | bytes 114720 | tf_op jit(solution)/shard_map/ppermute | solution.py:392
  46.6 2.5 %collective-permute-done.12.refs_4_ = bf16[112,512]{1,0:T(8,128)(2,1)S(1)} collective-permute-done((bf16[112,512]{1,0:T(8,128)(2,1)S(1)}, bf16[112,512]{1,0:T(8,128)(2,1)S(1)}, u32[]{:S(2)}, u32[]{:S(2)}) %collective-permute-start.12) | collective-permute-done | bytes 114720 | tf_op jit(solution)/shard_map/ppermute | solution.py:392
  49.2 1.0 %finish.1 = bf16[256,512]{1,0:T(8,128)(2,1)} custom-call(f32[256,512]{1,0:T(8,128)S(1)} %get-tuple-element.46.refs_0_, f32[256,128]{1,0:T(8,128)S(1)} %get-tuple-element.47.refs_1_, f32[256,128]{1,0:T(8,128)S(1)} %get-tuple-element.54.refs_6_.refs_2_, f32[256,128]{1,0:T(8,128)S(1)} %get-tuple-element.55.refs_7_.refs_3_, ...), custom_call_target="tpu_custom_call" | custom-call | flops 33554432 | tf_op jit(solution)/shard_map/finish/pallas_call | solution.py:28
  (36 shorter events, 3.0 us)
Async XLA Ops:
  3.5 23.0 %collective-permute-start = (bf16[112,2048]{1,0:T(8,128)(2,1)}, bf16[112,2048]{1,0:T(8,128)(2,1)S(1)}, u32[]{:S(2)}, u32[]{:S(2)}) collective-permute-start(bf16[112,2048]{1,0:T(8,128)(2,1)} %get-tuple-element.28), channel_id=1, source_target_pairs={{0,8},{4,12},{8,0},{12,4},{1,9},{5,13},{9,1},{13,5},{2,10},{6,14},... | collective-permute-start | bytes 1376264 | tf_op jit(solution)/shard_map/ppermute | solution.py:392
  6.5 20.0 %collective-permute-start.1 = (bf16[112,2048]{1,0:T(8,128)(2,1)}, bf16[112,2048]{1,0:T(8,128)(2,1)S(1)}, u32[]{:S(2)}, u32[]{:S(2)}) collective-permute-start(bf16[112,2048]{1,0:T(8,128)(2,1)} %get-tuple-element.29), channel_id=1, source_target_pairs={{0,12},{4,8},{8,4},{12,0},{1,13},{5,9},{9,5},{13,1},{2,14},{6,10},... | collective-permute-start | bytes 1376264 | tf_op jit(solution)/shard_map/ppermute | solution.py:392
  6.5 10.4 %collective-permute-start.2 = (bf16[112,2048]{1,0:T(8,128)(2,1)}, bf16[112,2048]{1,0:T(8,128)(2,1)S(1)}, u32[]{:S(2)}, u32[]{:S(2)}) collective-permute-start(bf16[112,2048]{1,0:T(8,128)(2,1)} %get-tuple-element.33), channel_id=1, source_target_pairs={{0,4},{4,0},{8,12},{12,8},{1,5},{5,1},{9,13},{13,9},{2,6},{6,2},{1... | collective-permute-start | bytes 1376264 | tf_op jit(solution)/shard_map/ppermute | solution.py:392
  6.7 0.7 %copy-start.4 = (f32[16,128]{1,0:T(8,128)S(1)}, f32[16,128]{1,0:T(8,128)}, u32[]{:S(2)}) copy-start(f32[16,128]{1,0:T(8,128)} %get-tuple-element.30.refs_0_) | copy-start | bytes 24580
  7.4 6.9 %copy-start.7 = (s32[256]{0:T(256)S(1)}, s32[256]{0:T(256)}, u32[]{:S(2)}) copy-start(s32[256]{0:T(256)} %param.15) | copy-start | bytes 3076
  7.4 7.5 %copy-start = (bf16[8,2048,128]{2,1,0:T(8,128)(2,1)S(1)}, bf16[8,2048,128]{2,1,0:T(8,128)(2,1)}, u32[]{:S(2)}) copy-start(bf16[8,2048,128]{2,1,0:T(8,128)(2,1)} %refs_1_.6) | copy-start | bytes 12582916
  12.2 8.9 %collective-permute-start.4 = (bf16[256,512]{1,0:T(8,128)(2,1)S(1)}, bf16[256,512]{1,0:T(8,128)(2,1)S(1)}, u32[]{:S(2)}, u32[]{:S(2)}) collective-permute-start(bf16[256,512]{1,0:T(8,128)(2,1)S(1)} %get-tuple-element.37), channel_id=1, source_target_pairs={{0,1},{1,0},{2,3},{3,2},{4,5},{5,4},{6,7},{7,6},{8,9},{9,8},{10,11... | collective-permute-start | bytes 786440 | tf_op jit(solution)/shard_map/ppermute | solution.py:392
  14.9 2.0 %copy-start.3 = (bf16[112,2048]{1,0:T(8,128)(2,1)S(1)}, bf16[112,2048]{1,0:T(8,128)(2,1)}, u32[]{:S(2)}) copy-start(bf16[112,2048]{1,0:T(8,128)(2,1)} %get-tuple-element.32.refs_0_) | copy-start | bytes 1376260
  16.8 1.4 %copy-start.1 = (bf16[256,2048]{1,0:T(8,128)(2,1)S(1)}, bf16[256,2048]{1,0:T(8,128)(2,1)}, u32[]{:S(2)}) copy-start(bf16[256,2048]{1,0:T(8,128)(2,1)} %refs_2_.5) | copy-start | bytes 3145732
  16.8 1.4 %copy-start.5 = (s32[256]{0:T(256)S(1)}, s32[256]{0:T(256)}, u32[]{:S(2)}) copy-start(s32[256]{0:T(256)} %param.13) | copy-start | bytes 3076
  16.9 1.4 %copy-start.6 = (s32[32]{0:T(128)S(1)}, s32[32]{0:T(128)}, u32[]{:S(2)}) copy-start(s32[32]{0:T(128)} %refs_1_.7) | copy-start | bytes 388
  18.0 4.2 %collective-permute-start.3 = (bf16[2,112,128]{2,1,0:T(8,128)(2,1)S(1)}, bf16[2,112,128]{2,1,0:T(8,128)(2,1)S(1)}, u32[]{:S(2)}, u32[]{:S(2)}) collective-permute-start(bf16[2,112,128]{2,1,0:T(8,128)(2,1)S(1)} %down_block.2.refs_3_.refs_1_), channel_id=1, source_target_pairs={{0,1},{1,0},{2,3},{3,2},{4,5},{5,4},{6,7},{7,6},{8,9},{9,8},{10,11... | collective-permute-start | bytes 172040 | tf_op jit(solution)/shard_map/ppermute | solution.py:392
  18.1 15.3 %copy-start.2 = (bf16[8,64,512]{2,1,0:T(8,128)(2,1)S(1)}, bf16[8,64,512]{2,1,0:T(8,128)(2,1)}, u32[]{:S(2)}) copy-start(bf16[8,64,512]{2,1,0:T(8,128)(2,1)} %refs_6_.1) | copy-start | bytes 1572868
  22.3 11.1 %collective-permute-start.8 = (bf16[736,128]{1,0:T(8,128)(2,1)S(1)}, bf16[736,128]{1,0:T(8,128)(2,1)S(1)}, u32[]{:S(2)}, u32[]{:S(2)}) collective-permute-start(bf16[736,128]{1,0:T(8,128)(2,1)S(1)} %get-tuple-element.38.refs_4_.refs_2_), channel_id=1, source_target_pairs={{0,2},{1,3},{2,0},{3,1},{4,6},{5,7},{6,4},{7,5},{8,10},{9,11},{10,... | collective-permute-start | bytes 565256 | tf_op jit(solution)/shard_map/ppermute | solution.py:392
  25.0 17.9 %collective-permute-start.9 = (bf16[256,512]{1,0:T(8,128)(2,1)S(1)}, bf16[256,512]{1,0:T(8,128)(2,1)S(1)}, u32[]{:S(2)}, u32[]{:S(2)}) collective-permute-start(bf16[256,512]{1,0:T(8,128)(2,1)S(1)} %get-tuple-element.41), channel_id=1, source_target_pairs={{0,1},{1,0},{2,3},{3,2},{4,5},{5,4},{6,7},{7,6},{8,9},{9,8},{10,11... | collective-permute-start | bytes 786440 | tf_op jit(solution)/shard_map/ppermute | solution.py:392
  27.6 11.7 %collective-permute-start.7 = (bf16[2,112,128]{2,1,0:T(8,128)(2,1)S(1)}, bf16[2,112,128]{2,1,0:T(8,128)(2,1)S(1)}, u32[]{:S(2)}, u32[]{:S(2)}) collective-permute-start(bf16[2,112,128]{2,1,0:T(8,128)(2,1)S(1)} %down_block.3.refs_5_.refs_2_), channel_id=1, source_target_pairs={{0,1},{1,0},{2,3},{3,2},{4,5},{5,4},{6,7},{7,6},{8,9},{9,8},{10,11... | collective-permute-start | bytes 172040 | tf_op jit(solution)/shard_map/ppermute | solution.py:392
  29.2 10.1 %collective-permute-start.6 = (bf16[2,112,128]{2,1,0:T(8,128)(2,1)S(1)}, bf16[2,112,128]{2,1,0:T(8,128)(2,1)S(1)}, u32[]{:S(2)}, u32[]{:S(2)}) collective-permute-start(bf16[2,112,128]{2,1,0:T(8,128)(2,1)S(1)} %down_block.3.refs_5_.refs_2_), channel_id=1, source_target_pairs={{0,2},{1,3},{2,0},{3,1},{4,6},{5,7},{6,4},{7,5},{8,10},{9,11},{10,... | collective-permute-start | bytes 172040 | tf_op jit(solution)/shard_map/ppermute | solution.py:392
  31.8 8.8 %collective-permute-start.5 = (bf16[2,112,128]{2,1,0:T(8,128)(2,1)S(1)}, bf16[2,112,128]{2,1,0:T(8,128)(2,1)S(1)}, u32[]{:S(2)}, u32[]{:S(2)}) collective-permute-start(bf16[2,112,128]{2,1,0:T(8,128)(2,1)S(1)} %down_block.3.refs_5_.refs_2_), channel_id=1, source_target_pairs={{0,3},{1,2},{2,1},{3,0},{4,7},{5,6},{6,5},{7,4},{8,11},{9,10},{10,... | collective-permute-start | bytes 172040 | tf_op jit(solution)/shard_map/ppermute | solution.py:392
  34.1 10.2 %collective-permute-start.10 = (bf16[128,512]{1,0:T(8,128)(2,1)S(1)}, bf16[128,512]{1,0:T(8,128)(2,1)S(1)}, u32[]{:S(2)}, u32[]{:S(2)}) collective-permute-start(bf16[128,512]{1,0:T(8,128)(2,1)S(1)} %pair_sums.1.refs_7_), channel_id=1, source_target_pairs={{0,2},{1,3},{2,0},{3,1},{4,6},{5,7},{6,4},{7,5},{8,10},{9,11},{10,... | collective-permute-start | bytes 393224 | tf_op jit(solution)/shard_map/ppermute | solution.py:392
  39.3 3.6 %collective-permute-start.11 = (bf16[112,512]{1,0:T(8,128)(2,1)S(1)}, bf16[112,512]{1,0:T(8,128)(2,1)S(1)}, u32[]{:S(2)}, u32[]{:S(2)}) collective-permute-start(bf16[112,512]{1,0:T(8,128)(2,1)S(1)} %get-tuple-element.42), channel_id=1, source_target_pairs={{0,4},{4,0},{8,12},{12,8},{1,5},{5,1},{9,13},{13,9},{2,6},{6,2},{1... | collective-permute-start | bytes 344072 | tf_op jit(solution)/shard_map/ppermute | solution.py:392
  41.2 5.4 %collective-permute-start.13 = (bf16[112,512]{1,0:T(8,128)(2,1)S(1)}, bf16[112,512]{1,0:T(8,128)(2,1)S(1)}, u32[]{:S(2)}, u32[]{:S(2)}) collective-permute-start(bf16[112,512]{1,0:T(8,128)(2,1)S(1)} %get-tuple-element.48), channel_id=1, source_target_pairs={{0,12},{4,8},{8,4},{12,0},{1,13},{5,9},{9,5},{13,1},{2,14},{6,10},... | collective-permute-start | bytes 344072 | tf_op jit(solution)/shard_map/ppermute | solution.py:392
  41.6 7.6 %collective-permute-start.12 = (bf16[112,512]{1,0:T(8,128)(2,1)S(1)}, bf16[112,512]{1,0:T(8,128)(2,1)S(1)}, u32[]{:S(2)}, u32[]{:S(2)}) collective-permute-start(bf16[112,512]{1,0:T(8,128)(2,1)S(1)} %get-tuple-element.45.refs_9_), channel_id=1, source_target_pairs={{0,8},{4,12},{8,0},{12,4},{1,9},{5,13},{9,1},{13,5},{2,10},{6,14},... | collective-permute-start | bytes 344072 | tf_op jit(solution)/shard_map/ppermute | solution.py:392

commit v4 on v3

--- a/solution.py
+++ b/solution.py
@@ -66,7 +66,7 @@
 
 def dispatch_kernel(order, n_wide, per_dev, cap, req_hbm, table_hbm, tok_hbm, gain_hbm, *refs):
     xs = refs[: len(order)]
-    wide_gain_ref, req_ref, table_ref, tok_ref, gain_ref, x_ref, sems, out_sems = refs[
+    xg_hbm, req_ref, table_ref, tok_ref, gain_ref, x_ref, xg_ref, sems, out_sems = refs[
         len(order) :
     ]
     rows, depth = tok_ref.shape
@@ -91,10 +91,17 @@
         )
         picks.append(pick[:height])
     loads[3].wait()
-    wide_gain_ref[...] = gain_ref[...].astype(F32)
     loads[2].wait()
     stores = []
     for j, k in enumerate(order):
+        if k == 1:
+            for b in range(depth // HEAD):
+                span = slice(b * HEAD, (b + 1) * HEAD)
+                piece = tok_ref[:, span].astype(F32) * gain_ref[b : b + 1].astype(F32)
+                xg_ref[:, span] = piece.astype(BF16)
+            copy = pltpu.make_async_copy(xg_ref, xg_hbm, out_sems.at[len(order)])
+            copy.start()
+            stores.append(copy)
         y = jnp.dot(picks[j], tok_ref[...], preferred_element_type=F32)
         first = jnp.where(iota((height, HEAD), 0) == cap, slot_rows[j][:1], y[:, :HEAD])
         x_ref[j, :, :HEAD] = first.astype(BF16)
@@ -106,30 +113,48 @@
         copy.wait()
 
 
-def base_kernel(offsets, cols, gain_hbm, tok_hbm, weight_hbm, *refs):
+def base_far_kernel(offsets, cols, xg_hbm, weight_hbm, *refs):
+    outs = refs[: len(offsets)]
+    x_ref, buf, sems = refs[len(offsets) :]
+    _, steps, chunk, _ = buf.shape
+    spot = lax.axis_index("tensor").astype(jnp.int32)
+    load = pltpu.make_async_copy(xg_hbm, x_ref, sems.at[0])
+    load.start()
+    copies = []
+    for j, k in enumerate(offsets):
+        start = pl.multiple_of((spot ^ k) * cols, HEAD)
+        for i in range(steps):
+            source = weight_hbm.at[pl.ds(i * chunk, chunk), pl.ds(start, cols)]
+            copy = pltpu.make_async_copy(source, buf.at[j, i], sems.at[1 + len(copies)])
+            copy.start()
+            copies.append(copy)
+    load.wait()
+    for j in range(len(offsets)):
+        total = None
+        for i in range(steps):
+            copies[j * steps + i].wait()
+            x = x_ref[:, i * chunk : (i + 1) * chunk]
+            y = jnp.dot(x, buf[j, i], preferred_element_type=F32)
+            total = y if total is None else total + y
+        outs[j][...] = total.astype(BF16)
+
+
+def base_kernel(offsets, cols, xg_hbm, weight_hbm, *refs):
     count = len(offsets)
     outs = refs[:count]
-    gain_ref, tok_ref, buf, acc_ref, sems = refs[count:]
+    x_ref, buf, acc_ref, sems = refs[count:]
     steps, chunk, _ = buf.shape
+    load = pltpu.make_async_copy(xg_hbm, x_ref, sems.at[0])
     copies = [
-        pltpu.make_async_copy(weight_hbm.at[pl.ds(i * chunk, chunk)], buf.at[i], sems.at[2 + i])
+        pltpu.make_async_copy(weight_hbm.at[pl.ds(i * chunk, chunk)], buf.at[i], sems.at[1 + i])
         for i in range(steps)
     ]
-    loads = [
-        pltpu.make_async_copy(gain_hbm, gain_ref, sems.at[0]),
-        pltpu.make_async_copy(tok_hbm, tok_ref, sems.at[1]),
-    ]
-    for copy in loads + copies:
+    for copy in [load] + copies:
         copy.start()
-    for copy in loads:
-        copy.wait()
+    load.wait()
     spot = lax.axis_index("tensor").astype(jnp.int32)
     for i in range(steps):
-        pieces = []
-        for b in range(i * chunk // HEAD, (i + 1) * chunk // HEAD):
-            piece = tok_ref[:, b * HEAD : (b + 1) * HEAD].astype(F32) * gain_ref[b : b + 1]
-            pieces.append(piece.astype(BF16))
-        x = jnp.concatenate(pieces, axis=1)
+        x = x_ref[:, i * chunk : (i + 1) * chunk]
         copies[i].wait()
         for j, k in enumerate(offsets):
             start = pl.multiple_of((spot ^ k) * cols, HEAD)
@@ -142,15 +167,16 @@
                 outs[j][...] = y.astype(outs[j].dtype)
 
 
-def pair_kernel(count, start, *refs):
+def pair_kernel(count, start, base_ref, near_ref, *refs):
+    refs[-1][...] = base_ref[...] + near_ref[...].astype(F32)
     for j in range(count):
         out_ref = refs[2 * count + j]
         rows = slice(start, start + out_ref.shape[0])
         out_ref[...] = (refs[j][rows] + refs[count + j][rows].astype(F32)).astype(BF16)
 
 
-def pair_low_kernel(count, near_ref, low_ref, other_ref, *refs):
-    outs, sent_ref = refs[2 * count : -1], refs[-1]
+def pair_low_kernel(count, low_ref, other_ref, *refs):
+    outs = refs[2 * count :]
     cols = refs[0].shape[1]
     half = refs[0].shape[0] // 2
     for j in range(count):
@@ -162,7 +188,6 @@
     for i in range(groups):
         total = low_ref[i].astype(F32) + other_ref[i].astype(F32)
         outs[0][base + i * height : base + (i + 1) * height] = total.astype(BF16)
-    sent_ref[...] = near_ref[...]
 
 
 def scaled_down_kernel(gain_ref, down_hbm, out_ref, buf, sems):
@@ -172,7 +197,7 @@
         copy.start()
     columns = []
     for b in range(depth // HEAD):
-        columns.append(to_column(gain_ref[b : b + 1], HEAD))
+        columns.append(to_column(gain_ref[b : b + 1].astype(F32), HEAD))
     for a in range(per_dev):
         copies[a].wait()
         for b in range(depth // HEAD):
@@ -318,7 +343,7 @@
     return jnp.dot(lhs, jnp.concatenate(blocks, axis=0), preferred_element_type=F32)
 
 
-def gather_kernel(n_pairs, count, sq_ref, base_ref, near_ref, *refs):
+def gather_kernel(n_pairs, count, sq_ref, base_ref, *refs):
     tops, bottoms = refs[:n_pairs], refs[n_pairs : 2 * n_pairs]
     deltas = refs[2 * n_pairs : 2 * n_pairs + count]
     sels = refs[2 * n_pairs + count : 2 * n_pairs + 2 * count]
@@ -334,7 +359,7 @@
     square = to_column(jnp.concatenate(squares, axis=1), rows)
     scale = lax.rsqrt(square * (1.0 / MODEL_WIDTH) + EPSILON)
     scale_ref[...] = jnp.broadcast_to(scale, (rows, HEAD))
-    total = base_ref[...] + near_ref[...].astype(F32) + placed(sels, deltas)
+    total = base_ref[...] + placed(sels, deltas)
     half = rows // 2
     lower = total[half:]
     for bottom in bottoms:
@@ -394,63 +419,56 @@
     small = [pltpu.VMEM((1, rows), jnp.int32), pltpu.SMEM(adapter_storage_row.shape, jnp.int32)]
     first, last = [0, 1], list(range(2, n_wide))
 
-    def dispatch(order, after):
-        *blocks, wide_gain = call(
-            functools.partial(dispatch_kernel, order, n_wide, per_dev, cap),
-            "dispatch",
-            [shape((height, depth), BF16)] * len(order) + [shape(gain.shape, F32)],
-            hbm=(req, adapter_storage_row, tokens, gain),
-            hbm_outs=len(order),
-            after=after,
-            scratch=small
-            + [
-                pltpu.VMEM((rows, depth), BF16),
-                pltpu.VMEM(gain.shape, BF16),
-                pltpu.VMEM((len(order), height, depth), BF16),
-                pltpu.SemaphoreType.DMA((4,)),
-                pltpu.SemaphoreType.DMA((len(order),)),
-            ],
-            flops=2 * len(order) * height * rows * depth,
-            moved=2 * rows * depth * 4,
-            limit=63,
-        )
-        return blocks, wide_gain
-
     order = list(range(n_wide - 1, -1, -1))
-    blocks, wide_gain = dispatch(order, ())
+    *blocks, xg = call(
+        functools.partial(dispatch_kernel, order, n_wide, per_dev, cap),
+        "dispatch",
+        [shape((height, depth), BF16)] * n_wide + [shape((rows, depth), BF16)],
+        hbm=(req, adapter_storage_row, tokens, gain),
+        hbm_outs=n_wide + 1,
+        scratch=small
+        + [
+            pltpu.VMEM((rows, depth), BF16),
+            pltpu.VMEM(gain.shape, BF16),
+            pltpu.VMEM((n_wide, height, depth), BF16),
+            pltpu.VMEM((rows, depth), BF16),
+            pltpu.SemaphoreType.DMA((4,)),
+            pltpu.SemaphoreType.DMA((n_wide + 1,)),
+        ],
+        flops=2 * n_wide * height * rows * depth,
+        moved=2 * rows * depth * 4,
+        limit=63,
+    )
     held = [blocks[n_wide - 1 - k] for k in range(n_wide)]
     held[1:] = [over("wide", held[k], k) for k in range(1, n_wide)]
 
     twos = list(range(2, n_tensor, 2))
     far = [k ^ 1 for k in twos]
-    offsets = far + [1] + twos + [0]
+    offsets = [1] + twos + [0]
     chunk = math.gcd(depth, 512)
     steps = depth // chunk
-    sums = call(
-        functools.partial(base_kernel, offsets, cols),
-        "base",
-        [shape((rows, cols), BF16)] * (len(far) + 1) + [shape((rows, cols), F32)] * (len(twos) + 1),
-        hbm=(wide_gain, tokens, key_value_weight),
+    away = call(
+        functools.partial(base_far_kernel, far, cols),
+        "base_far",
+        [shape((rows, cols), BF16)] * len(far),
+        hbm=(xg, key_value_weight),
         scratch=[
-            pltpu.VMEM(gain.shape, F32),
             pltpu.VMEM((rows, depth), BF16),
-            pltpu.VMEM((steps, chunk, key_value_weight.shape[1]), BF16),
-            pltpu.VMEM((len(offsets), rows, cols), F32),
-            pltpu.SemaphoreType.DMA((2 + steps,)),
+            pltpu.VMEM((len(far), steps, chunk, cols), BF16),
+            pltpu.SemaphoreType.DMA((1 + len(far) * steps,)),
         ],
-        flops=2 * rows * depth * cols * n_tensor,
-        moved=2 * depth * cols * n_tensor,
-        limit=52,
-    )
-    away, near, own, base = sums[: len(far)], sums[len(far)], sums[len(far) + 1 : -1], sums[-1]
+        flops=2 * rows * depth * cols * len(far),
+        moved=2 * depth * cols * len(far),
+        limit=58,
+    )
     beside = [over("tensor", p, 1) for p in away]
     (down,) = call(
         scaled_down_kernel,
         "scaled_down",
         [shape((depth, per_dev * rank), BF16)],
-        vmem=(wide_gain,),
+        vmem=(gain,),
         hbm=(adapter_down_weight,),
-        after=(base,),
+        after=(away[0],),
         scratch=[
             pltpu.VMEM((per_dev, depth, rank), BF16),
             pltpu.SemaphoreType.DMA((per_dev,)),
@@ -458,6 +476,7 @@
         flops=4 * depth * per_dev * rank,
         moved=4 * depth * per_dev * rank,
     )
+
     half_size = HEAD // 2
     freq_index = jnp.arange(half_size).astype(F32)
     inverse = jnp.exp(freq_index * (-2.0 / HEAD) * math.log(ROPE_BASE))
@@ -495,32 +514,46 @@
         )
 
     low = down_block(first, (), ())
+    other = over("tensor", low, 1)
+    near, *own, base = call(
+        functools.partial(base_kernel, offsets, cols),
+        "base",
+        [shape((rows, cols), BF16)] + [shape((rows, cols), F32)] * (len(twos) + 1),
+        hbm=(xg, key_value_weight),
+        after=(low,),
+        scratch=[
+            pltpu.VMEM((rows, depth), BF16),
+            pltpu.VMEM((steps, chunk, key_value_weight.shape[1]), BF16),
+            pltpu.VMEM((len(offsets), rows, cols), F32),
+            pltpu.SemaphoreType.DMA((1 + steps,)),
+        ],
+        flops=2 * rows * depth * cols * len(offsets),
+        moved=2 * depth * cols * n_tensor,
+        limit=52,
+    )
+    near = over("tensor", near, 1)
+    half = rows // 2
+    upper = cols // HEAD * half
+    pairs = call(
+        functools.partial(pair_low_kernel, len(twos)),
+        "pair_low_sums",
+        [shape((upper + len(first) * height, HEAD), BF16)]
+        + [shape((upper, HEAD), BF16)] * (len(twos) - 1),
+        vmem=(low, other, *own, *beside),
+    )
+    tops = [over("tensor", p, k) for p, k in zip(pairs, twos)]
+    done = pairs[0]
+    low, other = pairs[0], tops[0]
     sq, *sels = call(
         functools.partial(aux_kernel, n_wide, per_dev),
         "aux",
         [shape((8, HEAD), F32)] + [shape((rows, HEAD), BF16)] * n_wide,
         hbm=(req, adapter_storage_row, tokens),
-        after=(low,),
+        after=(done,),
         scratch=small + [pltpu.VMEM((rows, depth), BF16), pltpu.SemaphoreType.DMA((3,))],
         flops=2 * rows * rows * depth,
         moved=2 * rows * depth,
     )
-    half = rows // 2
-    upper = cols // HEAD * half
-    other = over("tensor", low, 1)
-    *pairs, near = call(
-        functools.partial(pair_low_kernel, len(twos)),
-        "pair_low_sums",
-        [shape((upper + len(first) * height, HEAD), BF16)]
-        + [shape((upper, HEAD), BF16)] * (len(twos) - 1)
-        + [shape((rows, cols), BF16)],
-        vmem=(near, low, other, *own, *beside),
-        after=(sq, cosine, sine),
-    )
-    tops = [over("tensor", p, k) for p, k in zip(pairs, twos)]
-    near = over("tensor", near, 1)
-    done = pairs[0]
-    low, other = pairs[0], tops[0]
     for step in range(2, n_tensor.bit_length() - 1):
         (low,) = call(
             low_sum_kernel,
@@ -529,15 +562,15 @@
             vmem=(low, other),
         )
         other = over("tensor", low, 2**step)
-    low_last = down_block(last, (sq,), (done,))
+    low_last = down_block(last, (sq,), (cosine, sine))
     last_parts = [low_last] + [over("tensor", low_last, k) for k in range(n_tensor - 1, 0, -1)]
     ups = up_block(first, [low, other], False, (low_last,))
     deltas = [u if k == 0 else over("wide", u, k) for k, u in zip(first, ups)]
-    pairs = call(
+    *pairs, base = call(
         functools.partial(pair_kernel, len(twos), half),
         "pair_sums",
-        [shape((half, cols), BF16)] * len(twos),
-        vmem=(*own, *beside),
+        [shape((half, cols), BF16)] * len(twos) + [shape((rows, cols), F32)],
+        vmem=(base, near, *own, *beside),
         after=(ups[0],),
     )
     bottoms = [over("tensor", p, k) for p, k in zip(pairs, twos)]
@@ -547,7 +580,7 @@
         functools.partial(gather_kernel, len(bottoms), len(first)),
         "gather",
         [shape((rows, cols), F32), shape((rows, HEAD), F32)],
-        vmem=(square, base, near, *tops, *bottoms, *deltas, *[sels[k] for k in first]),
+        vmem=(square, base, *tops, *bottoms, *deltas, *[sels[k] for k in first]),
         after=(ups[0],),
         flops=2 * rows * cols * HEAD * len(first),
     )

time: 50.4 us -> 51.5 us (1.022)
  waiting for transfers between devices: 16.4 us -> 10.3 us
  starting transfers between devices: 16 us -> 19.3 us
  Pallas kernels: 16.2 us -> 19.3 us
  other arithmetic: 0.68 us -> 1.36 us
    ppermute x14, waiting for transfers between devices: 16.4 us -> 10.3 us  [over(): return lax.ppermute(array, axis, [(i, i ^ k) for i in range(size)])]
    ppermute x14, starting transfers between devices: 16 us -> 19.3 us  [over(): return lax.ppermute(array, axis, [(i, i ^ k) for i in range(size)])]
    pallas_call x12 -> x13, Pallas kernels: 16.2 us -> 19.3 us  [call(): pl.pallas_call(body, out_shape=outs, in_specs=[pl.BlockSpec(memory_space=...]
    neg x1, other arithmetic: 0.54 us -> 1.22 us  [local(): sine = jnp.concatenate([-sine, sine], axis=1)]
  transfers between devices with their start and end apart: 14 -> 14, of which waited for: 8 -> 6; matrix products, arithmetic and copies ran while one was open for 1% -> 3% of each run, Pallas kernels for 23% -> 28%
where the time goes in v4:
time: 51.5 us; the launch traced here: 51.4 us
  Pallas kernels  19.3 us (37%)
  starting transfers between devices  19.3 us (37%)
  waiting for transfers between devices  10.3 us (20%)
  other arithmetic  1.36 us (3%)
  local copies, waits for them, and re-layouts  0.99 us (2%)
    ppermute x14, starting transfers between devices, over(): return lax.ppermute(array, axis, [(i, i ^ k) for i in range(size)])  19.3 us
    pallas_call x13, Pallas kernels, call(): pl.pallas_call(body, out_shape=outs, in_specs=[pl.BlockSpec(memory_space=...  19.3 us
    ppermute x14, waiting for transfers between devices, over(): return lax.ppermute(array, axis, [(i, i ^ k) for i in range(size)])  10.3 us
    neg x1, other arithmetic, local(): sine = jnp.concatenate([-sine, sine], axis=1)  1.22 us
  transfers between devices with their start and end apart: 14, of which 6 were waited for; matrix products, arithmetic and copies ran while one was open for 3% of the time, Pallas kernels for 28%

profile of v4, /device:TPU:0, one launch (start us, length us, event | category | flops | bytes accessed | tf_op | source)
XLA Modules:
  0.0 51.4 jit_solution(4481426051842928029)
XLA Ops:
  0.0 3.6 %dispatch.1 = (bf16[112,2048]{1,0:T(8,128)(2,1)}, bf16[112,2048]{1,0:T(8,128)(2,1)}, bf16[112,2048]{1,0:T(8,128)(2,1)}, bf16[112,2048]{1,0:T(8,128)(2,1)}, bf16[256,2048]{1,0:T(8,128)(2,1)}) custom-call(s32[1,256]{1,0:T(1,128)} %bitcast.4, s32[32]{0:T(128)} %refs_1_.9, bf16[256,2048]{1,0:T(8,128)(2,1)} %refs_2_.3, bf16[16,128]{1,0:T(8,128)(2,1)} %bitcast.2), custom_call_target="tpu_custom_call" | custom-call | flops 469762048 | bytes 4194304 | tf_op jit(solution)/shard_map/dispatch/pallas_call | solution.py:28
  4.1 2.6 %collective-permute-start = (bf16[112,2048]{1,0:T(8,128)(2,1)}, bf16[112,2048]{1,0:T(8,128)(2,1)S(1)}, u32[]{:S(2)}, u32[]{:S(2)}) collective-permute-start(bf16[112,2048]{1,0:T(8,128)(2,1)} %get-tuple-element.27), channel_id=1, source_target_pairs={{0,8},{4,12},{8,0},{12,4},{1,9},{5,13},{9,1},{13,5},{2,10},{6,14},... | collective-permute-start | bytes 1376264 | tf_op jit(solution)/shard_map/ppermute | solution.py:417
  6.8 3.2 %base_far.1.refs_2_ = bf16[256,512]{1,0:T(8,128)(2,1)} custom-call(bf16[256,2048]{1,0:T(8,128)(2,1)} %get-tuple-element.29.refs_0_, bf16[2048,2048]{1,0:T(8,128)(2,1)} %refs_1_.8), custom_call_target="tpu_custom_call" | custom-call | flops 536870912 | bytes 2097152 | tf_op jit(solution)/shard_map/base_far/pallas_call | solution.py:28
  10.0 1.9 %collective-permute-start.4 = (bf16[256,512]{1,0:T(8,128)(2,1)}, bf16[256,512]{1,0:T(8,128)(2,1)S(1)}, u32[]{:S(2)}, u32[]{:S(2)}) collective-permute-start(bf16[256,512]{1,0:T(8,128)(2,1)} %base_far.1.refs_2_), channel_id=1, source_target_pairs={{0,1},{1,0},{2,3},{3,2},{4,5},{5,4},{6,7},{7,6},{8,9},{9,8},{10,11... | collective-permute-start | bytes 786440 | tf_op jit(solution)/shard_map/ppermute | solution.py:417
  11.9 1.2 %fusion = (f32[256,64]{1,0:T(8,128)S(1)}, f32[256,64]{1,0:T(8,128)S(1)}, f32[256,64]{1,0:T(8,128)}) fusion(f32[64]{0:T(128)S(1)} %multiply_exponential_fusion, f32[256]{0:T(256)S(1)} %convert_element_type.10), kind=kLoop, calls=%fused_computation.4 | loop fusion | flops 32768 | bytes 197888 | tf_op jit(solution)/shard_map/neg | solution.py:486
  13.1 0.9 %copy-done.3 = bf16[256,512]{1,0:T(8,128)(2,1)S(1)} copy-done((bf16[256,512]{1,0:T(8,128)(2,1)S(1)}, bf16[256,512]{1,0:T(8,128)(2,1)}, u32[]{:S(2)}) %copy-start.3) | copy-done | bytes 262168
  14.1 2.0 %scaled_down.1.refs_2_ = bf16[2048,1024]{1,0:T(8,128)(2,1)S(1)} custom-call(bf16[16,128]{1,0:T(8,128)(2,1)S(1)} %bitcast.3, bf16[8,2048,128]{2,1,0:T(8,128)(2,1)S(1)} %copy-done, bf16[256,512]{1,0:T(8,128)(2,1)S(1)} %copy-done.3), custom_call_target="tpu_custom_call" | custom-call | flops 8388608 | bytes 8388608 | tf_op jit(solution)/shard_map/scaled_down/pallas_call | solution.py:28
  16.1 1.1 %down_block.2.refs_2_.refs_0_ = bf16[2,112,128]{2,1,0:T(8,128)(2,1)S(1)} custom-call(bf16[112,2048]{1,0:T(8,128)(2,1)S(1)} %copy-done.2, bf16[112,2048]{1,0:T(8,128)(2,1)S(1)} %collective-permute-done.2.refs_1_, bf16[2048,1024]{1,0:T(8,128)(2,1)S(1)} %scaled_down.1.refs_2_), custom_call_target="tpu_custom_call" | custom-call | flops 939524096 | bytes 4194304 | tf_op jit(solution)/shard_map/down_block/pallas_call | solution.py:28
  17.6 4.5 %base.1 = (bf16[256,512]{1,0:T(8,128)(2,1)S(1)}, f32[256,512]{1,0:T(8,128)S(1)}, f32[256,512]{1,0:T(8,128)S(1)}) custom-call(bf16[256,2048]{1,0:T(8,128)(2,1)} %get-tuple-element.29.refs_0_, bf16[2048,2048]{1,0:T(8,128)(2,1)} %refs_1_.8, bf16[2,112,128]{2,1,0:T(8,128)(2,1)S(1)} %down_block.2.refs_2_.refs_0_), custom_call_target="tpu_custom_call" | custom-call | flops 1610612736 | bytes 8388608 | tf_op jit(solution)/shard_map/base/pallas_call | solution.py:28
  22.0 1.8 %collective-permute-start.8 = (bf16[256,512]{1,0:T(8,128)(2,1)S(1)}, bf16[256,512]{1,0:T(8,128)(2,1)S(1)}, u32[]{:S(2)}, u32[]{:S(2)}) collective-permute-start(bf16[256,512]{1,0:T(8,128)(2,1)S(1)} %get-tuple-element.35), channel_id=1, source_target_pairs={{0,1},{1,0},{2,3},{3,2},{4,5},{5,4},{6,7},{7,6},{8,9},{9,8},{10,11... | collective-permute-start | bytes 786440 | tf_op jit(solution)/shard_map/ppermute | solution.py:417
  23.9 2.7 %collective-permute-start.9 = (bf16[736,128]{1,0:T(8,128)(2,1)S(1)}, bf16[736,128]{1,0:T(8,128)(2,1)S(1)}, u32[]{:S(2)}, u32[]{:S(2)}) collective-permute-start(bf16[736,128]{1,0:T(8,128)(2,1)S(1)} %pair_low_sums.1.refs_3_.refs_2_), channel_id=1, source_target_pairs={{0,2},{1,3},{2,0},{3,1},{4,6},{5,7},{6,4},{7,5},{8,10},{9,11},{10,... | collective-permute-start | bytes 565256 | tf_op jit(solution)/shard_map/ppermute | solution.py:417
  26.7 1.1 %aux.1 = (f32[8,128]{1,0:T(8,128)S(1)}, bf16[256,128]{1,0:T(8,128)(2,1)S(1)}, bf16[256,128]{1,0:T(8,128)(2,1)S(1)}, bf16[256,128]{1,0:T(8,128)(2,1)S(1)}, bf16[256,128]{1,0:T(8,128)(2,1)S(1)}) custom-call(s32[1,256]{1,0:T(1,128)S(1)} %bitcast.5, s32[32]{0:T(128)S(1)} %copy-done.7, bf16[256,2048]{1,0:T(8,128)(2,1)S(1)} %copy-done.4, ...), custom_call_target="tpu_custom_call" | custom-call | flops 268435456 | bytes 1048576 | tf_op jit(solution)/shard_map/aux/pallas_call | solution.py:28
  27.9 1.1 %down_block.3.refs_5_.refs_2_ = bf16[2,112,128]{2,1,0:T(8,128)(2,1)S(1)} custom-call(bf16[112,2048]{1,0:T(8,128)(2,1)S(1)} %collective-permute-done.refs_0_, bf16[112,2048]{1,0:T(8,128)(2,1)S(1)} %collective-permute-done.1.refs_1_, bf16[2048,1024]{1,0:T(8,128)(2,1)S(1)} %scaled_down.1.refs_2_, f32[8,128]{1,0:T(8,128)S(1)} %get-tuple-element.33.refs_3_, ...), custom_call_target="tpu_custom_call" | custom-call | flops 939524096 | bytes 4194304 | tf_op jit(solution)/shard_map/down_block/pallas_call | solution.py:28
  29.0 3.5 %collective-permute-start.5 = (bf16[2,112,128]{2,1,0:T(8,128)(2,1)S(1)}, bf16[2,112,128]{2,1,0:T(8,128)(2,1)S(1)}, u32[]{:S(2)}, u32[]{:S(2)}) collective-permute-start(bf16[2,112,128]{2,1,0:T(8,128)(2,1)S(1)} %down_block.3.refs_5_.refs_2_), channel_id=1, source_target_pairs={{0,3},{1,2},{2,1},{3,0},{4,7},{5,6},{6,5},{7,4},{8,11},{9,10},{10,... | collective-permute-start | bytes 172040 | tf_op jit(solution)/shard_map/ppermute | solution.py:417
  32.5 1.0 %collective-permute-start.7 = (bf16[2,112,128]{2,1,0:T(8,128)(2,1)S(1)}, bf16[2,112,128]{2,1,0:T(8,128)(2,1)S(1)}, u32[]{:S(2)}, u32[]{:S(2)}) collective-permute-start(bf16[2,112,128]{2,1,0:T(8,128)(2,1)S(1)} %down_block.3.refs_5_.refs_2_), channel_id=1, source_target_pairs={{0,1},{1,0},{2,3},{3,2},{4,5},{5,4},{6,7},{7,6},{8,9},{9,8},{10,11... | collective-permute-start | bytes 172040 | tf_op jit(solution)/shard_map/ppermute | solution.py:417
  33.6 0.6 %up_block.2 = (bf16[112,512]{1,0:T(8,128)(2,1)S(1)}, bf16[112,512]{1,0:T(8,128)(2,1)S(1)}) custom-call(bf16[112,2048]{1,0:T(8,128)(2,1)S(1)} %copy-done.2, bf16[112,2048]{1,0:T(8,128)(2,1)S(1)} %collective-permute-done.2.refs_1_, bf16[736,128]{1,0:T(8,128)(2,1)S(1)} %pair_low_sums.1.refs_3_.refs_2_, ...), custom_call_target="tpu_custom_call" | custom-call | flops 234881024 | bytes 1048576 | tf_op jit(solution)/shard_map/up_block/pallas_call | solution.py:28
  34.4 3.5 %collective-permute-start.10 = (bf16[128,512]{1,0:T(8,128)(2,1)S(1)}, bf16[128,512]{1,0:T(8,128)(2,1)S(1)}, u32[]{:S(2)}, u32[]{:S(2)}) collective-permute-start(bf16[128,512]{1,0:T(8,128)(2,1)S(1)} %get-tuple-element.37.refs_7_), channel_id=1, source_target_pairs={{0,2},{1,3},{2,0},{3,1},{4,6},{5,7},{6,4},{7,5},{8,10},{9,11},{10,... | collective-permute-start | bytes 393224 | tf_op jit(solution)/shard_map/ppermute | solution.py:417
  37.9 0.9 %collective-permute-done.5.refs_3_ = bf16[2,112,128]{2,1,0:T(8,128)(2,1)S(1)} collective-permute-done((bf16[2,112,128]{2,1,0:T(8,128)(2,1)S(1)}, bf16[2,112,128]{2,1,0:T(8,128)(2,1)S(1)}, u32[]{:S(2)}, u32[]{:S(2)}) %collective-permute-start.5) | collective-permute-done | bytes 57376 | tf_op jit(solution)/shard_map/ppermute | solution.py:417
  38.8 3.9 %collective-permute-done.6.refs_4_ = bf16[2,112,128]{2,1,0:T(8,128)(2,1)S(1)} collective-permute-done((bf16[2,112,128]{2,1,0:T(8,128)(2,1)S(1)}, bf16[2,112,128]{2,1,0:T(8,128)(2,1)S(1)}, u32[]{:S(2)}, u32[]{:S(2)}) %collective-permute-start.6) | collective-permute-done | bytes 57376 | tf_op jit(solution)/shard_map/ppermute | solution.py:417
  43.4 1.6 %collective-permute-start.12 = (bf16[112,512]{1,0:T(8,128)(2,1)S(1)}, bf16[112,512]{1,0:T(8,128)(2,1)S(1)}, u32[]{:S(2)}, u32[]{:S(2)}) collective-permute-start(bf16[112,512]{1,0:T(8,128)(2,1)S(1)} %get-tuple-element.43.refs_8_), channel_id=1, source_target_pairs={{0,8},{4,12},{8,0},{12,4},{1,9},{5,13},{9,1},{13,5},{2,10},{6,14},... | collective-permute-start | bytes 344072 | tf_op jit(solution)/shard_map/ppermute | solution.py:417
  44.9 1.8 %collective-permute-done.10.refs_3_ = bf16[128,512]{1,0:T(8,128)(2,1)S(1)} collective-permute-done((bf16[128,512]{1,0:T(8,128)(2,1)S(1)}, bf16[128,512]{1,0:T(8,128)(2,1)S(1)}, u32[]{:S(2)}, u32[]{:S(2)}) %collective-permute-start.10) | collective-permute-done | bytes 131104 | tf_op jit(solution)/shard_map/ppermute | solution.py:417
  47.0 1.5 %collective-permute-done.12.refs_4_ = bf16[112,512]{1,0:T(8,128)(2,1)S(1)} collective-permute-done((bf16[112,512]{1,0:T(8,128)(2,1)S(1)}, bf16[112,512]{1,0:T(8,128)(2,1)S(1)}, u32[]{:S(2)}, u32[]{:S(2)}) %collective-permute-start.12) | collective-permute-done | bytes 114720 | tf_op jit(solution)/shard_map/ppermute | solution.py:417
  48.5 1.8 %collective-permute-done.13.refs_5_ = bf16[112,512]{1,0:T(8,128)(2,1)S(1)} collective-permute-done((bf16[112,512]{1,0:T(8,128)(2,1)S(1)}, bf16[112,512]{1,0:T(8,128)(2,1)S(1)}, u32[]{:S(2)}, u32[]{:S(2)}) %collective-permute-start.13) | collective-permute-done | bytes 114720 | tf_op jit(solution)/shard_map/ppermute | solution.py:417
  50.3 1.0 %finish.1 = bf16[256,512]{1,0:T(8,128)(2,1)} custom-call(f32[256,512]{1,0:T(8,128)S(1)} %get-tuple-element.44.refs_0_, f32[256,128]{1,0:T(8,128)S(1)} %get-tuple-element.45.refs_1_, f32[256,128]{1,0:T(8,128)S(1)} %get-tuple-element.52.refs_4_.refs_2_, f32[256,128]{1,0:T(8,128)S(1)} %get-tuple-element.53.refs_5_.refs_3_, ...), custom_call_target="tpu_custom_call" | custom-call | flops 33554432 | tf_op jit(solution)/shard_map/finish/pallas_call | solution.py:28
  (41 shorter events, 2.2 us)
Async XLA Ops:
  3.6 12.4 %collective-permute-start.2 = (bf16[112,2048]{1,0:T(8,128)(2,1)}, bf16[112,2048]{1,0:T(8,128)(2,1)S(1)}, u32[]{:S(2)}, u32[]{:S(2)}) collective-permute-start(bf16[112,2048]{1,0:T(8,128)(2,1)} %get-tuple-element.31), channel_id=1, source_target_pairs={{0,4},{4,0},{8,12},{12,8},{1,5},{5,1},{9,13},{13,9},{2,6},{6,2},{1... | collective-permute-start | bytes 1376264 | tf_op jit(solution)/shard_map/ppermute | solution.py:417
  4.1 23.7 %collective-permute-start = (bf16[112,2048]{1,0:T(8,128)(2,1)}, bf16[112,2048]{1,0:T(8,128)(2,1)S(1)}, u32[]{:S(2)}, u32[]{:S(2)}) collective-permute-start(bf16[112,2048]{1,0:T(8,128)(2,1)} %get-tuple-element.27), channel_id=1, source_target_pairs={{0,8},{4,12},{8,0},{12,4},{1,9},{5,13},{9,1},{13,5},{2,10},{6,14},... | collective-permute-start | bytes 1376264 | tf_op jit(solution)/shard_map/ppermute | solution.py:417
  6.7 21.1 %collective-permute-start.1 = (bf16[112,2048]{1,0:T(8,128)(2,1)}, bf16[112,2048]{1,0:T(8,128)(2,1)S(1)}, u32[]{:S(2)}, u32[]{:S(2)}) collective-permute-start(bf16[112,2048]{1,0:T(8,128)(2,1)} %get-tuple-element.28), channel_id=1, source_target_pairs={{0,12},{4,8},{8,4},{12,0},{1,13},{5,9},{9,5},{13,1},{2,14},{6,10},... | collective-permute-start | bytes 1376264 | tf_op jit(solution)/shard_map/ppermute | solution.py:417
  6.8 5.1 %copy-start.9 = (s32[256]{0:T(256)S(1)}, s32[256]{0:T(256)}, u32[]{:S(2)}) copy-start(s32[256]{0:T(256)} %param.15) | copy-start | bytes 3076
  6.8 6.4 %copy-start = (bf16[8,2048,128]{2,1,0:T(8,128)(2,1)S(1)}, bf16[8,2048,128]{2,1,0:T(8,128)(2,1)}, u32[]{:S(2)}) copy-start(bf16[8,2048,128]{2,1,0:T(8,128)(2,1)} %refs_1_.7) | copy-start | bytes 12582916
  6.8 6.4 %copy-start.5 = (bf16[2048]{0:T(1024)(128)(2,1)S(1)}, bf16[2048]{0:T(1024)(128)(2,1)}, u32[]{:S(2)}) copy-start(bf16[2048]{0:T(1024)(128)(2,1)} %param.9) | copy-start | bytes 12292
  10.0 13.8 %collective-permute-start.4 = (bf16[256,512]{1,0:T(8,128)(2,1)}, bf16[256,512]{1,0:T(8,128)(2,1)S(1)}, u32[]{:S(2)}, u32[]{:S(2)}) collective-permute-start(bf16[256,512]{1,0:T(8,128)(2,1)} %base_far.1.refs_2_), channel_id=1, source_target_pairs={{0,1},{1,0},{2,3},{3,2},{4,5},{5,4},{6,7},{7,6},{8,9},{9,8},{10,11... | collective-permute-start | bytes 786440 | tf_op jit(solution)/shard_map/ppermute | solution.py:417
  13.1 1.0 %copy-start.3 = (bf16[256,512]{1,0:T(8,128)(2,1)S(1)}, bf16[256,512]{1,0:T(8,128)(2,1)}, u32[]{:S(2)}) copy-start(bf16[256,512]{1,0:T(8,128)(2,1)} %base_far.1.refs_2_) | copy-start | bytes 786436
  14.1 2.0 %copy-start.2 = (bf16[112,2048]{1,0:T(8,128)(2,1)S(1)}, bf16[112,2048]{1,0:T(8,128)(2,1)}, u32[]{:S(2)}) copy-start(bf16[112,2048]{1,0:T(8,128)(2,1)} %get-tuple-element.30.refs_0_) | copy-start | bytes 1376260
  17.2 9.3 %copy-start.8 = (f32[256,64]{1,0:T(8,128)S(1)}, f32[256,64]{1,0:T(8,128)}, u32[]{:S(2)}) copy-start(f32[256,64]{1,0:T(8,128)} %get-tuple-element.51) | copy-start | bytes 196612
  17.3 9.5 %copy-start.4 = (bf16[256,2048]{1,0:T(8,128)(2,1)S(1)}, bf16[256,2048]{1,0:T(8,128)(2,1)}, u32[]{:S(2)}) copy-start(bf16[256,2048]{1,0:T(8,128)(2,1)} %refs_2_.3) | copy-start | bytes 3145732
  17.3 9.5 %copy-start.6 = (s32[256]{0:T(256)S(1)}, s32[256]{0:T(256)}, u32[]{:S(2)}) copy-start(s32[256]{0:T(256)} %param.13) | copy-start | bytes 3076
  17.3 9.5 %copy-start.7 = (s32[32]{0:T(128)S(1)}, s32[32]{0:T(128)}, u32[]{:S(2)}) copy-start(s32[32]{0:T(128)} %refs_1_.9) | copy-start | bytes 388
  17.3 6.6 %collective-permute-start.3 = (bf16[2,112,128]{2,1,0:T(8,128)(2,1)S(1)}, bf16[2,112,128]{2,1,0:T(8,128)(2,1)S(1)}, u32[]{:S(2)}, u32[]{:S(2)}) collective-permute-start(bf16[2,112,128]{2,1,0:T(8,128)(2,1)S(1)} %down_block.2.refs_2_.refs_0_), channel_id=1, source_target_pairs={{0,1},{1,0},{2,3},{3,2},{4,5},{5,4},{6,7},{7,6},{8,9},{9,8},{10,11... | collective-permute-start | bytes 172040 | tf_op jit(solution)/shard_map/ppermute | solution.py:417
  22.0 12.2 %collective-permute-start.8 = (bf16[256,512]{1,0:T(8,128)(2,1)S(1)}, bf16[256,512]{1,0:T(8,128)(2,1)S(1)}, u32[]{:S(2)}, u32[]{:S(2)}) collective-permute-start(bf16[256,512]{1,0:T(8,128)(2,1)S(1)} %get-tuple-element.35), channel_id=1, source_target_pairs={{0,1},{1,0},{2,3},{3,2},{4,5},{5,4},{6,7},{7,6},{8,9},{9,8},{10,11... | collective-permute-start | bytes 786440 | tf_op jit(solution)/shard_map/ppermute | solution.py:417
  23.9 9.8 %copy-start.1 = (bf16[8,64,512]{2,1,0:T(8,128)(2,1)S(1)}, bf16[8,64,512]{2,1,0:T(8,128)(2,1)}, u32[]{:S(2)}) copy-start(bf16[8,64,512]{2,1,0:T(8,128)(2,1)} %refs_6_.1) | copy-start | bytes 1572868
  23.9 9.7 %collective-permute-start.9 = (bf16[736,128]{1,0:T(8,128)(2,1)S(1)}, bf16[736,128]{1,0:T(8,128)(2,1)S(1)}, u32[]{:S(2)}, u32[]{:S(2)}) collective-permute-start(bf16[736,128]{1,0:T(8,128)(2,1)S(1)} %pair_low_sums.1.refs_3_.refs_2_), channel_id=1, source_target_pairs={{0,2},{1,3},{2,0},{3,1},{4,6},{5,7},{6,4},{7,5},{8,10},{9,11},{10,... | collective-permute-start | bytes 565256 | tf_op jit(solution)/shard_map/ppermute | solution.py:417
  29.0 9.8 %collective-permute-start.5 = (bf16[2,112,128]{2,1,0:T(8,128)(2,1)S(1)}, bf16[2,112,128]{2,1,0:T(8,128)(2,1)S(1)}, u32[]{:S(2)}, u32[]{:S(2)}) collective-permute-start(bf16[2,112,128]{2,1,0:T(8,128)(2,1)S(1)} %down_block.3.refs_5_.refs_2_), channel_id=1, source_target_pairs={{0,3},{1,2},{2,1},{3,0},{4,7},{5,6},{6,5},{7,4},{8,11},{9,10},{10,... | collective-permute-start | bytes 172040 | tf_op jit(solution)/shard_map/ppermute | solution.py:417
  32.5 10.2 %collective-permute-start.6 = (bf16[2,112,128]{2,1,0:T(8,128)(2,1)S(1)}, bf16[2,112,128]{2,1,0:T(8,128)(2,1)S(1)}, u32[]{:S(2)}, u32[]{:S(2)}) collective-permute-start(bf16[2,112,128]{2,1,0:T(8,128)(2,1)S(1)} %down_block.3.refs_5_.refs_2_), channel_id=1, source_target_pairs={{0,2},{1,3},{2,0},{3,1},{4,6},{5,7},{6,4},{7,5},{8,10},{9,11},{10,... | collective-permute-start | bytes 172040 | tf_op jit(solution)/shard_map/ppermute | solution.py:417
  32.5 10.2 %collective-permute-start.7 = (bf16[2,112,128]{2,1,0:T(8,128)(2,1)S(1)}, bf16[2,112,128]{2,1,0:T(8,128)(2,1)S(1)}, u32[]{:S(2)}, u32[]{:S(2)}) collective-permute-start(bf16[2,112,128]{2,1,0:T(8,128)(2,1)S(1)} %down_block.3.refs_5_.refs_2_), channel_id=1, source_target_pairs={{0,1},{1,0},{2,3},{3,2},{4,5},{5,4},{6,7},{7,6},{8,9},{9,8},{10,11... | collective-permute-start | bytes 172040 | tf_op jit(solution)/shard_map/ppermute | solution.py:417
  34.4 12.4 %collective-permute-start.10 = (bf16[128,512]{1,0:T(8,128)(2,1)S(1)}, bf16[128,512]{1,0:T(8,128)(2,1)S(1)}, u32[]{:S(2)}, u32[]{:S(2)}) collective-permute-start(bf16[128,512]{1,0:T(8,128)(2,1)S(1)} %get-tuple-element.37.refs_7_), channel_id=1, source_target_pairs={{0,2},{1,3},{2,0},{3,1},{4,6},{5,7},{6,4},{7,5},{8,10},{9,11},{10,... | collective-permute-start | bytes 393224 | tf_op jit(solution)/shard_map/ppermute | solution.py:417
  37.9 7.1 %collective-permute-start.11 = (bf16[112,512]{1,0:T(8,128)(2,1)S(1)}, bf16[112,512]{1,0:T(8,128)(2,1)S(1)}, u32[]{:S(2)}, u32[]{:S(2)}) collective-permute-start(bf16[112,512]{1,0:T(8,128)(2,1)S(1)} %get-tuple-element.40), channel_id=1, source_target_pairs={{0,4},{4,0},{8,12},{12,8},{1,5},{5,1},{9,13},{13,9},{2,6},{6,2},{1... | collective-permute-start | bytes 344072 | tf_op jit(solution)/shard_map/ppermute | solution.py:417
  43.4 5.2 %collective-permute-start.12 = (bf16[112,512]{1,0:T(8,128)(2,1)S(1)}, bf16[112,512]{1,0:T(8,128)(2,1)S(1)}, u32[]{:S(2)}, u32[]{:S(2)}) collective-permute-start(bf16[112,512]{1,0:T(8,128)(2,1)S(1)} %get-tuple-element.43.refs_8_), channel_id=1, source_target_pairs={{0,8},{4,12},{8,0},{12,4},{1,9},{5,13},{9,1},{13,5},{2,10},{6,14},... | collective-permute-start | bytes 344072 | tf_op jit(solution)/shard_map/ppermute | solution.py:417
  44.9 5.4 %collective-permute-start.13 = (bf16[112,512]{1,0:T(8,128)(2,1)S(1)}, bf16[112,512]{1,0:T(8,128)(2,1)S(1)}, u32[]{:S(2)}, u32[]{:S(2)}) collective-permute-start(bf16[112,512]{1,0:T(8,128)(2,1)S(1)} %get-tuple-element.46), channel_id=1, source_target_pairs={{0,12},{4,8},{8,4},{12,0},{1,13},{5,9},{9,5},{13,1},{2,14},{6,10},... | collective-permute-start | bytes 344072 | tf_op jit(solution)/shard_map/ppermute | solution.py:417

commit v5 on v3

--- a/solution.py
+++ b/solution.py
@@ -142,15 +142,16 @@
                 outs[j][...] = y.astype(outs[j].dtype)
 
 
-def pair_kernel(count, start, *refs):
+def pair_kernel(count, start, base_ref, near_ref, *refs):
+    refs[-1][...] = base_ref[...] + near_ref[...].astype(F32)
     for j in range(count):
         out_ref = refs[2 * count + j]
         rows = slice(start, start + out_ref.shape[0])
         out_ref[...] = (refs[j][rows] + refs[count + j][rows].astype(F32)).astype(BF16)
 
 
-def pair_low_kernel(count, near_ref, low_ref, other_ref, *refs):
-    outs, sent_ref = refs[2 * count : -1], refs[-1]
+def pair_low_kernel(count, low_ref, other_ref, *refs):
+    outs = refs[2 * count :]
     cols = refs[0].shape[1]
     half = refs[0].shape[0] // 2
     for j in range(count):
@@ -162,7 +163,6 @@
     for i in range(groups):
         total = low_ref[i].astype(F32) + other_ref[i].astype(F32)
         outs[0][base + i * height : base + (i + 1) * height] = total.astype(BF16)
-    sent_ref[...] = near_ref[...]
 
 
 def scaled_down_kernel(gain_ref, down_hbm, out_ref, buf, sems):
@@ -182,9 +182,9 @@
             ).astype(BF16)
 
 
-def aux_kernel(n_wide, per_dev, req_hbm, table_hbm, tok_hbm, sq_ref, *refs):
+def aux_kernel(n_wide, per_dev, near_ref, req_hbm, table_hbm, tok_hbm, sq_ref, *refs):
     sels = refs[:n_wide]
-    req_ref, table_ref, tok_ref, sems = refs[n_wide:]
+    sent_ref, req_ref, table_ref, tok_ref, sems = refs[n_wide:]
     copies = [
         pltpu.make_async_copy(req_hbm, req_ref, sems.at[0]),
         pltpu.make_async_copy(table_hbm, table_ref, sems.at[1]),
@@ -192,6 +192,7 @@
     ]
     for copy in copies:
         copy.start()
+    sent_ref[...] = near_ref[...]
     for copy in copies:
         copy.wait()
     rows = tok_ref.shape[0]
@@ -318,7 +319,7 @@
     return jnp.dot(lhs, jnp.concatenate(blocks, axis=0), preferred_element_type=F32)
 
 
-def gather_kernel(n_pairs, count, sq_ref, base_ref, near_ref, *refs):
+def gather_kernel(n_pairs, count, sq_ref, base_ref, *refs):
     tops, bottoms = refs[:n_pairs], refs[n_pairs : 2 * n_pairs]
     deltas = refs[2 * n_pairs : 2 * n_pairs + count]
     sels = refs[2 * n_pairs + count : 2 * n_pairs + 2 * count]
@@ -334,7 +335,7 @@
     square = to_column(jnp.concatenate(squares, axis=1), rows)
     scale = lax.rsqrt(square * (1.0 / MODEL_WIDTH) + EPSILON)
     scale_ref[...] = jnp.broadcast_to(scale, (rows, HEAD))
-    total = base_ref[...] + near_ref[...].astype(F32) + placed(sels, deltas)
+    total = base_ref[...] + placed(sels, deltas)
     half = rows // 2
     lower = total[half:]
     for bottom in bottoms:
@@ -495,10 +496,13 @@
         )
 
     low = down_block(first, (), ())
-    sq, *sels = call(
+    sq, *sels, near = call(
         functools.partial(aux_kernel, n_wide, per_dev),
         "aux",
-        [shape((8, HEAD), F32)] + [shape((rows, HEAD), BF16)] * n_wide,
+        [shape((8, HEAD), F32)]
+        + [shape((rows, HEAD), BF16)] * n_wide
+        + [shape((rows, cols), BF16)],
+        vmem=(near,),
         hbm=(req, adapter_storage_row, tokens),
         after=(low,),
         scratch=small + [pltpu.VMEM((rows, depth), BF16), pltpu.SemaphoreType.DMA((3,))],
@@ -508,17 +512,16 @@
     half = rows // 2
     upper = cols // HEAD * half
     other = over("tensor", low, 1)
-    *pairs, near = call(
+    near = over("tensor", near, 1)
+    pairs = call(
         functools.partial(pair_low_kernel, len(twos)),
         "pair_low_sums",
         [shape((upper + len(first) * height, HEAD), BF16)]
-        + [shape((upper, HEAD), BF16)] * (len(twos) - 1)
-        + [shape((rows, cols), BF16)],
-        vmem=(near, low, other, *own, *beside),
+        + [shape((upper, HEAD), BF16)] * (len(twos) - 1),
+        vmem=(low, other, *own, *beside),
         after=(sq, cosine, sine),
     )
     tops = [over("tensor", p, k) for p, k in zip(pairs, twos)]
-    near = over("tensor", near, 1)
     done = pairs[0]
     low, other = pairs[0], tops[0]
     for step in range(2, n_tensor.bit_length() - 1):
@@ -533,11 +536,11 @@
     last_parts = [low_last] + [over("tensor", low_last, k) for k in range(n_tensor - 1, 0, -1)]
     ups = up_block(first, [low, other], False, (low_last,))
     deltas = [u if k == 0 else over("wide", u, k) for k, u in zip(first, ups)]
-    pairs = call(
+    *pairs, base = call(
         functools.partial(pair_kernel, len(twos), half),
         "pair_sums",
-        [shape((half, cols), BF16)] * len(twos),
-        vmem=(*own, *beside),
+        [shape((half, cols), BF16)] * len(twos) + [shape((rows, cols), F32)],
+        vmem=(base, near, *own, *beside),
         after=(ups[0],),
     )
     bottoms = [over("tensor", p, k) for p, k in zip(pairs, twos)]
@@ -547,7 +550,7 @@
         functools.partial(gather_kernel, len(bottoms), len(first)),
         "gather",
         [shape((rows, cols), F32), shape((rows, HEAD), F32)],
-        vmem=(square, base, near, *tops, *bottoms, *deltas, *[sels[k] for k in first]),
+        vmem=(square, base, *tops, *bottoms, *deltas, *[sels[k] for k in first]),
         after=(ups[0],),
         flops=2 * rows * cols * HEAD * len(first),
     )

time: 50.4 us -> 50.8 us (level)
  the two profiles are of different devices: /device:TPU:0 before, /device:TPU:12 now
where the time goes in v5:
time: 50.8 us; the launch traced here: 50.6 us
  starting transfers between devices  18.3 us (36%)
  Pallas kernels  16.2 us (32%)
  waiting for transfers between devices  14.5 us (29%)
  local copies, waits for them, and re-layouts  0.73 us (1%)
  other arithmetic  0.68 us (1%)
    ppermute x14, starting transfers between devices, over(): return lax.ppermute(array, axis, [(i, i ^ k) for i in range(size)])  18.3 us
    pallas_call x12, Pallas kernels, call(): pl.pallas_call(body, out_shape=outs, in_specs=[pl.BlockSpec(memory_space=...  16.2 us
    ppermute x14, waiting for transfers between devices, over(): return lax.ppermute(array, axis, [(i, i ^ k) for i in range(size)])  14.5 us
  transfers between devices with their start and end apart: 14, of which 7 were waited for; matrix products, arithmetic and copies ran while one was open for 1% of the time, Pallas kernels for 23%

profile of v5, /device:TPU:12, one launch (start us, length us, event | category | flops | bytes accessed | tf_op | source)
XLA Modules:
  0.0 50.6 jit_solution(5657327539357578752)
XLA Ops:
  0.0 3.5 %dispatch.1 = (bf16[112,2048]{1,0:T(8,128)(2,1)}, bf16[112,2048]{1,0:T(8,128)(2,1)}, bf16[112,2048]{1,0:T(8,128)(2,1)}, bf16[112,2048]{1,0:T(8,128)(2,1)}, f32[16,128]{1,0:T(8,128)}) custom-call(s32[1,256]{1,0:T(1,128)} %bitcast.2, s32[32]{0:T(128)} %refs_2_.5, bf16[256,2048]{1,0:T(8,128)(2,1)} %refs_3_.1, bf16[16,128]{1,0:T(8,128)(2,1)} %bitcast.4), custom_call_target="tpu_custom_call" | custom-call | flops 469762048 | bytes 4194304 | tf_op jit(solution)/shard_map/dispatch/pallas_call | solution.py:28
  3.5 1.6 %collective-permute-start = (bf16[112,2048]{1,0:T(8,128)(2,1)}, bf16[112,2048]{1,0:T(8,128)(2,1)S(1)}, u32[]{:S(2)}, u32[]{:S(2)}) collective-permute-start(bf16[112,2048]{1,0:T(8,128)(2,1)} %get-tuple-element.29), channel_id=1, source_target_pairs={{0,8},{4,12},{8,0},{12,4},{1,9},{5,13},{9,1},{13,5},{2,10},{6,14},... | collective-permute-start | bytes 1376264 | tf_op jit(solution)/shard_map/ppermute | solution.py:393
  5.0 0.7 %collective-permute-start.2 = (bf16[112,2048]{1,0:T(8,128)(2,1)}, bf16[112,2048]{1,0:T(8,128)(2,1)S(1)}, u32[]{:S(2)}, u32[]{:S(2)}) collective-permute-start(bf16[112,2048]{1,0:T(8,128)(2,1)} %get-tuple-element.35), channel_id=1, source_target_pairs={{0,4},{4,0},{8,12},{12,8},{1,5},{5,1},{9,13},{13,9},{2,6},{6,2},{1... | collective-permute-start | bytes 1376264 | tf_op jit(solution)/shard_map/ppermute | solution.py:393
  5.7 0.7 %copy-done.4 = f32[16,128]{1,0:T(8,128)S(1)} copy-done((f32[16,128]{1,0:T(8,128)S(1)}, f32[16,128]{1,0:T(8,128)}, u32[]{:S(2)}) %copy-start.4) | copy-done | bytes 8216
  6.4 4.8 %base.1 = (bf16[256,512]{1,0:T(8,128)(2,1)S(1)}, bf16[256,512]{1,0:T(8,128)(2,1)S(1)}, f32[256,512]{1,0:T(8,128)S(1)}, f32[256,512]{1,0:T(8,128)S(1)}) custom-call(f32[16,128]{1,0:T(8,128)S(1)} %copy-done.4, bf16[256,2048]{1,0:T(8,128)(2,1)} %refs_3_.1, bf16[2048,2048]{1,0:T(8,128)(2,1)} %refs_2_.4), custom_call_target="tpu_custom_call" | custom-call | flops 2147483648 | bytes 8388608 | tf_op jit(solution)/shard_map/base/pallas_call | solution.py:28
  12.3 2.0 %scaled_down.1.refs_2_ = bf16[2048,1024]{1,0:T(8,128)(2,1)S(1)} custom-call(f32[16,128]{1,0:T(8,128)S(1)} %copy-done.4, bf16[8,2048,128]{2,1,0:T(8,128)(2,1)S(1)} %copy-done, f32[256,512]{1,0:T(8,128)S(1)} %get-tuple-element.32.refs_2_.refs_0_), custom_call_target="tpu_custom_call" | custom-call | flops 8388608 | bytes 8388608 | tf_op jit(solution)/shard_map/scaled_down/pallas_call | solution.py:28
  14.3 1.2 %down_block.2.refs_4_.refs_0_ = bf16[2,112,128]{2,1,0:T(8,128)(2,1)S(1)} custom-call(bf16[112,2048]{1,0:T(8,128)(2,1)S(1)} %copy-done.3, bf16[112,2048]{1,0:T(8,128)(2,1)S(1)} %collective-permute-done.2.refs_1_, bf16[2048,1024]{1,0:T(8,128)(2,1)S(1)} %scaled_down.1.refs_2_), custom_call_target="tpu_custom_call" | custom-call | flops 939524096 | bytes 4194304 | tf_op jit(solution)/shard_map/down_block/pallas_call | solution.py:28
  15.5 1.6 %collective-permute-start.3 = (bf16[2,112,128]{2,1,0:T(8,128)(2,1)S(1)}, bf16[2,112,128]{2,1,0:T(8,128)(2,1)S(1)}, u32[]{:S(2)}, u32[]{:S(2)}) collective-permute-start(bf16[2,112,128]{2,1,0:T(8,128)(2,1)S(1)} %down_block.2.refs_4_.refs_0_), channel_id=1, source_target_pairs={{0,1},{1,0},{2,3},{3,2},{4,5},{5,4},{6,7},{7,6},{8,9},{9,8},{10,11... | collective-permute-start | bytes 172040 | tf_op jit(solution)/shard_map/ppermute | solution.py:393
  17.1 1.1 %aux.1 = (f32[8,128]{1,0:T(8,128)S(1)}, bf16[256,128]{1,0:T(8,128)(2,1)S(1)}, bf16[256,128]{1,0:T(8,128)(2,1)S(1)}, bf16[256,128]{1,0:T(8,128)(2,1)S(1)}, bf16[2...) custom-call(bf16[256,512]{1,0:T(8,128)(2,1)S(1)} %get-tuple-element.33.refs_0_, s32[1,256]{1,0:T(1,128)S(1)} %bitcast.3, ...), custom_call_target="tpu_custom_call" | custom-call | flops 268435456 | bytes 1048576 | tf_op jit(solution)/shard_map/aux/pallas_call | solution.py:28
  18.9 1.2 %collective-permute-done.4.refs_3_ = bf16[256,512]{1,0:T(8,128)(2,1)S(1)} collective-permute-done((bf16[256,512]{1,0:T(8,128)(2,1)S(1)}, bf16[256,512]{1,0:T(8,128)(2,1)S(1)}, u32[]{:S(2)}, u32[]{:S(2)}) %collective-permute-start.4) | collective-permute-done | bytes 262176 | tf_op jit(solution)/shard_map/ppermute | solution.py:393
  20.1 0.9 %collective-permute-done.3.refs_1_ = bf16[2,112,128]{2,1,0:T(8,128)(2,1)S(1)} collective-permute-done((bf16[2,112,128]{2,1,0:T(8,128)(2,1)S(1)}, bf16[2,112,128]{2,1,0:T(8,128)(2,1)S(1)}, u32[]{:S(2)}, u32[]{:S(2)}) %collective-permute-start.3) | collective-permute-done | bytes 57376 | tf_op jit(solution)/shard_map/ppermute | solution.py:393
  21.1 2.7 %collective-permute-start.9 = (bf16[736,128]{1,0:T(8,128)(2,1)S(1)}, bf16[736,128]{1,0:T(8,128)(2,1)S(1)}, u32[]{:S(2)}, u32[]{:S(2)}) collective-permute-start(bf16[736,128]{1,0:T(8,128)(2,1)S(1)} %pair_low_sums.1.refs_4_.refs_2_), channel_id=1, source_target_pairs={{0,2},{1,3},{2,0},{3,1},{4,6},{5,7},{6,4},{7,5},{8,10},{9,11},{10,... | collective-permute-start | bytes 565256 | tf_op jit(solution)/shard_map/ppermute | solution.py:393
  23.8 1.2 %collective-permute-done.1.refs_1_ = bf16[112,2048]{1,0:T(8,128)(2,1)S(1)} collective-permute-done((bf16[112,2048]{1,0:T(8,128)(2,1)}, bf16[112,2048]{1,0:T(8,128)(2,1)S(1)}, u32[]{:S(2)}, u32[]{:S(2)}) %collective-permute-start.1) | collective-permute-done | bytes 458784 | tf_op jit(solution)/shard_map/ppermute | solution.py:393
  25.0 1.1 %down_block.3.refs_5_.refs_2_ = bf16[2,112,128]{2,1,0:T(8,128)(2,1)S(1)} custom-call(bf16[112,2048]{1,0:T(8,128)(2,1)S(1)} %collective-permute-done.refs_0_, bf16[112,2048]{1,0:T(8,128)(2,1)S(1)} %collective-permute-done.1.refs_1_, bf16[2048,1024]{1,0:T(8,128)(2,1)S(1)} %scaled_down.1.refs_2_, f32[8,128]{1,0:T(8,128)S(1)} %get-tuple-element.36.refs_4_.refs_3_, ...), custom_call_target="tpu_custom_call" | custom-call | flops 939524096 | bytes 4194304 | tf_op jit(solution)/shard_map/down_block/pallas_call | solution.py:28
  26.6 2.6 %collective-permute-start.6 = (bf16[2,112,128]{2,1,0:T(8,128)(2,1)S(1)}, bf16[2,112,128]{2,1,0:T(8,128)(2,1)S(1)}, u32[]{:S(2)}, u32[]{:S(2)}) collective-permute-start(bf16[2,112,128]{2,1,0:T(8,128)(2,1)S(1)} %down_block.3.refs_5_.refs_2_), channel_id=1, source_target_pairs={{0,2},{1,3},{2,0},{3,1},{4,6},{5,7},{6,4},{7,5},{8,10},{9,11},{10,... | collective-permute-start | bytes 172040 | tf_op jit(solution)/shard_map/ppermute | solution.py:393
  29.7 5.6 %collective-permute-done.9.refs_3_.refs_2_ = bf16[736,128]{1,0:T(8,128)(2,1)S(1)} collective-permute-done((bf16[736,128]{1,0:T(8,128)(2,1)S(1)}, bf16[736,128]{1,0:T(8,128)(2,1)S(1)}, u32[]{:S(2)}, u32[]{:S(2)}) %collective-permute-start.9) | collective-permute-done | bytes 188448 | tf_op jit(solution)/shard_map/ppermute | solution.py:393
  35.3 0.6 %up_block.2 = (bf16[112,512]{1,0:T(8,128)(2,1)S(1)}, bf16[112,512]{1,0:T(8,128)(2,1)S(1)}) custom-call(bf16[112,2048]{1,0:T(8,128)(2,1)S(1)} %copy-done.3, bf16[112,2048]{1,0:T(8,128)(2,1)S(1)} %collective-permute-done.2.refs_1_, bf16[736,128]{1,0:T(8,128)(2,1)S(1)} %pair_low_sums.1.refs_4_.refs_2_, ...), custom_call_target="tpu_custom_call" | custom-call | flops 234881024 | bytes 1048576 | tf_op jit(solution)/shard_map/up_block/pallas_call | solution.py:28
  36.0 5.0 %collective-permute-start.10 = (bf16[128,512]{1,0:T(8,128)(2,1)S(1)}, bf16[128,512]{1,0:T(8,128)(2,1)S(1)}, u32[]{:S(2)}, u32[]{:S(2)}) collective-permute-start(bf16[128,512]{1,0:T(8,128)(2,1)S(1)} %get-tuple-element.41.refs_7_), channel_id=1, source_target_pairs={{0,2},{1,3},{2,0},{3,1},{4,6},{5,7},{6,4},{7,5},{8,10},{9,11},{10,... | collective-permute-start | bytes 393224 | tf_op jit(solution)/shard_map/ppermute | solution.py:393
  41.0 0.6 %up_block.3 = (bf16[112,512]{1,0:T(8,128)(2,1)S(1)}, bf16[112,512]{1,0:T(8,128)(2,1)S(1)}, f32[8,128]{1,0:T(8,128)S(1)}) custom-call(bf16[112,2048]{1,0:T(8,128)(2,1)S(1)} %collective-permute-done.refs_0_, bf16[112,2048]{1,0:T(8,128)(2,1)S(1)} %collective-permute-done.1.refs_1_, bf16[2,112,128]{2,1,0:T(8,128)(2,1)S(1)} %down_block.3.refs_5_.refs_2_, ...), custom_call_target="tpu_custom_call" | custom-call | flops 234881024 | bytes 1048576 | tf_op jit(solution)/shard_map/up_block/pallas_call | solution.py:28
  41.6 1.6 %collective-permute-start.13 = (bf16[112,512]{1,0:T(8,128)(2,1)S(1)}, bf16[112,512]{1,0:T(8,128)(2,1)S(1)}, u32[]{:S(2)}, u32[]{:S(2)}) collective-permute-start(bf16[112,512]{1,0:T(8,128)(2,1)S(1)} %get-tuple-element.50), channel_id=1, source_target_pairs={{0,12},{4,8},{8,4},{12,0},{1,13},{5,9},{9,5},{13,1},{2,14},{6,10},... | collective-permute-start | bytes 344072 | tf_op jit(solution)/shard_map/ppermute | solution.py:393
  43.3 0.6 %collective-permute-start.12 = (bf16[112,512]{1,0:T(8,128)(2,1)S(1)}, bf16[112,512]{1,0:T(8,128)(2,1)S(1)}, u32[]{:S(2)}, u32[]{:S(2)}) collective-permute-start(bf16[112,512]{1,0:T(8,128)(2,1)S(1)} %get-tuple-element.47.refs_8_), channel_id=1, source_target_pairs={{0,8},{4,12},{8,0},{12,4},{1,9},{5,13},{9,1},{13,5},{2,10},{6,14},... | collective-permute-start | bytes 344072 | tf_op jit(solution)/shard_map/ppermute | solution.py:393
  44.2 2.6 %collective-permute-done.13.refs_5_ = bf16[112,512]{1,0:T(8,128)(2,1)S(1)} collective-permute-done((bf16[112,512]{1,0:T(8,128)(2,1)S(1)}, bf16[112,512]{1,0:T(8,128)(2,1)S(1)}, u32[]{:S(2)}, u32[]{:S(2)}) %collective-permute-start.13) | collective-permute-done | bytes 114720 | tf_op jit(solution)/shard_map/ppermute | solution.py:393
  46.8 2.8 %collective-permute-done.12.refs_4_ = bf16[112,512]{1,0:T(8,128)(2,1)S(1)} collective-permute-done((bf16[112,512]{1,0:T(8,128)(2,1)S(1)}, bf16[112,512]{1,0:T(8,128)(2,1)S(1)}, u32[]{:S(2)}, u32[]{:S(2)}) %collective-permute-start.12) | collective-permute-done | bytes 114720 | tf_op jit(solution)/shard_map/ppermute | solution.py:393
  49.6 1.0 %finish.1 = bf16[256,512]{1,0:T(8,128)(2,1)} custom-call(f32[256,512]{1,0:T(8,128)S(1)} %get-tuple-element.48.refs_0_, f32[256,128]{1,0:T(8,128)S(1)} %get-tuple-element.49.refs_1_, f32[256,128]{1,0:T(8,128)S(1)} %get-tuple-element.56.refs_5_.refs_2_, f32[256,128]{1,0:T(8,128)S(1)} %get-tuple-element.57.refs_6_.refs_3_, ...), custom_call_target="tpu_custom_call" | custom-call | flops 33554432 | tf_op jit(solution)/shard_map/finish/pallas_call | solution.py:28
  (36 shorter events, 3.2 us)
Async XLA Ops:
  3.5 20.3 %collective-permute-start = (bf16[112,2048]{1,0:T(8,128)(2,1)}, bf16[112,2048]{1,0:T(8,128)(2,1)S(1)}, u32[]{:S(2)}, u32[]{:S(2)}) collective-permute-start(bf16[112,2048]{1,0:T(8,128)(2,1)} %get-tuple-element.29), channel_id=1, source_target_pairs={{0,8},{4,12},{8,0},{12,4},{1,9},{5,13},{9,1},{13,5},{2,10},{6,14},... | collective-permute-start | bytes 1376264 | tf_op jit(solution)/shard_map/ppermute | solution.py:393
  5.0 19.9 %collective-permute-start.1 = (bf16[112,2048]{1,0:T(8,128)(2,1)}, bf16[112,2048]{1,0:T(8,128)(2,1)S(1)}, u32[]{:S(2)}, u32[]{:S(2)}) collective-permute-start(bf16[112,2048]{1,0:T(8,128)(2,1)} %get-tuple-element.30), channel_id=1, source_target_pairs={{0,12},{4,8},{8,4},{12,0},{1,13},{5,9},{9,5},{13,1},{2,14},{6,10},... | collective-permute-start | bytes 1376264 | tf_op jit(solution)/shard_map/ppermute | solution.py:393
  5.0 9.3 %collective-permute-start.2 = (bf16[112,2048]{1,0:T(8,128)(2,1)}, bf16[112,2048]{1,0:T(8,128)(2,1)S(1)}, u32[]{:S(2)}, u32[]{:S(2)}) collective-permute-start(bf16[112,2048]{1,0:T(8,128)(2,1)} %get-tuple-element.35), channel_id=1, source_target_pairs={{0,4},{4,0},{8,12},{12,8},{1,5},{5,1},{9,13},{13,9},{2,6},{6,2},{1... | collective-permute-start | bytes 1376264 | tf_op jit(solution)/shard_map/ppermute | solution.py:393
  5.7 0.7 %copy-start.4 = (f32[16,128]{1,0:T(8,128)S(1)}, f32[16,128]{1,0:T(8,128)}, u32[]{:S(2)}) copy-start(f32[16,128]{1,0:T(8,128)} %get-tuple-element.31.refs_0_) | copy-start | bytes 24580
  6.4 5.3 %copy-start.7 = (s32[256]{0:T(256)S(1)}, s32[256]{0:T(256)}, u32[]{:S(2)}) copy-start(s32[256]{0:T(256)} %param.15) | copy-start | bytes 3076
  6.4 5.9 %copy-start = (bf16[8,2048,128]{2,1,0:T(8,128)(2,1)S(1)}, bf16[8,2048,128]{2,1,0:T(8,128)(2,1)}, u32[]{:S(2)}) copy-start(bf16[8,2048,128]{2,1,0:T(8,128)(2,1)} %refs_1_.5) | copy-start | bytes 12582916
  11.2 8.9 %collective-permute-start.4 = (bf16[256,512]{1,0:T(8,128)(2,1)S(1)}, bf16[256,512]{1,0:T(8,128)(2,1)S(1)}, u32[]{:S(2)}, u32[]{:S(2)}) collective-permute-start(bf16[256,512]{1,0:T(8,128)(2,1)S(1)} %get-tuple-element.38), channel_id=1, source_target_pairs={{0,1},{1,0},{2,3},{3,2},{4,5},{5,4},{6,7},{7,6},{8,9},{9,8},{10,11... | collective-permute-start | bytes 786440 | tf_op jit(solution)/shard_map/ppermute | solution.py:393
  12.3 2.0 %copy-start.3 = (bf16[112,2048]{1,0:T(8,128)(2,1)S(1)}, bf16[112,2048]{1,0:T(8,128)(2,1)}, u32[]{:S(2)}) copy-start(bf16[112,2048]{1,0:T(8,128)(2,1)} %get-tuple-element.34.refs_0_) | copy-start | bytes 1376260
  14.3 2.9 %copy-start.1 = (bf16[256,2048]{1,0:T(8,128)(2,1)S(1)}, bf16[256,2048]{1,0:T(8,128)(2,1)}, u32[]{:S(2)}) copy-start(bf16[256,2048]{1,0:T(8,128)(2,1)} %refs_3_.1) | copy-start | bytes 3145732
  14.3 2.8 %copy-start.5 = (s32[256]{0:T(256)S(1)}, s32[256]{0:T(256)}, u32[]{:S(2)}) copy-start(s32[256]{0:T(256)} %param.13) | copy-start | bytes 3076
  14.3 2.8 %copy-start.6 = (s32[32]{0:T(128)S(1)}, s32[32]{0:T(128)}, u32[]{:S(2)}) copy-start(s32[32]{0:T(128)} %refs_2_.5) | copy-start | bytes 388
  15.5 5.6 %collective-permute-start.3 = (bf16[2,112,128]{2,1,0:T(8,128)(2,1)S(1)}, bf16[2,112,128]{2,1,0:T(8,128)(2,1)S(1)}, u32[]{:S(2)}, u32[]{:S(2)}) collective-permute-start(bf16[2,112,128]{2,1,0:T(8,128)(2,1)S(1)} %down_block.2.refs_4_.refs_0_), channel_id=1, source_target_pairs={{0,1},{1,0},{2,3},{3,2},{4,5},{5,4},{6,7},{7,6},{8,9},{9,8},{10,11... | collective-permute-start | bytes 172040 | tf_op jit(solution)/shard_map/ppermute | solution.py:393
  17.1 18.2 %copy-start.2 = (bf16[8,64,512]{2,1,0:T(8,128)(2,1)S(1)}, bf16[8,64,512]{2,1,0:T(8,128)(2,1)}, u32[]{:S(2)}) copy-start(bf16[8,64,512]{2,1,0:T(8,128)(2,1)} %refs_6_.1) | copy-start | bytes 1572868
  18.2 17.7 %collective-permute-start.8 = (bf16[256,512]{1,0:T(8,128)(2,1)S(1)}, bf16[256,512]{1,0:T(8,128)(2,1)S(1)}, u32[]{:S(2)}, u32[]{:S(2)}) collective-permute-start(bf16[256,512]{1,0:T(8,128)(2,1)S(1)} %get-tuple-element.39), channel_id=1, source_target_pairs={{0,1},{1,0},{2,3},{3,2},{4,5},{5,4},{6,7},{7,6},{8,9},{9,8},{10,11... | collective-permute-start | bytes 786440 | tf_op jit(solution)/shard_map/ppermute | solution.py:393
  21.1 14.2 %collective-permute-start.9 = (bf16[736,128]{1,0:T(8,128)(2,1)S(1)}, bf16[736,128]{1,0:T(8,128)(2,1)S(1)}, u32[]{:S(2)}, u32[]{:S(2)}) collective-permute-start(bf16[736,128]{1,0:T(8,128)(2,1)S(1)} %pair_low_sums.1.refs_4_.refs_2_), channel_id=1, source_target_pairs={{0,2},{1,3},{2,0},{3,1},{4,6},{5,7},{6,4},{7,5},{8,10},{9,11},{10,... | collective-permute-start | bytes 565256 | tf_op jit(solution)/shard_map/ppermute | solution.py:393
  26.1 14.9 %collective-permute-start.7 = (bf16[2,112,128]{2,1,0:T(8,128)(2,1)S(1)}, bf16[2,112,128]{2,1,0:T(8,128)(2,1)S(1)}, u32[]{:S(2)}, u32[]{:S(2)}) collective-permute-start(bf16[2,112,128]{2,1,0:T(8,128)(2,1)S(1)} %down_block.3.refs_5_.refs_2_), channel_id=1, source_target_pairs={{0,1},{1,0},{2,3},{3,2},{4,5},{5,4},{6,7},{7,6},{8,9},{9,8},{10,11... | collective-permute-start | bytes 172040 | tf_op jit(solution)/shard_map/ppermute | solution.py:393
  26.6 14.4 %collective-permute-start.6 = (bf16[2,112,128]{2,1,0:T(8,128)(2,1)S(1)}, bf16[2,112,128]{2,1,0:T(8,128)(2,1)S(1)}, u32[]{:S(2)}, u32[]{:S(2)}) collective-permute-start(bf16[2,112,128]{2,1,0:T(8,128)(2,1)S(1)} %down_block.3.refs_5_.refs_2_), channel_id=1, source_target_pairs={{0,2},{1,3},{2,0},{3,1},{4,6},{5,7},{6,4},{7,5},{8,10},{9,11},{10,... | collective-permute-start | bytes 172040 | tf_op jit(solution)/shard_map/ppermute | solution.py:393
  29.2 11.8 %collective-permute-start.5 = (bf16[2,112,128]{2,1,0:T(8,128)(2,1)S(1)}, bf16[2,112,128]{2,1,0:T(8,128)(2,1)S(1)}, u32[]{:S(2)}, u32[]{:S(2)}) collective-permute-start(bf16[2,112,128]{2,1,0:T(8,128)(2,1)S(1)} %down_block.3.refs_5_.refs_2_), channel_id=1, source_target_pairs={{0,3},{1,2},{2,1},{3,0},{4,7},{5,6},{6,5},{7,4},{8,11},{9,10},{10,... | collective-permute-start | bytes 172040 | tf_op jit(solution)/shard_map/ppermute | solution.py:393
  36.0 7.9 %collective-permute-start.10 = (bf16[128,512]{1,0:T(8,128)(2,1)S(1)}, bf16[128,512]{1,0:T(8,128)(2,1)S(1)}, u32[]{:S(2)}, u32[]{:S(2)}) collective-permute-start(bf16[128,512]{1,0:T(8,128)(2,1)S(1)} %get-tuple-element.41.refs_7_), channel_id=1, source_target_pairs={{0,2},{1,3},{2,0},{3,1},{4,6},{5,7},{6,4},{7,5},{8,10},{9,11},{10,... | collective-permute-start | bytes 393224 | tf_op jit(solution)/shard_map/ppermute | solution.py:393
  41.0 2.8 %collective-permute-start.11 = (bf16[112,512]{1,0:T(8,128)(2,1)S(1)}, bf16[112,512]{1,0:T(8,128)(2,1)S(1)}, u32[]{:S(2)}, u32[]{:S(2)}) collective-permute-start(bf16[112,512]{1,0:T(8,128)(2,1)S(1)} %get-tuple-element.44), channel_id=1, source_target_pairs={{0,4},{4,0},{8,12},{12,8},{1,5},{5,1},{9,13},{13,9},{2,6},{6,2},{1... | collective-permute-start | bytes 344072 | tf_op jit(solution)/shard_map/ppermute | solution.py:393
  41.6 5.1 %collective-permute-start.13 = (bf16[112,512]{1,0:T(8,128)(2,1)S(1)}, bf16[112,512]{1,0:T(8,128)(2,1)S(1)}, u32[]{:S(2)}, u32[]{:S(2)}) collective-permute-start(bf16[112,512]{1,0:T(8,128)(2,1)S(1)} %get-tuple-element.50), channel_id=1, source_target_pairs={{0,12},{4,8},{8,4},{12,0},{1,13},{5,9},{9,5},{13,1},{2,14},{6,10},... | collective-permute-start | bytes 344072 | tf_op jit(solution)/shard_map/ppermute | solution.py:393
  43.3 6.3 %collective-permute-start.12 = (bf16[112,512]{1,0:T(8,128)(2,1)S(1)}, bf16[112,512]{1,0:T(8,128)(2,1)S(1)}, u32[]{:S(2)}, u32[]{:S(2)}) collective-permute-start(bf16[112,512]{1,0:T(8,128)(2,1)S(1)} %get-tuple-element.47.refs_8_), channel_id=1, source_target_pairs={{0,8},{4,12},{8,0},{12,4},{1,9},{5,13},{9,1},{13,5},{2,10},{6,14},... | collective-permute-start | bytes 344072 | tf_op jit(solution)/shard_map/ppermute | solution.py:393

commit v6 on v5

--- a/solution.py
+++ b/solution.py
@@ -142,8 +142,7 @@
                 outs[j][...] = y.astype(outs[j].dtype)
 
 
-def pair_kernel(count, start, base_ref, near_ref, *refs):
-    refs[-1][...] = base_ref[...] + near_ref[...].astype(F32)
+def pair_kernel(count, start, *refs):
     for j in range(count):
         out_ref = refs[2 * count + j]
         rows = slice(start, start + out_ref.shape[0])
@@ -182,9 +181,9 @@
             ).astype(BF16)
 
 
-def aux_kernel(n_wide, per_dev, near_ref, req_hbm, table_hbm, tok_hbm, sq_ref, *refs):
+def aux_kernel(n_wide, per_dev, req_hbm, table_hbm, tok_hbm, sq_ref, *refs):
     sels = refs[:n_wide]
-    sent_ref, req_ref, table_ref, tok_ref, sems = refs[n_wide:]
+    req_ref, table_ref, tok_ref, sems = refs[n_wide:]
     copies = [
         pltpu.make_async_copy(req_hbm, req_ref, sems.at[0]),
         pltpu.make_async_copy(table_hbm, table_ref, sems.at[1]),
@@ -192,7 +191,6 @@
     ]
     for copy in copies:
         copy.start()
-    sent_ref[...] = near_ref[...]
     for copy in copies:
         copy.wait()
     rows = tok_ref.shape[0]
@@ -273,7 +271,7 @@
     xs = refs[:count]
     parts = refs[count : count + n_parts]
     up_ref = refs[count + n_parts]
-    outs = refs[count + n_parts + 1 :]
+    outs = refs[count + n_parts + (2 if with_sq else 1) :]
     per_dev, half, cols = up_ref.shape
     heads = cols // HEAD
     height, rank = outs[0].shape[0], 2 * half
@@ -284,6 +282,7 @@
         sums.append(sum(terms[1:], terms[0]))
     if with_sq:
         outs[count][...] = sums[0][cap : cap + 8]
+        outs[count + 1][...] = refs[count + n_parts + 1][...]
     low = jnp.concatenate(sums, axis=0) if count > 1 else sums[0]
     slot = [slot_column(x, cap) for x in xs]
     slot = jnp.concatenate(slot, axis=0) if count > 1 else slot[0]
@@ -349,10 +348,10 @@
         out_ref[:half, span] = upper
 
 
-def finish_kernel(count, sum_ref, scale_ref, cos_ref, sin_ref, *refs):
+def finish_kernel(count, sum_ref, near_ref, scale_ref, cos_ref, sin_ref, *refs):
     deltas, sels, out_ref = refs[:count], refs[count : 2 * count], refs[2 * count]
     rows, cols = out_ref.shape
-    total = sum_ref[...] + placed(sels, deltas)
+    total = sum_ref[...] + near_ref[...].astype(F32) + placed(sels, deltas)
     heads = cols // HEAD
     scale = scale_ref[...]
     for h in range(heads):
@@ -480,29 +479,27 @@
         )
         return low
 
-    def up_block(group, parts, with_sq, after):
+    def up_block(group, parts, extra, after):
         xs = [held[k] for k in group]
         outs = [shape((height, cols), BF16)] * len(xs)
-        if with_sq:
-            outs = outs + [shape((8, HEAD), F32)]
+        if extra:
+            outs = outs + [shape((8, HEAD), F32), shape((rows, cols), BF16)]
         return call(
-            functools.partial(up_kernel, len(xs), len(parts), cap, with_sq),
+            functools.partial(up_kernel, len(xs), len(parts), cap, bool(extra)),
             "up_block",
             outs,
-            vmem=(*xs, *parts, adapter_up_weight),
+            vmem=(*xs, *parts, adapter_up_weight, *extra),
             after=after,
             flops=2 * len(xs) * height * per_dev * rank * cols,
             moved=2 * per_dev * rank * cols,
         )
 
     low = down_block(first, (), ())
-    sq, *sels, near = call(
+    sq, *sels = call(
         functools.partial(aux_kernel, n_wide, per_dev),
         "aux",
         [shape((8, HEAD), F32)]
-        + [shape((rows, HEAD), BF16)] * n_wide
-        + [shape((rows, cols), BF16)],
-        vmem=(near,),
+        + [shape((rows, HEAD), BF16)] * n_wide,
         hbm=(req, adapter_storage_row, tokens),
         after=(low,),
         scratch=small + [pltpu.VMEM((rows, depth), BF16), pltpu.SemaphoreType.DMA((3,))],
@@ -512,14 +509,13 @@
     half = rows // 2
     upper = cols // HEAD * half
     other = over("tensor", low, 1)
-    near = over("tensor", near, 1)
     pairs = call(
         functools.partial(pair_low_kernel, len(twos)),
         "pair_low_sums",
         [shape((upper + len(first) * height, HEAD), BF16)]
         + [shape((upper, HEAD), BF16)] * (len(twos) - 1),
         vmem=(low, other, *own, *beside),
-        after=(sq, cosine, sine),
+        after=(sq,),
     )
     tops = [over("tensor", p, k) for p, k in zip(pairs, twos)]
     done = pairs[0]
@@ -534,17 +530,18 @@
         other = over("tensor", low, 2**step)
     low_last = down_block(last, (sq,), (done,))
     last_parts = [low_last] + [over("tensor", low_last, k) for k in range(n_tensor - 1, 0, -1)]
-    ups = up_block(first, [low, other], False, (low_last,))
+    ups = up_block(first, [low, other], (), (low_last,))
     deltas = [u if k == 0 else over("wide", u, k) for k, u in zip(first, ups)]
-    *pairs, base = call(
+    pairs = call(
         functools.partial(pair_kernel, len(twos), half),
         "pair_sums",
-        [shape((half, cols), BF16)] * len(twos) + [shape((rows, cols), F32)],
-        vmem=(base, near, *own, *beside),
+        [shape((half, cols), BF16)] * len(twos),
+        vmem=(*own, *beside),
         after=(ups[0],),
     )
     bottoms = [over("tensor", p, k) for p, k in zip(pairs, twos)]
-    *ups, square = up_block(last, last_parts, True, (pairs[0],))
+    *ups, square, near = up_block(last, last_parts, (near,), (pairs[0],))
+    near = over("tensor", near, 1)
     last_deltas = [over("wide", u, k) for k, u in zip(last, ups)]
     total, scale = call(
         functools.partial(gather_kernel, len(bottoms), len(first)),
@@ -558,7 +555,7 @@
         functools.partial(finish_kernel, len(last)),
         "finish",
         [shape((rows, cols), BF16)],
-        vmem=(total, scale, cosine, sine, *last_deltas, *[sels[k] for k in last]),
+        vmem=(total, near, scale, cosine, sine, *last_deltas, *[sels[k] for k in last]),
         flops=2 * rows * cols * HEAD,
     )[0]
 

time: 50.8 us -> 52.1 us (1.026)
  the two profiles are of different devices: /device:TPU:12 before, /device:TPU:0 now
where the time goes in v6:
time: 52.1 us; the launch traced here: 51.8 us
  starting transfers between devices  17.9 us (34%)
  waiting for transfers between devices  16.2 us (31%)
  Pallas kernels  16.1 us (31%)
  local copies, waits for them, and re-layouts  0.74 us (1%)
  other arithmetic  0.67 us (1%)
    ppermute x14, starting transfers between devices, over(): return lax.ppermute(array, axis, [(i, i ^ k) for i in range(size)])  17.9 us
    ppermute x14, waiting for transfers between devices, over(): return lax.ppermute(array, axis, [(i, i ^ k) for i in range(size)])  16.2 us
    pallas_call x12, Pallas kernels, call(): pl.pallas_call(body, out_shape=outs, in_specs=[pl.BlockSpec(memory_space=...  16.1 us
  transfers between devices with their start and end apart: 14, of which 7 were waited for; matrix products, arithmetic and copies ran while one was open for 1% of the time, Pallas kernels for 22%

profile of v6, /device:TPU:0, one launch (start us, length us, event | category | flops | bytes accessed | tf_op | source)
XLA Modules:
  0.0 51.8 jit_solution(16417195119794474709)
XLA Ops:
  0.0 3.5 %dispatch.1 = (bf16[112,2048]{1,0:T(8,128)(2,1)}, bf16[112,2048]{1,0:T(8,128)(2,1)}, bf16[112,2048]{1,0:T(8,128)(2,1)}, bf16[112,2048]{1,0:T(8,128)(2,1)}, f32[16,128]{1,0:T(8,128)}) custom-call(s32[1,256]{1,0:T(1,128)} %bitcast.2, s32[32]{0:T(128)} %refs_1_.7, bf16[256,2048]{1,0:T(8,128)(2,1)} %refs_2_.5, bf16[16,128]{1,0:T(8,128)(2,1)} %bitcast.4), custom_call_target="tpu_custom_call" | custom-call | flops 469762048 | bytes 4194304 | tf_op jit(solution)/shard_map/dispatch/pallas_call | solution.py:28
  4.0 2.6 %collective-permute-start = (bf16[112,2048]{1,0:T(8,128)(2,1)}, bf16[112,2048]{1,0:T(8,128)(2,1)S(1)}, u32[]{:S(2)}, u32[]{:S(2)}) collective-permute-start(bf16[112,2048]{1,0:T(8,128)(2,1)} %get-tuple-element.27), channel_id=1, source_target_pairs={{0,8},{4,12},{8,0},{12,4},{1,9},{5,13},{9,1},{13,5},{2,10},{6,14},... | collective-permute-start | bytes 1376264 | tf_op jit(solution)/shard_map/ppermute | solution.py:392
  6.6 0.7 %copy-done.4 = f32[16,128]{1,0:T(8,128)S(1)} copy-done((f32[16,128]{1,0:T(8,128)S(1)}, f32[16,128]{1,0:T(8,128)}, u32[]{:S(2)}) %copy-start.4) | copy-done | bytes 8216
  7.3 4.8 %base.1 = (bf16[256,512]{1,0:T(8,128)(2,1)S(1)}, bf16[256,512]{1,0:T(8,128)(2,1)S(1)}, f32[256,512]{1,0:T(8,128)S(1)}, f32[256,512]{1,0:T(8,128)S(1)}) custom-call(f32[16,128]{1,0:T(8,128)S(1)} %copy-done.4, bf16[256,2048]{1,0:T(8,128)(2,1)} %refs_2_.5, bf16[2048,2048]{1,0:T(8,128)(2,1)} %refs_2_.4), custom_call_target="tpu_custom_call" | custom-call | flops 2147483648 | bytes 8388608 | tf_op jit(solution)/shard_map/base/pallas_call | solution.py:28
  12.1 1.9 %collective-permute-start.4 = (bf16[256,512]{1,0:T(8,128)(2,1)S(1)}, bf16[256,512]{1,0:T(8,128)(2,1)S(1)}, u32[]{:S(2)}, u32[]{:S(2)}) collective-permute-start(bf16[256,512]{1,0:T(8,128)(2,1)S(1)} %get-tuple-element.35), channel_id=1, source_target_pairs={{0,1},{1,0},{2,3},{3,2},{4,5},{5,4},{6,7},{7,6},{8,9},{9,8},{10,11... | collective-permute-start | bytes 786440 | tf_op jit(solution)/shard_map/ppermute | solution.py:392
  14.0 1.9 %scaled_down.1.refs_2_ = bf16[2048,1024]{1,0:T(8,128)(2,1)S(1)} custom-call(f32[16,128]{1,0:T(8,128)S(1)} %copy-done.4, bf16[8,2048,128]{2,1,0:T(8,128)(2,1)S(1)} %copy-done, f32[256,512]{1,0:T(8,128)S(1)} %get-tuple-element.30.refs_2_.refs_1_), custom_call_target="tpu_custom_call" | custom-call | flops 8388608 | bytes 8388608 | tf_op jit(solution)/shard_map/scaled_down/pallas_call | solution.py:28
  16.0 1.1 %down_block.2.refs_3_.refs_0_ = bf16[2,112,128]{2,1,0:T(8,128)(2,1)S(1)} custom-call(bf16[112,2048]{1,0:T(8,128)(2,1)S(1)} %copy-done.3, bf16[112,2048]{1,0:T(8,128)(2,1)S(1)} %collective-permute-done.2.refs_1_, bf16[2048,1024]{1,0:T(8,128)(2,1)S(1)} %scaled_down.1.refs_2_), custom_call_target="tpu_custom_call" | custom-call | flops 939524096 | bytes 4194304 | tf_op jit(solution)/shard_map/down_block/pallas_call | solution.py:28
  17.5 1.1 %aux.1 = (f32[8,128]{1,0:T(8,128)S(1)}, bf16[256,128]{1,0:T(8,128)(2,1)S(1)}, bf16[256,128]{1,0:T(8,128)(2,1)S(1)}, bf16[256,128]{1,0:T(8,128)(2,1)S(1)}, bf16[256,128]{1,0:T(8,128)(2,1)S(1)}) custom-call(s32[1,256]{1,0:T(1,128)S(1)} %bitcast.3, s32[32]{0:T(128)S(1)} %copy-done.6, bf16[256,2048]{1,0:T(8,128)(2,1)S(1)} %copy-done.1, ...), custom_call_target="tpu_custom_call" | custom-call | flops 268435456 | bytes 1048576 | tf_op jit(solution)/shard_map/aux/pallas_call | solution.py:28
  18.6 2.7 %collective-permute-done.4.refs_3_.refs_1_ = bf16[256,512]{1,0:T(8,128)(2,1)S(1)} collective-permute-done((bf16[256,512]{1,0:T(8,128)(2,1)S(1)}, bf16[256,512]{1,0:T(8,128)(2,1)S(1)}, u32[]{:S(2)}, u32[]{:S(2)}) %collective-permute-start.4) | collective-permute-done | bytes 262176 | tf_op jit(solution)/shard_map/ppermute | solution.py:392
  21.3 0.7 %collective-permute-done.3.refs_1_ = bf16[2,112,128]{2,1,0:T(8,128)(2,1)S(1)} collective-permute-done((bf16[2,112,128]{2,1,0:T(8,128)(2,1)S(1)}, bf16[2,112,128]{2,1,0:T(8,128)(2,1)S(1)}, u32[]{:S(2)}, u32[]{:S(2)}) %collective-permute-start.3) | collective-permute-done | bytes 57376 | tf_op jit(solution)/shard_map/ppermute | solution.py:392
  22.1 2.8 %collective-permute-start.8 = (bf16[736,128]{1,0:T(8,128)(2,1)S(1)}, bf16[736,128]{1,0:T(8,128)(2,1)S(1)}, u32[]{:S(2)}, u32[]{:S(2)}) collective-permute-start(bf16[736,128]{1,0:T(8,128)(2,1)S(1)} %pair_low_sums.1.refs_4_.refs_2_), channel_id=1, source_target_pairs={{0,2},{1,3},{2,0},{3,1},{4,6},{5,7},{6,4},{7,5},{8,10},{9,11},{10,... | collective-permute-start | bytes 565256 | tf_op jit(solution)/shard_map/ppermute | solution.py:392
  24.9 2.5 %collective-permute-done.1.refs_1_ = bf16[112,2048]{1,0:T(8,128)(2,1)S(1)} collective-permute-done((bf16[112,2048]{1,0:T(8,128)(2,1)}, bf16[112,2048]{1,0:T(8,128)(2,1)S(1)}, u32[]{:S(2)}, u32[]{:S(2)}) %collective-permute-start.1) | collective-permute-done | bytes 458784 | tf_op jit(solution)/shard_map/ppermute | solution.py:392
  27.4 1.1 %down_block.3.refs_5_.refs_2_ = bf16[2,112,128]{2,1,0:T(8,128)(2,1)S(1)} custom-call(bf16[112,2048]{1,0:T(8,128)(2,1)S(1)} %collective-permute-done.refs_0_, bf16[112,2048]{1,0:T(8,128)(2,1)S(1)} %collective-permute-done.1.refs_1_, bf16[2048,1024]{1,0:T(8,128)(2,1)S(1)} %scaled_down.1.refs_2_, f32[8,128]{1,0:T(8,128)S(1)} %get-tuple-element.33.refs_4_.refs_3_, ...), custom_call_target="tpu_custom_call" | custom-call | flops 939524096 | bytes 4194304 | tf_op jit(solution)/shard_map/down_block/pallas_call | solution.py:28
  28.6 3.8 %collective-permute-start.5 = (bf16[2,112,128]{2,1,0:T(8,128)(2,1)S(1)}, bf16[2,112,128]{2,1,0:T(8,128)(2,1)S(1)}, u32[]{:S(2)}, u32[]{:S(2)}) collective-permute-start(bf16[2,112,128]{2,1,0:T(8,128)(2,1)S(1)} %down_block.3.refs_5_.refs_2_), channel_id=1, source_target_pairs={{0,3},{1,2},{2,1},{3,0},{4,7},{5,6},{6,5},{7,4},{8,11},{9,10},{10,... | collective-permute-start | bytes 172040 | tf_op jit(solution)/shard_map/ppermute | solution.py:392
  32.3 0.7 %collective-permute-start.7 = (bf16[2,112,128]{2,1,0:T(8,128)(2,1)S(1)}, bf16[2,112,128]{2,1,0:T(8,128)(2,1)S(1)}, u32[]{:S(2)}, u32[]{:S(2)}) collective-permute-start(bf16[2,112,128]{2,1,0:T(8,128)(2,1)S(1)} %down_block.3.refs_5_.refs_2_), channel_id=1, source_target_pairs={{0,1},{1,0},{2,3},{3,2},{4,5},{5,4},{6,7},{7,6},{8,9},{9,8},{10,11... | collective-permute-start | bytes 172040 | tf_op jit(solution)/shard_map/ppermute | solution.py:392
  33.0 2.0 %collective-permute-done.8.refs_3_.refs_2_ = bf16[736,128]{1,0:T(8,128)(2,1)S(1)} collective-permute-done((bf16[736,128]{1,0:T(8,128)(2,1)S(1)}, bf16[736,128]{1,0:T(8,128)(2,1)S(1)}, u32[]{:S(2)}, u32[]{:S(2)}) %collective-permute-start.8) | collective-permute-done | bytes 188448 | tf_op jit(solution)/shard_map/ppermute | solution.py:392
  35.0 0.6 %up_block.2 = (bf16[112,512]{1,0:T(8,128)(2,1)S(1)}, bf16[112,512]{1,0:T(8,128)(2,1)S(1)}) custom-call(bf16[112,2048]{1,0:T(8,128)(2,1)S(1)} %copy-done.3, bf16[112,2048]{1,0:T(8,128)(2,1)S(1)} %collective-permute-done.2.refs_1_, bf16[736,128]{1,0:T(8,128)(2,1)S(1)} %pair_low_sums.1.refs_4_.refs_2_, ...), custom_call_target="tpu_custom_call" | custom-call | flops 234881024 | bytes 1048576 | tf_op jit(solution)/shard_map/up_block/pallas_call | solution.py:28
  36.0 2.9 %collective-permute-done.6.refs_4_ = bf16[2,112,128]{2,1,0:T(8,128)(2,1)S(1)} collective-permute-done((bf16[2,112,128]{2,1,0:T(8,128)(2,1)S(1)}, bf16[2,112,128]{2,1,0:T(8,128)(2,1)S(1)}, u32[]{:S(2)}, u32[]{:S(2)}) %collective-permute-start.6) | collective-permute-done | bytes 57376 | tf_op jit(solution)/shard_map/ppermute | solution.py:392
  38.9 0.6 %up_block.3 = (bf16[112,512]{1,0:T(8,128)(2,1)S(1)}, bf16[112,512]{1,0:T(8,128)(2,1)S(1)}, f32[8,128]{1,0:T(8,128)S(1)}, bf16[256,512]{1,0:T(8,128)(2,1)S(1)}) custom-call(bf16[112,2048]{1,0:T(8,128)(2,1)S(1)} %collective-permute-done.refs_0_, bf16[112,2048]{1,0:T(8,128)(2,1)S(1)} %collective-permute-done.1.refs_1_, ...), custom_call_target="tpu_custom_call" | custom-call | flops 234881024 | bytes 1048576 | tf_op jit(solution)/shard_map/up_block/pallas_call | solution.py:28
  39.5 3.1 %collective-permute-start.11 = (bf16[256,512]{1,0:T(8,128)(2,1)S(1)}, bf16[256,512]{1,0:T(8,128)(2,1)S(1)}, u32[]{:S(2)}, u32[]{:S(2)}) collective-permute-start(bf16[256,512]{1,0:T(8,128)(2,1)S(1)} %get-tuple-element.44), channel_id=1, source_target_pairs={{0,1},{1,0},{2,3},{3,2},{4,5},{5,4},{6,7},{7,6},{8,9},{9,8},{10,11... | collective-permute-start | bytes 786440 | tf_op jit(solution)/shard_map/ppermute | solution.py:392
  43.2 1.6 %collective-permute-start.12 = (bf16[112,512]{1,0:T(8,128)(2,1)S(1)}, bf16[112,512]{1,0:T(8,128)(2,1)S(1)}, u32[]{:S(2)}, u32[]{:S(2)}) collective-permute-start(bf16[112,512]{1,0:T(8,128)(2,1)S(1)} %get-tuple-element.42.refs_8_), channel_id=1, source_target_pairs={{0,8},{4,12},{8,0},{12,4},{1,9},{5,13},{9,1},{13,5},{2,10},{6,14},... | collective-permute-start | bytes 344072 | tf_op jit(solution)/shard_map/ppermute | solution.py:392
  45.5 3.8 %collective-permute-done.12.refs_5_ = bf16[112,512]{1,0:T(8,128)(2,1)S(1)} collective-permute-done((bf16[112,512]{1,0:T(8,128)(2,1)S(1)}, bf16[112,512]{1,0:T(8,128)(2,1)S(1)}, u32[]{:S(2)}, u32[]{:S(2)}) %collective-permute-start.12) | collective-permute-done | bytes 114720 | tf_op jit(solution)/shard_map/ppermute | solution.py:392
  49.2 1.6 %collective-permute-done.13.refs_6_ = bf16[112,512]{1,0:T(8,128)(2,1)S(1)} collective-permute-done((bf16[112,512]{1,0:T(8,128)(2,1)S(1)}, bf16[112,512]{1,0:T(8,128)(2,1)S(1)}, u32[]{:S(2)}, u32[]{:S(2)}) %collective-permute-start.13) | collective-permute-done | bytes 114720 | tf_op jit(solution)/shard_map/ppermute | solution.py:392
  50.8 1.0 %finish.1 = bf16[256,512]{1,0:T(8,128)(2,1)} custom-call(f32[256,512]{1,0:T(8,128)S(1)} %get-tuple-element.43.refs_0_, bf16[256,512]{1,0:T(8,128)(2,1)S(1)} %collective-permute-done.11.refs_1_, f32[256,128]{1,0:T(8,128)S(1)} %get-tuple-element.45.refs_2_, f32[256,128]{1,0:T(8,128)S(1)} %get-tuple-element.52.refs_3_, ...), custom_call_target="tpu_custom_call" | custom-call | flops 33554432 | tf_op jit(solution)/shard_map/finish/pallas_call | solution.py:28
  (36 shorter events, 2.6 us)
Async XLA Ops:
  3.5 12.5 %collective-permute-start.2 = (bf16[112,2048]{1,0:T(8,128)(2,1)}, bf16[112,2048]{1,0:T(8,128)(2,1)S(1)}, u32[]{:S(2)}, u32[]{:S(2)}) collective-permute-start(bf16[112,2048]{1,0:T(8,128)(2,1)} %get-tuple-element.32), channel_id=1, source_target_pairs={{0,4},{4,0},{8,12},{12,8},{1,5},{5,1},{9,13},{13,9},{2,6},{6,2},{1... | collective-permute-start | bytes 1376264 | tf_op jit(solution)/shard_map/ppermute | solution.py:392
  4.0 20.9 %collective-permute-start = (bf16[112,2048]{1,0:T(8,128)(2,1)}, bf16[112,2048]{1,0:T(8,128)(2,1)S(1)}, u32[]{:S(2)}, u32[]{:S(2)}) collective-permute-start(bf16[112,2048]{1,0:T(8,128)(2,1)} %get-tuple-element.27), channel_id=1, source_target_pairs={{0,8},{4,12},{8,0},{12,4},{1,9},{5,13},{9,1},{13,5},{2,10},{6,14},... | collective-permute-start | bytes 1376264 | tf_op jit(solution)/shard_map/ppermute | solution.py:392
  6.6 20.9 %collective-permute-start.1 = (bf16[112,2048]{1,0:T(8,128)(2,1)}, bf16[112,2048]{1,0:T(8,128)(2,1)S(1)}, u32[]{:S(2)}, u32[]{:S(2)}) collective-permute-start(bf16[112,2048]{1,0:T(8,128)(2,1)} %get-tuple-element.28), channel_id=1, source_target_pairs={{0,12},{4,8},{8,4},{12,0},{1,13},{5,9},{9,5},{13,1},{2,14},{6,10},... | collective-permute-start | bytes 1376264 | tf_op jit(solution)/shard_map/ppermute | solution.py:392
  6.6 0.7 %copy-start.4 = (f32[16,128]{1,0:T(8,128)S(1)}, f32[16,128]{1,0:T(8,128)}, u32[]{:S(2)}) copy-start(f32[16,128]{1,0:T(8,128)} %get-tuple-element.29.refs_0_) | copy-start | bytes 24580
  7.3 6.7 %copy-start = (bf16[8,2048,128]{2,1,0:T(8,128)(2,1)S(1)}, bf16[8,2048,128]{2,1,0:T(8,128)(2,1)}, u32[]{:S(2)}) copy-start(bf16[8,2048,128]{2,1,0:T(8,128)(2,1)} %refs_1_.6) | copy-start | bytes 12582916
  12.1 9.2 %collective-permute-start.4 = (bf16[256,512]{1,0:T(8,128)(2,1)S(1)}, bf16[256,512]{1,0:T(8,128)(2,1)S(1)}, u32[]{:S(2)}, u32[]{:S(2)}) collective-permute-start(bf16[256,512]{1,0:T(8,128)(2,1)S(1)} %get-tuple-element.35), channel_id=1, source_target_pairs={{0,1},{1,0},{2,3},{3,2},{4,5},{5,4},{6,7},{7,6},{8,9},{9,8},{10,11... | collective-permute-start | bytes 786440 | tf_op jit(solution)/shard_map/ppermute | solution.py:392
  14.0 2.0 %copy-start.3 = (bf16[112,2048]{1,0:T(8,128)(2,1)S(1)}, bf16[112,2048]{1,0:T(8,128)(2,1)}, u32[]{:S(2)}) copy-start(bf16[112,2048]{1,0:T(8,128)(2,1)} %get-tuple-element.31.refs_0_) | copy-start | bytes 1376260
  16.0 1.5 %copy-start.1 = (bf16[256,2048]{1,0:T(8,128)(2,1)S(1)}, bf16[256,2048]{1,0:T(8,128)(2,1)}, u32[]{:S(2)}) copy-start(bf16[256,2048]{1,0:T(8,128)(2,1)} %refs_2_.5) | copy-start | bytes 3145732
  16.0 1.5 %copy-start.5 = (s32[256]{0:T(256)S(1)}, s32[256]{0:T(256)}, u32[]{:S(2)}) copy-start(s32[256]{0:T(256)} %param.13) | copy-start | bytes 3076
  16.0 1.5 %copy-start.6 = (s32[32]{0:T(128)S(1)}, s32[32]{0:T(128)}, u32[]{:S(2)}) copy-start(s32[32]{0:T(128)} %refs_1_.7) | copy-start | bytes 388
  17.2 15.9 %copy-start.7 = (s32[256]{0:T(256)S(1)}, s32[256]{0:T(256)}, u32[]{:S(2)}) copy-start(s32[256]{0:T(256)} %param.15) | copy-start | bytes 3076
  17.2 17.9 %copy-start.2 = (bf16[8,64,512]{2,1,0:T(8,128)(2,1)S(1)}, bf16[8,64,512]{2,1,0:T(8,128)(2,1)}, u32[]{:S(2)}) copy-start(bf16[8,64,512]{2,1,0:T(8,128)(2,1)} %refs_6_.1) | copy-start | bytes 1572868
  17.2 4.9 %collective-permute-start.3 = (bf16[2,112,128]{2,1,0:T(8,128)(2,1)S(1)}, bf16[2,112,128]{2,1,0:T(8,128)(2,1)S(1)}, u32[]{:S(2)}, u32[]{:S(2)}) collective-permute-start(bf16[2,112,128]{2,1,0:T(8,128)(2,1)S(1)} %down_block.2.refs_3_.refs_0_), channel_id=1, source_target_pairs={{0,1},{1,0},{2,3},{3,2},{4,5},{5,4},{6,7},{7,6},{8,9},{9,8},{10,11... | collective-permute-start | bytes 172040 | tf_op jit(solution)/shard_map/ppermute | solution.py:392
  22.1 12.9 %collective-permute-start.8 = (bf16[736,128]{1,0:T(8,128)(2,1)S(1)}, bf16[736,128]{1,0:T(8,128)(2,1)S(1)}, u32[]{:S(2)}, u32[]{:S(2)}) collective-permute-start(bf16[736,128]{1,0:T(8,128)(2,1)S(1)} %pair_low_sums.1.refs_4_.refs_2_), channel_id=1, source_target_pairs={{0,2},{1,3},{2,0},{3,1},{4,6},{5,7},{6,4},{7,5},{8,10},{9,11},{10,... | collective-permute-start | bytes 565256 | tf_op jit(solution)/shard_map/ppermute | solution.py:392
  28.6 7.4 %collective-permute-start.5 = (bf16[2,112,128]{2,1,0:T(8,128)(2,1)S(1)}, bf16[2,112,128]{2,1,0:T(8,128)(2,1)S(1)}, u32[]{:S(2)}, u32[]{:S(2)}) collective-permute-start(bf16[2,112,128]{2,1,0:T(8,128)(2,1)S(1)} %down_block.3.refs_5_.refs_2_), channel_id=1, source_target_pairs={{0,3},{1,2},{2,1},{3,0},{4,7},{5,6},{6,5},{7,4},{8,11},{9,10},{10,... | collective-permute-start | bytes 172040 | tf_op jit(solution)/shard_map/ppermute | solution.py:392
  32.3 6.6 %collective-permute-start.6 = (bf16[2,112,128]{2,1,0:T(8,128)(2,1)S(1)}, bf16[2,112,128]{2,1,0:T(8,128)(2,1)S(1)}, u32[]{:S(2)}, u32[]{:S(2)}) collective-permute-start(bf16[2,112,128]{2,1,0:T(8,128)(2,1)S(1)} %down_block.3.refs_5_.refs_2_), channel_id=1, source_target_pairs={{0,2},{1,3},{2,0},{3,1},{4,6},{5,7},{6,4},{7,5},{8,10},{9,11},{10,... | collective-permute-start | bytes 172040 | tf_op jit(solution)/shard_map/ppermute | solution.py:392
  32.3 6.6 %collective-permute-start.7 = (bf16[2,112,128]{2,1,0:T(8,128)(2,1)S(1)}, bf16[2,112,128]{2,1,0:T(8,128)(2,1)S(1)}, u32[]{:S(2)}, u32[]{:S(2)}) collective-permute-start(bf16[2,112,128]{2,1,0:T(8,128)(2,1)S(1)} %down_block.3.refs_5_.refs_2_), channel_id=1, source_target_pairs={{0,1},{1,0},{2,3},{3,2},{4,5},{5,4},{6,7},{7,6},{8,9},{9,8},{10,11... | collective-permute-start | bytes 172040 | tf_op jit(solution)/shard_map/ppermute | solution.py:392
  35.7 9.6 %collective-permute-start.9 = (bf16[128,512]{1,0:T(8,128)(2,1)S(1)}, bf16[128,512]{1,0:T(8,128)(2,1)S(1)}, u32[]{:S(2)}, u32[]{:S(2)}) collective-permute-start(bf16[128,512]{1,0:T(8,128)(2,1)S(1)} %pair_sums.1.refs_8_), channel_id=1, source_target_pairs={{0,2},{1,3},{2,0},{3,1},{4,6},{5,7},{6,4},{7,5},{8,10},{9,11},{10,... | collective-permute-start | bytes 393224 | tf_op jit(solution)/shard_map/ppermute | solution.py:392
  39.5 11.3 %collective-permute-start.11 = (bf16[256,512]{1,0:T(8,128)(2,1)S(1)}, bf16[256,512]{1,0:T(8,128)(2,1)S(1)}, u32[]{:S(2)}, u32[]{:S(2)}) collective-permute-start(bf16[256,512]{1,0:T(8,128)(2,1)S(1)} %get-tuple-element.44), channel_id=1, source_target_pairs={{0,1},{1,0},{2,3},{3,2},{4,5},{5,4},{6,7},{7,6},{8,9},{9,8},{10,11... | collective-permute-start | bytes 786440 | tf_op jit(solution)/shard_map/ppermute | solution.py:392
  43.2 2.1 %collective-permute-start.10 = (bf16[112,512]{1,0:T(8,128)(2,1)S(1)}, bf16[112,512]{1,0:T(8,128)(2,1)S(1)}, u32[]{:S(2)}, u32[]{:S(2)}) collective-permute-start(bf16[112,512]{1,0:T(8,128)(2,1)S(1)} %get-tuple-element.39), channel_id=1, source_target_pairs={{0,4},{4,0},{8,12},{12,8},{1,5},{5,1},{9,13},{13,9},{2,6},{6,2},{1... | collective-permute-start | bytes 344072 | tf_op jit(solution)/shard_map/ppermute | solution.py:392
  43.2 6.0 %collective-permute-start.12 = (bf16[112,512]{1,0:T(8,128)(2,1)S(1)}, bf16[112,512]{1,0:T(8,128)(2,1)S(1)}, u32[]{:S(2)}, u32[]{:S(2)}) collective-permute-start(bf16[112,512]{1,0:T(8,128)(2,1)S(1)} %get-tuple-element.42.refs_8_), channel_id=1, source_target_pairs={{0,8},{4,12},{8,0},{12,4},{1,9},{5,13},{9,1},{13,5},{2,10},{6,14},... | collective-permute-start | bytes 344072 | tf_op jit(solution)/shard_map/ppermute | solution.py:392
  44.8 6.0 %collective-permute-start.13 = (bf16[112,512]{1,0:T(8,128)(2,1)S(1)}, bf16[112,512]{1,0:T(8,128)(2,1)S(1)}, u32[]{:S(2)}, u32[]{:S(2)}) collective-permute-start(bf16[112,512]{1,0:T(8,128)(2,1)S(1)} %get-tuple-element.46), channel_id=1, source_target_pairs={{0,12},{4,8},{8,4},{12,0},{1,13},{5,9},{9,5},{13,1},{2,14},{6,10},... | collective-permute-start | bytes 344072 | tf_op jit(solution)/shard_map/ppermute | solution.py:392

commit v7 on v6

--- a/solution.py
+++ b/solution.py
@@ -142,7 +142,8 @@
                 outs[j][...] = y.astype(outs[j].dtype)
 
 
-def pair_kernel(count, start, *refs):
+def pair_kernel(count, start, near_ref, *refs):
+    refs[-1][...] = near_ref[...]
     for j in range(count):
         out_ref = refs[2 * count + j]
         rows = slice(start, start + out_ref.shape[0])
@@ -271,7 +272,7 @@
     xs = refs[:count]
     parts = refs[count : count + n_parts]
     up_ref = refs[count + n_parts]
-    outs = refs[count + n_parts + (2 if with_sq else 1) :]
+    outs = refs[count + n_parts + 1 :]
     per_dev, half, cols = up_ref.shape
     heads = cols // HEAD
     height, rank = outs[0].shape[0], 2 * half
@@ -282,7 +283,6 @@
         sums.append(sum(terms[1:], terms[0]))
     if with_sq:
         outs[count][...] = sums[0][cap : cap + 8]
-        outs[count + 1][...] = refs[count + n_parts + 1][...]
     low = jnp.concatenate(sums, axis=0) if count > 1 else sums[0]
     slot = [slot_column(x, cap) for x in xs]
     slot = jnp.concatenate(slot, axis=0) if count > 1 else slot[0]
@@ -479,16 +479,16 @@
         )
         return low
 
-    def up_block(group, parts, extra, after):
+    def up_block(group, parts, with_sq, after):
         xs = [held[k] for k in group]
         outs = [shape((height, cols), BF16)] * len(xs)
-        if extra:
-            outs = outs + [shape((8, HEAD), F32), shape((rows, cols), BF16)]
+        if with_sq:
+            outs = outs + [shape((8, HEAD), F32)]
         return call(
-            functools.partial(up_kernel, len(xs), len(parts), cap, bool(extra)),
+            functools.partial(up_kernel, len(xs), len(parts), cap, with_sq),
             "up_block",
             outs,
-            vmem=(*xs, *parts, adapter_up_weight, *extra),
+            vmem=(*xs, *parts, adapter_up_weight),
             after=after,
             flops=2 * len(xs) * height * per_dev * rank * cols,
             moved=2 * per_dev * rank * cols,
@@ -530,18 +530,18 @@
         other = over("tensor", low, 2**step)
     low_last = down_block(last, (sq,), (done,))
     last_parts = [low_last] + [over("tensor", low_last, k) for k in range(n_tensor - 1, 0, -1)]
-    ups = up_block(first, [low, other], (), (low_last,))
+    ups = up_block(first, [low, other], False, (low_last,))
     deltas = [u if k == 0 else over("wide", u, k) for k, u in zip(first, ups)]
-    pairs = call(
+    *pairs, near = call(
         functools.partial(pair_kernel, len(twos), half),
         "pair_sums",
-        [shape((half, cols), BF16)] * len(twos),
-        vmem=(*own, *beside),
+        [shape((half, cols), BF16)] * len(twos) + [shape((rows, cols), BF16)],
+        vmem=(near, *own, *beside),
         after=(ups[0],),
     )
+    near = over("tensor", near, 1)
     bottoms = [over("tensor", p, k) for p, k in zip(pairs, twos)]
-    *ups, square, near = up_block(last, last_parts, (near,), (pairs[0],))
-    near = over("tensor", near, 1)
+    *ups, square = up_block(last, last_parts, True, (pairs[0],))
     last_deltas = [over("wide", u, k) for k, u in zip(last, ups)]
     total, scale = call(
         functools.partial(gather_kernel, len(bottoms), len(first)),

time: 52.1 us -> 48.5 us (0.931)
  waiting for transfers between devices: 16.2 us -> 13.4 us
  starting transfers between devices: 17.9 us -> 17.2 us
    ppermute x14, waiting for transfers between devices: 16.2 us -> 13.4 us  [over(): return lax.ppermute(array, axis, [(i, i ^ k) for i in range(size)])]
    ppermute x14, starting transfers between devices: 17.9 us -> 17.2 us  [over(): return lax.ppermute(array, axis, [(i, i ^ k) for i in range(size)])]
  transfers between devices with their start and end apart: 14 -> 14, of which waited for: 7 -> 7; matrix products, arithmetic and copies ran while one was open for 1% -> 1% of each run, Pallas kernels for 22% -> 24%
where the time goes in v7:
time: 48.5 us; the launch traced here: 48.3 us
  starting transfers between devices  17.2 us (35%)
  Pallas kernels  16.1 us (33%)
  waiting for transfers between devices  13.4 us (28%)
  local copies, waits for them, and re-layouts  0.74 us (2%)
  other arithmetic  0.68 us (1%)
    ppermute x14, starting transfers between devices, over(): return lax.ppermute(array, axis, [(i, i ^ k) for i in range(size)])  17.2 us
    pallas_call x12, Pallas kernels, call(): pl.pallas_call(body, out_shape=outs, in_specs=[pl.BlockSpec(memory_space=...  16.1 us
    ppermute x14, waiting for transfers between devices, over(): return lax.ppermute(array, axis, [(i, i ^ k) for i in range(size)])  13.4 us
  transfers between devices with their start and end apart: 14, of which 7 were waited for; matrix products, arithmetic and copies ran while one was open for 1% of the time, Pallas kernels for 24%

profile of v7, /device:TPU:0, one launch (start us, length us, event | category | flops | bytes accessed | tf_op | source)
XLA Modules:
  0.0 48.3 jit_solution(15945066699548612350)
XLA Ops:
  0.0 3.5 %dispatch.1 = (bf16[112,2048]{1,0:T(8,128)(2,1)}, bf16[112,2048]{1,0:T(8,128)(2,1)}, bf16[112,2048]{1,0:T(8,128)(2,1)}, bf16[112,2048]{1,0:T(8,128)(2,1)}, f32[16,128]{1,0:T(8,128)}) custom-call(s32[1,256]{1,0:T(1,128)} %bitcast.2, s32[32]{0:T(128)} %refs_1_.7, bf16[256,2048]{1,0:T(8,128)(2,1)} %refs_2_.5, bf16[16,128]{1,0:T(8,128)(2,1)} %bitcast.4), custom_call_target="tpu_custom_call" | custom-call | flops 469762048 | bytes 4194304 | tf_op jit(solution)/shard_map/dispatch/pallas_call | solution.py:28
  4.0 2.6 %collective-permute-start = (bf16[112,2048]{1,0:T(8,128)(2,1)}, bf16[112,2048]{1,0:T(8,128)(2,1)S(1)}, u32[]{:S(2)}, u32[]{:S(2)}) collective-permute-start(bf16[112,2048]{1,0:T(8,128)(2,1)} %get-tuple-element.28), channel_id=1, source_target_pairs={{0,8},{4,12},{8,0},{12,4},{1,9},{5,13},{9,1},{13,5},{2,10},{6,14},... | collective-permute-start | bytes 1376264 | tf_op jit(solution)/shard_map/ppermute | solution.py:392
  6.6 0.7 %copy-done.4 = f32[16,128]{1,0:T(8,128)S(1)} copy-done((f32[16,128]{1,0:T(8,128)S(1)}, f32[16,128]{1,0:T(8,128)}, u32[]{:S(2)}) %copy-start.4) | copy-done | bytes 8216
  7.3 4.8 %base.1 = (bf16[256,512]{1,0:T(8,128)(2,1)S(1)}, bf16[256,512]{1,0:T(8,128)(2,1)S(1)}, f32[256,512]{1,0:T(8,128)S(1)}, f32[256,512]{1,0:T(8,128)S(1)}) custom-call(f32[16,128]{1,0:T(8,128)S(1)} %copy-done.4, bf16[256,2048]{1,0:T(8,128)(2,1)} %refs_2_.5, bf16[2048,2048]{1,0:T(8,128)(2,1)} %refs_2_.4), custom_call_target="tpu_custom_call" | custom-call | flops 2147483648 | bytes 8388608 | tf_op jit(solution)/shard_map/base/pallas_call | solution.py:28
  12.1 1.9 %collective-permute-start.4 = (bf16[256,512]{1,0:T(8,128)(2,1)S(1)}, bf16[256,512]{1,0:T(8,128)(2,1)S(1)}, u32[]{:S(2)}, u32[]{:S(2)}) collective-permute-start(bf16[256,512]{1,0:T(8,128)(2,1)S(1)} %get-tuple-element.36), channel_id=1, source_target_pairs={{0,1},{1,0},{2,3},{3,2},{4,5},{5,4},{6,7},{7,6},{8,9},{9,8},{10,11... | collective-permute-start | bytes 786440 | tf_op jit(solution)/shard_map/ppermute | solution.py:392
  14.0 1.9 %scaled_down.1.refs_2_ = bf16[2048,1024]{1,0:T(8,128)(2,1)S(1)} custom-call(f32[16,128]{1,0:T(8,128)S(1)} %copy-done.4, bf16[8,2048,128]{2,1,0:T(8,128)(2,1)S(1)} %copy-done, f32[256,512]{1,0:T(8,128)S(1)} %get-tuple-element.31.refs_2_.refs_1_), custom_call_target="tpu_custom_call" | custom-call | flops 8388608 | bytes 8388608 | tf_op jit(solution)/shard_map/scaled_down/pallas_call | solution.py:28
  16.1 1.1 %down_block.2.refs_3_.refs_0_ = bf16[2,112,128]{2,1,0:T(8,128)(2,1)S(1)} custom-call(bf16[112,2048]{1,0:T(8,128)(2,1)S(1)} %copy-done.3, bf16[112,2048]{1,0:T(8,128)(2,1)S(1)} %collective-permute-done.2.refs_1_, bf16[2048,1024]{1,0:T(8,128)(2,1)S(1)} %scaled_down.1.refs_2_), custom_call_target="tpu_custom_call" | custom-call | flops 939524096 | bytes 4194304 | tf_op jit(solution)/shard_map/down_block/pallas_call | solution.py:28
  17.5 1.1 %aux.1 = (f32[8,128]{1,0:T(8,128)S(1)}, bf16[256,128]{1,0:T(8,128)(2,1)S(1)}, bf16[256,128]{1,0:T(8,128)(2,1)S(1)}, bf16[256,128]{1,0:T(8,128)(2,1)S(1)}, bf16[256,128]{1,0:T(8,128)(2,1)S(1)}) custom-call(s32[1,256]{1,0:T(1,128)S(1)} %bitcast.3, s32[32]{0:T(128)S(1)} %copy-done.6, bf16[256,2048]{1,0:T(8,128)(2,1)S(1)} %copy-done.1, ...), custom_call_target="tpu_custom_call" | custom-call | flops 268435456 | bytes 1048576 | tf_op jit(solution)/shard_map/aux/pallas_call | solution.py:28
  18.6 2.7 %collective-permute-done.4.refs_3_.refs_2_ = bf16[256,512]{1,0:T(8,128)(2,1)S(1)} collective-permute-done((bf16[256,512]{1,0:T(8,128)(2,1)S(1)}, bf16[256,512]{1,0:T(8,128)(2,1)S(1)}, u32[]{:S(2)}, u32[]{:S(2)}) %collective-permute-start.4) | collective-permute-done | bytes 262176 | tf_op jit(solution)/shard_map/ppermute | solution.py:392
  21.3 0.7 %collective-permute-done.3.refs_1_ = bf16[2,112,128]{2,1,0:T(8,128)(2,1)S(1)} collective-permute-done((bf16[2,112,128]{2,1,0:T(8,128)(2,1)S(1)}, bf16[2,112,128]{2,1,0:T(8,128)(2,1)S(1)}, u32[]{:S(2)}, u32[]{:S(2)}) %collective-permute-start.3) | collective-permute-done | bytes 57376 | tf_op jit(solution)/shard_map/ppermute | solution.py:392
  22.1 2.8 %collective-permute-start.8 = (bf16[736,128]{1,0:T(8,128)(2,1)S(1)}, bf16[736,128]{1,0:T(8,128)(2,1)S(1)}, u32[]{:S(2)}, u32[]{:S(2)}) collective-permute-start(bf16[736,128]{1,0:T(8,128)(2,1)S(1)} %pair_low_sums.1.refs_4_.refs_2_), channel_id=1, source_target_pairs={{0,2},{1,3},{2,0},{3,1},{4,6},{5,7},{6,4},{7,5},{8,10},{9,11},{10,... | collective-permute-start | bytes 565256 | tf_op jit(solution)/shard_map/ppermute | solution.py:392
  25.0 2.5 %collective-permute-done.1.refs_1_ = bf16[112,2048]{1,0:T(8,128)(2,1)S(1)} collective-permute-done((bf16[112,2048]{1,0:T(8,128)(2,1)}, bf16[112,2048]{1,0:T(8,128)(2,1)S(1)}, u32[]{:S(2)}, u32[]{:S(2)}) %collective-permute-start.1) | collective-permute-done | bytes 458784 | tf_op jit(solution)/shard_map/ppermute | solution.py:392
  27.5 1.1 %down_block.3.refs_5_.refs_2_ = bf16[2,112,128]{2,1,0:T(8,128)(2,1)S(1)} custom-call(bf16[112,2048]{1,0:T(8,128)(2,1)S(1)} %collective-permute-done.refs_0_, bf16[112,2048]{1,0:T(8,128)(2,1)S(1)} %collective-permute-done.1.refs_1_, bf16[2048,1024]{1,0:T(8,128)(2,1)S(1)} %scaled_down.1.refs_2_, f32[8,128]{1,0:T(8,128)S(1)} %get-tuple-element.34.refs_4_.refs_3_, ...), custom_call_target="tpu_custom_call" | custom-call | flops 939524096 | bytes 4194304 | tf_op jit(solution)/shard_map/down_block/pallas_call | solution.py:28
  28.6 3.7 %collective-permute-start.5 = (bf16[2,112,128]{2,1,0:T(8,128)(2,1)S(1)}, bf16[2,112,128]{2,1,0:T(8,128)(2,1)S(1)}, u32[]{:S(2)}, u32[]{:S(2)}) collective-permute-start(bf16[2,112,128]{2,1,0:T(8,128)(2,1)S(1)} %down_block.3.refs_5_.refs_2_), channel_id=1, source_target_pairs={{0,3},{1,2},{2,1},{3,0},{4,7},{5,6},{6,5},{7,4},{8,11},{9,10},{10,... | collective-permute-start | bytes 172040 | tf_op jit(solution)/shard_map/ppermute | solution.py:392
  32.4 0.7 %collective-permute-start.7 = (bf16[2,112,128]{2,1,0:T(8,128)(2,1)S(1)}, bf16[2,112,128]{2,1,0:T(8,128)(2,1)S(1)}, u32[]{:S(2)}, u32[]{:S(2)}) collective-permute-start(bf16[2,112,128]{2,1,0:T(8,128)(2,1)S(1)} %down_block.3.refs_5_.refs_2_), channel_id=1, source_target_pairs={{0,1},{1,0},{2,3},{3,2},{4,5},{5,4},{6,7},{7,6},{8,9},{9,8},{10,11... | collective-permute-start | bytes 172040 | tf_op jit(solution)/shard_map/ppermute | solution.py:392
  33.1 2.0 %collective-permute-done.8.refs_3_.refs_2_ = bf16[736,128]{1,0:T(8,128)(2,1)S(1)} collective-permute-done((bf16[736,128]{1,0:T(8,128)(2,1)S(1)}, bf16[736,128]{1,0:T(8,128)(2,1)S(1)}, u32[]{:S(2)}, u32[]{:S(2)}) %collective-permute-start.8) | collective-permute-done | bytes 188448 | tf_op jit(solution)/shard_map/ppermute | solution.py:392
  35.1 0.6 %up_block.2 = (bf16[112,512]{1,0:T(8,128)(2,1)S(1)}, bf16[112,512]{1,0:T(8,128)(2,1)S(1)}) custom-call(bf16[112,2048]{1,0:T(8,128)(2,1)S(1)} %copy-done.3, bf16[112,2048]{1,0:T(8,128)(2,1)S(1)} %collective-permute-done.2.refs_1_, bf16[736,128]{1,0:T(8,128)(2,1)S(1)} %pair_low_sums.1.refs_4_.refs_2_, ...), custom_call_target="tpu_custom_call" | custom-call | flops 234881024 | bytes 1048576 | tf_op jit(solution)/shard_map/up_block/pallas_call | solution.py:28
  35.8 0.5 %fusion = (f32[256,64]{1,0:T(8,128)S(1)}, f32[256,64]{1,0:T(8,128)S(1)}, f32[256,64]{1,0:T(8,128)S(1)}) fusion(f32[64]{0:T(128)S(1)} %multiply_exponential_fusion, f32[256]{0:T(256)S(1)} %convert_element_type.10), kind=kLoop, calls=%fused_computation.4 | loop fusion | flops 32768 | bytes 197888 | tf_op jit(solution)/shard_map/neg | solution.py:467
  36.4 2.6 %collective-permute-start.9 = (bf16[128,512]{1,0:T(8,128)(2,1)S(1)}, bf16[128,512]{1,0:T(8,128)(2,1)S(1)}, u32[]{:S(2)}, u32[]{:S(2)}) collective-permute-start(bf16[128,512]{1,0:T(8,128)(2,1)S(1)} %get-tuple-element.39.refs_7_), channel_id=1, source_target_pairs={{0,2},{1,3},{2,0},{3,1},{4,6},{5,7},{6,4},{7,5},{8,10},{9,11},{10,... | collective-permute-start | bytes 393224 | tf_op jit(solution)/shard_map/ppermute | solution.py:392
  39.0 0.6 %up_block.3 = (bf16[112,512]{1,0:T(8,128)(2,1)S(1)}, bf16[112,512]{1,0:T(8,128)(2,1)S(1)}, f32[8,128]{1,0:T(8,128)S(1)}) custom-call(bf16[112,2048]{1,0:T(8,128)(2,1)S(1)} %collective-permute-done.refs_0_, bf16[112,2048]{1,0:T(8,128)(2,1)S(1)} %collective-permute-done.1.refs_1_, bf16[2,112,128]{2,1,0:T(8,128)(2,1)S(1)} %down_block.3.refs_5_.refs_2_, ...), custom_call_target="tpu_custom_call" | custom-call | flops 234881024 | bytes 1048576 | tf_op jit(solution)/shard_map/up_block/pallas_call | solution.py:28
  39.6 1.6 %collective-permute-start.12 = (bf16[112,512]{1,0:T(8,128)(2,1)S(1)}, bf16[112,512]{1,0:T(8,128)(2,1)S(1)}, u32[]{:S(2)}, u32[]{:S(2)}) collective-permute-start(bf16[112,512]{1,0:T(8,128)(2,1)S(1)} %get-tuple-element.44.refs_8_), channel_id=1, source_target_pairs={{0,8},{4,12},{8,0},{12,4},{1,9},{5,13},{9,1},{13,5},{2,10},{6,14},... | collective-permute-start | bytes 344072 | tf_op jit(solution)/shard_map/ppermute | solution.py:392
  41.7 3.2 %collective-permute-done.9.refs_3_ = bf16[128,512]{1,0:T(8,128)(2,1)S(1)} collective-permute-done((bf16[128,512]{1,0:T(8,128)(2,1)S(1)}, bf16[128,512]{1,0:T(8,128)(2,1)S(1)}, u32[]{:S(2)}, u32[]{:S(2)}) %collective-permute-start.9) | collective-permute-done | bytes 131104 | tf_op jit(solution)/shard_map/ppermute | solution.py:392
  45.6 1.7 %collective-permute-done.13.refs_6_ = bf16[112,512]{1,0:T(8,128)(2,1)S(1)} collective-permute-done((bf16[112,512]{1,0:T(8,128)(2,1)S(1)}, bf16[112,512]{1,0:T(8,128)(2,1)S(1)}, u32[]{:S(2)}, u32[]{:S(2)}) %collective-permute-start.13) | collective-permute-done | bytes 114720 | tf_op jit(solution)/shard_map/ppermute | solution.py:392
  47.3 1.0 %finish.1 = bf16[256,512]{1,0:T(8,128)(2,1)} custom-call(f32[256,512]{1,0:T(8,128)S(1)} %get-tuple-element.45.refs_0_, bf16[256,512]{1,0:T(8,128)(2,1)S(1)} %collective-permute-done.11.refs_1_, f32[256,128]{1,0:T(8,128)S(1)} %get-tuple-element.47.refs_2_, f32[256,128]{1,0:T(8,128)S(1)} %get-tuple-element.54.refs_3_, ...), custom_call_target="tpu_custom_call" | custom-call | flops 33554432 | tf_op jit(solution)/shard_map/finish/pallas_call | solution.py:28
  (36 shorter events, 2.3 us)
Async XLA Ops:
  3.5 12.6 %collective-permute-start.2 = (bf16[112,2048]{1,0:T(8,128)(2,1)}, bf16[112,2048]{1,0:T(8,128)(2,1)S(1)}, u32[]{:S(2)}, u32[]{:S(2)}) collective-permute-start(bf16[112,2048]{1,0:T(8,128)(2,1)} %get-tuple-element.33), channel_id=1, source_target_pairs={{0,4},{4,0},{8,12},{12,8},{1,5},{5,1},{9,13},{13,9},{2,6},{6,2},{1... | collective-permute-start | bytes 1376264 | tf_op jit(solution)/shard_map/ppermute | solution.py:392
  4.0 20.9 %collective-permute-start = (bf16[112,2048]{1,0:T(8,128)(2,1)}, bf16[112,2048]{1,0:T(8,128)(2,1)S(1)}, u32[]{:S(2)}, u32[]{:S(2)}) collective-permute-start(bf16[112,2048]{1,0:T(8,128)(2,1)} %get-tuple-element.28), channel_id=1, source_target_pairs={{0,8},{4,12},{8,0},{12,4},{1,9},{5,13},{9,1},{13,5},{2,10},{6,14},... | collective-permute-start | bytes 1376264 | tf_op jit(solution)/shard_map/ppermute | solution.py:392
  6.6 20.9 %collective-permute-start.1 = (bf16[112,2048]{1,0:T(8,128)(2,1)}, bf16[112,2048]{1,0:T(8,128)(2,1)S(1)}, u32[]{:S(2)}, u32[]{:S(2)}) collective-permute-start(bf16[112,2048]{1,0:T(8,128)(2,1)} %get-tuple-element.29), channel_id=1, source_target_pairs={{0,12},{4,8},{8,4},{12,0},{1,13},{5,9},{9,5},{13,1},{2,14},{6,10},... | collective-permute-start | bytes 1376264 | tf_op jit(solution)/shard_map/ppermute | solution.py:392
  6.6 0.7 %copy-start.4 = (f32[16,128]{1,0:T(8,128)S(1)}, f32[16,128]{1,0:T(8,128)}, u32[]{:S(2)}) copy-start(f32[16,128]{1,0:T(8,128)} %get-tuple-element.30.refs_0_) | copy-start | bytes 24580
  7.3 6.7 %copy-start = (bf16[8,2048,128]{2,1,0:T(8,128)(2,1)S(1)}, bf16[8,2048,128]{2,1,0:T(8,128)(2,1)}, u32[]{:S(2)}) copy-start(bf16[8,2048,128]{2,1,0:T(8,128)(2,1)} %refs_1_.6) | copy-start | bytes 12582916
  12.1 9.2 %collective-permute-start.4 = (bf16[256,512]{1,0:T(8,128)(2,1)S(1)}, bf16[256,512]{1,0:T(8,128)(2,1)S(1)}, u32[]{:S(2)}, u32[]{:S(2)}) collective-permute-start(bf16[256,512]{1,0:T(8,128)(2,1)S(1)} %get-tuple-element.36), channel_id=1, source_target_pairs={{0,1},{1,0},{2,3},{3,2},{4,5},{5,4},{6,7},{7,6},{8,9},{9,8},{10,11... | collective-permute-start | bytes 786440 | tf_op jit(solution)/shard_map/ppermute | solution.py:392
  14.0 2.0 %copy-start.3 = (bf16[112,2048]{1,0:T(8,128)(2,1)S(1)}, bf16[112,2048]{1,0:T(8,128)(2,1)}, u32[]{:S(2)}) copy-start(bf16[112,2048]{1,0:T(8,128)(2,1)} %get-tuple-element.32.refs_0_) | copy-start | bytes 1376260
  16.0 1.5 %copy-start.7 = (s32[256]{0:T(256)S(1)}, s32[256]{0:T(256)}, u32[]{:S(2)}) copy-start(s32[256]{0:T(256)} %param.15) | copy-start | bytes 3076
  16.0 1.5 %copy-start.1 = (bf16[256,2048]{1,0:T(8,128)(2,1)S(1)}, bf16[256,2048]{1,0:T(8,128)(2,1)}, u32[]{:S(2)}) copy-start(bf16[256,2048]{1,0:T(8,128)(2,1)} %refs_2_.5) | copy-start | bytes 3145732
  16.0 1.5 %copy-start.5 = (s32[256]{0:T(256)S(1)}, s32[256]{0:T(256)}, u32[]{:S(2)}) copy-start(s32[256]{0:T(256)} %param.13) | copy-start | bytes 3076
  16.0 1.5 %copy-start.6 = (s32[32]{0:T(128)S(1)}, s32[32]{0:T(128)}, u32[]{:S(2)}) copy-start(s32[32]{0:T(128)} %refs_1_.7) | copy-start | bytes 388
  17.2 17.9 %copy-start.2 = (bf16[8,64,512]{2,1,0:T(8,128)(2,1)S(1)}, bf16[8,64,512]{2,1,0:T(8,128)(2,1)}, u32[]{:S(2)}) copy-start(bf16[8,64,512]{2,1,0:T(8,128)(2,1)} %refs_6_.1) | copy-start | bytes 1572868
  17.2 4.8 %collective-permute-start.3 = (bf16[2,112,128]{2,1,0:T(8,128)(2,1)S(1)}, bf16[2,112,128]{2,1,0:T(8,128)(2,1)S(1)}, u32[]{:S(2)}, u32[]{:S(2)}) collective-permute-start(bf16[2,112,128]{2,1,0:T(8,128)(2,1)S(1)} %down_block.2.refs_3_.refs_0_), channel_id=1, source_target_pairs={{0,1},{1,0},{2,3},{3,2},{4,5},{5,4},{6,7},{7,6},{8,9},{9,8},{10,11... | collective-permute-start | bytes 172040 | tf_op jit(solution)/shard_map/ppermute | solution.py:392
  22.1 12.9 %collective-permute-start.8 = (bf16[736,128]{1,0:T(8,128)(2,1)S(1)}, bf16[736,128]{1,0:T(8,128)(2,1)S(1)}, u32[]{:S(2)}, u32[]{:S(2)}) collective-permute-start(bf16[736,128]{1,0:T(8,128)(2,1)S(1)} %pair_low_sums.1.refs_4_.refs_2_), channel_id=1, source_target_pairs={{0,2},{1,3},{2,0},{3,1},{4,6},{5,7},{6,4},{7,5},{8,10},{9,11},{10,... | collective-permute-start | bytes 565256 | tf_op jit(solution)/shard_map/ppermute | solution.py:392
  28.6 10.4 %collective-permute-start.5 = (bf16[2,112,128]{2,1,0:T(8,128)(2,1)S(1)}, bf16[2,112,128]{2,1,0:T(8,128)(2,1)S(1)}, u32[]{:S(2)}, u32[]{:S(2)}) collective-permute-start(bf16[2,112,128]{2,1,0:T(8,128)(2,1)S(1)} %down_block.3.refs_5_.refs_2_), channel_id=1, source_target_pairs={{0,3},{1,2},{2,1},{3,0},{4,7},{5,6},{6,5},{7,4},{8,11},{9,10},{10,... | collective-permute-start | bytes 172040 | tf_op jit(solution)/shard_map/ppermute | solution.py:392
  32.4 6.6 %collective-permute-start.6 = (bf16[2,112,128]{2,1,0:T(8,128)(2,1)S(1)}, bf16[2,112,128]{2,1,0:T(8,128)(2,1)S(1)}, u32[]{:S(2)}, u32[]{:S(2)}) collective-permute-start(bf16[2,112,128]{2,1,0:T(8,128)(2,1)S(1)} %down_block.3.refs_5_.refs_2_), channel_id=1, source_target_pairs={{0,2},{1,3},{2,0},{3,1},{4,6},{5,7},{6,4},{7,5},{8,10},{9,11},{10,... | collective-permute-start | bytes 172040 | tf_op jit(solution)/shard_map/ppermute | solution.py:392
  32.4 6.6 %collective-permute-start.7 = (bf16[2,112,128]{2,1,0:T(8,128)(2,1)S(1)}, bf16[2,112,128]{2,1,0:T(8,128)(2,1)S(1)}, u32[]{:S(2)}, u32[]{:S(2)}) collective-permute-start(bf16[2,112,128]{2,1,0:T(8,128)(2,1)S(1)} %down_block.3.refs_5_.refs_2_), channel_id=1, source_target_pairs={{0,1},{1,0},{2,3},{3,2},{4,5},{5,4},{6,7},{7,6},{8,9},{9,8},{10,11... | collective-permute-start | bytes 172040 | tf_op jit(solution)/shard_map/ppermute | solution.py:392
  35.7 11.5 %collective-permute-start.11 = (bf16[256,512]{1,0:T(8,128)(2,1)S(1)}, bf16[256,512]{1,0:T(8,128)(2,1)S(1)}, u32[]{:S(2)}, u32[]{:S(2)}) collective-permute-start(bf16[256,512]{1,0:T(8,128)(2,1)S(1)} %get-tuple-element.46), channel_id=1, source_target_pairs={{0,1},{1,0},{2,3},{3,2},{4,5},{5,4},{6,7},{7,6},{8,9},{9,8},{10,11... | collective-permute-start | bytes 786440 | tf_op jit(solution)/shard_map/ppermute | solution.py:392
  36.4 8.5 %collective-permute-start.9 = (bf16[128,512]{1,0:T(8,128)(2,1)S(1)}, bf16[128,512]{1,0:T(8,128)(2,1)S(1)}, u32[]{:S(2)}, u32[]{:S(2)}) collective-permute-start(bf16[128,512]{1,0:T(8,128)(2,1)S(1)} %get-tuple-element.39.refs_7_), channel_id=1, source_target_pairs={{0,2},{1,3},{2,0},{3,1},{4,6},{5,7},{6,4},{7,5},{8,10},{9,11},{10,... | collective-permute-start | bytes 393224 | tf_op jit(solution)/shard_map/ppermute | solution.py:392
  39.0 2.7 %collective-permute-start.10 = (bf16[112,512]{1,0:T(8,128)(2,1)S(1)}, bf16[112,512]{1,0:T(8,128)(2,1)S(1)}, u32[]{:S(2)}, u32[]{:S(2)}) collective-permute-start(bf16[112,512]{1,0:T(8,128)(2,1)S(1)} %get-tuple-element.41), channel_id=1, source_target_pairs={{0,4},{4,0},{8,12},{12,8},{1,5},{5,1},{9,13},{13,9},{2,6},{6,2},{1... | collective-permute-start | bytes 344072 | tf_op jit(solution)/shard_map/ppermute | solution.py:392
  39.6 6.0 %collective-permute-start.12 = (bf16[112,512]{1,0:T(8,128)(2,1)S(1)}, bf16[112,512]{1,0:T(8,128)(2,1)S(1)}, u32[]{:S(2)}, u32[]{:S(2)}) collective-permute-start(bf16[112,512]{1,0:T(8,128)(2,1)S(1)} %get-tuple-element.44.refs_8_), channel_id=1, source_target_pairs={{0,8},{4,12},{8,0},{12,4},{1,9},{5,13},{9,1},{13,5},{2,10},{6,14},... | collective-permute-start | bytes 344072 | tf_op jit(solution)/shard_map/ppermute | solution.py:392
  41.2 6.1 %collective-permute-start.13 = (bf16[112,512]{1,0:T(8,128)(2,1)S(1)}, bf16[112,512]{1,0:T(8,128)(2,1)S(1)}, u32[]{:S(2)}, u32[]{:S(2)}) collective-permute-start(bf16[112,512]{1,0:T(8,128)(2,1)S(1)} %get-tuple-element.48), channel_id=1, source_target_pairs={{0,12},{4,8},{8,4},{12,0},{1,13},{5,9},{9,5},{13,1},{2,14},{6,10},... | collective-permute-start | bytes 344072 | tf_op jit(solution)/shard_map/ppermute | solution.py:392

commit v8 on v7

--- a/solution.py
+++ b/solution.py
@@ -66,7 +66,7 @@
 
 def dispatch_kernel(order, n_wide, per_dev, cap, req_hbm, table_hbm, tok_hbm, gain_hbm, *refs):
     xs = refs[: len(order)]
-    wide_gain_ref, req_ref, table_ref, tok_ref, gain_ref, x_ref, sems, out_sems = refs[
+    xg_hbm, req_ref, table_ref, tok_ref, gain_ref, x_ref, xg_ref, sems, out_sems = refs[
         len(order) :
     ]
     rows, depth = tok_ref.shape
@@ -91,10 +91,17 @@
         )
         picks.append(pick[:height])
     loads[3].wait()
-    wide_gain_ref[...] = gain_ref[...].astype(F32)
     loads[2].wait()
     stores = []
     for j, k in enumerate(order):
+        if k == 1:
+            for b in range(depth // HEAD):
+                span = slice(b * HEAD, (b + 1) * HEAD)
+                piece = tok_ref[:, span].astype(F32) * gain_ref[b : b + 1].astype(F32)
+                xg_ref[:, span] = piece.astype(BF16)
+            copy = pltpu.make_async_copy(xg_ref, xg_hbm, out_sems.at[len(order)])
+            copy.start()
+            stores.append(copy)
         y = jnp.dot(picks[j], tok_ref[...], preferred_element_type=F32)
         first = jnp.where(iota((height, HEAD), 0) == cap, slot_rows[j][:1], y[:, :HEAD])
         x_ref[j, :, :HEAD] = first.astype(BF16)
@@ -106,30 +113,22 @@
         copy.wait()
 
 
-def base_kernel(offsets, cols, gain_hbm, tok_hbm, weight_hbm, *refs):
+def base_kernel(offsets, cols, xg_hbm, weight_hbm, *refs):
     count = len(offsets)
     outs = refs[:count]
-    gain_ref, tok_ref, buf, acc_ref, sems = refs[count:]
+    x_ref, buf, acc_ref, sems = refs[count:]
     steps, chunk, _ = buf.shape
+    load = pltpu.make_async_copy(xg_hbm, x_ref, sems.at[0])
     copies = [
-        pltpu.make_async_copy(weight_hbm.at[pl.ds(i * chunk, chunk)], buf.at[i], sems.at[2 + i])
+        pltpu.make_async_copy(weight_hbm.at[pl.ds(i * chunk, chunk)], buf.at[i], sems.at[1 + i])
         for i in range(steps)
     ]
-    loads = [
-        pltpu.make_async_copy(gain_hbm, gain_ref, sems.at[0]),
-        pltpu.make_async_copy(tok_hbm, tok_ref, sems.at[1]),
-    ]
-    for copy in loads + copies:
+    for copy in [load] + copies:
         copy.start()
-    for copy in loads:
-        copy.wait()
+    load.wait()
     spot = lax.axis_index("tensor").astype(jnp.int32)
     for i in range(steps):
-        pieces = []
-        for b in range(i * chunk // HEAD, (i + 1) * chunk // HEAD):
-            piece = tok_ref[:, b * HEAD : (b + 1) * HEAD].astype(F32) * gain_ref[b : b + 1]
-            pieces.append(piece.astype(BF16))
-        x = jnp.concatenate(pieces, axis=1)
+        x = x_ref[:, i * chunk : (i + 1) * chunk]
         copies[i].wait()
         for j, k in enumerate(offsets):
             start = pl.multiple_of((spot ^ k) * cols, HEAD)
@@ -172,7 +171,7 @@
         copy.start()
     columns = []
     for b in range(depth // HEAD):
-        columns.append(to_column(gain_ref[b : b + 1], HEAD))
+        columns.append(to_column(gain_ref[b : b + 1].astype(F32), HEAD))
     for a in range(per_dev):
         copies[a].wait()
         for b in range(depth // HEAD):
@@ -394,30 +393,26 @@
     small = [pltpu.VMEM((1, rows), jnp.int32), pltpu.SMEM(adapter_storage_row.shape, jnp.int32)]
     first, last = [0, 1], list(range(2, n_wide))
 
-    def dispatch(order, after):
-        *blocks, wide_gain = call(
-            functools.partial(dispatch_kernel, order, n_wide, per_dev, cap),
-            "dispatch",
-            [shape((height, depth), BF16)] * len(order) + [shape(gain.shape, F32)],
-            hbm=(req, adapter_storage_row, tokens, gain),
-            hbm_outs=len(order),
-            after=after,
-            scratch=small
-            + [
-                pltpu.VMEM((rows, depth), BF16),
-                pltpu.VMEM(gain.shape, BF16),
-                pltpu.VMEM((len(order), height, depth), BF16),
-                pltpu.SemaphoreType.DMA((4,)),
-                pltpu.SemaphoreType.DMA((len(order),)),
-            ],
-            flops=2 * len(order) * height * rows * depth,
-            moved=2 * rows * depth * 4,
-            limit=63,
-        )
-        return blocks, wide_gain
-
     order = list(range(n_wide - 1, -1, -1))
-    blocks, wide_gain = dispatch(order, ())
+    *blocks, xg = call(
+        functools.partial(dispatch_kernel, order, n_wide, per_dev, cap),
+        "dispatch",
+        [shape((height, depth), BF16)] * n_wide + [shape((rows, depth), BF16)],
+        hbm=(req, adapter_storage_row, tokens, gain),
+        hbm_outs=n_wide + 1,
+        scratch=small
+        + [
+            pltpu.VMEM((rows, depth), BF16),
+            pltpu.VMEM(gain.shape, BF16),
+            pltpu.VMEM((n_wide, height, depth), BF16),
+            pltpu.VMEM((rows, depth), BF16),
+            pltpu.SemaphoreType.DMA((4,)),
+            pltpu.SemaphoreType.DMA((n_wide + 1,)),
+        ],
+        flops=2 * n_wide * height * rows * depth,
+        moved=2 * rows * depth * 4,
+        limit=63,
+    )
     held = [blocks[n_wide - 1 - k] for k in range(n_wide)]
     held[1:] = [over("wide", held[k], k) for k in range(1, n_wide)]
 
@@ -430,13 +425,12 @@
         functools.partial(base_kernel, offsets, cols),
         "base",
         [shape((rows, cols), BF16)] * (len(far) + 1) + [shape((rows, cols), F32)] * (len(twos) + 1),
-        hbm=(wide_gain, tokens, key_value_weight),
+        hbm=(xg, key_value_weight),
         scratch=[
-            pltpu.VMEM(gain.shape, F32),
             pltpu.VMEM((rows, depth), BF16),
             pltpu.VMEM((steps, chunk, key_value_weight.shape[1]), BF16),
             pltpu.VMEM((len(offsets), rows, cols), F32),
-            pltpu.SemaphoreType.DMA((2 + steps,)),
+            pltpu.SemaphoreType.DMA((1 + steps,)),
         ],
         flops=2 * rows * depth * cols * n_tensor,
         moved=2 * depth * cols * n_tensor,
@@ -448,7 +442,7 @@
         scaled_down_kernel,
         "scaled_down",
         [shape((depth, per_dev * rank), BF16)],
-        vmem=(wide_gain,),
+        vmem=(gain,),
         hbm=(adapter_down_weight,),
         after=(base,),
         scratch=[

time: 48.5 us -> 48.3 us (level)
  starting transfers between devices: 17.2 us -> 18.9 us
  waiting for transfers between devices: 13.4 us -> 12.1 us
  local copies, waits for them, and re-layouts: 0.74 us -> 0.04 us
    ppermute x14, starting transfers between devices: 17.2 us -> 18.9 us  [over(): return lax.ppermute(array, axis, [(i, i ^ k) for i in range(size)])]
    ppermute x14, waiting for transfers between devices: 13.4 us -> 12.1 us  [over(): return lax.ppermute(array, axis, [(i, i ^ k) for i in range(size)])]
    unnamed x16, local copies, waits for them, and re-layouts: 0.74 us -> 0.04 us
  transfers between devices with their start and end apart: 14 -> 14, of which waited for: 7 -> 6; matrix products, arithmetic and copies ran while one was open for 1% -> 1% of each run, Pallas kernels for 24% -> 24%
where the time goes in v8:
time: 48.3 us; the launch traced here: 48.1 us
  starting transfers between devices  18.9 us (39%)
  Pallas kernels  16.2 us (34%)
  waiting for transfers between devices  12.1 us (25%)
  other arithmetic  0.68 us (1%)
    ppermute x14, starting transfers between devices, over(): return lax.ppermute(array, axis, [(i, i ^ k) for i in range(size)])  18.9 us
    pallas_call x12, Pallas kernels, call(): pl.pallas_call(body, out_shape=outs, in_specs=[pl.BlockSpec(memory_space=...  16.2 us
    ppermute x14, waiting for transfers between devices, over(): return lax.ppermute(array, axis, [(i, i ^ k) for i in range(size)])  12.1 us
  transfers between devices with their start and end apart: 14, of which 6 were waited for; matrix products, arithmetic and copies ran while one was open for 1% of the time, Pallas kernels for 24%

profile of v8, /device:TPU:0, one launch (start us, length us, event | category | flops | bytes accessed | tf_op | source)
XLA Modules:
  0.0 48.1 jit_solution(9082753659016327142)
XLA Ops:
  0.0 3.6 %dispatch.1 = (bf16[112,2048]{1,0:T(8,128)(2,1)}, bf16[112,2048]{1,0:T(8,128)(2,1)}, bf16[112,2048]{1,0:T(8,128)(2,1)}, bf16[112,2048]{1,0:T(8,128)(2,1)}, bf16[256,2048]{1,0:T(8,128)(2,1)}) custom-call(s32[1,256]{1,0:T(1,128)} %bitcast.4, s32[32]{0:T(128)} %refs_1_.7, bf16[256,2048]{1,0:T(8,128)(2,1)} %refs_2_.3, bf16[16,128]{1,0:T(8,128)(2,1)} %bitcast.2), custom_call_target="tpu_custom_call" | custom-call | flops 469762048 | bytes 4194304 | tf_op jit(solution)/shard_map/dispatch/pallas_call | solution.py:28
  3.6 0.5 %collective-permute-start.2 = (bf16[112,2048]{1,0:T(8,128)(2,1)}, bf16[112,2048]{1,0:T(8,128)(2,1)S(1)}, u32[]{:S(2)}, u32[]{:S(2)}) collective-permute-start(bf16[112,2048]{1,0:T(8,128)(2,1)} %get-tuple-element.33), channel_id=1, source_target_pairs={{0,4},{4,0},{8,12},{12,8},{1,5},{5,1},{9,13},{13,9},{2,6},{6,2},{1... | collective-permute-start | bytes 1376264 | tf_op jit(solution)/shard_map/ppermute | solution.py:391
  4.2 2.6 %collective-permute-start = (bf16[112,2048]{1,0:T(8,128)(2,1)}, bf16[112,2048]{1,0:T(8,128)(2,1)S(1)}, u32[]{:S(2)}, u32[]{:S(2)}) collective-permute-start(bf16[112,2048]{1,0:T(8,128)(2,1)} %get-tuple-element.28), channel_id=1, source_target_pairs={{0,8},{4,12},{8,0},{12,4},{1,9},{5,13},{9,1},{13,5},{2,10},{6,14},... | collective-permute-start | bytes 1376264 | tf_op jit(solution)/shard_map/ppermute | solution.py:391
  6.8 4.7 %base.1 = (bf16[256,512]{1,0:T(8,128)(2,1)S(1)}, bf16[256,512]{1,0:T(8,128)(2,1)S(1)}, f32[256,512]{1,0:T(8,128)S(1)}, f32[256,512]{1,0:T(8,128)S(1)}) custom-call(bf16[256,2048]{1,0:T(8,128)(2,1)} %get-tuple-element.30.refs_0_, bf16[2048,2048]{1,0:T(8,128)(2,1)} %refs_1_.5), custom_call_target="tpu_custom_call" | custom-call | flops 2147483648 | bytes 8388608 | tf_op jit(solution)/shard_map/base/pallas_call | solution.py:28
  11.5 1.9 %collective-permute-start.4 = (bf16[256,512]{1,0:T(8,128)(2,1)S(1)}, bf16[256,512]{1,0:T(8,128)(2,1)S(1)}, u32[]{:S(2)}, u32[]{:S(2)}) collective-permute-start(bf16[256,512]{1,0:T(8,128)(2,1)S(1)} %get-tuple-element.36), channel_id=1, source_target_pairs={{0,1},{1,0},{2,3},{3,2},{4,5},{5,4},{6,7},{7,6},{8,9},{9,8},{10,11... | collective-permute-start | bytes 786440 | tf_op jit(solution)/shard_map/ppermute | solution.py:391
  13.4 2.0 %scaled_down.1.refs_2_ = bf16[2048,1024]{1,0:T(8,128)(2,1)S(1)} custom-call(bf16[16,128]{1,0:T(8,128)(2,1)S(1)} %bitcast.3, bf16[8,2048,128]{2,1,0:T(8,128)(2,1)S(1)} %copy-done, f32[256,512]{1,0:T(8,128)S(1)} %get-tuple-element.31.refs_2_.refs_1_), custom_call_target="tpu_custom_call" | custom-call | flops 8388608 | bytes 8388608 | tf_op jit(solution)/shard_map/scaled_down/pallas_call | solution.py:28
  15.4 1.1 %down_block.2.refs_3_.refs_0_ = bf16[2,112,128]{2,1,0:T(8,128)(2,1)S(1)} custom-call(bf16[112,2048]{1,0:T(8,128)(2,1)S(1)} %copy-done.2, bf16[112,2048]{1,0:T(8,128)(2,1)S(1)} %collective-permute-done.2.refs_1_, bf16[2048,1024]{1,0:T(8,128)(2,1)S(1)} %scaled_down.1.refs_2_), custom_call_target="tpu_custom_call" | custom-call | flops 939524096 | bytes 4194304 | tf_op jit(solution)/shard_map/down_block/pallas_call | solution.py:28
  16.9 1.1 %aux.1 = (f32[8,128]{1,0:T(8,128)S(1)}, bf16[256,128]{1,0:T(8,128)(2,1)S(1)}, bf16[256,128]{1,0:T(8,128)(2,1)S(1)}, bf16[256,128]{1,0:T(8,128)(2,1)S(1)}, bf16[256,128]{1,0:T(8,128)(2,1)S(1)}) custom-call(s32[1,256]{1,0:T(1,128)S(1)} %bitcast.5, s32[32]{0:T(128)S(1)} %copy-done.6, bf16[256,2048]{1,0:T(8,128)(2,1)S(1)} %copy-done.3, ...), custom_call_target="tpu_custom_call" | custom-call | flops 268435456 | bytes 1048576 | tf_op jit(solution)/shard_map/aux/pallas_call | solution.py:28
  18.0 2.7 %collective-permute-done.4.refs_3_.refs_2_ = bf16[256,512]{1,0:T(8,128)(2,1)S(1)} collective-permute-done((bf16[256,512]{1,0:T(8,128)(2,1)S(1)}, bf16[256,512]{1,0:T(8,128)(2,1)S(1)}, u32[]{:S(2)}, u32[]{:S(2)}) %collective-permute-start.4) | collective-permute-done | bytes 262176 | tf_op jit(solution)/shard_map/ppermute | solution.py:391
  20.7 0.7 %collective-permute-done.3.refs_1_ = bf16[2,112,128]{2,1,0:T(8,128)(2,1)S(1)} collective-permute-done((bf16[2,112,128]{2,1,0:T(8,128)(2,1)S(1)}, bf16[2,112,128]{2,1,0:T(8,128)(2,1)S(1)}, u32[]{:S(2)}, u32[]{:S(2)}) %collective-permute-start.3) | collective-permute-done | bytes 57376 | tf_op jit(solution)/shard_map/ppermute | solution.py:391
  21.5 2.8 %collective-permute-start.8 = (bf16[736,128]{1,0:T(8,128)(2,1)S(1)}, bf16[736,128]{1,0:T(8,128)(2,1)S(1)}, u32[]{:S(2)}, u32[]{:S(2)}) collective-permute-start(bf16[736,128]{1,0:T(8,128)(2,1)S(1)} %pair_low_sums.1.refs_4_.refs_2_), channel_id=1, source_target_pairs={{0,2},{1,3},{2,0},{3,1},{4,6},{5,7},{6,4},{7,5},{8,10},{9,11},{10,... | collective-permute-start | bytes 565256 | tf_op jit(solution)/shard_map/ppermute | solution.py:391
  24.3 3.3 %collective-permute-done.1.refs_1_ = bf16[112,2048]{1,0:T(8,128)(2,1)S(1)} collective-permute-done((bf16[112,2048]{1,0:T(8,128)(2,1)}, bf16[112,2048]{1,0:T(8,128)(2,1)S(1)}, u32[]{:S(2)}, u32[]{:S(2)}) %collective-permute-start.1) | collective-permute-done | bytes 458784 | tf_op jit(solution)/shard_map/ppermute | solution.py:391
  27.6 1.1 %down_block.3.refs_5_.refs_2_ = bf16[2,112,128]{2,1,0:T(8,128)(2,1)S(1)} custom-call(bf16[112,2048]{1,0:T(8,128)(2,1)S(1)} %collective-permute-done.refs_0_, bf16[112,2048]{1,0:T(8,128)(2,1)S(1)} %collective-permute-done.1.refs_1_, bf16[2048,1024]{1,0:T(8,128)(2,1)S(1)} %scaled_down.1.refs_2_, f32[8,128]{1,0:T(8,128)S(1)} %get-tuple-element.34.refs_4_.refs_3_, ...), custom_call_target="tpu_custom_call" | custom-call | flops 939524096 | bytes 4194304 | tf_op jit(solution)/shard_map/down_block/pallas_call | solution.py:28
  28.8 3.7 %collective-permute-start.5 = (bf16[2,112,128]{2,1,0:T(8,128)(2,1)S(1)}, bf16[2,112,128]{2,1,0:T(8,128)(2,1)S(1)}, u32[]{:S(2)}, u32[]{:S(2)}) collective-permute-start(bf16[2,112,128]{2,1,0:T(8,128)(2,1)S(1)} %down_block.3.refs_5_.refs_2_), channel_id=1, source_target_pairs={{0,3},{1,2},{2,1},{3,0},{4,7},{5,6},{6,5},{7,4},{8,11},{9,10},{10,... | collective-permute-start | bytes 172040 | tf_op jit(solution)/shard_map/ppermute | solution.py:391
  32.5 0.7 %collective-permute-start.7 = (bf16[2,112,128]{2,1,0:T(8,128)(2,1)S(1)}, bf16[2,112,128]{2,1,0:T(8,128)(2,1)S(1)}, u32[]{:S(2)}, u32[]{:S(2)}) collective-permute-start(bf16[2,112,128]{2,1,0:T(8,128)(2,1)S(1)} %down_block.3.refs_5_.refs_2_), channel_id=1, source_target_pairs={{0,1},{1,0},{2,3},{3,2},{4,5},{5,4},{6,7},{7,6},{8,9},{9,8},{10,11... | collective-permute-start | bytes 172040 | tf_op jit(solution)/shard_map/ppermute | solution.py:391
  33.2 0.6 %up_block.2 = (bf16[112,512]{1,0:T(8,128)(2,1)S(1)}, bf16[112,512]{1,0:T(8,128)(2,1)S(1)}) custom-call(bf16[112,2048]{1,0:T(8,128)(2,1)S(1)} %copy-done.2, bf16[112,2048]{1,0:T(8,128)(2,1)S(1)} %collective-permute-done.2.refs_1_, bf16[736,128]{1,0:T(8,128)(2,1)S(1)} %pair_low_sums.1.refs_4_.refs_2_, ...), custom_call_target="tpu_custom_call" | custom-call | flops 234881024 | bytes 1048576 | tf_op jit(solution)/shard_map/up_block/pallas_call | solution.py:28
  33.9 1.4 %collective-permute-start.11 = (bf16[256,512]{1,0:T(8,128)(2,1)S(1)}, bf16[256,512]{1,0:T(8,128)(2,1)S(1)}, u32[]{:S(2)}, u32[]{:S(2)}) collective-permute-start(bf16[256,512]{1,0:T(8,128)(2,1)S(1)} %get-tuple-element.46), channel_id=1, source_target_pairs={{0,1},{1,0},{2,3},{3,2},{4,5},{5,4},{6,7},{7,6},{8,9},{9,8},{10,11... | collective-permute-start | bytes 786440 | tf_op jit(solution)/shard_map/ppermute | solution.py:391
  35.3 0.5 %fusion = (f32[256,64]{1,0:T(8,128)S(1)}, f32[256,64]{1,0:T(8,128)S(1)}, f32[256,64]{1,0:T(8,128)S(1)}) fusion(f32[64]{0:T(128)S(1)} %multiply_exponential_fusion, f32[256]{0:T(256)S(1)} %convert_element_type.10), kind=kLoop, calls=%fused_computation.4 | loop fusion | flops 32768 | bytes 197888 | tf_op jit(solution)/shard_map/neg | solution.py:461
  35.8 3.0 %collective-permute-start.9 = (bf16[128,512]{1,0:T(8,128)(2,1)S(1)}, bf16[128,512]{1,0:T(8,128)(2,1)S(1)}, u32[]{:S(2)}, u32[]{:S(2)}) collective-permute-start(bf16[128,512]{1,0:T(8,128)(2,1)S(1)} %get-tuple-element.39.refs_7_), channel_id=1, source_target_pairs={{0,2},{1,3},{2,0},{3,1},{4,6},{5,7},{6,4},{7,5},{8,10},{9,11},{10,... | collective-permute-start | bytes 393224 | tf_op jit(solution)/shard_map/ppermute | solution.py:391
  38.8 0.6 %up_block.3 = (bf16[112,512]{1,0:T(8,128)(2,1)S(1)}, bf16[112,512]{1,0:T(8,128)(2,1)S(1)}, f32[8,128]{1,0:T(8,128)S(1)}) custom-call(bf16[112,2048]{1,0:T(8,128)(2,1)S(1)} %collective-permute-done.refs_0_, bf16[112,2048]{1,0:T(8,128)(2,1)S(1)} %collective-permute-done.1.refs_1_, bf16[2,112,128]{2,1,0:T(8,128)(2,1)S(1)} %down_block.3.refs_5_.refs_2_, ...), custom_call_target="tpu_custom_call" | custom-call | flops 234881024 | bytes 1048576 | tf_op jit(solution)/shard_map/up_block/pallas_call | solution.py:28
  39.4 1.6 %collective-permute-start.12 = (bf16[112,512]{1,0:T(8,128)(2,1)S(1)}, bf16[112,512]{1,0:T(8,128)(2,1)S(1)}, u32[]{:S(2)}, u32[]{:S(2)}) collective-permute-start(bf16[112,512]{1,0:T(8,128)(2,1)S(1)} %get-tuple-element.44.refs_8_), channel_id=1, source_target_pairs={{0,8},{4,12},{8,0},{12,4},{1,9},{5,13},{9,1},{13,5},{2,10},{6,14},... | collective-permute-start | bytes 344072 | tf_op jit(solution)/shard_map/ppermute | solution.py:391
  41.5 3.6 %collective-permute-done.9.refs_3_ = bf16[128,512]{1,0:T(8,128)(2,1)S(1)} collective-permute-done((bf16[128,512]{1,0:T(8,128)(2,1)S(1)}, bf16[128,512]{1,0:T(8,128)(2,1)S(1)}, u32[]{:S(2)}, u32[]{:S(2)}) %collective-permute-start.9) | collective-permute-done | bytes 131104 | tf_op jit(solution)/shard_map/ppermute | solution.py:391
  45.5 1.7 %collective-permute-done.13.refs_6_ = bf16[112,512]{1,0:T(8,128)(2,1)S(1)} collective-permute-done((bf16[112,512]{1,0:T(8,128)(2,1)S(1)}, bf16[112,512]{1,0:T(8,128)(2,1)S(1)}, u32[]{:S(2)}, u32[]{:S(2)}) %collective-permute-start.13) | collective-permute-done | bytes 114720 | tf_op jit(solution)/shard_map/ppermute | solution.py:391
  47.1 1.0 %finish.1 = bf16[256,512]{1,0:T(8,128)(2,1)} custom-call(f32[256,512]{1,0:T(8,128)S(1)} %get-tuple-element.45.refs_0_, bf16[256,512]{1,0:T(8,128)(2,1)S(1)} %collective-permute-done.11.refs_1_, f32[256,128]{1,0:T(8,128)S(1)} %get-tuple-element.47.refs_2_, f32[256,128]{1,0:T(8,128)S(1)} %get-tuple-element.54.refs_3_, ...), custom_call_target="tpu_custom_call" | custom-call | flops 33554432 | tf_op jit(solution)/shard_map/finish/pallas_call | solution.py:28
  (36 shorter events, 1.4 us)
Async XLA Ops:
  3.6 11.8 %collective-permute-start.2 = (bf16[112,2048]{1,0:T(8,128)(2,1)}, bf16[112,2048]{1,0:T(8,128)(2,1)S(1)}, u32[]{:S(2)}, u32[]{:S(2)}) collective-permute-start(bf16[112,2048]{1,0:T(8,128)(2,1)} %get-tuple-element.33), channel_id=1, source_target_pairs={{0,4},{4,0},{8,12},{12,8},{1,5},{5,1},{9,13},{13,9},{2,6},{6,2},{1... | collective-permute-start | bytes 1376264 | tf_op jit(solution)/shard_map/ppermute | solution.py:391
  4.2 20.1 %collective-permute-start = (bf16[112,2048]{1,0:T(8,128)(2,1)}, bf16[112,2048]{1,0:T(8,128)(2,1)S(1)}, u32[]{:S(2)}, u32[]{:S(2)}) collective-permute-start(bf16[112,2048]{1,0:T(8,128)(2,1)} %get-tuple-element.28), channel_id=1, source_target_pairs={{0,8},{4,12},{8,0},{12,4},{1,9},{5,13},{9,1},{13,5},{2,10},{6,14},... | collective-permute-start | bytes 1376264 | tf_op jit(solution)/shard_map/ppermute | solution.py:391
  6.7 20.9 %collective-permute-start.1 = (bf16[112,2048]{1,0:T(8,128)(2,1)}, bf16[112,2048]{1,0:T(8,128)(2,1)S(1)}, u32[]{:S(2)}, u32[]{:S(2)}) collective-permute-start(bf16[112,2048]{1,0:T(8,128)(2,1)} %get-tuple-element.29), channel_id=1, source_target_pairs={{0,12},{4,8},{8,4},{12,0},{1,13},{5,9},{9,5},{13,1},{2,14},{6,10},... | collective-permute-start | bytes 1376264 | tf_op jit(solution)/shard_map/ppermute | solution.py:391
  6.8 6.6 %copy-start = (bf16[8,2048,128]{2,1,0:T(8,128)(2,1)S(1)}, bf16[8,2048,128]{2,1,0:T(8,128)(2,1)}, u32[]{:S(2)}) copy-start(bf16[8,2048,128]{2,1,0:T(8,128)(2,1)} %refs_1_.6) | copy-start | bytes 12582916
  6.8 6.6 %copy-start.4 = (bf16[2048]{0:T(1024)(128)(2,1)S(1)}, bf16[2048]{0:T(1024)(128)(2,1)}, u32[]{:S(2)}) copy-start(bf16[2048]{0:T(1024)(128)(2,1)} %param.9) | copy-start | bytes 12292
  11.5 9.2 %collective-permute-start.4 = (bf16[256,512]{1,0:T(8,128)(2,1)S(1)}, bf16[256,512]{1,0:T(8,128)(2,1)S(1)}, u32[]{:S(2)}, u32[]{:S(2)}) collective-permute-start(bf16[256,512]{1,0:T(8,128)(2,1)S(1)} %get-tuple-element.36), channel_id=1, source_target_pairs={{0,1},{1,0},{2,3},{3,2},{4,5},{5,4},{6,7},{7,6},{8,9},{9,8},{10,11... | collective-permute-start | bytes 786440 | tf_op jit(solution)/shard_map/ppermute | solution.py:391
  13.4 2.0 %copy-start.2 = (bf16[112,2048]{1,0:T(8,128)(2,1)S(1)}, bf16[112,2048]{1,0:T(8,128)(2,1)}, u32[]{:S(2)}) copy-start(bf16[112,2048]{1,0:T(8,128)(2,1)} %get-tuple-element.32.refs_0_) | copy-start | bytes 1376260
  15.3 1.5 %copy-start.7 = (s32[256]{0:T(256)S(1)}, s32[256]{0:T(256)}, u32[]{:S(2)}) copy-start(s32[256]{0:T(256)} %param.15) | copy-start | bytes 3076
  15.4 1.5 %copy-start.3 = (bf16[256,2048]{1,0:T(8,128)(2,1)S(1)}, bf16[256,2048]{1,0:T(8,128)(2,1)}, u32[]{:S(2)}) copy-start(bf16[256,2048]{1,0:T(8,128)(2,1)} %refs_2_.3) | copy-start | bytes 3145732
  15.4 1.5 %copy-start.5 = (s32[256]{0:T(256)S(1)}, s32[256]{0:T(256)}, u32[]{:S(2)}) copy-start(s32[256]{0:T(256)} %param.13) | copy-start | bytes 3076
  15.4 1.5 %copy-start.6 = (s32[32]{0:T(128)S(1)}, s32[32]{0:T(128)}, u32[]{:S(2)}) copy-start(s32[32]{0:T(128)} %refs_1_.7) | copy-start | bytes 388
  16.6 16.7 %copy-start.1 = (bf16[8,64,512]{2,1,0:T(8,128)(2,1)S(1)}, bf16[8,64,512]{2,1,0:T(8,128)(2,1)}, u32[]{:S(2)}) copy-start(bf16[8,64,512]{2,1,0:T(8,128)(2,1)} %refs_6_.1) | copy-start | bytes 1572868
  16.6 4.8 %collective-permute-start.3 = (bf16[2,112,128]{2,1,0:T(8,128)(2,1)S(1)}, bf16[2,112,128]{2,1,0:T(8,128)(2,1)S(1)}, u32[]{:S(2)}, u32[]{:S(2)}) collective-permute-start(bf16[2,112,128]{2,1,0:T(8,128)(2,1)S(1)} %down_block.2.refs_3_.refs_0_), channel_id=1, source_target_pairs={{0,1},{1,0},{2,3},{3,2},{4,5},{5,4},{6,7},{7,6},{8,9},{9,8},{10,11... | collective-permute-start | bytes 172040 | tf_op jit(solution)/shard_map/ppermute | solution.py:391
  21.5 11.8 %collective-permute-start.8 = (bf16[736,128]{1,0:T(8,128)(2,1)S(1)}, bf16[736,128]{1,0:T(8,128)(2,1)S(1)}, u32[]{:S(2)}, u32[]{:S(2)}) collective-permute-start(bf16[736,128]{1,0:T(8,128)(2,1)S(1)} %pair_low_sums.1.refs_4_.refs_2_), channel_id=1, source_target_pairs={{0,2},{1,3},{2,0},{3,1},{4,6},{5,7},{6,4},{7,5},{8,10},{9,11},{10,... | collective-permute-start | bytes 565256 | tf_op jit(solution)/shard_map/ppermute | solution.py:391
  28.8 10.0 %collective-permute-start.5 = (bf16[2,112,128]{2,1,0:T(8,128)(2,1)S(1)}, bf16[2,112,128]{2,1,0:T(8,128)(2,1)S(1)}, u32[]{:S(2)}, u32[]{:S(2)}) collective-permute-start(bf16[2,112,128]{2,1,0:T(8,128)(2,1)S(1)} %down_block.3.refs_5_.refs_2_), channel_id=1, source_target_pairs={{0,3},{1,2},{2,1},{3,0},{4,7},{5,6},{6,5},{7,4},{8,11},{9,10},{10,... | collective-permute-start | bytes 172040 | tf_op jit(solution)/shard_map/ppermute | solution.py:391
  32.5 6.3 %collective-permute-start.6 = (bf16[2,112,128]{2,1,0:T(8,128)(2,1)S(1)}, bf16[2,112,128]{2,1,0:T(8,128)(2,1)S(1)}, u32[]{:S(2)}, u32[]{:S(2)}) collective-permute-start(bf16[2,112,128]{2,1,0:T(8,128)(2,1)S(1)} %down_block.3.refs_5_.refs_2_), channel_id=1, source_target_pairs={{0,2},{1,3},{2,0},{3,1},{4,6},{5,7},{6,4},{7,5},{8,10},{9,11},{10,... | collective-permute-start | bytes 172040 | tf_op jit(solution)/shard_map/ppermute | solution.py:391
  32.5 6.3 %collective-permute-start.7 = (bf16[2,112,128]{2,1,0:T(8,128)(2,1)S(1)}, bf16[2,112,128]{2,1,0:T(8,128)(2,1)S(1)}, u32[]{:S(2)}, u32[]{:S(2)}) collective-permute-start(bf16[2,112,128]{2,1,0:T(8,128)(2,1)S(1)} %down_block.3.refs_5_.refs_2_), channel_id=1, source_target_pairs={{0,1},{1,0},{2,3},{3,2},{4,5},{5,4},{6,7},{7,6},{8,9},{9,8},{10,11... | collective-permute-start | bytes 172040 | tf_op jit(solution)/shard_map/ppermute | solution.py:391
  33.9 13.2 %collective-permute-start.11 = (bf16[256,512]{1,0:T(8,128)(2,1)S(1)}, bf16[256,512]{1,0:T(8,128)(2,1)S(1)}, u32[]{:S(2)}, u32[]{:S(2)}) collective-permute-start(bf16[256,512]{1,0:T(8,128)(2,1)S(1)} %get-tuple-element.46), channel_id=1, source_target_pairs={{0,1},{1,0},{2,3},{3,2},{4,5},{5,4},{6,7},{7,6},{8,9},{9,8},{10,11... | collective-permute-start | bytes 786440 | tf_op jit(solution)/shard_map/ppermute | solution.py:391
  35.8 9.2 %collective-permute-start.9 = (bf16[128,512]{1,0:T(8,128)(2,1)S(1)}, bf16[128,512]{1,0:T(8,128)(2,1)S(1)}, u32[]{:S(2)}, u32[]{:S(2)}) collective-permute-start(bf16[128,512]{1,0:T(8,128)(2,1)S(1)} %get-tuple-element.39.refs_7_), channel_id=1, source_target_pairs={{0,2},{1,3},{2,0},{3,1},{4,6},{5,7},{6,4},{7,5},{8,10},{9,11},{10,... | collective-permute-start | bytes 393224 | tf_op jit(solution)/shard_map/ppermute | solution.py:391
  38.8 2.7 %collective-permute-start.10 = (bf16[112,512]{1,0:T(8,128)(2,1)S(1)}, bf16[112,512]{1,0:T(8,128)(2,1)S(1)}, u32[]{:S(2)}, u32[]{:S(2)}) collective-permute-start(bf16[112,512]{1,0:T(8,128)(2,1)S(1)} %get-tuple-element.41), channel_id=1, source_target_pairs={{0,4},{4,0},{8,12},{12,8},{1,5},{5,1},{9,13},{13,9},{2,6},{6,2},{1... | collective-permute-start | bytes 344072 | tf_op jit(solution)/shard_map/ppermute | solution.py:391
  39.4 6.0 %collective-permute-start.12 = (bf16[112,512]{1,0:T(8,128)(2,1)S(1)}, bf16[112,512]{1,0:T(8,128)(2,1)S(1)}, u32[]{:S(2)}, u32[]{:S(2)}) collective-permute-start(bf16[112,512]{1,0:T(8,128)(2,1)S(1)} %get-tuple-element.44.refs_8_), channel_id=1, source_target_pairs={{0,8},{4,12},{8,0},{12,4},{1,9},{5,13},{9,1},{13,5},{2,10},{6,14},... | collective-permute-start | bytes 344072 | tf_op jit(solution)/shard_map/ppermute | solution.py:391
  41.0 6.1 %collective-permute-start.13 = (bf16[112,512]{1,0:T(8,128)(2,1)S(1)}, bf16[112,512]{1,0:T(8,128)(2,1)S(1)}, u32[]{:S(2)}, u32[]{:S(2)}) collective-permute-start(bf16[112,512]{1,0:T(8,128)(2,1)S(1)} %get-tuple-element.48), channel_id=1, source_target_pairs={{0,12},{4,8},{8,4},{12,0},{1,13},{5,9},{9,5},{13,1},{2,14},{6,10},... | collective-permute-start | bytes 344072 | tf_op jit(solution)/shard_map/ppermute | solution.py:391

commit v9 on v8

--- a/solution.py
+++ b/solution.py
@@ -149,10 +149,9 @@
         out_ref[...] = (refs[j][rows] + refs[count + j][rows].astype(F32)).astype(BF16)
 
 
-def pair_low_kernel(count, low_ref, other_ref, *refs):
+def pair_low_kernel(count, half, low_ref, other_ref, *refs):
     outs = refs[2 * count :]
     cols = refs[0].shape[1]
-    half = refs[0].shape[0] // 2
     for j in range(count):
         total = (refs[j][:half] + refs[count + j][:half].astype(F32)).astype(BF16)
         for h in range(cols // HEAD):
@@ -317,7 +316,7 @@
     return jnp.dot(lhs, jnp.concatenate(blocks, axis=0), preferred_element_type=F32)
 
 
-def gather_kernel(n_pairs, count, sq_ref, base_ref, *refs):
+def gather_kernel(n_pairs, count, half, sq_ref, base_ref, *refs):
     tops, bottoms = refs[:n_pairs], refs[n_pairs : 2 * n_pairs]
     deltas = refs[2 * n_pairs : 2 * n_pairs + count]
     sels = refs[2 * n_pairs + count : 2 * n_pairs + 2 * count]
@@ -334,7 +333,6 @@
     scale = lax.rsqrt(square * (1.0 / MODEL_WIDTH) + EPSILON)
     scale_ref[...] = jnp.broadcast_to(scale, (rows, HEAD))
     total = base_ref[...] + placed(sels, deltas)
-    half = rows // 2
     lower = total[half:]
     for bottom in bottoms:
         lower = lower + bottom[...].astype(F32)
@@ -500,11 +498,11 @@
         flops=2 * rows * rows * depth,
         moved=2 * rows * depth,
     )
-    half = rows // 2
+    half = rows * 3 // 128 * 16
     upper = cols // HEAD * half
     other = over("tensor", low, 1)
     pairs = call(
-        functools.partial(pair_low_kernel, len(twos)),
+        functools.partial(pair_low_kernel, len(twos), half),
         "pair_low_sums",
         [shape((upper + len(first) * height, HEAD), BF16)]
         + [shape((upper, HEAD), BF16)] * (len(twos) - 1),
@@ -529,7 +527,7 @@
     *pairs, near = call(
         functools.partial(pair_kernel, len(twos), half),
         "pair_sums",
-        [shape((half, cols), BF16)] * len(twos) + [shape((rows, cols), BF16)],
+        [shape((rows - half, cols), BF16)] * len(twos) + [shape((rows, cols), BF16)],
         vmem=(near, *own, *beside),
         after=(ups[0],),
     )
@@ -538,7 +536,7 @@
     *ups, square = up_block(last, last_parts, True, (pairs[0],))
     last_deltas = [over("wide", u, k) for k, u in zip(last, ups)]
     total, scale = call(
-        functools.partial(gather_kernel, len(bottoms), len(first)),
+        functools.partial(gather_kernel, len(tops), len(first), half),
         "gather",
         [shape((rows, cols), F32), shape((rows, HEAD), F32)],
         vmem=(square, base, *tops, *bottoms, *deltas, *[sels[k] for k in first]),

time: 48.3 us -> 48.5 us (level)
  transfers between devices with their start and end apart: 14 -> 14, of which waited for: 6 -> 7; matrix products, arithmetic and copies ran while one was open for 1% -> 1% of each run, Pallas kernels for 24% -> 24%
where the time goes in v9:
time: 48.5 us; the launch traced here: 48.3 us
  starting transfers between devices  18.9 us (39%)
  Pallas kernels  16.2 us (33%)
  waiting for transfers between devices  12.3 us (25%)
  other arithmetic  0.67 us (1%)
    ppermute x14, starting transfers between devices, over(): return lax.ppermute(array, axis, [(i, i ^ k) for i in range(size)])  18.9 us
    pallas_call x12, Pallas kernels, call(): pl.pallas_call(body, out_shape=outs, in_specs=[pl.BlockSpec(memory_space=...  16.2 us
    ppermute x14, waiting for transfers between devices, over(): return lax.ppermute(array, axis, [(i, i ^ k) for i in range(size)])  12.3 us
  transfers between devices with their start and end apart: 14, of which 7 were waited for; matrix products, arithmetic and copies ran while one was open for 1% of the time, Pallas kernels for 24%

profile of v9, /device:TPU:0, one launch (start us, length us, event | category | flops | bytes accessed | tf_op | source)
XLA Modules:
  0.0 48.3 jit_solution(11920770495728772576)
XLA Ops:
  0.0 3.6 %dispatch.1 = (bf16[112,2048]{1,0:T(8,128)(2,1)}, bf16[112,2048]{1,0:T(8,128)(2,1)}, bf16[112,2048]{1,0:T(8,128)(2,1)}, bf16[112,2048]{1,0:T(8,128)(2,1)}, bf16[256,2048]{1,0:T(8,128)(2,1)}) custom-call(s32[1,256]{1,0:T(1,128)} %bitcast.4, s32[32]{0:T(128)} %refs_1_.7, bf16[256,2048]{1,0:T(8,128)(2,1)} %refs_2_.3, bf16[16,128]{1,0:T(8,128)(2,1)} %bitcast.2), custom_call_target="tpu_custom_call" | custom-call | flops 469762048 | bytes 4194304 | tf_op jit(solution)/shard_map/dispatch/pallas_call | solution.py:28
  3.6 0.5 %collective-permute-start.2 = (bf16[112,2048]{1,0:T(8,128)(2,1)}, bf16[112,2048]{1,0:T(8,128)(2,1)S(1)}, u32[]{:S(2)}, u32[]{:S(2)}) collective-permute-start(bf16[112,2048]{1,0:T(8,128)(2,1)} %get-tuple-element.33), channel_id=1, source_target_pairs={{0,4},{4,0},{8,12},{12,8},{1,5},{5,1},{9,13},{13,9},{2,6},{6,2},{1... | collective-permute-start | bytes 1376264 | tf_op jit(solution)/shard_map/ppermute | solution.py:389
  4.2 2.6 %collective-permute-start = (bf16[112,2048]{1,0:T(8,128)(2,1)}, bf16[112,2048]{1,0:T(8,128)(2,1)S(1)}, u32[]{:S(2)}, u32[]{:S(2)}) collective-permute-start(bf16[112,2048]{1,0:T(8,128)(2,1)} %get-tuple-element.28), channel_id=1, source_target_pairs={{0,8},{4,12},{8,0},{12,4},{1,9},{5,13},{9,1},{13,5},{2,10},{6,14},... | collective-permute-start | bytes 1376264 | tf_op jit(solution)/shard_map/ppermute | solution.py:389
  6.8 4.7 %base.1 = (bf16[256,512]{1,0:T(8,128)(2,1)S(1)}, bf16[256,512]{1,0:T(8,128)(2,1)S(1)}, f32[256,512]{1,0:T(8,128)S(1)}, f32[256,512]{1,0:T(8,128)S(1)}) custom-call(bf16[256,2048]{1,0:T(8,128)(2,1)} %get-tuple-element.30.refs_0_, bf16[2048,2048]{1,0:T(8,128)(2,1)} %refs_1_.5), custom_call_target="tpu_custom_call" | custom-call | flops 2147483648 | bytes 8388608 | tf_op jit(solution)/shard_map/base/pallas_call | solution.py:28
  11.5 1.9 %collective-permute-start.4 = (bf16[256,512]{1,0:T(8,128)(2,1)S(1)}, bf16[256,512]{1,0:T(8,128)(2,1)S(1)}, u32[]{:S(2)}, u32[]{:S(2)}) collective-permute-start(bf16[256,512]{1,0:T(8,128)(2,1)S(1)} %get-tuple-element.36), channel_id=1, source_target_pairs={{0,1},{1,0},{2,3},{3,2},{4,5},{5,4},{6,7},{7,6},{8,9},{9,8},{10,11... | collective-permute-start | bytes 786440 | tf_op jit(solution)/shard_map/ppermute | solution.py:389
  13.4 2.0 %scaled_down.1.refs_2_ = bf16[2048,1024]{1,0:T(8,128)(2,1)S(1)} custom-call(bf16[16,128]{1,0:T(8,128)(2,1)S(1)} %bitcast.3, bf16[8,2048,128]{2,1,0:T(8,128)(2,1)S(1)} %copy-done, f32[256,512]{1,0:T(8,128)S(1)} %get-tuple-element.31.refs_2_.refs_1_), custom_call_target="tpu_custom_call" | custom-call | flops 8388608 | bytes 8388608 | tf_op jit(solution)/shard_map/scaled_down/pallas_call | solution.py:28
  15.4 1.1 %down_block.2.refs_3_.refs_0_ = bf16[2,112,128]{2,1,0:T(8,128)(2,1)S(1)} custom-call(bf16[112,2048]{1,0:T(8,128)(2,1)S(1)} %copy-done.2, bf16[112,2048]{1,0:T(8,128)(2,1)S(1)} %collective-permute-done.2.refs_1_, bf16[2048,1024]{1,0:T(8,128)(2,1)S(1)} %scaled_down.1.refs_2_), custom_call_target="tpu_custom_call" | custom-call | flops 939524096 | bytes 4194304 | tf_op jit(solution)/shard_map/down_block/pallas_call | solution.py:28
  16.9 1.1 %aux.1 = (f32[8,128]{1,0:T(8,128)S(1)}, bf16[256,128]{1,0:T(8,128)(2,1)S(1)}, bf16[256,128]{1,0:T(8,128)(2,1)S(1)}, bf16[256,128]{1,0:T(8,128)(2,1)S(1)}, bf16[256,128]{1,0:T(8,128)(2,1)S(1)}) custom-call(s32[1,256]{1,0:T(1,128)S(1)} %bitcast.5, s32[32]{0:T(128)S(1)} %copy-done.6, bf16[256,2048]{1,0:T(8,128)(2,1)S(1)} %copy-done.3, ...), custom_call_target="tpu_custom_call" | custom-call | flops 268435456 | bytes 1048576 | tf_op jit(solution)/shard_map/aux/pallas_call | solution.py:28
  18.0 2.7 %collective-permute-done.4.refs_3_.refs_2_ = bf16[256,512]{1,0:T(8,128)(2,1)S(1)} collective-permute-done((bf16[256,512]{1,0:T(8,128)(2,1)S(1)}, bf16[256,512]{1,0:T(8,128)(2,1)S(1)}, u32[]{:S(2)}, u32[]{:S(2)}) %collective-permute-start.4) | collective-permute-done | bytes 262176 | tf_op jit(solution)/shard_map/ppermute | solution.py:389
  20.7 0.7 %collective-permute-done.3.refs_1_ = bf16[2,112,128]{2,1,0:T(8,128)(2,1)S(1)} collective-permute-done((bf16[2,112,128]{2,1,0:T(8,128)(2,1)S(1)}, bf16[2,112,128]{2,1,0:T(8,128)(2,1)S(1)}, u32[]{:S(2)}, u32[]{:S(2)}) %collective-permute-start.3) | collective-permute-done | bytes 57376 | tf_op jit(solution)/shard_map/ppermute | solution.py:389
  21.5 2.8 %collective-permute-start.8 = (bf16[608,128]{1,0:T(8,128)(2,1)S(1)}, bf16[608,128]{1,0:T(8,128)(2,1)S(1)}, u32[]{:S(2)}, u32[]{:S(2)}) collective-permute-start(bf16[608,128]{1,0:T(8,128)(2,1)S(1)} %pair_low_sums.1.refs_4_.refs_2_), channel_id=1, source_target_pairs={{0,2},{1,3},{2,0},{3,1},{4,6},{5,7},{6,4},{7,5},{8,10},{9,11},{10,... | collective-permute-start | bytes 466952 | tf_op jit(solution)/shard_map/ppermute | solution.py:389
  24.3 3.3 %collective-permute-done.1.refs_1_ = bf16[112,2048]{1,0:T(8,128)(2,1)S(1)} collective-permute-done((bf16[112,2048]{1,0:T(8,128)(2,1)}, bf16[112,2048]{1,0:T(8,128)(2,1)S(1)}, u32[]{:S(2)}, u32[]{:S(2)}) %collective-permute-start.1) | collective-permute-done | bytes 458784 | tf_op jit(solution)/shard_map/ppermute | solution.py:389
  27.6 1.1 %down_block.3.refs_5_.refs_2_ = bf16[2,112,128]{2,1,0:T(8,128)(2,1)S(1)} custom-call(bf16[112,2048]{1,0:T(8,128)(2,1)S(1)} %collective-permute-done.refs_0_, bf16[112,2048]{1,0:T(8,128)(2,1)S(1)} %collective-permute-done.1.refs_1_, bf16[2048,1024]{1,0:T(8,128)(2,1)S(1)} %scaled_down.1.refs_2_, f32[8,128]{1,0:T(8,128)S(1)} %get-tuple-element.34.refs_4_.refs_3_, ...), custom_call_target="tpu_custom_call" | custom-call | flops 939524096 | bytes 4194304 | tf_op jit(solution)/shard_map/down_block/pallas_call | solution.py:28
  28.8 3.7 %collective-permute-start.5 = (bf16[2,112,128]{2,1,0:T(8,128)(2,1)S(1)}, bf16[2,112,128]{2,1,0:T(8,128)(2,1)S(1)}, u32[]{:S(2)}, u32[]{:S(2)}) collective-permute-start(bf16[2,112,128]{2,1,0:T(8,128)(2,1)S(1)} %down_block.3.refs_5_.refs_2_), channel_id=1, source_target_pairs={{0,3},{1,2},{2,1},{3,0},{4,7},{5,6},{6,5},{7,4},{8,11},{9,10},{10,... | collective-permute-start | bytes 172040 | tf_op jit(solution)/shard_map/ppermute | solution.py:389
  32.5 0.7 %collective-permute-start.7 = (bf16[2,112,128]{2,1,0:T(8,128)(2,1)S(1)}, bf16[2,112,128]{2,1,0:T(8,128)(2,1)S(1)}, u32[]{:S(2)}, u32[]{:S(2)}) collective-permute-start(bf16[2,112,128]{2,1,0:T(8,128)(2,1)S(1)} %down_block.3.refs_5_.refs_2_), channel_id=1, source_target_pairs={{0,1},{1,0},{2,3},{3,2},{4,5},{5,4},{6,7},{7,6},{8,9},{9,8},{10,11... | collective-permute-start | bytes 172040 | tf_op jit(solution)/shard_map/ppermute | solution.py:389
  33.2 0.6 %up_block.2 = (bf16[112,512]{1,0:T(8,128)(2,1)S(1)}, bf16[112,512]{1,0:T(8,128)(2,1)S(1)}) custom-call(bf16[112,2048]{1,0:T(8,128)(2,1)S(1)} %copy-done.2, bf16[112,2048]{1,0:T(8,128)(2,1)S(1)} %collective-permute-done.2.refs_1_, bf16[608,128]{1,0:T(8,128)(2,1)S(1)} %pair_low_sums.1.refs_4_.refs_2_, ...), custom_call_target="tpu_custom_call" | custom-call | flops 234881024 | bytes 1048576 | tf_op jit(solution)/shard_map/up_block/pallas_call | solution.py:28
  33.9 2.3 %collective-permute-start.9 = (bf16[160,512]{1,0:T(8,128)(2,1)S(1)}, bf16[160,512]{1,0:T(8,128)(2,1)S(1)}, u32[]{:S(2)}, u32[]{:S(2)}) collective-permute-start(bf16[160,512]{1,0:T(8,128)(2,1)S(1)} %get-tuple-element.39.refs_7_), channel_id=1, source_target_pairs={{0,2},{1,3},{2,0},{3,1},{4,6},{5,7},{6,4},{7,5},{8,10},{9,11},{10,... | collective-permute-start | bytes 491528 | tf_op jit(solution)/shard_map/ppermute | solution.py:389
  36.2 2.0 %collective-permute-start.11 = (bf16[256,512]{1,0:T(8,128)(2,1)S(1)}, bf16[256,512]{1,0:T(8,128)(2,1)S(1)}, u32[]{:S(2)}, u32[]{:S(2)}) collective-permute-start(bf16[256,512]{1,0:T(8,128)(2,1)S(1)} %get-tuple-element.46), channel_id=1, source_target_pairs={{0,1},{1,0},{2,3},{3,2},{4,5},{5,4},{6,7},{7,6},{8,9},{9,8},{10,11... | collective-permute-start | bytes 786440 | tf_op jit(solution)/shard_map/ppermute | solution.py:389
  38.2 0.5 %fusion = (f32[256,64]{1,0:T(8,128)S(1)}, f32[256,64]{1,0:T(8,128)S(1)}, f32[256,64]{1,0:T(8,128)S(1)}) fusion(f32[64]{0:T(128)S(1)} %multiply_exponential_fusion, f32[256]{0:T(256)S(1)} %convert_element_type.10), kind=kLoop, calls=%fused_computation.4 | loop fusion | flops 32768 | bytes 197888 | tf_op jit(solution)/shard_map/neg | solution.py:459
  38.9 0.6 %up_block.3 = (bf16[112,512]{1,0:T(8,128)(2,1)S(1)}, bf16[112,512]{1,0:T(8,128)(2,1)S(1)}, f32[8,128]{1,0:T(8,128)S(1)}) custom-call(bf16[112,2048]{1,0:T(8,128)(2,1)S(1)} %collective-permute-done.refs_0_, bf16[112,2048]{1,0:T(8,128)(2,1)S(1)} %collective-permute-done.1.refs_1_, bf16[2,112,128]{2,1,0:T(8,128)(2,1)S(1)} %down_block.3.refs_5_.refs_2_, ...), custom_call_target="tpu_custom_call" | custom-call | flops 234881024 | bytes 1048576 | tf_op jit(solution)/shard_map/up_block/pallas_call | solution.py:28
  39.5 1.6 %collective-permute-start.12 = (bf16[112,512]{1,0:T(8,128)(2,1)S(1)}, bf16[112,512]{1,0:T(8,128)(2,1)S(1)}, u32[]{:S(2)}, u32[]{:S(2)}) collective-permute-start(bf16[112,512]{1,0:T(8,128)(2,1)S(1)} %get-tuple-element.44.refs_8_), channel_id=1, source_target_pairs={{0,8},{4,12},{8,0},{12,4},{1,9},{5,13},{9,1},{13,5},{2,10},{6,14},... | collective-permute-start | bytes 344072 | tf_op jit(solution)/shard_map/ppermute | solution.py:389
  41.5 3.6 %collective-permute-done.9.refs_3_ = bf16[160,512]{1,0:T(8,128)(2,1)S(1)} collective-permute-done((bf16[160,512]{1,0:T(8,128)(2,1)S(1)}, bf16[160,512]{1,0:T(8,128)(2,1)S(1)}, u32[]{:S(2)}, u32[]{:S(2)}) %collective-permute-start.9) | collective-permute-done | bytes 163872 | tf_op jit(solution)/shard_map/ppermute | solution.py:389
  45.5 1.6 %collective-permute-done.13.refs_6_ = bf16[112,512]{1,0:T(8,128)(2,1)S(1)} collective-permute-done((bf16[112,512]{1,0:T(8,128)(2,1)S(1)}, bf16[112,512]{1,0:T(8,128)(2,1)S(1)}, u32[]{:S(2)}, u32[]{:S(2)}) %collective-permute-start.13) | collective-permute-done | bytes 114720 | tf_op jit(solution)/shard_map/ppermute | solution.py:389
  47.3 1.0 %finish.1 = bf16[256,512]{1,0:T(8,128)(2,1)} custom-call(f32[256,512]{1,0:T(8,128)S(1)} %get-tuple-element.45.refs_0_, bf16[256,512]{1,0:T(8,128)(2,1)S(1)} %collective-permute-done.11.refs_1_, f32[256,128]{1,0:T(8,128)S(1)} %get-tuple-element.47.refs_2_, f32[256,128]{1,0:T(8,128)S(1)} %get-tuple-element.54.refs_3_, ...), custom_call_target="tpu_custom_call" | custom-call | flops 33554432 | tf_op jit(solution)/shard_map/finish/pallas_call | solution.py:28
  (36 shorter events, 1.6 us)
Async XLA Ops:
  3.6 11.8 %collective-permute-start.2 = (bf16[112,2048]{1,0:T(8,128)(2,1)}, bf16[112,2048]{1,0:T(8,128)(2,1)S(1)}, u32[]{:S(2)}, u32[]{:S(2)}) collective-permute-start(bf16[112,2048]{1,0:T(8,128)(2,1)} %get-tuple-element.33), channel_id=1, source_target_pairs={{0,4},{4,0},{8,12},{12,8},{1,5},{5,1},{9,13},{13,9},{2,6},{6,2},{1... | collective-permute-start | bytes 1376264 | tf_op jit(solution)/shard_map/ppermute | solution.py:389
  4.2 20.1 %collective-permute-start = (bf16[112,2048]{1,0:T(8,128)(2,1)}, bf16[112,2048]{1,0:T(8,128)(2,1)S(1)}, u32[]{:S(2)}, u32[]{:S(2)}) collective-permute-start(bf16[112,2048]{1,0:T(8,128)(2,1)} %get-tuple-element.28), channel_id=1, source_target_pairs={{0,8},{4,12},{8,0},{12,4},{1,9},{5,13},{9,1},{13,5},{2,10},{6,14},... | collective-permute-start | bytes 1376264 | tf_op jit(solution)/shard_map/ppermute | solution.py:389
  6.7 20.9 %collective-permute-start.1 = (bf16[112,2048]{1,0:T(8,128)(2,1)}, bf16[112,2048]{1,0:T(8,128)(2,1)S(1)}, u32[]{:S(2)}, u32[]{:S(2)}) collective-permute-start(bf16[112,2048]{1,0:T(8,128)(2,1)} %get-tuple-element.29), channel_id=1, source_target_pairs={{0,12},{4,8},{8,4},{12,0},{1,13},{5,9},{9,5},{13,1},{2,14},{6,10},... | collective-permute-start | bytes 1376264 | tf_op jit(solution)/shard_map/ppermute | solution.py:389
  6.8 6.6 %copy-start = (bf16[8,2048,128]{2,1,0:T(8,128)(2,1)S(1)}, bf16[8,2048,128]{2,1,0:T(8,128)(2,1)}, u32[]{:S(2)}) copy-start(bf16[8,2048,128]{2,1,0:T(8,128)(2,1)} %refs_1_.6) | copy-start | bytes 12582916
  6.8 6.6 %copy-start.4 = (bf16[2048]{0:T(1024)(128)(2,1)S(1)}, bf16[2048]{0:T(1024)(128)(2,1)}, u32[]{:S(2)}) copy-start(bf16[2048]{0:T(1024)(128)(2,1)} %param.9) | copy-start | bytes 12292
  11.5 9.2 %collective-permute-start.4 = (bf16[256,512]{1,0:T(8,128)(2,1)S(1)}, bf16[256,512]{1,0:T(8,128)(2,1)S(1)}, u32[]{:S(2)}, u32[]{:S(2)}) collective-permute-start(bf16[256,512]{1,0:T(8,128)(2,1)S(1)} %get-tuple-element.36), channel_id=1, source_target_pairs={{0,1},{1,0},{2,3},{3,2},{4,5},{5,4},{6,7},{7,6},{8,9},{9,8},{10,11... | collective-permute-start | bytes 786440 | tf_op jit(solution)/shard_map/ppermute | solution.py:389
  13.4 2.0 %copy-start.2 = (bf16[112,2048]{1,0:T(8,128)(2,1)S(1)}, bf16[112,2048]{1,0:T(8,128)(2,1)}, u32[]{:S(2)}) copy-start(bf16[112,2048]{1,0:T(8,128)(2,1)} %get-tuple-element.32.refs_0_) | copy-start | bytes 1376260
  15.3 1.5 %copy-start.7 = (s32[256]{0:T(256)S(1)}, s32[256]{0:T(256)}, u32[]{:S(2)}) copy-start(s32[256]{0:T(256)} %param.15) | copy-start | bytes 3076
  15.4 1.5 %copy-start.3 = (bf16[256,2048]{1,0:T(8,128)(2,1)S(1)}, bf16[256,2048]{1,0:T(8,128)(2,1)}, u32[]{:S(2)}) copy-start(bf16[256,2048]{1,0:T(8,128)(2,1)} %refs_2_.3) | copy-start | bytes 3145732
  15.4 1.5 %copy-start.5 = (s32[256]{0:T(256)S(1)}, s32[256]{0:T(256)}, u32[]{:S(2)}) copy-start(s32[256]{0:T(256)} %param.13) | copy-start | bytes 3076
  15.4 1.5 %copy-start.6 = (s32[32]{0:T(128)S(1)}, s32[32]{0:T(128)}, u32[]{:S(2)}) copy-start(s32[32]{0:T(128)} %refs_1_.7) | copy-start | bytes 388
  16.6 16.7 %copy-start.1 = (bf16[8,64,512]{2,1,0:T(8,128)(2,1)S(1)}, bf16[8,64,512]{2,1,0:T(8,128)(2,1)}, u32[]{:S(2)}) copy-start(bf16[8,64,512]{2,1,0:T(8,128)(2,1)} %refs_6_.1) | copy-start | bytes 1572868
  16.6 4.8 %collective-permute-start.3 = (bf16[2,112,128]{2,1,0:T(8,128)(2,1)S(1)}, bf16[2,112,128]{2,1,0:T(8,128)(2,1)S(1)}, u32[]{:S(2)}, u32[]{:S(2)}) collective-permute-start(bf16[2,112,128]{2,1,0:T(8,128)(2,1)S(1)} %down_block.2.refs_3_.refs_0_), channel_id=1, source_target_pairs={{0,1},{1,0},{2,3},{3,2},{4,5},{5,4},{6,7},{7,6},{8,9},{9,8},{10,11... | collective-permute-start | bytes 172040 | tf_op jit(solution)/shard_map/ppermute | solution.py:389
  21.5 11.8 %collective-permute-start.8 = (bf16[608,128]{1,0:T(8,128)(2,1)S(1)}, bf16[608,128]{1,0:T(8,128)(2,1)S(1)}, u32[]{:S(2)}, u32[]{:S(2)}) collective-permute-start(bf16[608,128]{1,0:T(8,128)(2,1)S(1)} %pair_low_sums.1.refs_4_.refs_2_), channel_id=1, source_target_pairs={{0,2},{1,3},{2,0},{3,1},{4,6},{5,7},{6,4},{7,5},{8,10},{9,11},{10,... | collective-permute-start | bytes 466952 | tf_op jit(solution)/shard_map/ppermute | solution.py:389
  28.8 10.0 %collective-permute-start.5 = (bf16[2,112,128]{2,1,0:T(8,128)(2,1)S(1)}, bf16[2,112,128]{2,1,0:T(8,128)(2,1)S(1)}, u32[]{:S(2)}, u32[]{:S(2)}) collective-permute-start(bf16[2,112,128]{2,1,0:T(8,128)(2,1)S(1)} %down_block.3.refs_5_.refs_2_), channel_id=1, source_target_pairs={{0,3},{1,2},{2,1},{3,0},{4,7},{5,6},{6,5},{7,4},{8,11},{9,10},{10,... | collective-permute-start | bytes 172040 | tf_op jit(solution)/shard_map/ppermute | solution.py:389
  32.5 6.3 %collective-permute-start.6 = (bf16[2,112,128]{2,1,0:T(8,128)(2,1)S(1)}, bf16[2,112,128]{2,1,0:T(8,128)(2,1)S(1)}, u32[]{:S(2)}, u32[]{:S(2)}) collective-permute-start(bf16[2,112,128]{2,1,0:T(8,128)(2,1)S(1)} %down_block.3.refs_5_.refs_2_), channel_id=1, source_target_pairs={{0,2},{1,3},{2,0},{3,1},{4,6},{5,7},{6,4},{7,5},{8,10},{9,11},{10,... | collective-permute-start | bytes 172040 | tf_op jit(solution)/shard_map/ppermute | solution.py:389
  32.5 6.3 %collective-permute-start.7 = (bf16[2,112,128]{2,1,0:T(8,128)(2,1)S(1)}, bf16[2,112,128]{2,1,0:T(8,128)(2,1)S(1)}, u32[]{:S(2)}, u32[]{:S(2)}) collective-permute-start(bf16[2,112,128]{2,1,0:T(8,128)(2,1)S(1)} %down_block.3.refs_5_.refs_2_), channel_id=1, source_target_pairs={{0,1},{1,0},{2,3},{3,2},{4,5},{5,4},{6,7},{7,6},{8,9},{9,8},{10,11... | collective-permute-start | bytes 172040 | tf_op jit(solution)/shard_map/ppermute | solution.py:389
  33.9 11.2 %collective-permute-start.9 = (bf16[160,512]{1,0:T(8,128)(2,1)S(1)}, bf16[160,512]{1,0:T(8,128)(2,1)S(1)}, u32[]{:S(2)}, u32[]{:S(2)}) collective-permute-start(bf16[160,512]{1,0:T(8,128)(2,1)S(1)} %get-tuple-element.39.refs_7_), channel_id=1, source_target_pairs={{0,2},{1,3},{2,0},{3,1},{4,6},{5,7},{6,4},{7,5},{8,10},{9,11},{10,... | collective-permute-start | bytes 491528 | tf_op jit(solution)/shard_map/ppermute | solution.py:389
  36.2 11.1 %collective-permute-start.11 = (bf16[256,512]{1,0:T(8,128)(2,1)S(1)}, bf16[256,512]{1,0:T(8,128)(2,1)S(1)}, u32[]{:S(2)}, u32[]{:S(2)}) collective-permute-start(bf16[256,512]{1,0:T(8,128)(2,1)S(1)} %get-tuple-element.46), channel_id=1, source_target_pairs={{0,1},{1,0},{2,3},{3,2},{4,5},{5,4},{6,7},{7,6},{8,9},{9,8},{10,11... | collective-permute-start | bytes 786440 | tf_op jit(solution)/shard_map/ppermute | solution.py:389
  38.8 2.8 %collective-permute-start.10 = (bf16[112,512]{1,0:T(8,128)(2,1)S(1)}, bf16[112,512]{1,0:T(8,128)(2,1)S(1)}, u32[]{:S(2)}, u32[]{:S(2)}) collective-permute-start(bf16[112,512]{1,0:T(8,128)(2,1)S(1)} %get-tuple-element.41), channel_id=1, source_target_pairs={{0,4},{4,0},{8,12},{12,8},{1,5},{5,1},{9,13},{13,9},{2,6},{6,2},{1... | collective-permute-start | bytes 344072 | tf_op jit(solution)/shard_map/ppermute | solution.py:389
  39.5 6.0 %collective-permute-start.12 = (bf16[112,512]{1,0:T(8,128)(2,1)S(1)}, bf16[112,512]{1,0:T(8,128)(2,1)S(1)}, u32[]{:S(2)}, u32[]{:S(2)}) collective-permute-start(bf16[112,512]{1,0:T(8,128)(2,1)S(1)} %get-tuple-element.44.refs_8_), channel_id=1, source_target_pairs={{0,8},{4,12},{8,0},{12,4},{1,9},{5,13},{9,1},{13,5},{2,10},{6,14},... | collective-permute-start | bytes 344072 | tf_op jit(solution)/shard_map/ppermute | solution.py:389
  41.0 6.1 %collective-permute-start.13 = (bf16[112,512]{1,0:T(8,128)(2,1)S(1)}, bf16[112,512]{1,0:T(8,128)(2,1)S(1)}, u32[]{:S(2)}, u32[]{:S(2)}) collective-permute-start(bf16[112,512]{1,0:T(8,128)(2,1)S(1)} %get-tuple-element.48), channel_id=1, source_target_pairs={{0,12},{4,8},{8,4},{12,0},{1,13},{5,9},{9,5},{13,1},{2,14},{6,10},... | collective-permute-start | bytes 344072 | tf_op jit(solution)/shard_map/ppermute | solution.py:389

commit v10 on v9

--- a/solution.py
+++ b/solution.py
@@ -498,7 +498,7 @@
         flops=2 * rows * rows * depth,
         moved=2 * rows * depth,
     )
-    half = rows * 3 // 128 * 16
+    half = rows // 64 * 16
     upper = cols // HEAD * half
     other = over("tensor", low, 1)
     pairs = call(

time: 48.5 us -> 49 us (1.010)
  waiting for transfers between devices: 12.3 us -> 12.9 us
    ppermute x14, waiting for transfers between devices: 12.3 us -> 12.9 us  [over(): return lax.ppermute(array, axis, [(i, i ^ k) for i in range(size)])]
  transfers between devices with their start and end apart: 14 -> 14, of which waited for: 7 -> 6; matrix products, arithmetic and copies ran while one was open for 1% -> 1% of each run, Pallas kernels for 24% -> 24%
where the time goes in v10:
time: 49 us; the launch traced here: 48.9 us
  starting transfers between devices  18.9 us (39%)
  Pallas kernels  16.2 us (33%)
  waiting for transfers between devices  12.9 us (26%)
  other arithmetic  0.67 us (1%)
    ppermute x14, starting transfers between devices, over(): return lax.ppermute(array, axis, [(i, i ^ k) for i in range(size)])  18.9 us
    pallas_call x12, Pallas kernels, call(): pl.pallas_call(body, out_shape=outs, in_specs=[pl.BlockSpec(memory_space=...  16.2 us
    ppermute x14, waiting for transfers between devices, over(): return lax.ppermute(array, axis, [(i, i ^ k) for i in range(size)])  12.9 us
  transfers between devices with their start and end apart: 14, of which 6 were waited for; matrix products, arithmetic and copies ran while one was open for 1% of the time, Pallas kernels for 24%

profile of v10, /device:TPU:0, one launch (start us, length us, event | category | flops | bytes accessed | tf_op | source)
XLA Modules:
  0.0 48.9 jit_solution(11723768040053354438)
XLA Ops:
  0.0 3.6 %dispatch.1 = (bf16[112,2048]{1,0:T(8,128)(2,1)}, bf16[112,2048]{1,0:T(8,128)(2,1)}, bf16[112,2048]{1,0:T(8,128)(2,1)}, bf16[112,2048]{1,0:T(8,128)(2,1)}, bf16[256,2048]{1,0:T(8,128)(2,1)}) custom-call(s32[1,256]{1,0:T(1,128)} %bitcast.4, s32[32]{0:T(128)} %refs_1_.7, bf16[256,2048]{1,0:T(8,128)(2,1)} %refs_2_.3, bf16[16,128]{1,0:T(8,128)(2,1)} %bitcast.2), custom_call_target="tpu_custom_call" | custom-call | flops 469762048 | bytes 4194304 | tf_op jit(solution)/shard_map/dispatch/pallas_call | solution.py:28
  4.2 2.6 %collective-permute-start = (bf16[112,2048]{1,0:T(8,128)(2,1)}, bf16[112,2048]{1,0:T(8,128)(2,1)S(1)}, u32[]{:S(2)}, u32[]{:S(2)}) collective-permute-start(bf16[112,2048]{1,0:T(8,128)(2,1)} %get-tuple-element.28), channel_id=1, source_target_pairs={{0,8},{4,12},{8,0},{12,4},{1,9},{5,13},{9,1},{13,5},{2,10},{6,14},... | collective-permute-start | bytes 1376264 | tf_op jit(solution)/shard_map/ppermute | solution.py:389
  6.8 4.7 %base.1 = (bf16[256,512]{1,0:T(8,128)(2,1)S(1)}, bf16[256,512]{1,0:T(8,128)(2,1)S(1)}, f32[256,512]{1,0:T(8,128)S(1)}, f32[256,512]{1,0:T(8,128)S(1)}) custom-call(bf16[256,2048]{1,0:T(8,128)(2,1)} %get-tuple-element.30.refs_0_, bf16[2048,2048]{1,0:T(8,128)(2,1)} %refs_1_.5), custom_call_target="tpu_custom_call" | custom-call | flops 2147483648 | bytes 8388608 | tf_op jit(solution)/shard_map/base/pallas_call | solution.py:28
  11.5 1.9 %collective-permute-start.4 = (bf16[256,512]{1,0:T(8,128)(2,1)S(1)}, bf16[256,512]{1,0:T(8,128)(2,1)S(1)}, u32[]{:S(2)}, u32[]{:S(2)}) collective-permute-start(bf16[256,512]{1,0:T(8,128)(2,1)S(1)} %get-tuple-element.36), channel_id=1, source_target_pairs={{0,1},{1,0},{2,3},{3,2},{4,5},{5,4},{6,7},{7,6},{8,9},{9,8},{10,11... | collective-permute-start | bytes 786440 | tf_op jit(solution)/shard_map/ppermute | solution.py:389
  13.4 2.0 %scaled_down.1.refs_2_ = bf16[2048,1024]{1,0:T(8,128)(2,1)S(1)} custom-call(bf16[16,128]{1,0:T(8,128)(2,1)S(1)} %bitcast.3, bf16[8,2048,128]{2,1,0:T(8,128)(2,1)S(1)} %copy-done, f32[256,512]{1,0:T(8,128)S(1)} %get-tuple-element.31.refs_2_.refs_1_), custom_call_target="tpu_custom_call" | custom-call | flops 8388608 | bytes 8388608 | tf_op jit(solution)/shard_map/scaled_down/pallas_call | solution.py:28
  15.4 1.1 %down_block.2.refs_3_.refs_0_ = bf16[2,112,128]{2,1,0:T(8,128)(2,1)S(1)} custom-call(bf16[112,2048]{1,0:T(8,128)(2,1)S(1)} %copy-done.2, bf16[112,2048]{1,0:T(8,128)(2,1)S(1)} %collective-permute-done.2.refs_1_, bf16[2048,1024]{1,0:T(8,128)(2,1)S(1)} %scaled_down.1.refs_2_), custom_call_target="tpu_custom_call" | custom-call | flops 939524096 | bytes 4194304 | tf_op jit(solution)/shard_map/down_block/pallas_call | solution.py:28
  16.9 1.1 %aux.1 = (f32[8,128]{1,0:T(8,128)S(1)}, bf16[256,128]{1,0:T(8,128)(2,1)S(1)}, bf16[256,128]{1,0:T(8,128)(2,1)S(1)}, bf16[256,128]{1,0:T(8,128)(2,1)S(1)}, bf16[256,128]{1,0:T(8,128)(2,1)S(1)}) custom-call(s32[1,256]{1,0:T(1,128)S(1)} %bitcast.5, s32[32]{0:T(128)S(1)} %copy-done.6, bf16[256,2048]{1,0:T(8,128)(2,1)S(1)} %copy-done.3, ...), custom_call_target="tpu_custom_call" | custom-call | flops 268435456 | bytes 1048576 | tf_op jit(solution)/shard_map/aux/pallas_call | solution.py:28
  17.9 2.7 %collective-permute-done.4.refs_3_.refs_2_ = bf16[256,512]{1,0:T(8,128)(2,1)S(1)} collective-permute-done((bf16[256,512]{1,0:T(8,128)(2,1)S(1)}, bf16[256,512]{1,0:T(8,128)(2,1)S(1)}, u32[]{:S(2)}, u32[]{:S(2)}) %collective-permute-start.4) | collective-permute-done | bytes 262176 | tf_op jit(solution)/shard_map/ppermute | solution.py:389
  20.7 0.7 %collective-permute-done.3.refs_1_ = bf16[2,112,128]{2,1,0:T(8,128)(2,1)S(1)} collective-permute-done((bf16[2,112,128]{2,1,0:T(8,128)(2,1)S(1)}, bf16[2,112,128]{2,1,0:T(8,128)(2,1)S(1)}, u32[]{:S(2)}, u32[]{:S(2)}) %collective-permute-start.3) | collective-permute-done | bytes 57376 | tf_op jit(solution)/shard_map/ppermute | solution.py:389
  21.4 2.8 %collective-permute-start.8 = (bf16[480,128]{1,0:T(8,128)(2,1)S(1)}, bf16[480,128]{1,0:T(8,128)(2,1)S(1)}, u32[]{:S(2)}, u32[]{:S(2)}) collective-permute-start(bf16[480,128]{1,0:T(8,128)(2,1)S(1)} %pair_low_sums.1.refs_4_.refs_2_), channel_id=1, source_target_pairs={{0,2},{1,3},{2,0},{3,1},{4,6},{5,7},{6,4},{7,5},{8,10},{9,11},{10,... | collective-permute-start | bytes 368648 | tf_op jit(solution)/shard_map/ppermute | solution.py:389
  24.3 3.3 %collective-permute-done.1.refs_1_ = bf16[112,2048]{1,0:T(8,128)(2,1)S(1)} collective-permute-done((bf16[112,2048]{1,0:T(8,128)(2,1)}, bf16[112,2048]{1,0:T(8,128)(2,1)S(1)}, u32[]{:S(2)}, u32[]{:S(2)}) %collective-permute-start.1) | collective-permute-done | bytes 458784 | tf_op jit(solution)/shard_map/ppermute | solution.py:389
  27.6 1.1 %down_block.3.refs_5_.refs_2_ = bf16[2,112,128]{2,1,0:T(8,128)(2,1)S(1)} custom-call(bf16[112,2048]{1,0:T(8,128)(2,1)S(1)} %collective-permute-done.refs_0_, bf16[112,2048]{1,0:T(8,128)(2,1)S(1)} %collective-permute-done.1.refs_1_, bf16[2048,1024]{1,0:T(8,128)(2,1)S(1)} %scaled_down.1.refs_2_, f32[8,128]{1,0:T(8,128)S(1)} %get-tuple-element.34.refs_4_.refs_3_, ...), custom_call_target="tpu_custom_call" | custom-call | flops 939524096 | bytes 4194304 | tf_op jit(solution)/shard_map/down_block/pallas_call | solution.py:28
  28.8 3.7 %collective-permute-start.5 = (bf16[2,112,128]{2,1,0:T(8,128)(2,1)S(1)}, bf16[2,112,128]{2,1,0:T(8,128)(2,1)S(1)}, u32[]{:S(2)}, u32[]{:S(2)}) collective-permute-start(bf16[2,112,128]{2,1,0:T(8,128)(2,1)S(1)} %down_block.3.refs_5_.refs_2_), channel_id=1, source_target_pairs={{0,3},{1,2},{2,1},{3,0},{4,7},{5,6},{6,5},{7,4},{8,11},{9,10},{10,... | collective-permute-start | bytes 172040 | tf_op jit(solution)/shard_map/ppermute | solution.py:389
  32.5 0.7 %collective-permute-start.7 = (bf16[2,112,128]{2,1,0:T(8,128)(2,1)S(1)}, bf16[2,112,128]{2,1,0:T(8,128)(2,1)S(1)}, u32[]{:S(2)}, u32[]{:S(2)}) collective-permute-start(bf16[2,112,128]{2,1,0:T(8,128)(2,1)S(1)} %down_block.3.refs_5_.refs_2_), channel_id=1, source_target_pairs={{0,1},{1,0},{2,3},{3,2},{4,5},{5,4},{6,7},{7,6},{8,9},{9,8},{10,11... | collective-permute-start | bytes 172040 | tf_op jit(solution)/shard_map/ppermute | solution.py:389
  33.2 0.6 %up_block.2 = (bf16[112,512]{1,0:T(8,128)(2,1)S(1)}, bf16[112,512]{1,0:T(8,128)(2,1)S(1)}) custom-call(bf16[112,2048]{1,0:T(8,128)(2,1)S(1)} %copy-done.2, bf16[112,2048]{1,0:T(8,128)(2,1)S(1)} %collective-permute-done.2.refs_1_, bf16[480,128]{1,0:T(8,128)(2,1)S(1)} %pair_low_sums.1.refs_4_.refs_2_, ...), custom_call_target="tpu_custom_call" | custom-call | flops 234881024 | bytes 1048576 | tf_op jit(solution)/shard_map/up_block/pallas_call | solution.py:28
  33.9 2.3 %collective-permute-start.9 = (bf16[192,512]{1,0:T(8,128)(2,1)S(1)}, bf16[192,512]{1,0:T(8,128)(2,1)S(1)}, u32[]{:S(2)}, u32[]{:S(2)}) collective-permute-start(bf16[192,512]{1,0:T(8,128)(2,1)S(1)} %get-tuple-element.39.refs_7_), channel_id=1, source_target_pairs={{0,2},{1,3},{2,0},{3,1},{4,6},{5,7},{6,4},{7,5},{8,10},{9,11},{10,... | collective-permute-start | bytes 589832 | tf_op jit(solution)/shard_map/ppermute | solution.py:389
  36.2 2.0 %collective-permute-start.11 = (bf16[256,512]{1,0:T(8,128)(2,1)S(1)}, bf16[256,512]{1,0:T(8,128)(2,1)S(1)}, u32[]{:S(2)}, u32[]{:S(2)}) collective-permute-start(bf16[256,512]{1,0:T(8,128)(2,1)S(1)} %get-tuple-element.46), channel_id=1, source_target_pairs={{0,1},{1,0},{2,3},{3,2},{4,5},{5,4},{6,7},{7,6},{8,9},{9,8},{10,11... | collective-permute-start | bytes 786440 | tf_op jit(solution)/shard_map/ppermute | solution.py:389
  38.2 0.5 %fusion = (f32[256,64]{1,0:T(8,128)S(1)}, f32[256,64]{1,0:T(8,128)S(1)}, f32[256,64]{1,0:T(8,128)S(1)}) fusion(f32[64]{0:T(128)S(1)} %multiply_exponential_fusion, f32[256]{0:T(256)S(1)} %convert_element_type.10), kind=kLoop, calls=%fused_computation.4 | loop fusion | flops 32768 | bytes 197888 | tf_op jit(solution)/shard_map/neg | solution.py:459
  38.9 0.6 %up_block.3 = (bf16[112,512]{1,0:T(8,128)(2,1)S(1)}, bf16[112,512]{1,0:T(8,128)(2,1)S(1)}, f32[8,128]{1,0:T(8,128)S(1)}) custom-call(bf16[112,2048]{1,0:T(8,128)(2,1)S(1)} %collective-permute-done.refs_0_, bf16[112,2048]{1,0:T(8,128)(2,1)S(1)} %collective-permute-done.1.refs_1_, bf16[2,112,128]{2,1,0:T(8,128)(2,1)S(1)} %down_block.3.refs_5_.refs_2_, ...), custom_call_target="tpu_custom_call" | custom-call | flops 234881024 | bytes 1048576 | tf_op jit(solution)/shard_map/up_block/pallas_call | solution.py:28
  39.5 1.6 %collective-permute-start.12 = (bf16[112,512]{1,0:T(8,128)(2,1)S(1)}, bf16[112,512]{1,0:T(8,128)(2,1)S(1)}, u32[]{:S(2)}, u32[]{:S(2)}) collective-permute-start(bf16[112,512]{1,0:T(8,128)(2,1)S(1)} %get-tuple-element.44.refs_8_), channel_id=1, source_target_pairs={{0,8},{4,12},{8,0},{12,4},{1,9},{5,13},{9,1},{13,5},{2,10},{6,14},... | collective-permute-start | bytes 344072 | tf_op jit(solution)/shard_map/ppermute | solution.py:389
  41.5 4.8 %collective-permute-done.9.refs_3_ = bf16[192,512]{1,0:T(8,128)(2,1)S(1)} collective-permute-done((bf16[192,512]{1,0:T(8,128)(2,1)S(1)}, bf16[192,512]{1,0:T(8,128)(2,1)S(1)}, u32[]{:S(2)}, u32[]{:S(2)}) %collective-permute-start.9) | collective-permute-done | bytes 196640 | tf_op jit(solution)/shard_map/ppermute | solution.py:389
  46.6 0.5 %collective-permute-done.13.refs_6_ = bf16[112,512]{1,0:T(8,128)(2,1)S(1)} collective-permute-done((bf16[112,512]{1,0:T(8,128)(2,1)S(1)}, bf16[112,512]{1,0:T(8,128)(2,1)S(1)}, u32[]{:S(2)}, u32[]{:S(2)}) %collective-permute-start.13) | collective-permute-done | bytes 114720 | tf_op jit(solution)/shard_map/ppermute | solution.py:389
  47.1 0.7 %collective-permute-done.11.refs_1_ = bf16[256,512]{1,0:T(8,128)(2,1)S(1)} collective-permute-done((bf16[256,512]{1,0:T(8,128)(2,1)S(1)}, bf16[256,512]{1,0:T(8,128)(2,1)S(1)}, u32[]{:S(2)}, u32[]{:S(2)}) %collective-permute-start.11) | collective-permute-done | bytes 262176 | tf_op jit(solution)/shard_map/ppermute | solution.py:389
  47.9 1.0 %finish.1 = bf16[256,512]{1,0:T(8,128)(2,1)} custom-call(f32[256,512]{1,0:T(8,128)S(1)} %get-tuple-element.45.refs_0_, bf16[256,512]{1,0:T(8,128)(2,1)S(1)} %collective-permute-done.11.refs_1_, f32[256,128]{1,0:T(8,128)S(1)} %get-tuple-element.47.refs_2_, f32[256,128]{1,0:T(8,128)S(1)} %get-tuple-element.54.refs_3_, ...), custom_call_target="tpu_custom_call" | custom-call | flops 33554432 | tf_op jit(solution)/shard_map/finish/pallas_call | solution.py:28
  (36 shorter events, 1.8 us)
Async XLA Ops:
  3.6 11.8 %collective-permute-start.2 = (bf16[112,2048]{1,0:T(8,128)(2,1)}, bf16[112,2048]{1,0:T(8,128)(2,1)S(1)}, u32[]{:S(2)}, u32[]{:S(2)}) collective-permute-start(bf16[112,2048]{1,0:T(8,128)(2,1)} %get-tuple-element.33), channel_id=1, source_target_pairs={{0,4},{4,0},{8,12},{12,8},{1,5},{5,1},{9,13},{13,9},{2,6},{6,2},{1... | collective-permute-start | bytes 1376264 | tf_op jit(solution)/shard_map/ppermute | solution.py:389
  4.2 20.1 %collective-permute-start = (bf16[112,2048]{1,0:T(8,128)(2,1)}, bf16[112,2048]{1,0:T(8,128)(2,1)S(1)}, u32[]{:S(2)}, u32[]{:S(2)}) collective-permute-start(bf16[112,2048]{1,0:T(8,128)(2,1)} %get-tuple-element.28), channel_id=1, source_target_pairs={{0,8},{4,12},{8,0},{12,4},{1,9},{5,13},{9,1},{13,5},{2,10},{6,14},... | collective-permute-start | bytes 1376264 | tf_op jit(solution)/shard_map/ppermute | solution.py:389
  6.7 20.9 %collective-permute-start.1 = (bf16[112,2048]{1,0:T(8,128)(2,1)}, bf16[112,2048]{1,0:T(8,128)(2,1)S(1)}, u32[]{:S(2)}, u32[]{:S(2)}) collective-permute-start(bf16[112,2048]{1,0:T(8,128)(2,1)} %get-tuple-element.29), channel_id=1, source_target_pairs={{0,12},{4,8},{8,4},{12,0},{1,13},{5,9},{9,5},{13,1},{2,14},{6,10},... | collective-permute-start | bytes 1376264 | tf_op jit(solution)/shard_map/ppermute | solution.py:389
  6.8 6.6 %copy-start = (bf16[8,2048,128]{2,1,0:T(8,128)(2,1)S(1)}, bf16[8,2048,128]{2,1,0:T(8,128)(2,1)}, u32[]{:S(2)}) copy-start(bf16[8,2048,128]{2,1,0:T(8,128)(2,1)} %refs_1_.6) | copy-start | bytes 12582916
  6.8 6.6 %copy-start.4 = (bf16[2048]{0:T(1024)(128)(2,1)S(1)}, bf16[2048]{0:T(1024)(128)(2,1)}, u32[]{:S(2)}) copy-start(bf16[2048]{0:T(1024)(128)(2,1)} %param.9) | copy-start | bytes 12292
  11.5 9.2 %collective-permute-start.4 = (bf16[256,512]{1,0:T(8,128)(2,1)S(1)}, bf16[256,512]{1,0:T(8,128)(2,1)S(1)}, u32[]{:S(2)}, u32[]{:S(2)}) collective-permute-start(bf16[256,512]{1,0:T(8,128)(2,1)S(1)} %get-tuple-element.36), channel_id=1, source_target_pairs={{0,1},{1,0},{2,3},{3,2},{4,5},{5,4},{6,7},{7,6},{8,9},{9,8},{10,11... | collective-permute-start | bytes 786440 | tf_op jit(solution)/shard_map/ppermute | solution.py:389
  13.4 2.0 %copy-start.2 = (bf16[112,2048]{1,0:T(8,128)(2,1)S(1)}, bf16[112,2048]{1,0:T(8,128)(2,1)}, u32[]{:S(2)}) copy-start(bf16[112,2048]{1,0:T(8,128)(2,1)} %get-tuple-element.32.refs_0_) | copy-start | bytes 1376260
  15.3 1.5 %copy-start.3 = (bf16[256,2048]{1,0:T(8,128)(2,1)S(1)}, bf16[256,2048]{1,0:T(8,128)(2,1)}, u32[]{:S(2)}) copy-start(bf16[256,2048]{1,0:T(8,128)(2,1)} %refs_2_.3) | copy-start | bytes 3145732
  15.4 1.5 %copy-start.5 = (s32[256]{0:T(256)S(1)}, s32[256]{0:T(256)}, u32[]{:S(2)}) copy-start(s32[256]{0:T(256)} %param.13) | copy-start | bytes 3076
  15.4 1.5 %copy-start.6 = (s32[32]{0:T(128)S(1)}, s32[32]{0:T(128)}, u32[]{:S(2)}) copy-start(s32[32]{0:T(128)} %refs_1_.7) | copy-start | bytes 388
  15.4 8.9 %copy-start.7 = (s32[256]{0:T(256)S(1)}, s32[256]{0:T(256)}, u32[]{:S(2)}) copy-start(s32[256]{0:T(256)} %param.15) | copy-start | bytes 3076
  16.6 16.7 %copy-start.1 = (bf16[8,64,512]{2,1,0:T(8,128)(2,1)S(1)}, bf16[8,64,512]{2,1,0:T(8,128)(2,1)}, u32[]{:S(2)}) copy-start(bf16[8,64,512]{2,1,0:T(8,128)(2,1)} %refs_6_.1) | copy-start | bytes 1572868
  16.6 4.8 %collective-permute-start.3 = (bf16[2,112,128]{2,1,0:T(8,128)(2,1)S(1)}, bf16[2,112,128]{2,1,0:T(8,128)(2,1)S(1)}, u32[]{:S(2)}, u32[]{:S(2)}) collective-permute-start(bf16[2,112,128]{2,1,0:T(8,128)(2,1)S(1)} %down_block.2.refs_3_.refs_0_), channel_id=1, source_target_pairs={{0,1},{1,0},{2,3},{3,2},{4,5},{5,4},{6,7},{7,6},{8,9},{9,8},{10,11... | collective-permute-start | bytes 172040 | tf_op jit(solution)/shard_map/ppermute | solution.py:389
  21.4 11.8 %collective-permute-start.8 = (bf16[480,128]{1,0:T(8,128)(2,1)S(1)}, bf16[480,128]{1,0:T(8,128)(2,1)S(1)}, u32[]{:S(2)}, u32[]{:S(2)}) collective-permute-start(bf16[480,128]{1,0:T(8,128)(2,1)S(1)} %pair_low_sums.1.refs_4_.refs_2_), channel_id=1, source_target_pairs={{0,2},{1,3},{2,0},{3,1},{4,6},{5,7},{6,4},{7,5},{8,10},{9,11},{10,... | collective-permute-start | bytes 368648 | tf_op jit(solution)/shard_map/ppermute | solution.py:389
  28.8 10.0 %collective-permute-start.5 = (bf16[2,112,128]{2,1,0:T(8,128)(2,1)S(1)}, bf16[2,112,128]{2,1,0:T(8,128)(2,1)S(1)}, u32[]{:S(2)}, u32[]{:S(2)}) collective-permute-start(bf16[2,112,128]{2,1,0:T(8,128)(2,1)S(1)} %down_block.3.refs_5_.refs_2_), channel_id=1, source_target_pairs={{0,3},{1,2},{2,1},{3,0},{4,7},{5,6},{6,5},{7,4},{8,11},{9,10},{10,... | collective-permute-start | bytes 172040 | tf_op jit(solution)/shard_map/ppermute | solution.py:389
  32.5 6.3 %collective-permute-start.6 = (bf16[2,112,128]{2,1,0:T(8,128)(2,1)S(1)}, bf16[2,112,128]{2,1,0:T(8,128)(2,1)S(1)}, u32[]{:S(2)}, u32[]{:S(2)}) collective-permute-start(bf16[2,112,128]{2,1,0:T(8,128)(2,1)S(1)} %down_block.3.refs_5_.refs_2_), channel_id=1, source_target_pairs={{0,2},{1,3},{2,0},{3,1},{4,6},{5,7},{6,4},{7,5},{8,10},{9,11},{10,... | collective-permute-start | bytes 172040 | tf_op jit(solution)/shard_map/ppermute | solution.py:389
  32.5 6.4 %collective-permute-start.7 = (bf16[2,112,128]{2,1,0:T(8,128)(2,1)S(1)}, bf16[2,112,128]{2,1,0:T(8,128)(2,1)S(1)}, u32[]{:S(2)}, u32[]{:S(2)}) collective-permute-start(bf16[2,112,128]{2,1,0:T(8,128)(2,1)S(1)} %down_block.3.refs_5_.refs_2_), channel_id=1, source_target_pairs={{0,1},{1,0},{2,3},{3,2},{4,5},{5,4},{6,7},{7,6},{8,9},{9,8},{10,11... | collective-permute-start | bytes 172040 | tf_op jit(solution)/shard_map/ppermute | solution.py:389
  33.9 12.5 %collective-permute-start.9 = (bf16[192,512]{1,0:T(8,128)(2,1)S(1)}, bf16[192,512]{1,0:T(8,128)(2,1)S(1)}, u32[]{:S(2)}, u32[]{:S(2)}) collective-permute-start(bf16[192,512]{1,0:T(8,128)(2,1)S(1)} %get-tuple-element.39.refs_7_), channel_id=1, source_target_pairs={{0,2},{1,3},{2,0},{3,1},{4,6},{5,7},{6,4},{7,5},{8,10},{9,11},{10,... | collective-permute-start | bytes 589832 | tf_op jit(solution)/shard_map/ppermute | solution.py:389
  36.2 11.7 %collective-permute-start.11 = (bf16[256,512]{1,0:T(8,128)(2,1)S(1)}, bf16[256,512]{1,0:T(8,128)(2,1)S(1)}, u32[]{:S(2)}, u32[]{:S(2)}) collective-permute-start(bf16[256,512]{1,0:T(8,128)(2,1)S(1)} %get-tuple-element.46), channel_id=1, source_target_pairs={{0,1},{1,0},{2,3},{3,2},{4,5},{5,4},{6,7},{7,6},{8,9},{9,8},{10,11... | collective-permute-start | bytes 786440 | tf_op jit(solution)/shard_map/ppermute | solution.py:389
  38.8 2.8 %collective-permute-start.10 = (bf16[112,512]{1,0:T(8,128)(2,1)S(1)}, bf16[112,512]{1,0:T(8,128)(2,1)S(1)}, u32[]{:S(2)}, u32[]{:S(2)}) collective-permute-start(bf16[112,512]{1,0:T(8,128)(2,1)S(1)} %get-tuple-element.41), channel_id=1, source_target_pairs={{0,4},{4,0},{8,12},{12,8},{1,5},{5,1},{9,13},{13,9},{2,6},{6,2},{1... | collective-permute-start | bytes 344072 | tf_op jit(solution)/shard_map/ppermute | solution.py:389
  39.5 7.1 %collective-permute-start.12 = (bf16[112,512]{1,0:T(8,128)(2,1)S(1)}, bf16[112,512]{1,0:T(8,128)(2,1)S(1)}, u32[]{:S(2)}, u32[]{:S(2)}) collective-permute-start(bf16[112,512]{1,0:T(8,128)(2,1)S(1)} %get-tuple-element.44.refs_8_), channel_id=1, source_target_pairs={{0,8},{4,12},{8,0},{12,4},{1,9},{5,13},{9,1},{13,5},{2,10},{6,14},... | collective-permute-start | bytes 344072 | tf_op jit(solution)/shard_map/ppermute | solution.py:389
  41.1 6.1 %collective-permute-start.13 = (bf16[112,512]{1,0:T(8,128)(2,1)S(1)}, bf16[112,512]{1,0:T(8,128)(2,1)S(1)}, u32[]{:S(2)}, u32[]{:S(2)}) collective-permute-start(bf16[112,512]{1,0:T(8,128)(2,1)S(1)} %get-tuple-element.48), channel_id=1, source_target_pairs={{0,12},{4,8},{8,4},{12,0},{1,13},{5,9},{9,5},{13,1},{2,14},{6,10},... | collective-permute-start | bytes 344072 | tf_op jit(solution)/shard_map/ppermute | solution.py:389

commit v11 on v8

--- a/solution.py
+++ b/solution.py
@@ -74,9 +74,12 @@
     loads = [
         pltpu.make_async_copy(req_hbm, req_ref, sems.at[0]),
         pltpu.make_async_copy(table_hbm, table_ref, sems.at[1]),
-        pltpu.make_async_copy(tok_hbm, tok_ref, sems.at[2]),
-        pltpu.make_async_copy(gain_hbm, gain_ref, sems.at[3]),
+        pltpu.make_async_copy(gain_hbm, gain_ref, sems.at[2]),
     ]
+    part = rows // 4
+    for i in range(4):
+        span = pl.ds(i * part, part)
+        loads.append(pltpu.make_async_copy(tok_hbm.at[span], tok_ref.at[span], sems.at[3 + i]))
     for copy in loads:
         copy.start()
     loads[0].wait()
@@ -90,8 +93,8 @@
             lax.dot_general(slots, pick, (((1,), (1,)), ((), ())), preferred_element_type=F32)
         )
         picks.append(pick[:height])
-    loads[3].wait()
-    loads[2].wait()
+    for copy in loads[2:]:
+        copy.wait()
     stores = []
     for j, k in enumerate(order):
         if k == 1:
@@ -406,7 +409,7 @@
             pltpu.VMEM(gain.shape, BF16),
             pltpu.VMEM((n_wide, height, depth), BF16),
             pltpu.VMEM((rows, depth), BF16),
-            pltpu.SemaphoreType.DMA((4,)),
+            pltpu.SemaphoreType.DMA((7,)),
             pltpu.SemaphoreType.DMA((n_wide + 1,)),
         ],
         flops=2 * n_wide * height * rows * depth,
@@ -419,7 +422,7 @@
     twos = list(range(2, n_tensor, 2))
     far = [k ^ 1 for k in twos]
     offsets = far + [1] + twos + [0]
-    chunk = math.gcd(depth, 512)
+    chunk = math.gcd(depth, 256)
     steps = depth // chunk
     sums = call(
         functools.partial(base_kernel, offsets, cols),

time: 48.3 us -> 48.3 us (level)
  no operation moved by 1% of the time
where the time goes in v11:
time: 48.3 us; the launch traced here: 48.1 us
  starting transfers between devices  19 us (39%)
  Pallas kernels  16.1 us (33%)
  waiting for transfers between devices  12.1 us (25%)
  other arithmetic  0.68 us (1%)
    ppermute x14, starting transfers between devices, over(): return lax.ppermute(array, axis, [(i, i ^ k) for i in range(size)])  19 us
    pallas_call x12, Pallas kernels, call(): pl.pallas_call(body, out_shape=outs, in_specs=[pl.BlockSpec(memory_space=...  16.1 us
    ppermute x14, waiting for transfers between devices, over(): return lax.ppermute(array, axis, [(i, i ^ k) for i in range(size)])  12.1 us
  transfers between devices with their start and end apart: 14, of which 6 were waited for; matrix products, arithmetic and copies ran while one was open for 1% of the time, Pallas kernels for 24%

profile of v11, /device:TPU:0, one launch (start us, length us, event | category | flops | bytes accessed | tf_op | source)
XLA Modules:
  0.0 48.1 jit_solution(7471237568629759710)
XLA Ops:
  0.0 3.6 %dispatch.1 = (bf16[112,2048]{1,0:T(8,128)(2,1)}, bf16[112,2048]{1,0:T(8,128)(2,1)}, bf16[112,2048]{1,0:T(8,128)(2,1)}, bf16[112,2048]{1,0:T(8,128)(2,1)}, bf16[256,2048]{1,0:T(8,128)(2,1)}) custom-call(s32[1,256]{1,0:T(1,128)} %bitcast.4, s32[32]{0:T(128)} %refs_1_.7, bf16[256,2048]{1,0:T(8,128)(2,1)} %refs_2_.3, bf16[16,128]{1,0:T(8,128)(2,1)} %bitcast.2), custom_call_target="tpu_custom_call" | custom-call | flops 469762048 | bytes 4194304 | tf_op jit(solution)/shard_map/dispatch/pallas_call | solution.py:28
  3.6 0.5 %collective-permute-start.2 = (bf16[112,2048]{1,0:T(8,128)(2,1)}, bf16[112,2048]{1,0:T(8,128)(2,1)S(1)}, u32[]{:S(2)}, u32[]{:S(2)}) collective-permute-start(bf16[112,2048]{1,0:T(8,128)(2,1)} %get-tuple-element.33), channel_id=1, source_target_pairs={{0,4},{4,0},{8,12},{12,8},{1,5},{5,1},{9,13},{13,9},{2,6},{6,2},{1... | collective-permute-start | bytes 1376264 | tf_op jit(solution)/shard_map/ppermute | solution.py:394
  4.2 2.6 %collective-permute-start = (bf16[112,2048]{1,0:T(8,128)(2,1)}, bf16[112,2048]{1,0:T(8,128)(2,1)S(1)}, u32[]{:S(2)}, u32[]{:S(2)}) collective-permute-start(bf16[112,2048]{1,0:T(8,128)(2,1)} %get-tuple-element.28), channel_id=1, source_target_pairs={{0,8},{4,12},{8,0},{12,4},{1,9},{5,13},{9,1},{13,5},{2,10},{6,14},... | collective-permute-start | bytes 1376264 | tf_op jit(solution)/shard_map/ppermute | solution.py:394
  6.8 4.6 %base.1 = (bf16[256,512]{1,0:T(8,128)(2,1)S(1)}, bf16[256,512]{1,0:T(8,128)(2,1)S(1)}, f32[256,512]{1,0:T(8,128)S(1)}, f32[256,512]{1,0:T(8,128)S(1)}) custom-call(bf16[256,2048]{1,0:T(8,128)(2,1)} %get-tuple-element.30.refs_0_, bf16[2048,2048]{1,0:T(8,128)(2,1)} %refs_1_.5), custom_call_target="tpu_custom_call" | custom-call | flops 2147483648 | bytes 8388608 | tf_op jit(solution)/shard_map/base/pallas_call | solution.py:28
  11.4 1.9 %collective-permute-start.4 = (bf16[256,512]{1,0:T(8,128)(2,1)S(1)}, bf16[256,512]{1,0:T(8,128)(2,1)S(1)}, u32[]{:S(2)}, u32[]{:S(2)}) collective-permute-start(bf16[256,512]{1,0:T(8,128)(2,1)S(1)} %get-tuple-element.36), channel_id=1, source_target_pairs={{0,1},{1,0},{2,3},{3,2},{4,5},{5,4},{6,7},{7,6},{8,9},{9,8},{10,11... | collective-permute-start | bytes 786440 | tf_op jit(solution)/shard_map/ppermute | solution.py:394
  13.3 2.0 %scaled_down.1.refs_2_ = bf16[2048,1024]{1,0:T(8,128)(2,1)S(1)} custom-call(bf16[16,128]{1,0:T(8,128)(2,1)S(1)} %bitcast.3, bf16[8,2048,128]{2,1,0:T(8,128)(2,1)S(1)} %copy-done, f32[256,512]{1,0:T(8,128)S(1)} %get-tuple-element.31.refs_2_.refs_1_), custom_call_target="tpu_custom_call" | custom-call | flops 8388608 | bytes 8388608 | tf_op jit(solution)/shard_map/scaled_down/pallas_call | solution.py:28
  15.3 1.1 %down_block.2.refs_3_.refs_0_ = bf16[2,112,128]{2,1,0:T(8,128)(2,1)S(1)} custom-call(bf16[112,2048]{1,0:T(8,128)(2,1)S(1)} %copy-done.2, bf16[112,2048]{1,0:T(8,128)(2,1)S(1)} %collective-permute-done.2.refs_1_, bf16[2048,1024]{1,0:T(8,128)(2,1)S(1)} %scaled_down.1.refs_2_), custom_call_target="tpu_custom_call" | custom-call | flops 939524096 | bytes 4194304 | tf_op jit(solution)/shard_map/down_block/pallas_call | solution.py:28
  16.9 1.1 %aux.1 = (f32[8,128]{1,0:T(8,128)S(1)}, bf16[256,128]{1,0:T(8,128)(2,1)S(1)}, bf16[256,128]{1,0:T(8,128)(2,1)S(1)}, bf16[256,128]{1,0:T(8,128)(2,1)S(1)}, bf16[256,128]{1,0:T(8,128)(2,1)S(1)}) custom-call(s32[1,256]{1,0:T(1,128)S(1)} %bitcast.5, s32[32]{0:T(128)S(1)} %copy-done.6, bf16[256,2048]{1,0:T(8,128)(2,1)S(1)} %copy-done.3, ...), custom_call_target="tpu_custom_call" | custom-call | flops 268435456 | bytes 1048576 | tf_op jit(solution)/shard_map/aux/pallas_call | solution.py:28
  17.9 2.6 %collective-permute-done.4.refs_3_.refs_2_ = bf16[256,512]{1,0:T(8,128)(2,1)S(1)} collective-permute-done((bf16[256,512]{1,0:T(8,128)(2,1)S(1)}, bf16[256,512]{1,0:T(8,128)(2,1)S(1)}, u32[]{:S(2)}, u32[]{:S(2)}) %collective-permute-start.4) | collective-permute-done | bytes 262176 | tf_op jit(solution)/shard_map/ppermute | solution.py:394
  20.6 0.7 %collective-permute-done.3.refs_1_ = bf16[2,112,128]{2,1,0:T(8,128)(2,1)S(1)} collective-permute-done((bf16[2,112,128]{2,1,0:T(8,128)(2,1)S(1)}, bf16[2,112,128]{2,1,0:T(8,128)(2,1)S(1)}, u32[]{:S(2)}, u32[]{:S(2)}) %collective-permute-start.3) | collective-permute-done | bytes 57376 | tf_op jit(solution)/shard_map/ppermute | solution.py:394
  21.3 2.8 %collective-permute-start.8 = (bf16[736,128]{1,0:T(8,128)(2,1)S(1)}, bf16[736,128]{1,0:T(8,128)(2,1)S(1)}, u32[]{:S(2)}, u32[]{:S(2)}) collective-permute-start(bf16[736,128]{1,0:T(8,128)(2,1)S(1)} %pair_low_sums.1.refs_4_.refs_2_), channel_id=1, source_target_pairs={{0,2},{1,3},{2,0},{3,1},{4,6},{5,7},{6,4},{7,5},{8,10},{9,11},{10,... | collective-permute-start | bytes 565256 | tf_op jit(solution)/shard_map/ppermute | solution.py:394
  24.2 3.4 %collective-permute-done.1.refs_1_ = bf16[112,2048]{1,0:T(8,128)(2,1)S(1)} collective-permute-done((bf16[112,2048]{1,0:T(8,128)(2,1)}, bf16[112,2048]{1,0:T(8,128)(2,1)S(1)}, u32[]{:S(2)}, u32[]{:S(2)}) %collective-permute-start.1) | collective-permute-done | bytes 458784 | tf_op jit(solution)/shard_map/ppermute | solution.py:394
  27.6 1.1 %down_block.3.refs_5_.refs_2_ = bf16[2,112,128]{2,1,0:T(8,128)(2,1)S(1)} custom-call(bf16[112,2048]{1,0:T(8,128)(2,1)S(1)} %collective-permute-done.refs_0_, bf16[112,2048]{1,0:T(8,128)(2,1)S(1)} %collective-permute-done.1.refs_1_, bf16[2048,1024]{1,0:T(8,128)(2,1)S(1)} %scaled_down.1.refs_2_, f32[8,128]{1,0:T(8,128)S(1)} %get-tuple-element.34.refs_4_.refs_3_, ...), custom_call_target="tpu_custom_call" | custom-call | flops 939524096 | bytes 4194304 | tf_op jit(solution)/shard_map/down_block/pallas_call | solution.py:28
  28.8 3.7 %collective-permute-start.5 = (bf16[2,112,128]{2,1,0:T(8,128)(2,1)S(1)}, bf16[2,112,128]{2,1,0:T(8,128)(2,1)S(1)}, u32[]{:S(2)}, u32[]{:S(2)}) collective-permute-start(bf16[2,112,128]{2,1,0:T(8,128)(2,1)S(1)} %down_block.3.refs_5_.refs_2_), channel_id=1, source_target_pairs={{0,3},{1,2},{2,1},{3,0},{4,7},{5,6},{6,5},{7,4},{8,11},{9,10},{10,... | collective-permute-start | bytes 172040 | tf_op jit(solution)/shard_map/ppermute | solution.py:394
  32.5 0.7 %collective-permute-start.7 = (bf16[2,112,128]{2,1,0:T(8,128)(2,1)S(1)}, bf16[2,112,128]{2,1,0:T(8,128)(2,1)S(1)}, u32[]{:S(2)}, u32[]{:S(2)}) collective-permute-start(bf16[2,112,128]{2,1,0:T(8,128)(2,1)S(1)} %down_block.3.refs_5_.refs_2_), channel_id=1, source_target_pairs={{0,1},{1,0},{2,3},{3,2},{4,5},{5,4},{6,7},{7,6},{8,9},{9,8},{10,11... | collective-permute-start | bytes 172040 | tf_op jit(solution)/shard_map/ppermute | solution.py:394
  33.2 0.6 %up_block.2 = (bf16[112,512]{1,0:T(8,128)(2,1)S(1)}, bf16[112,512]{1,0:T(8,128)(2,1)S(1)}) custom-call(bf16[112,2048]{1,0:T(8,128)(2,1)S(1)} %copy-done.2, bf16[112,2048]{1,0:T(8,128)(2,1)S(1)} %collective-permute-done.2.refs_1_, bf16[736,128]{1,0:T(8,128)(2,1)S(1)} %pair_low_sums.1.refs_4_.refs_2_, ...), custom_call_target="tpu_custom_call" | custom-call | flops 234881024 | bytes 1048576 | tf_op jit(solution)/shard_map/up_block/pallas_call | solution.py:28
  33.9 1.4 %collective-permute-start.11 = (bf16[256,512]{1,0:T(8,128)(2,1)S(1)}, bf16[256,512]{1,0:T(8,128)(2,1)S(1)}, u32[]{:S(2)}, u32[]{:S(2)}) collective-permute-start(bf16[256,512]{1,0:T(8,128)(2,1)S(1)} %get-tuple-element.46), channel_id=1, source_target_pairs={{0,1},{1,0},{2,3},{3,2},{4,5},{5,4},{6,7},{7,6},{8,9},{9,8},{10,11... | collective-permute-start | bytes 786440 | tf_op jit(solution)/shard_map/ppermute | solution.py:394
  35.3 0.5 %fusion = (f32[256,64]{1,0:T(8,128)S(1)}, f32[256,64]{1,0:T(8,128)S(1)}, f32[256,64]{1,0:T(8,128)S(1)}) fusion(f32[64]{0:T(128)S(1)} %multiply_exponential_fusion, f32[256]{0:T(256)S(1)} %convert_element_type.10), kind=kLoop, calls=%fused_computation.4 | loop fusion | flops 32768 | bytes 197888 | tf_op jit(solution)/shard_map/neg | solution.py:464
  35.8 3.0 %collective-permute-start.9 = (bf16[128,512]{1,0:T(8,128)(2,1)S(1)}, bf16[128,512]{1,0:T(8,128)(2,1)S(1)}, u32[]{:S(2)}, u32[]{:S(2)}) collective-permute-start(bf16[128,512]{1,0:T(8,128)(2,1)S(1)} %get-tuple-element.39.refs_7_), channel_id=1, source_target_pairs={{0,2},{1,3},{2,0},{3,1},{4,6},{5,7},{6,4},{7,5},{8,10},{9,11},{10,... | collective-permute-start | bytes 393224 | tf_op jit(solution)/shard_map/ppermute | solution.py:394
  38.8 0.6 %up_block.3 = (bf16[112,512]{1,0:T(8,128)(2,1)S(1)}, bf16[112,512]{1,0:T(8,128)(2,1)S(1)}, f32[8,128]{1,0:T(8,128)S(1)}) custom-call(bf16[112,2048]{1,0:T(8,128)(2,1)S(1)} %collective-permute-done.refs_0_, bf16[112,2048]{1,0:T(8,128)(2,1)S(1)} %collective-permute-done.1.refs_1_, bf16[2,112,128]{2,1,0:T(8,128)(2,1)S(1)} %down_block.3.refs_5_.refs_2_, ...), custom_call_target="tpu_custom_call" | custom-call | flops 234881024 | bytes 1048576 | tf_op jit(solution)/shard_map/up_block/pallas_call | solution.py:28
  39.4 1.6 %collective-permute-start.12 = (bf16[112,512]{1,0:T(8,128)(2,1)S(1)}, bf16[112,512]{1,0:T(8,128)(2,1)S(1)}, u32[]{:S(2)}, u32[]{:S(2)}) collective-permute-start(bf16[112,512]{1,0:T(8,128)(2,1)S(1)} %get-tuple-element.44.refs_8_), channel_id=1, source_target_pairs={{0,8},{4,12},{8,0},{12,4},{1,9},{5,13},{9,1},{13,5},{2,10},{6,14},... | collective-permute-start | bytes 344072 | tf_op jit(solution)/shard_map/ppermute | solution.py:394
  41.5 3.6 %collective-permute-done.9.refs_3_ = bf16[128,512]{1,0:T(8,128)(2,1)S(1)} collective-permute-done((bf16[128,512]{1,0:T(8,128)(2,1)S(1)}, bf16[128,512]{1,0:T(8,128)(2,1)S(1)}, u32[]{:S(2)}, u32[]{:S(2)}) %collective-permute-start.9) | collective-permute-done | bytes 131104 | tf_op jit(solution)/shard_map/ppermute | solution.py:394
  45.5 1.7 %collective-permute-done.13.refs_6_ = bf16[112,512]{1,0:T(8,128)(2,1)S(1)} collective-permute-done((bf16[112,512]{1,0:T(8,128)(2,1)S(1)}, bf16[112,512]{1,0:T(8,128)(2,1)S(1)}, u32[]{:S(2)}, u32[]{:S(2)}) %collective-permute-start.13) | collective-permute-done | bytes 114720 | tf_op jit(solution)/shard_map/ppermute | solution.py:394
  47.1 1.0 %finish.1 = bf16[256,512]{1,0:T(8,128)(2,1)} custom-call(f32[256,512]{1,0:T(8,128)S(1)} %get-tuple-element.45.refs_0_, bf16[256,512]{1,0:T(8,128)(2,1)S(1)} %collective-permute-done.11.refs_1_, f32[256,128]{1,0:T(8,128)S(1)} %get-tuple-element.47.refs_2_, f32[256,128]{1,0:T(8,128)S(1)} %get-tuple-element.54.refs_3_, ...), custom_call_target="tpu_custom_call" | custom-call | flops 33554432 | tf_op jit(solution)/shard_map/finish/pallas_call | solution.py:28
  (36 shorter events, 1.5 us)
Async XLA Ops:
  3.6 11.6 %collective-permute-start.2 = (bf16[112,2048]{1,0:T(8,128)(2,1)}, bf16[112,2048]{1,0:T(8,128)(2,1)S(1)}, u32[]{:S(2)}, u32[]{:S(2)}) collective-permute-start(bf16[112,2048]{1,0:T(8,128)(2,1)} %get-tuple-element.33), channel_id=1, source_target_pairs={{0,4},{4,0},{8,12},{12,8},{1,5},{5,1},{9,13},{13,9},{2,6},{6,2},{1... | collective-permute-start | bytes 1376264 | tf_op jit(solution)/shard_map/ppermute | solution.py:394
  4.2 20.0 %collective-permute-start = (bf16[112,2048]{1,0:T(8,128)(2,1)}, bf16[112,2048]{1,0:T(8,128)(2,1)S(1)}, u32[]{:S(2)}, u32[]{:S(2)}) collective-permute-start(bf16[112,2048]{1,0:T(8,128)(2,1)} %get-tuple-element.28), channel_id=1, source_target_pairs={{0,8},{4,12},{8,0},{12,4},{1,9},{5,13},{9,1},{13,5},{2,10},{6,14},... | collective-permute-start | bytes 1376264 | tf_op jit(solution)/shard_map/ppermute | solution.py:394
  6.7 20.9 %collective-permute-start.1 = (bf16[112,2048]{1,0:T(8,128)(2,1)}, bf16[112,2048]{1,0:T(8,128)(2,1)S(1)}, u32[]{:S(2)}, u32[]{:S(2)}) collective-permute-start(bf16[112,2048]{1,0:T(8,128)(2,1)} %get-tuple-element.29), channel_id=1, source_target_pairs={{0,12},{4,8},{8,4},{12,0},{1,13},{5,9},{9,5},{13,1},{2,14},{6,10},... | collective-permute-start | bytes 1376264 | tf_op jit(solution)/shard_map/ppermute | solution.py:394
  6.8 6.5 %copy-start = (bf16[8,2048,128]{2,1,0:T(8,128)(2,1)S(1)}, bf16[8,2048,128]{2,1,0:T(8,128)(2,1)}, u32[]{:S(2)}) copy-start(bf16[8,2048,128]{2,1,0:T(8,128)(2,1)} %refs_1_.6) | copy-start | bytes 12582916
  6.8 6.5 %copy-start.4 = (bf16[2048]{0:T(1024)(128)(2,1)S(1)}, bf16[2048]{0:T(1024)(128)(2,1)}, u32[]{:S(2)}) copy-start(bf16[2048]{0:T(1024)(128)(2,1)} %param.9) | copy-start | bytes 12292
  11.4 9.2 %collective-permute-start.4 = (bf16[256,512]{1,0:T(8,128)(2,1)S(1)}, bf16[256,512]{1,0:T(8,128)(2,1)S(1)}, u32[]{:S(2)}, u32[]{:S(2)}) collective-permute-start(bf16[256,512]{1,0:T(8,128)(2,1)S(1)} %get-tuple-element.36), channel_id=1, source_target_pairs={{0,1},{1,0},{2,3},{3,2},{4,5},{5,4},{6,7},{7,6},{8,9},{9,8},{10,11... | collective-permute-start | bytes 786440 | tf_op jit(solution)/shard_map/ppermute | solution.py:394
  13.3 2.0 %copy-start.2 = (bf16[112,2048]{1,0:T(8,128)(2,1)S(1)}, bf16[112,2048]{1,0:T(8,128)(2,1)}, u32[]{:S(2)}) copy-start(bf16[112,2048]{1,0:T(8,128)(2,1)} %get-tuple-element.32.refs_0_) | copy-start | bytes 1376260
  15.2 1.6 %copy-start.7 = (s32[256]{0:T(256)S(1)}, s32[256]{0:T(256)}, u32[]{:S(2)}) copy-start(s32[256]{0:T(256)} %param.15) | copy-start | bytes 3076
  15.2 1.6 %copy-start.3 = (bf16[256,2048]{1,0:T(8,128)(2,1)S(1)}, bf16[256,2048]{1,0:T(8,128)(2,1)}, u32[]{:S(2)}) copy-start(bf16[256,2048]{1,0:T(8,128)(2,1)} %refs_2_.3) | copy-start | bytes 3145732
  15.3 1.6 %copy-start.5 = (s32[256]{0:T(256)S(1)}, s32[256]{0:T(256)}, u32[]{:S(2)}) copy-start(s32[256]{0:T(256)} %param.13) | copy-start | bytes 3076
  15.3 1.6 %copy-start.6 = (s32[32]{0:T(128)S(1)}, s32[32]{0:T(128)}, u32[]{:S(2)}) copy-start(s32[32]{0:T(128)} %refs_1_.7) | copy-start | bytes 388
  16.4 16.8 %copy-start.1 = (bf16[8,64,512]{2,1,0:T(8,128)(2,1)S(1)}, bf16[8,64,512]{2,1,0:T(8,128)(2,1)}, u32[]{:S(2)}) copy-start(bf16[8,64,512]{2,1,0:T(8,128)(2,1)} %refs_6_.1) | copy-start | bytes 1572868
  16.5 4.8 %collective-permute-start.3 = (bf16[2,112,128]{2,1,0:T(8,128)(2,1)S(1)}, bf16[2,112,128]{2,1,0:T(8,128)(2,1)S(1)}, u32[]{:S(2)}, u32[]{:S(2)}) collective-permute-start(bf16[2,112,128]{2,1,0:T(8,128)(2,1)S(1)} %down_block.2.refs_3_.refs_0_), channel_id=1, source_target_pairs={{0,1},{1,0},{2,3},{3,2},{4,5},{5,4},{6,7},{7,6},{8,9},{9,8},{10,11... | collective-permute-start | bytes 172040 | tf_op jit(solution)/shard_map/ppermute | solution.py:394
  21.3 11.9 %collective-permute-start.8 = (bf16[736,128]{1,0:T(8,128)(2,1)S(1)}, bf16[736,128]{1,0:T(8,128)(2,1)S(1)}, u32[]{:S(2)}, u32[]{:S(2)}) collective-permute-start(bf16[736,128]{1,0:T(8,128)(2,1)S(1)} %pair_low_sums.1.refs_4_.refs_2_), channel_id=1, source_target_pairs={{0,2},{1,3},{2,0},{3,1},{4,6},{5,7},{6,4},{7,5},{8,10},{9,11},{10,... | collective-permute-start | bytes 565256 | tf_op jit(solution)/shard_map/ppermute | solution.py:394
  28.8 10.0 %collective-permute-start.5 = (bf16[2,112,128]{2,1,0:T(8,128)(2,1)S(1)}, bf16[2,112,128]{2,1,0:T(8,128)(2,1)S(1)}, u32[]{:S(2)}, u32[]{:S(2)}) collective-permute-start(bf16[2,112,128]{2,1,0:T(8,128)(2,1)S(1)} %down_block.3.refs_5_.refs_2_), channel_id=1, source_target_pairs={{0,3},{1,2},{2,1},{3,0},{4,7},{5,6},{6,5},{7,4},{8,11},{9,10},{10,... | collective-permute-start | bytes 172040 | tf_op jit(solution)/shard_map/ppermute | solution.py:394
  32.5 6.3 %collective-permute-start.6 = (bf16[2,112,128]{2,1,0:T(8,128)(2,1)S(1)}, bf16[2,112,128]{2,1,0:T(8,128)(2,1)S(1)}, u32[]{:S(2)}, u32[]{:S(2)}) collective-permute-start(bf16[2,112,128]{2,1,0:T(8,128)(2,1)S(1)} %down_block.3.refs_5_.refs_2_), channel_id=1, source_target_pairs={{0,2},{1,3},{2,0},{3,1},{4,6},{5,7},{6,4},{7,5},{8,10},{9,11},{10,... | collective-permute-start | bytes 172040 | tf_op jit(solution)/shard_map/ppermute | solution.py:394
  32.5 6.3 %collective-permute-start.7 = (bf16[2,112,128]{2,1,0:T(8,128)(2,1)S(1)}, bf16[2,112,128]{2,1,0:T(8,128)(2,1)S(1)}, u32[]{:S(2)}, u32[]{:S(2)}) collective-permute-start(bf16[2,112,128]{2,1,0:T(8,128)(2,1)S(1)} %down_block.3.refs_5_.refs_2_), channel_id=1, source_target_pairs={{0,1},{1,0},{2,3},{3,2},{4,5},{5,4},{6,7},{7,6},{8,9},{9,8},{10,11... | collective-permute-start | bytes 172040 | tf_op jit(solution)/shard_map/ppermute | solution.py:394
  33.9 13.2 %collective-permute-start.11 = (bf16[256,512]{1,0:T(8,128)(2,1)S(1)}, bf16[256,512]{1,0:T(8,128)(2,1)S(1)}, u32[]{:S(2)}, u32[]{:S(2)}) collective-permute-start(bf16[256,512]{1,0:T(8,128)(2,1)S(1)} %get-tuple-element.46), channel_id=1, source_target_pairs={{0,1},{1,0},{2,3},{3,2},{4,5},{5,4},{6,7},{7,6},{8,9},{9,8},{10,11... | collective-permute-start | bytes 786440 | tf_op jit(solution)/shard_map/ppermute | solution.py:394
  35.8 9.2 %collective-permute-start.9 = (bf16[128,512]{1,0:T(8,128)(2,1)S(1)}, bf16[128,512]{1,0:T(8,128)(2,1)S(1)}, u32[]{:S(2)}, u32[]{:S(2)}) collective-permute-start(bf16[128,512]{1,0:T(8,128)(2,1)S(1)} %get-tuple-element.39.refs_7_), channel_id=1, source_target_pairs={{0,2},{1,3},{2,0},{3,1},{4,6},{5,7},{6,4},{7,5},{8,10},{9,11},{10,... | collective-permute-start | bytes 393224 | tf_op jit(solution)/shard_map/ppermute | solution.py:394
  38.8 2.7 %collective-permute-start.10 = (bf16[112,512]{1,0:T(8,128)(2,1)S(1)}, bf16[112,512]{1,0:T(8,128)(2,1)S(1)}, u32[]{:S(2)}, u32[]{:S(2)}) collective-permute-start(bf16[112,512]{1,0:T(8,128)(2,1)S(1)} %get-tuple-element.41), channel_id=1, source_target_pairs={{0,4},{4,0},{8,12},{12,8},{1,5},{5,1},{9,13},{13,9},{2,6},{6,2},{1... | collective-permute-start | bytes 344072 | tf_op jit(solution)/shard_map/ppermute | solution.py:394
  39.4 6.0 %collective-permute-start.12 = (bf16[112,512]{1,0:T(8,128)(2,1)S(1)}, bf16[112,512]{1,0:T(8,128)(2,1)S(1)}, u32[]{:S(2)}, u32[]{:S(2)}) collective-permute-start(bf16[112,512]{1,0:T(8,128)(2,1)S(1)} %get-tuple-element.44.refs_8_), channel_id=1, source_target_pairs={{0,8},{4,12},{8,0},{12,4},{1,9},{5,13},{9,1},{13,5},{2,10},{6,14},... | collective-permute-start | bytes 344072 | tf_op jit(solution)/shard_map/ppermute | solution.py:394
  41.0 6.1 %collective-permute-start.13 = (bf16[112,512]{1,0:T(8,128)(2,1)S(1)}, bf16[112,512]{1,0:T(8,128)(2,1)S(1)}, u32[]{:S(2)}, u32[]{:S(2)}) collective-permute-start(bf16[112,512]{1,0:T(8,128)(2,1)S(1)} %get-tuple-element.48), channel_id=1, source_target_pairs={{0,12},{4,8},{8,4},{12,0},{1,13},{5,9},{9,5},{13,1},{2,14},{6,10},... | collective-permute-start | bytes 344072 | tf_op jit(solution)/shard_map/ppermute | solution.py:394

commit v12 on v11

--- a/solution.py
+++ b/solution.py
@@ -152,10 +152,9 @@
         out_ref[...] = (refs[j][rows] + refs[count + j][rows].astype(F32)).astype(BF16)
 
 
-def pair_low_kernel(count, low_ref, other_ref, *refs):
+def pair_low_kernel(count, half, low_ref, other_ref, *refs):
     outs = refs[2 * count :]
     cols = refs[0].shape[1]
-    half = refs[0].shape[0] // 2
     for j in range(count):
         total = (refs[j][:half] + refs[count + j][:half].astype(F32)).astype(BF16)
         for h in range(cols // HEAD):
@@ -320,7 +319,7 @@
     return jnp.dot(lhs, jnp.concatenate(blocks, axis=0), preferred_element_type=F32)
 
 
-def gather_kernel(n_pairs, count, sq_ref, base_ref, *refs):
+def gather_kernel(n_pairs, count, half, sq_ref, base_ref, *refs):
     tops, bottoms = refs[:n_pairs], refs[n_pairs : 2 * n_pairs]
     deltas = refs[2 * n_pairs : 2 * n_pairs + count]
     sels = refs[2 * n_pairs + count : 2 * n_pairs + 2 * count]
@@ -337,7 +336,6 @@
     scale = lax.rsqrt(square * (1.0 / MODEL_WIDTH) + EPSILON)
     scale_ref[...] = jnp.broadcast_to(scale, (rows, HEAD))
     total = base_ref[...] + placed(sels, deltas)
-    half = rows // 2
     lower = total[half:]
     for bottom in bottoms:
         lower = lower + bottom[...].astype(F32)
@@ -503,11 +501,11 @@
         flops=2 * rows * rows * depth,
         moved=2 * rows * depth,
     )
-    half = rows // 2
+    half = rows * 3 // 128 * 16
     upper = cols // HEAD * half
     other = over("tensor", low, 1)
     pairs = call(
-        functools.partial(pair_low_kernel, len(twos)),
+        functools.partial(pair_low_kernel, len(twos), half),
         "pair_low_sums",
         [shape((upper + len(first) * height, HEAD), BF16)]
         + [shape((upper, HEAD), BF16)] * (len(twos) - 1),
@@ -532,7 +530,7 @@
     *pairs, near = call(
         functools.partial(pair_kernel, len(twos), half),
         "pair_sums",
-        [shape((half, cols), BF16)] * len(twos) + [shape((rows, cols), BF16)],
+        [shape((rows - half, cols), BF16)] * len(twos) + [shape((rows, cols), BF16)],
         vmem=(near, *own, *beside),
         after=(ups[0],),
     )
@@ -541,7 +539,7 @@
     *ups, square = up_block(last, last_parts, True, (pairs[0],))
     last_deltas = [over("wide", u, k) for k, u in zip(last, ups)]
     total, scale = call(
-        functools.partial(gather_kernel, len(bottoms), len(first)),
+        functools.partial(gather_kernel, len(tops), len(first), half),
         "gather",
         [shape((rows, cols), F32), shape((rows, HEAD), F32)],
         vmem=(square, base, *tops, *bottoms, *deltas, *[sels[k] for k in first]),

time: 48.3 us -> 48.3 us (level)
  no operation moved by 1% of the time
where the time goes in v12:
time: 48.3 us; the launch traced here: 48.2 us
  starting transfers between devices  19 us (39%)
  Pallas kernels  16.1 us (33%)
  waiting for transfers between devices  12.2 us (25%)
  other arithmetic  0.67 us (1%)
    ppermute x14, starting transfers between devices, over(): return lax.ppermute(array, axis, [(i, i ^ k) for i in range(size)])  19 us
    pallas_call x12, Pallas kernels, call(): pl.pallas_call(body, out_shape=outs, in_specs=[pl.BlockSpec(memory_space=...  16.1 us
    ppermute x14, waiting for transfers between devices, over(): return lax.ppermute(array, axis, [(i, i ^ k) for i in range(size)])  12.2 us
  transfers between devices with their start and end apart: 14, of which 6 were waited for; matrix products, arithmetic and copies ran while one was open for 1% of the time, Pallas kernels for 24%

profile of v12, /device:TPU:0, one launch (start us, length us, event | category | flops | bytes accessed | tf_op | source)
XLA Modules:
  0.0 48.2 jit_solution(17241594598978751622)
XLA Ops:
  0.0 3.6 %dispatch.1 = (bf16[112,2048]{1,0:T(8,128)(2,1)}, bf16[112,2048]{1,0:T(8,128)(2,1)}, bf16[112,2048]{1,0:T(8,128)(2,1)}, bf16[112,2048]{1,0:T(8,128)(2,1)}, bf16[256,2048]{1,0:T(8,128)(2,1)}) custom-call(s32[1,256]{1,0:T(1,128)} %bitcast.4, s32[32]{0:T(128)} %refs_1_.7, bf16[256,2048]{1,0:T(8,128)(2,1)} %refs_2_.3, bf16[16,128]{1,0:T(8,128)(2,1)} %bitcast.2), custom_call_target="tpu_custom_call" | custom-call | flops 469762048 | bytes 4194304 | tf_op jit(solution)/shard_map/dispatch/pallas_call | solution.py:28
  3.6 0.5 %collective-permute-start.2 = (bf16[112,2048]{1,0:T(8,128)(2,1)}, bf16[112,2048]{1,0:T(8,128)(2,1)S(1)}, u32[]{:S(2)}, u32[]{:S(2)}) collective-permute-start(bf16[112,2048]{1,0:T(8,128)(2,1)} %get-tuple-element.33), channel_id=1, source_target_pairs={{0,4},{4,0},{8,12},{12,8},{1,5},{5,1},{9,13},{13,9},{2,6},{6,2},{1... | collective-permute-start | bytes 1376264 | tf_op jit(solution)/shard_map/ppermute | solution.py:392
  4.2 2.6 %collective-permute-start = (bf16[112,2048]{1,0:T(8,128)(2,1)}, bf16[112,2048]{1,0:T(8,128)(2,1)S(1)}, u32[]{:S(2)}, u32[]{:S(2)}) collective-permute-start(bf16[112,2048]{1,0:T(8,128)(2,1)} %get-tuple-element.28), channel_id=1, source_target_pairs={{0,8},{4,12},{8,0},{12,4},{1,9},{5,13},{9,1},{13,5},{2,10},{6,14},... | collective-permute-start | bytes 1376264 | tf_op jit(solution)/shard_map/ppermute | solution.py:392
  6.8 4.6 %base.1 = (bf16[256,512]{1,0:T(8,128)(2,1)S(1)}, bf16[256,512]{1,0:T(8,128)(2,1)S(1)}, f32[256,512]{1,0:T(8,128)S(1)}, f32[256,512]{1,0:T(8,128)S(1)}) custom-call(bf16[256,2048]{1,0:T(8,128)(2,1)} %get-tuple-element.30.refs_0_, bf16[2048,2048]{1,0:T(8,128)(2,1)} %refs_1_.5), custom_call_target="tpu_custom_call" | custom-call | flops 2147483648 | bytes 8388608 | tf_op jit(solution)/shard_map/base/pallas_call | solution.py:28
  11.4 1.9 %collective-permute-start.4 = (bf16[256,512]{1,0:T(8,128)(2,1)S(1)}, bf16[256,512]{1,0:T(8,128)(2,1)S(1)}, u32[]{:S(2)}, u32[]{:S(2)}) collective-permute-start(bf16[256,512]{1,0:T(8,128)(2,1)S(1)} %get-tuple-element.36), channel_id=1, source_target_pairs={{0,1},{1,0},{2,3},{3,2},{4,5},{5,4},{6,7},{7,6},{8,9},{9,8},{10,11... | collective-permute-start | bytes 786440 | tf_op jit(solution)/shard_map/ppermute | solution.py:392
  13.3 2.0 %scaled_down.1.refs_2_ = bf16[2048,1024]{1,0:T(8,128)(2,1)S(1)} custom-call(bf16[16,128]{1,0:T(8,128)(2,1)S(1)} %bitcast.3, bf16[8,2048,128]{2,1,0:T(8,128)(2,1)S(1)} %copy-done, f32[256,512]{1,0:T(8,128)S(1)} %get-tuple-element.31.refs_2_.refs_1_), custom_call_target="tpu_custom_call" | custom-call | flops 8388608 | bytes 8388608 | tf_op jit(solution)/shard_map/scaled_down/pallas_call | solution.py:28
  15.3 1.1 %down_block.2.refs_3_.refs_0_ = bf16[2,112,128]{2,1,0:T(8,128)(2,1)S(1)} custom-call(bf16[112,2048]{1,0:T(8,128)(2,1)S(1)} %copy-done.2, bf16[112,2048]{1,0:T(8,128)(2,1)S(1)} %collective-permute-done.2.refs_1_, bf16[2048,1024]{1,0:T(8,128)(2,1)S(1)} %scaled_down.1.refs_2_), custom_call_target="tpu_custom_call" | custom-call | flops 939524096 | bytes 4194304 | tf_op jit(solution)/shard_map/down_block/pallas_call | solution.py:28
  16.9 1.1 %aux.1 = (f32[8,128]{1,0:T(8,128)S(1)}, bf16[256,128]{1,0:T(8,128)(2,1)S(1)}, bf16[256,128]{1,0:T(8,128)(2,1)S(1)}, bf16[256,128]{1,0:T(8,128)(2,1)S(1)}, bf16[256,128]{1,0:T(8,128)(2,1)S(1)}) custom-call(s32[1,256]{1,0:T(1,128)S(1)} %bitcast.5, s32[32]{0:T(128)S(1)} %copy-done.6, bf16[256,2048]{1,0:T(8,128)(2,1)S(1)} %copy-done.3, ...), custom_call_target="tpu_custom_call" | custom-call | flops 268435456 | bytes 1048576 | tf_op jit(solution)/shard_map/aux/pallas_call | solution.py:28
  17.9 2.6 %collective-permute-done.4.refs_3_.refs_2_ = bf16[256,512]{1,0:T(8,128)(2,1)S(1)} collective-permute-done((bf16[256,512]{1,0:T(8,128)(2,1)S(1)}, bf16[256,512]{1,0:T(8,128)(2,1)S(1)}, u32[]{:S(2)}, u32[]{:S(2)}) %collective-permute-start.4) | collective-permute-done | bytes 262176 | tf_op jit(solution)/shard_map/ppermute | solution.py:392
  20.6 0.7 %collective-permute-done.3.refs_1_ = bf16[2,112,128]{2,1,0:T(8,128)(2,1)S(1)} collective-permute-done((bf16[2,112,128]{2,1,0:T(8,128)(2,1)S(1)}, bf16[2,112,128]{2,1,0:T(8,128)(2,1)S(1)}, u32[]{:S(2)}, u32[]{:S(2)}) %collective-permute-start.3) | collective-permute-done | bytes 57376 | tf_op jit(solution)/shard_map/ppermute | solution.py:392
  21.3 2.8 %collective-permute-start.8 = (bf16[608,128]{1,0:T(8,128)(2,1)S(1)}, bf16[608,128]{1,0:T(8,128)(2,1)S(1)}, u32[]{:S(2)}, u32[]{:S(2)}) collective-permute-start(bf16[608,128]{1,0:T(8,128)(2,1)S(1)} %pair_low_sums.1.refs_4_.refs_2_), channel_id=1, source_target_pairs={{0,2},{1,3},{2,0},{3,1},{4,6},{5,7},{6,4},{7,5},{8,10},{9,11},{10,... | collective-permute-start | bytes 466952 | tf_op jit(solution)/shard_map/ppermute | solution.py:392
  24.2 3.4 %collective-permute-done.1.refs_1_ = bf16[112,2048]{1,0:T(8,128)(2,1)S(1)} collective-permute-done((bf16[112,2048]{1,0:T(8,128)(2,1)}, bf16[112,2048]{1,0:T(8,128)(2,1)S(1)}, u32[]{:S(2)}, u32[]{:S(2)}) %collective-permute-start.1) | collective-permute-done | bytes 458784 | tf_op jit(solution)/shard_map/ppermute | solution.py:392
  27.6 1.1 %down_block.3.refs_5_.refs_2_ = bf16[2,112,128]{2,1,0:T(8,128)(2,1)S(1)} custom-call(bf16[112,2048]{1,0:T(8,128)(2,1)S(1)} %collective-permute-done.refs_0_, bf16[112,2048]{1,0:T(8,128)(2,1)S(1)} %collective-permute-done.1.refs_1_, bf16[2048,1024]{1,0:T(8,128)(2,1)S(1)} %scaled_down.1.refs_2_, f32[8,128]{1,0:T(8,128)S(1)} %get-tuple-element.34.refs_4_.refs_3_, ...), custom_call_target="tpu_custom_call" | custom-call | flops 939524096 | bytes 4194304 | tf_op jit(solution)/shard_map/down_block/pallas_call | solution.py:28
  28.8 3.7 %collective-permute-start.5 = (bf16[2,112,128]{2,1,0:T(8,128)(2,1)S(1)}, bf16[2,112,128]{2,1,0:T(8,128)(2,1)S(1)}, u32[]{:S(2)}, u32[]{:S(2)}) collective-permute-start(bf16[2,112,128]{2,1,0:T(8,128)(2,1)S(1)} %down_block.3.refs_5_.refs_2_), channel_id=1, source_target_pairs={{0,3},{1,2},{2,1},{3,0},{4,7},{5,6},{6,5},{7,4},{8,11},{9,10},{10,... | collective-permute-start | bytes 172040 | tf_op jit(solution)/shard_map/ppermute | solution.py:392
  32.5 0.7 %collective-permute-start.7 = (bf16[2,112,128]{2,1,0:T(8,128)(2,1)S(1)}, bf16[2,112,128]{2,1,0:T(8,128)(2,1)S(1)}, u32[]{:S(2)}, u32[]{:S(2)}) collective-permute-start(bf16[2,112,128]{2,1,0:T(8,128)(2,1)S(1)} %down_block.3.refs_5_.refs_2_), channel_id=1, source_target_pairs={{0,1},{1,0},{2,3},{3,2},{4,5},{5,4},{6,7},{7,6},{8,9},{9,8},{10,11... | collective-permute-start | bytes 172040 | tf_op jit(solution)/shard_map/ppermute | solution.py:392
  33.2 0.6 %up_block.2 = (bf16[112,512]{1,0:T(8,128)(2,1)S(1)}, bf16[112,512]{1,0:T(8,128)(2,1)S(1)}) custom-call(bf16[112,2048]{1,0:T(8,128)(2,1)S(1)} %copy-done.2, bf16[112,2048]{1,0:T(8,128)(2,1)S(1)} %collective-permute-done.2.refs_1_, bf16[608,128]{1,0:T(8,128)(2,1)S(1)} %pair_low_sums.1.refs_4_.refs_2_, ...), custom_call_target="tpu_custom_call" | custom-call | flops 234881024 | bytes 1048576 | tf_op jit(solution)/shard_map/up_block/pallas_call | solution.py:28
  33.9 2.3 %collective-permute-start.9 = (bf16[160,512]{1,0:T(8,128)(2,1)S(1)}, bf16[160,512]{1,0:T(8,128)(2,1)S(1)}, u32[]{:S(2)}, u32[]{:S(2)}) collective-permute-start(bf16[160,512]{1,0:T(8,128)(2,1)S(1)} %get-tuple-element.39.refs_7_), channel_id=1, source_target_pairs={{0,2},{1,3},{2,0},{3,1},{4,6},{5,7},{6,4},{7,5},{8,10},{9,11},{10,... | collective-permute-start | bytes 491528 | tf_op jit(solution)/shard_map/ppermute | solution.py:392
  36.2 2.0 %collective-permute-start.11 = (bf16[256,512]{1,0:T(8,128)(2,1)S(1)}, bf16[256,512]{1,0:T(8,128)(2,1)S(1)}, u32[]{:S(2)}, u32[]{:S(2)}) collective-permute-start(bf16[256,512]{1,0:T(8,128)(2,1)S(1)} %get-tuple-element.46), channel_id=1, source_target_pairs={{0,1},{1,0},{2,3},{3,2},{4,5},{5,4},{6,7},{7,6},{8,9},{9,8},{10,11... | collective-permute-start | bytes 786440 | tf_op jit(solution)/shard_map/ppermute | solution.py:392
  38.2 0.5 %fusion = (f32[256,64]{1,0:T(8,128)S(1)}, f32[256,64]{1,0:T(8,128)S(1)}, f32[256,64]{1,0:T(8,128)S(1)}) fusion(f32[64]{0:T(128)S(1)} %multiply_exponential_fusion, f32[256]{0:T(256)S(1)} %convert_element_type.10), kind=kLoop, calls=%fused_computation.4 | loop fusion | flops 32768 | bytes 197888 | tf_op jit(solution)/shard_map/neg | solution.py:462
  38.9 0.6 %up_block.3 = (bf16[112,512]{1,0:T(8,128)(2,1)S(1)}, bf16[112,512]{1,0:T(8,128)(2,1)S(1)}, f32[8,128]{1,0:T(8,128)S(1)}) custom-call(bf16[112,2048]{1,0:T(8,128)(2,1)S(1)} %collective-permute-done.refs_0_, bf16[112,2048]{1,0:T(8,128)(2,1)S(1)} %collective-permute-done.1.refs_1_, bf16[2,112,128]{2,1,0:T(8,128)(2,1)S(1)} %down_block.3.refs_5_.refs_2_, ...), custom_call_target="tpu_custom_call" | custom-call | flops 234881024 | bytes 1048576 | tf_op jit(solution)/shard_map/up_block/pallas_call | solution.py:28
  39.5 1.6 %collective-permute-start.12 = (bf16[112,512]{1,0:T(8,128)(2,1)S(1)}, bf16[112,512]{1,0:T(8,128)(2,1)S(1)}, u32[]{:S(2)}, u32[]{:S(2)}) collective-permute-start(bf16[112,512]{1,0:T(8,128)(2,1)S(1)} %get-tuple-element.44.refs_8_), channel_id=1, source_target_pairs={{0,8},{4,12},{8,0},{12,4},{1,9},{5,13},{9,1},{13,5},{2,10},{6,14},... | collective-permute-start | bytes 344072 | tf_op jit(solution)/shard_map/ppermute | solution.py:392
  41.5 3.5 %collective-permute-done.9.refs_3_ = bf16[160,512]{1,0:T(8,128)(2,1)S(1)} collective-permute-done((bf16[160,512]{1,0:T(8,128)(2,1)S(1)}, bf16[160,512]{1,0:T(8,128)(2,1)S(1)}, u32[]{:S(2)}, u32[]{:S(2)}) %collective-permute-start.9) | collective-permute-done | bytes 163872 | tf_op jit(solution)/shard_map/ppermute | solution.py:392
  45.5 1.7 %collective-permute-done.13.refs_6_ = bf16[112,512]{1,0:T(8,128)(2,1)S(1)} collective-permute-done((bf16[112,512]{1,0:T(8,128)(2,1)S(1)}, bf16[112,512]{1,0:T(8,128)(2,1)S(1)}, u32[]{:S(2)}, u32[]{:S(2)}) %collective-permute-start.13) | collective-permute-done | bytes 114720 | tf_op jit(solution)/shard_map/ppermute | solution.py:392
  47.2 1.0 %finish.1 = bf16[256,512]{1,0:T(8,128)(2,1)} custom-call(f32[256,512]{1,0:T(8,128)S(1)} %get-tuple-element.45.refs_0_, bf16[256,512]{1,0:T(8,128)(2,1)S(1)} %collective-permute-done.11.refs_1_, f32[256,128]{1,0:T(8,128)S(1)} %get-tuple-element.47.refs_2_, f32[256,128]{1,0:T(8,128)S(1)} %get-tuple-element.54.refs_3_, ...), custom_call_target="tpu_custom_call" | custom-call | flops 33554432 | tf_op jit(solution)/shard_map/finish/pallas_call | solution.py:28
  (36 shorter events, 1.7 us)
Async XLA Ops:
  3.6 11.6 %collective-permute-start.2 = (bf16[112,2048]{1,0:T(8,128)(2,1)}, bf16[112,2048]{1,0:T(8,128)(2,1)S(1)}, u32[]{:S(2)}, u32[]{:S(2)}) collective-permute-start(bf16[112,2048]{1,0:T(8,128)(2,1)} %get-tuple-element.33), channel_id=1, source_target_pairs={{0,4},{4,0},{8,12},{12,8},{1,5},{5,1},{9,13},{13,9},{2,6},{6,2},{1... | collective-permute-start | bytes 1376264 | tf_op jit(solution)/shard_map/ppermute | solution.py:392
  4.2 20.0 %collective-permute-start = (bf16[112,2048]{1,0:T(8,128)(2,1)}, bf16[112,2048]{1,0:T(8,128)(2,1)S(1)}, u32[]{:S(2)}, u32[]{:S(2)}) collective-permute-start(bf16[112,2048]{1,0:T(8,128)(2,1)} %get-tuple-element.28), channel_id=1, source_target_pairs={{0,8},{4,12},{8,0},{12,4},{1,9},{5,13},{9,1},{13,5},{2,10},{6,14},... | collective-permute-start | bytes 1376264 | tf_op jit(solution)/shard_map/ppermute | solution.py:392
  6.7 20.9 %collective-permute-start.1 = (bf16[112,2048]{1,0:T(8,128)(2,1)}, bf16[112,2048]{1,0:T(8,128)(2,1)S(1)}, u32[]{:S(2)}, u32[]{:S(2)}) collective-permute-start(bf16[112,2048]{1,0:T(8,128)(2,1)} %get-tuple-element.29), channel_id=1, source_target_pairs={{0,12},{4,8},{8,4},{12,0},{1,13},{5,9},{9,5},{13,1},{2,14},{6,10},... | collective-permute-start | bytes 1376264 | tf_op jit(solution)/shard_map/ppermute | solution.py:392
  6.8 6.5 %copy-start = (bf16[8,2048,128]{2,1,0:T(8,128)(2,1)S(1)}, bf16[8,2048,128]{2,1,0:T(8,128)(2,1)}, u32[]{:S(2)}) copy-start(bf16[8,2048,128]{2,1,0:T(8,128)(2,1)} %refs_1_.6) | copy-start | bytes 12582916
  6.8 6.5 %copy-start.4 = (bf16[2048]{0:T(1024)(128)(2,1)S(1)}, bf16[2048]{0:T(1024)(128)(2,1)}, u32[]{:S(2)}) copy-start(bf16[2048]{0:T(1024)(128)(2,1)} %param.9) | copy-start | bytes 12292
  11.4 9.2 %collective-permute-start.4 = (bf16[256,512]{1,0:T(8,128)(2,1)S(1)}, bf16[256,512]{1,0:T(8,128)(2,1)S(1)}, u32[]{:S(2)}, u32[]{:S(2)}) collective-permute-start(bf16[256,512]{1,0:T(8,128)(2,1)S(1)} %get-tuple-element.36), channel_id=1, source_target_pairs={{0,1},{1,0},{2,3},{3,2},{4,5},{5,4},{6,7},{7,6},{8,9},{9,8},{10,11... | collective-permute-start | bytes 786440 | tf_op jit(solution)/shard_map/ppermute | solution.py:392
  13.3 2.0 %copy-start.2 = (bf16[112,2048]{1,0:T(8,128)(2,1)S(1)}, bf16[112,2048]{1,0:T(8,128)(2,1)}, u32[]{:S(2)}) copy-start(bf16[112,2048]{1,0:T(8,128)(2,1)} %get-tuple-element.32.refs_0_) | copy-start | bytes 1376260
  15.2 1.6 %copy-start.7 = (s32[256]{0:T(256)S(1)}, s32[256]{0:T(256)}, u32[]{:S(2)}) copy-start(s32[256]{0:T(256)} %param.15) | copy-start | bytes 3076
  15.2 1.6 %copy-start.3 = (bf16[256,2048]{1,0:T(8,128)(2,1)S(1)}, bf16[256,2048]{1,0:T(8,128)(2,1)}, u32[]{:S(2)}) copy-start(bf16[256,2048]{1,0:T(8,128)(2,1)} %refs_2_.3) | copy-start | bytes 3145732
  15.3 1.6 %copy-start.5 = (s32[256]{0:T(256)S(1)}, s32[256]{0:T(256)}, u32[]{:S(2)}) copy-start(s32[256]{0:T(256)} %param.13) | copy-start | bytes 3076
  15.3 1.6 %copy-start.6 = (s32[32]{0:T(128)S(1)}, s32[32]{0:T(128)}, u32[]{:S(2)}) copy-start(s32[32]{0:T(128)} %refs_1_.7) | copy-start | bytes 388
  16.4 16.8 %copy-start.1 = (bf16[8,64,512]{2,1,0:T(8,128)(2,1)S(1)}, bf16[8,64,512]{2,1,0:T(8,128)(2,1)}, u32[]{:S(2)}) copy-start(bf16[8,64,512]{2,1,0:T(8,128)(2,1)} %refs_6_.1) | copy-start | bytes 1572868
  16.5 4.8 %collective-permute-start.3 = (bf16[2,112,128]{2,1,0:T(8,128)(2,1)S(1)}, bf16[2,112,128]{2,1,0:T(8,128)(2,1)S(1)}, u32[]{:S(2)}, u32[]{:S(2)}) collective-permute-start(bf16[2,112,128]{2,1,0:T(8,128)(2,1)S(1)} %down_block.2.refs_3_.refs_0_), channel_id=1, source_target_pairs={{0,1},{1,0},{2,3},{3,2},{4,5},{5,4},{6,7},{7,6},{8,9},{9,8},{10,11... | collective-permute-start | bytes 172040 | tf_op jit(solution)/shard_map/ppermute | solution.py:392
  21.3 11.9 %collective-permute-start.8 = (bf16[608,128]{1,0:T(8,128)(2,1)S(1)}, bf16[608,128]{1,0:T(8,128)(2,1)S(1)}, u32[]{:S(2)}, u32[]{:S(2)}) collective-permute-start(bf16[608,128]{1,0:T(8,128)(2,1)S(1)} %pair_low_sums.1.refs_4_.refs_2_), channel_id=1, source_target_pairs={{0,2},{1,3},{2,0},{3,1},{4,6},{5,7},{6,4},{7,5},{8,10},{9,11},{10,... | collective-permute-start | bytes 466952 | tf_op jit(solution)/shard_map/ppermute | solution.py:392
  28.8 10.0 %collective-permute-start.5 = (bf16[2,112,128]{2,1,0:T(8,128)(2,1)S(1)}, bf16[2,112,128]{2,1,0:T(8,128)(2,1)S(1)}, u32[]{:S(2)}, u32[]{:S(2)}) collective-permute-start(bf16[2,112,128]{2,1,0:T(8,128)(2,1)S(1)} %down_block.3.refs_5_.refs_2_), channel_id=1, source_target_pairs={{0,3},{1,2},{2,1},{3,0},{4,7},{5,6},{6,5},{7,4},{8,11},{9,10},{10,... | collective-permute-start | bytes 172040 | tf_op jit(solution)/shard_map/ppermute | solution.py:392
  32.5 6.3 %collective-permute-start.6 = (bf16[2,112,128]{2,1,0:T(8,128)(2,1)S(1)}, bf16[2,112,128]{2,1,0:T(8,128)(2,1)S(1)}, u32[]{:S(2)}, u32[]{:S(2)}) collective-permute-start(bf16[2,112,128]{2,1,0:T(8,128)(2,1)S(1)} %down_block.3.refs_5_.refs_2_), channel_id=1, source_target_pairs={{0,2},{1,3},{2,0},{3,1},{4,6},{5,7},{6,4},{7,5},{8,10},{9,11},{10,... | collective-permute-start | bytes 172040 | tf_op jit(solution)/shard_map/ppermute | solution.py:392
  32.5 6.3 %collective-permute-start.7 = (bf16[2,112,128]{2,1,0:T(8,128)(2,1)S(1)}, bf16[2,112,128]{2,1,0:T(8,128)(2,1)S(1)}, u32[]{:S(2)}, u32[]{:S(2)}) collective-permute-start(bf16[2,112,128]{2,1,0:T(8,128)(2,1)S(1)} %down_block.3.refs_5_.refs_2_), channel_id=1, source_target_pairs={{0,1},{1,0},{2,3},{3,2},{4,5},{5,4},{6,7},{7,6},{8,9},{9,8},{10,11... | collective-permute-start | bytes 172040 | tf_op jit(solution)/shard_map/ppermute | solution.py:392
  33.9 11.1 %collective-permute-start.9 = (bf16[160,512]{1,0:T(8,128)(2,1)S(1)}, bf16[160,512]{1,0:T(8,128)(2,1)S(1)}, u32[]{:S(2)}, u32[]{:S(2)}) collective-permute-start(bf16[160,512]{1,0:T(8,128)(2,1)S(1)} %get-tuple-element.39.refs_7_), channel_id=1, source_target_pairs={{0,2},{1,3},{2,0},{3,1},{4,6},{5,7},{6,4},{7,5},{8,10},{9,11},{10,... | collective-permute-start | bytes 491528 | tf_op jit(solution)/shard_map/ppermute | solution.py:392
  36.2 11.0 %collective-permute-start.11 = (bf16[256,512]{1,0:T(8,128)(2,1)S(1)}, bf16[256,512]{1,0:T(8,128)(2,1)S(1)}, u32[]{:S(2)}, u32[]{:S(2)}) collective-permute-start(bf16[256,512]{1,0:T(8,128)(2,1)S(1)} %get-tuple-element.46), channel_id=1, source_target_pairs={{0,1},{1,0},{2,3},{3,2},{4,5},{5,4},{6,7},{7,6},{8,9},{9,8},{10,11... | collective-permute-start | bytes 786440 | tf_op jit(solution)/shard_map/ppermute | solution.py:392
  38.8 2.8 %collective-permute-start.10 = (bf16[112,512]{1,0:T(8,128)(2,1)S(1)}, bf16[112,512]{1,0:T(8,128)(2,1)S(1)}, u32[]{:S(2)}, u32[]{:S(2)}) collective-permute-start(bf16[112,512]{1,0:T(8,128)(2,1)S(1)} %get-tuple-element.41), channel_id=1, source_target_pairs={{0,4},{4,0},{8,12},{12,8},{1,5},{5,1},{9,13},{13,9},{2,6},{6,2},{1... | collective-permute-start | bytes 344072 | tf_op jit(solution)/shard_map/ppermute | solution.py:392
  39.5 6.0 %collective-permute-start.12 = (bf16[112,512]{1,0:T(8,128)(2,1)S(1)}, bf16[112,512]{1,0:T(8,128)(2,1)S(1)}, u32[]{:S(2)}, u32[]{:S(2)}) collective-permute-start(bf16[112,512]{1,0:T(8,128)(2,1)S(1)} %get-tuple-element.44.refs_8_), channel_id=1, source_target_pairs={{0,8},{4,12},{8,0},{12,4},{1,9},{5,13},{9,1},{13,5},{2,10},{6,14},... | collective-permute-start | bytes 344072 | tf_op jit(solution)/shard_map/ppermute | solution.py:392
  41.0 6.1 %collective-permute-start.13 = (bf16[112,512]{1,0:T(8,128)(2,1)S(1)}, bf16[112,512]{1,0:T(8,128)(2,1)S(1)}, u32[]{:S(2)}, u32[]{:S(2)}) collective-permute-start(bf16[112,512]{1,0:T(8,128)(2,1)S(1)} %get-tuple-element.48), channel_id=1, source_target_pairs={{0,12},{4,8},{8,4},{12,0},{1,13},{5,9},{9,5},{13,1},{2,14},{6,10},... | collective-permute-start | bytes 344072 | tf_op jit(solution)/shard_map/ppermute | solution.py:392
